TPU v7x, 32 devices: a whole 2x2x4 slice. The times are simulated.
32 devices in a mesh: dev: 8 (over z, x), ta: 4 (over y, core).
Axes of the slice: x: 2, y: 2, z: 4, core: 2. Of those that a mesh axis runs over, the one named last changes fastest.
Arguments:
- tokens: bfloat16 [4096, 2048], P(('dev', 'ta')), may hold values from -6 to 6
- cotangent: bfloat16 [4096, 2048], P(('dev', 'ta')), may hold values from -6 to 6
- lengths: int32 [6], replicated, may hold values from 1 to 3970, 4096 in all
- pad_mask: int32 [4096], P(('dev', 'ta')), may hold values 0 or 1
- attn_gain: float32 [2048], replicated, may hold values from 0.5 to 1.5
- projection_weight: bfloat16 [2048, 4, 2048], P(('dev', 'ta')), may hold values from -0.125 to 0.125
- w_beta: bfloat16 [2048, 16], P(('dev', 'ta')), may hold values from -0.125 to 0.125
- beta_bias: float32 [16], replicated, may hold values from -5 to 0
- conv_weight: float32 [3, 4, 2048], replicated, may hold values from -3 to 3
- head_gain: float32 [128], replicated, may hold values from 0.5 to 1.5
- mlp_gain: float32 [2048], replicated, may hold values from 0.5 to 1.5
- w_gate: bfloat16 [2048, 5632], P(None, 'ta'), may hold values from -0.125 to 0.125
- w_up: bfloat16 [2048, 5632], P(None, 'ta'), may hold values from -0.125 to 0.125
- w_down: bfloat16 [5632, 2048], P('ta'), may hold values from -0.078125 to 0.078125
Outputs:
- block_out: bfloat16 [4096, 2048], P(('dev', 'ta'))
- grad_tokens: float32 [4096, 2048], P(('dev', 'ta'))
- grad_attn_gain: float32 [2048], replicated
- gradient_projection_weight: float32 [2048, 4, 2048], P(('dev', 'ta'))
- grad_w_beta: float32 [2048, 16], P(('dev', 'ta'))
- grad_beta_bias: float32 [16], replicated
- grad_conv: float32 [3, 4, 2048], replicated
- grad_head_gain: float32 [128], replicated
- grad_mlp_gain: float32 [2048], replicated
- grad_w_gate: float32 [2048, 5632], P(None, 'ta')
- grad_w_up: float32 [2048, 5632], P(None, 'ta')
- grad_w_down: float32 [5632, 2048], P('ta')
Inputs may be any that keep to these rules, and one draw needn't show every extreme that they name: 6 documents lie end to end in this order from position 0; their lengths sum to 4096.
All inputs are finite; a program needn't handle non-finite values. No bound on the sum of `pad_mask` on one device may be relied on, other than what follows from the above.
Results may differ from a plain program's by a relative error of at most 0.024.
Values may be sent and summed in bfloat16 or wider, within the bound.
No kernel may reach another device: no remote copies, remote signals or barrier semaphores. Data moves between devices by JAX's collectives and lax.ppermute only.
A program may use at most 640 MiB of HBM per device.

v0:
```python
import jax
import jax.numpy as jnp
from jax import lax
from jax.sharding import PartitionSpec as P

SPAN = 64


HIGHEST_ACCURACY = lax.Precision.HIGHEST
NORM_EPS = 1e-06
HEAD_EPS = 1e-05
UNIT_EPS = 1e-06


def passed_along(block, axis, distance):
    devices = range(lax.axis_size(axis))
    route = [(i - distance, i) for i in devices if i - distance in devices]
    return lax.ppermute(block, axis, route)


def entering(value, axis, join, neutral):
    place = lax.axis_index(axis)
    gathered = jax.tree.map(
        lambda a, kind: lax.all_gather(a.astype(kind), axis), value, (jnp.bfloat16, jnp.bfloat16)
    )
    state = jax.tree.map(lambda a, e: jnp.zeros_like(a) + jnp.asarray(e, a.dtype), value, neutral)

    def one(turn, state):
        return join(
            state,
            jax.tree.map(
                lambda a, own: lax.dynamic_index_in_dim(a, turn, 0, False).astype(own.dtype),
                gathered,
                value,
            ),
        )

    return lax.fori_loop(0, place, one, state)


def prefix(value, axis, combine, identity):
    devices, place = (lax.axis_size(axis), lax.axis_index(axis))
    everything = jax.tree.map(
        lambda part, kind: lax.all_gather(part.astype(kind), axis),
        value,
        jax.tree.map(lambda a: jnp.bfloat16 if a.dtype == jnp.float32 else a.dtype, value),
    )
    start = jax.tree.map(
        lambda part, zero: jnp.broadcast_to(jnp.asarray(zero, part.dtype), part.shape),
        value,
        identity,
    )

    def turn(k, before):
        at = devices - 1 - k
        reached = at > place
        new = combine(
            before, jax.tree.map(lambda part, own: part[at].astype(own.dtype), everything, value)
        )
        return jax.tree.map(lambda a, b: jnp.where(reached, a, b), new, before)

    return lax.fori_loop(0, devices, turn, start)


def for_sending(value):

    def short(part):
        return part.astype(jnp.bfloat16) if part.dtype == jnp.float32 else part

    return jax.tree.map(short, value)


def rms_scale(values, gain):
    return values * lax.rsqrt(jnp.mean(values * values, axis=-1, keepdims=True) + NORM_EPS) * gain


def head_norm(heads_out, head_gain):
    scaled = (
        heads_out
        * lax.rsqrt(jnp.mean(heads_out * heads_out, axis=-1, keepdims=True) + HEAD_EPS)
        * head_gain
    )
    return scaled.reshape(heads_out.shape[0], -1)


def unit_rows(values):
    return values * lax.rsqrt(jnp.sum(values * values, axis=-1, keepdims=True) + UNIT_EPS)


def document_of(lengths, positions):
    starts = jnp.cumsum(lengths) - lengths
    above = (starts[None, :] <= positions[:, None]).astype(jnp.int32)
    return jnp.sum(above, axis=1) - 1


def contract_rows(left, right):
    return lax.dot_general(
        left, right, (((0,), (0,)), ((), ())), preferred_element_type=jnp.float32
    )


def contract_cols(left, right):
    return lax.dot_general(
        left, right, (((1,), (1,)), ((), ())), preferred_element_type=jnp.float32
    )


def combine(earlier, later):
    return (
        jnp.einsum("hde,hef->hdf", later[0], earlier[0], precision=HIGHEST_ACCURACY),
        jnp.einsum("hde,hef->hdf", later[0], earlier[1], precision=HIGHEST_ACCURACY) + later[1],
    )


def mixer_inputs(extended, conv_weight, valid, beta_logit, beta_bias, live):
    width, heads = beta_logit.shape
    ksize = conv_weight.shape[1]
    summed = extended[0:width] * conv_weight[:, 0, :][None] * valid[:, 0, None, None]
    for offset in range(1, ksize):
        summed = (
            summed
            + extended[offset : offset + width]
            * conv_weight[:, offset, :][None]
            * valid[:, offset, None, None]
        )
    active = jax.nn.silu(summed).reshape(width, 3, heads, -1)
    depth = active.shape[3]
    queries = unit_rows(active[:, 0]) * depth ** (-0.5)
    keys = unit_rows(active[:, 1])
    values = active[:, 2]
    beta = jax.nn.sigmoid(beta_logit + beta_bias) * live[:, None]
    return (queries, keys, values, beta)


def span_terms(queries, keys, values, beta, documents, previous):
    width, heads, depth = queries.shape
    count = width // SPAN
    query_blocks = queries.reshape(count, SPAN, heads, depth)
    key_blocks = keys.reshape(count, SPAN, heads, depth)
    value_blocks = values.reshape(count, SPAN, heads, depth)
    doc_blocks = documents.reshape(count, SPAN)
    same = doc_blocks[:, :, None] == doc_blocks[:, None, :]
    order = jnp.arange(SPAN, dtype=jnp.int32)
    strict = (same & (order[:, None] > order[None, :])[None]).astype(jnp.float32)
    weak = (same & (order[:, None] >= order[None, :])[None]).astype(jnp.float32)
    continuing = (doc_blocks == previous[:, None]).astype(jnp.float32)
    closing = (doc_blocks == doc_blocks[:, SPAN - 1 :]).astype(jnp.float32)
    rates = jnp.transpose(beta.reshape(count, SPAN, heads), (0, 2, 1))
    key_key = jnp.einsum("cthd,cshd->chts", key_blocks, key_blocks, precision=HIGHEST_ACCURACY)
    query_key = jnp.einsum("cthd,cshd->chts", query_blocks, key_blocks, precision=HIGHEST_ACCURACY)
    system = jnp.eye(SPAN, dtype=jnp.float32) + key_key * rates[:, :, None, :] * strict[:, None]
    inverse = jax.scipy.linalg.solve_triangular(
        system, jnp.broadcast_to(jnp.eye(SPAN, dtype=jnp.float32), system.shape), lower=True
    )
    plain = jnp.einsum("chts,cshe->chte", inverse, value_blocks, precision=HIGHEST_ACCURACY)
    reach = jnp.einsum(
        "chts,cshd->chtd",
        inverse,
        key_blocks * continuing[:, :, None, None],
        precision=HIGHEST_ACCURACY,
    )
    mixing = query_key * rates[:, :, None, :] * weak[:, None]
    written = rates * closing[:, None, :]
    transition = continuing[:, SPAN - 1, None, None, None] * jnp.eye(depth, dtype=jnp.float32)
    transition = transition - jnp.einsum(
        "cthd,cht,chte->chde", key_blocks, written, reach, precision=HIGHEST_ACCURACY
    )
    fresh = jnp.einsum(
        "cthd,cht,chte->chde", key_blocks, written, plain, precision=HIGHEST_ACCURACY
    )
    direct = jnp.einsum("chts,chse->chte", mixing, plain, precision=HIGHEST_ACCURACY)
    read = continuing[:, None, :, None] * jnp.transpose(query_blocks, (0, 2, 1, 3))
    read = read - jnp.einsum("chts,chsd->chtd", mixing, reach, precision=HIGHEST_ACCURACY)
    return (transition, fresh, read, direct)


def span_prefix(transition, fresh):
    heads, depth = (transition.shape[1], transition.shape[2])
    start = (
        jnp.broadcast_to(jnp.eye(depth, dtype=jnp.float32), (heads, depth, depth)),
        jnp.zeros((heads, depth, depth), jnp.float32),
    )

    def advance(carry, item):
        return (combine(carry, item), carry)

    whole, before = lax.scan(advance, start, (transition, fresh))
    return (before[0], before[1], whole[0], whole[1])


def read_out(read, direct, before_maps, before_adds, incoming):
    states = (
        jnp.einsum("chde,hef->chdf", before_maps, incoming, precision=HIGHEST_ACCURACY)
        + before_adds
    )
    outputs = direct + jnp.einsum("chtd,chdf->chtf", read, states, precision=HIGHEST_ACCURACY)
    count, heads, length, depth = outputs.shape
    return jnp.transpose(outputs, (0, 2, 1, 3)).reshape(count * length, heads, depth)


def mixer_core(queries, keys, values, beta, incoming, documents, previous):
    transition, fresh, read, direct = span_terms(queries, keys, values, beta, documents, previous)
    before_maps, before_adds, whole_map, whole_add = span_prefix(transition, fresh)
    outputs = read_out(read, direct, before_maps, before_adds, incoming)
    leaving = (
        jnp.einsum("hde,hef->hdf", whole_map, incoming, precision=HIGHEST_ACCURACY) + whole_add
    )
    return (outputs, leaving)


def body(
    tokens,
    cotangent,
    lengths,
    pad_mask,
    attn_gain,
    projection_weight,
    w_beta,
    beta_bias,
    conv_weight,
    head_gain,
    mlp_gain,
    w_gate,
    w_up,
    w_down,
):
    width, model = tokens.shape
    heads = w_beta.shape[1]
    depth = head_gain.shape[0]
    ksize = conv_weight.shape[1]
    margin = ksize - 1
    place = lax.axis_index(("dev", "ta"))
    positions = place * width + jnp.arange(width, dtype=jnp.int32)
    documents = document_of(lengths, positions)
    valid = jnp.stack(
        [
            (document_of(lengths, positions - margin + offset) == documents).astype(jnp.float32)
            for offset in range(ksize)
        ],
        axis=1,
    )
    previous = document_of(lengths, positions[::SPAN] - 1)
    live = pad_mask.astype(jnp.float32)
    proj_all, beta_all = (
        lax.all_gather(projection_weight, ("dev", "ta"), axis=0, tiled=True),
        lax.all_gather(w_beta, ("dev", "ta"), axis=0, tiled=True),
    )
    query_weights = proj_all[:, 0:3]
    output_weights = proj_all[:, 3]
    tokens_f = tokens.astype(jnp.float32)
    normalized_rows, attention_backward = jax.vjp(rms_scale, tokens_f, attn_gain)
    normed_low = normalized_rows.astype(jnp.bfloat16)
    projected_rows = jnp.einsum(
        "td,die->tie", normed_low, query_weights, preferred_element_type=jnp.float32
    )
    beta_logit = jnp.dot(normed_low, beta_all, preferred_element_type=jnp.float32)
    masked = projected_rows * live[:, None, None]
    arriving = passed_along(masked[width - margin :].astype(jnp.bfloat16), ("dev", "ta"), 1).astype(
        jnp.float32
    )
    extended = jnp.concatenate([arriving, masked], axis=0)

    def prepare(extended, conv_weight, beta_logit, beta_bias):
        return mixer_inputs(extended, conv_weight, valid, beta_logit, beta_bias, live)

    (queries, keys, values, beta), prepare_back = jax.vjp(
        prepare, extended, conv_weight, beta_logit, beta_bias
    )
    transition, fresh, read, direct = span_terms(queries, keys, values, beta, documents, previous)
    before_maps, before_adds, whole_map, whole_add = span_prefix(transition, fresh)
    identity = (
        jnp.broadcast_to(jnp.eye(depth, dtype=jnp.float32), (heads, depth, depth)),
        jnp.zeros((heads, depth, depth), jnp.float32),
    )
    incoming = entering((whole_map, whole_add), ("dev", "ta"), combine, identity)[1]
    outputs = read_out(read, direct, before_maps, before_adds, incoming)
    head_normed, head_back = jax.vjp(head_norm, outputs, head_gain)
    heads_low = head_normed.astype(jnp.bfloat16)
    residual = tokens_f + jnp.dot(heads_low, output_weights, preferred_element_type=jnp.float32)
    feed, feed_back = jax.vjp(rms_scale, residual, mlp_gain)
    feed_rows = lax.all_gather(feed.astype(jnp.bfloat16), "ta", axis=0, tiled=True)
    gate = jnp.dot(feed_rows, w_gate, preferred_element_type=jnp.float32)
    lifted = jnp.dot(feed_rows, w_up, preferred_element_type=jnp.float32)
    sigmoid_gate = jax.nn.sigmoid(gate)
    swish = gate * sigmoid_gate
    hidden_low = (swish * lifted).astype(jnp.bfloat16)
    branch = lax.psum_scatter(
        jnp.dot(hidden_low, w_down, preferred_element_type=jnp.float32).astype(jnp.bfloat16),
        "ta",
        scatter_dimension=0,
        tiled=True,
    ).astype(jnp.float32)
    block_out = (residual + branch).astype(jnp.bfloat16)
    upstream = cotangent.astype(jnp.float32)
    grad_rows = lax.all_gather(cotangent, "ta", axis=0, tiled=True)
    grad_hidden = contract_cols(grad_rows, w_down)
    grad_w_down = contract_rows(hidden_low, grad_rows)
    grad_gate_low = (
        grad_hidden * lifted * sigmoid_gate * (1.0 + gate * (1.0 - sigmoid_gate))
    ).astype(jnp.bfloat16)
    gradient_lifted_reduced = (grad_hidden * swish).astype(jnp.bfloat16)
    grad_w_gate = contract_rows(feed_rows, grad_gate_low)
    grad_w_up = contract_rows(feed_rows, gradient_lifted_reduced)
    grad_feed = lax.psum_scatter(
        (
            contract_cols(grad_gate_low, w_gate) + contract_cols(gradient_lifted_reduced, w_up)
        ).astype(jnp.bfloat16),
        "ta",
        scatter_dimension=0,
        tiled=True,
    ).astype(jnp.float32)
    grad_w_gate, grad_w_up, grad_w_down = (
        lax.psum(grad_w_gate.astype(jnp.bfloat16), "dev").astype(jnp.float32),
        lax.psum(grad_w_up.astype(jnp.bfloat16), "dev").astype(jnp.float32),
        lax.psum(grad_w_down.astype(jnp.bfloat16), "dev").astype(jnp.float32),
    )
    grad_from_feed, grad_mlp_gain = feed_back(grad_feed)
    grad_residual = upstream + grad_from_feed
    grad_mixed_low = grad_residual.astype(jnp.bfloat16)
    grad_heads = contract_cols(grad_mixed_low, output_weights)
    grad_outputs, grad_head_gain = head_back(grad_heads)
    count = width // SPAN
    grad_blocks = jnp.transpose(grad_outputs.reshape(count, SPAN, heads, depth), (0, 2, 1, 3))
    leaking = jnp.einsum(
        "ched,chte,chtf->hdf", before_maps, read, grad_blocks, precision=HIGHEST_ACCURACY
    )
    flipped = jnp.swapaxes(whole_map, 1, 2)
    leaving_grad = prefix((flipped, leaking), ("dev", "ta"), combine, identity)[1]

    def core(queries, keys, values, beta, incoming):
        return mixer_core(queries, keys, values, beta, incoming, documents, previous)

    _, core_back = jax.vjp(core, queries, keys, values, beta, incoming)
    grad_queries, grad_keys, grad_values, grad_beta, _ = core_back((grad_outputs, leaving_grad))
    grad_extended, grad_conv, grad_beta_logit, grad_beta_bias = prepare_back(
        (grad_queries, grad_keys, grad_values, grad_beta)
    )
    spilled = passed_along(for_sending(grad_extended[:margin]), ("dev", "ta"), -1)
    grad_masked = grad_extended[margin:] + jnp.concatenate(
        [jnp.zeros((width - margin,) + spilled.shape[1:], jnp.float32), spilled], axis=0
    )
    grad_projected_low = (grad_masked * live[:, None, None]).astype(jnp.bfloat16)
    grad_logit_low = grad_beta_logit.astype(jnp.bfloat16)
    grad_normed = jnp.einsum(
        "tie,die->td", grad_projected_low, query_weights, preferred_element_type=jnp.float32
    )
    grad_normed = grad_normed + contract_cols(grad_logit_low, beta_all)
    grad_from_norm, grad_attn_gain = attention_backward(grad_normed)
    grad_tokens = grad_residual + grad_from_norm
    group_normed, group_grads, group_heads, group_mixed = (
        lax.all_gather(normed_low, "ta", axis=0, tiled=True),
        lax.all_gather(grad_projected_low, "ta", axis=0, tiled=True),
        lax.all_gather(heads_low, "ta", axis=0, tiled=True),
        lax.all_gather(grad_mixed_low, "ta", axis=0, tiled=True),
    )
    lanes = lax.axis_size("ta")
    blocks = lax.axis_size("dev")
    rank = lax.axis_index("ta")
    stride = projection_weight.shape[0]

    def select(values):
        split = values.reshape(values.shape[0], blocks, lanes, stride)
        return lax.dynamic_index_in_dim(split, rank, axis=2, keepdims=False).reshape(
            values.shape[0], blocks * stride
        )

    inputs_term = jnp.einsum(
        "tr,tie->rie", select(group_normed), group_grads, preferred_element_type=jnp.float32
    )
    output_term = contract_rows(select(group_heads), group_mixed)[:, None, :]
    gradient_projection_weight = lax.psum_scatter(
        jnp.concatenate([inputs_term, output_term], axis=1).astype(jnp.bfloat16),
        "dev",
        scatter_dimension=0,
        tiled=True,
    ).astype(jnp.float32)
    grad_w_beta_full = contract_rows(normed_low, grad_logit_low)
    summed = lax.psum(
        (
            grad_attn_gain,
            grad_head_gain,
            grad_mlp_gain,
            grad_conv,
            grad_beta_bias,
            grad_w_beta_full,
        ),
        ("dev", "ta"),
    )
    beta_rows = w_beta.shape[0]
    grad_w_beta = lax.dynamic_slice_in_dim(summed[5], place * beta_rows, beta_rows, 0)
    return (
        block_out,
        grad_tokens,
        summed[0],
        gradient_projection_weight,
        grad_w_beta,
        summed[4],
        summed[3],
        summed[1],
        summed[2],
        grad_w_gate,
        grad_w_up,
        grad_w_down,
    )


def solution(mesh):
    placed = (
        P(("dev", "ta"), None),
        P(("dev", "ta"), None),
        P(),
        P(("dev", "ta")),
        P(),
        P(("dev", "ta"), None, None),
        P(("dev", "ta"), None),
        P(),
        P(),
        P(),
        P(),
        P(None, "ta"),
        P(None, "ta"),
        P("ta", None),
    )
    return jax.shard_map(
        body,
        mesh=mesh,
        in_specs=placed,
        out_specs=(
            P(("dev", "ta"), None),
            P(("dev", "ta"), None),
            P(),
            P(("dev", "ta"), None, None),
            P(("dev", "ta"), None),
            P(),
            P(),
            P(),
            P(),
            P(None, "ta"),
            P(None, "ta"),
            P("ta", None),
        ),
        check_vma=False,
    )
```

profile of v0, /device:TPU:0, one launch (start us, length us, event | category | flops | bytes accessed | tf_op | source)
XLA Modules:
  0.0 2308.6 jit_solution(14072569502405810885)
XLA Ops:
  10.2 44.6 %all-gather.4 = bf16[32,64,16]{1,2,0:T(8,128)(2,1)S(1)} all-gather(bf16[1,64,16]{1,2,0:T(8,128)(2,1)S(1)} %bitcast.413), channel_id=1, replica_groups=mesh['dev'=8,'ta'=4] {'dev','ta'}, dimensions={0}, use_global_device_ids=true | all-gather | bytes 67584 | tf_op jit(solution)/shard_map/all_gather | solution.py:246
  59.9 149.4 %all-gather.17.cloned.1.call-done = bf16[2048,4,2048]{2,0,1:T(8,128)(2,1)} async-done(((bf16[64,4,2048]{2,0,1:T(8,128)(2,1)}), bf16[2048,4,2048]{2,0,1:T(8,128)(2,1)}) %all-gather.17.cloned.1.call-update) | async-done | bytes 33554448 | tf_op jit(solution)/shard_map/all_gather | solution.py:245
  209.3 10.2 fusion.61
  224.5 4.2 fusion.49
  239.0 159.2 %custom-call.10 = f32[2,16,1,64,64]{3,4,2,1,0:T(8,128)} custom-call(f32[2,16,1,64,64]{4,3,2,1,0:T(8,128)} %select_bitcast_fusion), custom_call_target="InvertDiagBlocksLowerTriangular" | custom-call | tf_op jit(solution)/shard_map/jit(_solve_triangular)/vmap(vmap())/triangular_solve/custom-call.1 | solution.py:152
  404.1 5.1 fusion.151
  409.3 4.0 convolution_subtract_fusion
  417.7 16.8 while.74
  442.0 3.7 fusion.156
  451.0 102.0 %all-gather.31.cloned.1.call-done = bf16[512,128,128]{2,1,0:T(8,128)(2,1)} async-done(((bf16[16,128,128]{2,1,0:T(8,128)(2,1)}), bf16[512,128,128]{2,1,0:T(8,128)(2,1)}) %all-gather.31.cloned.1.call-update) | async-done | bytes 16777232 | tf_op jit(solution)/shard_map/all_gather | solution.py:24
  553.0 115.9 %all-gather.33.cloned.1.call-done = bf16[512,128,128]{2,1,0:T(8,128)(2,1)} async-done(((bf16[16,128,128]{2,1,0:T(8,128)(2,1)}), bf16[512,128,128]{2,1,0:T(8,128)(2,1)}) %all-gather.33.cloned.1.call-update) | async-done | bytes 16777232 | tf_op jit(solution)/shard_map/all_gather | solution.py:24
  670.3 4.7 bitcast_add_fusion
  675.1 4.3 multiply_reduce_fusion.11
  680.4 4.8 multiply_reduce_fusion.10
  688.2 146.9 %all-gather.19.cloned.1.call-done = bf16[512,2048]{1,0:T(8,128)(2,1)} async-done(((bf16[128,2048]{1,0:T(8,128)(2,1)}), bf16[512,2048]{1,0:T(8,128)(2,1)}) %all-gather.19.cloned.1.call-update) | async-done | bytes 2097168 | tf_op jit(solution)/shard_map/all_gather | solution.py:281
  835.1 8.4 fusion.222
  843.5 8.0 fusion.223
  851.5 7.6 all-gather.21.cloned.1.call-done
  859.1 10.6 multiply_convert_fusion
  869.7 6.5 fusion.224
  876.2 7.4 add_convert_fusion
  886.9 8.9 slice.93
  895.9 3.2 fusion.70
  900.7 14.5 reduce-scatter.6.cloned.1.call-done
  919.6 7.5 multiply_reduce_fusion.6
  937.1 4.1 fusion.66
  949.7 3.5 fusion.123
  954.6 5.6 fusion.78
  960.2 73.2 %all-gather.35.cloned.1.call-done = bf16[512,128,128]{2,1,0:T(8,128)(2,1)} async-done(((bf16[16,128,128]{2,1,0:T(8,128)(2,1)}), bf16[512,128,128]{2,1,0:T(8,128)(2,1)}) %all-gather.35.cloned.1.call-update) | async-done | bytes 16777232 | tf_op jit(solution)/shard_map/all_gather | solution.py:44
  1033.4 116.3 %all-gather.37.cloned.1.call-done = bf16[512,128,128]{2,1,0:T(8,128)(2,1)} async-done(((bf16[16,128,128]{2,1,0:T(8,128)(2,1)}), bf16[512,128,128]{2,1,0:T(8,128)(2,1)}) %all-gather.37.cloned.1.call-update) | async-done | bytes 16777232 | tf_op jit(solution)/shard_map/all_gather | solution.py:44
  1149.7 135.6 %while.75 = (s32[]{:T(128)}, f32[16,128,128]{2,1,0:T(8,128)}, s32[]{:T(128)}, bf16[32,16,128,128]{3,2,1,0:T(8,128)(2,1)}, bf16[32,16,128,128]{3,2,1,0:T(8,128)(2...) while((s32[]{:T(128)}, f32[16,128,128]{2,1,0:T(8,128)}, s32[]{:T(128)}, ...), condition=%wide.region_20.22_spmd.clone, body=%wide.region_19.21_spmd.clone.sunk | while | flops 403963904 | bytes 6294181 | solution.py:62
  1155.2 3.1 fusion.326
  1180.7 3.1 fusion.326
  1206.2 3.1 fusion.326
  1285.4 4.8 fusion.225
  1293.3 39.1 %while.73 = (s32[]{:T(128)}, f32[16,128,128]{2,1,0:T(8,128)}, f32[16,128,128]{2,1,0:T(8,128)}, f32[2,16,128,128]{2,3,1,0:T(8,128)}, f32[2,16,128,128]{3,2,1,0:T(...) while((s32[]{:T(128)}, f32[16,128,128]{2,1,0:T(8,128)}, ...), condition=%wide.region_22.24_spmd, body=%wide.region_21.23_spmd.sunk | while | flops 1611399168 | bytes 89131384 | solution.py:187
  1294.6 3.7 fusion.317
  1308.8 4.0 convolution_add_fusion.18
  1314.1 3.7 fusion.317
  1328.2 4.0 convolution_add_fusion.18
  1332.5 4.6 multiply_reduce_fusion.5
  1337.1 4.1 fusion.149
  1341.3 4.4 multiply_reduce_fusion.4
  1375.2 3.2 add_add_fusion.2
  1380.2 4.7 reshape.486
  1385.0 5.4 multiply_reduce_fusion.2
  1399.4 6.8 convolution_convert_fusion.2
  1406.1 5.3 convolution_convert_fusion.1
  1411.5 5.0 convolution_convert_fusion
  1417.8 7.2 convolution_convert_fusion.5
  1431.9 4.2 fusion.51
  1438.2 10.0 all-gather.25.cloned.1.call-done
  1448.2 6.4 convolution_convert_fusion.3
  1454.6 6.2 pad_maximum_fusion
  1460.9 520.1 %all-reduce.20.cloned.1.call-done = (bf16[2048,1408]{1,0:T(8,128)(2,1)}, bf16[2048,1408]{1,0:T(8,128)(2,1)}, bf16[1408,2048]{1,0:T(8,128)(2,1)}) async-done(((bf16[2048,1408]{1,0:T(8,128)(2,1)}, bf16[2048,1408]{1,0:T(8,128)(2,1)}, bf16[1408,2048]{1,0:T(8,128)(2,1)}), (bf16[2048,1408]{1,0:T(8,128)(2,1)}, bf16[2048,1408]{1,0:T(8,128)(2,1)}, bf16[1408,2048]{1,0:T(8,128)(2,1)})) %all-reduce.20.cloned.1.call-update) | async-done | bytes 17301520 | tf_op jit(solution)/shard_map/psum | solution.py:313
  1981.0 8.8 convert_element_type.266
  1989.8 5.2 convert_element_type.268
  1995.0 6.0 convert_element_type.270
  2002.4 14.5 fusion.111
  2016.9 40.1 %all-reduce.12 = (f32[2048]{0:T(1024)}, f32[16]{0:T(128)}, f32[128]{0:T(128)}, f32[2048]{0:T(1024)}) all-reduce(f32[2048]{0:T(1024)S(1)} %get-tuple-element.636, f32[16]{0:T(128)S(1)} %get-tuple-element.706, f32[128]{0:T(128)S(1)} %copy-done.118, f32[2048]{0:T(1024)S(1)} %copy-done.103), channel_id=1, replica_groups=mesh['dev'=8,'ta'=4] {'dev','ta'}, use_global_device_ids=true, to_apply=%region_29.31 | all-reduce | flops 4240 | bytes 33920 | tf_op jit(solution)/shard_map/psum | solution.py:378
  2057.1 3.3 fusion.115
  2060.4 85.6 %all-reduce.18.cloned.1.call-done = (f32[2048,16]{0,1:T(8,128)}, f32[3,4,2048]{2,0,1:T(4,128)}) async-done(((f32[2048,16]{0,1:T(8,128)}, f32[3,4,2048]{2,0,1:T(4,128)}), (f32[2048,16]{0,1:T(8,128)}, f32[3,4,2048]{2,0,1:T(4,128)})) %all-reduce.18.cloned.1.call-update) | async-done | bytes 229392 | tf_op jit(solution)/shard_map/psum | solution.py:378
  2149.0 149.4 %reduce-scatter.8.cloned.1.call-done = bf16[64,4,2048]{2,0,1:T(8,128)(2,1)} async-done(((bf16[512,4,2048]{2,0,1:T(8,128)(2,1)}), bf16[64,4,2048]{2,0,1:T(8,128)(2,1)}) %reduce-scatter.8.cloned.1.call-update) | async-done | bytes 1048592 | tf_op jit(solution)/shard_map/reduce_scatter | solution.py:371
  2298.4 3.4 copy.397
  (555 shorter events, 304.3 us)
Async XLA Ops:
  7.2 47.9 %copy-start.129 = (s32[128]{0:T(128)S(1)}, s32[128]{0:T(128)}, u32[]{:S(2)}) copy-start(s32[128]{0:T(128)} %param.27) | copy-start | bytes 1540
  7.2 48.0 %copy-start.130 = (s32[6]{0:T(128)S(1)}, s32[6]{0:T(128)}, u32[]{:S(2)}) copy-start(s32[6]{0:T(128)} %param.26) | copy-start | bytes 76
  7.2 49.2 %copy-start.67 = (bf16[128,2048]{1,0:T(8,128)(2,1)S(1)}, bf16[128,2048]{1,0:T(8,128)(2,1)}, u32[]{:S(2)}) copy-start(bf16[128,2048]{1,0:T(8,128)(2,1)} %param.24) | copy-start | bytes 1572868
  7.2 49.4 %copy-start.100 = (f32[2048]{0:T(1024)S(1)}, f32[2048]{0:T(1024)}, u32[]{:S(2)}) copy-start(f32[2048]{0:T(1024)} %param.28) | copy-start | bytes 24580
  7.2 49.6 %copy-start.123 = (f32[16]{0:T(128)S(1)}, f32[16]{0:T(128)}, u32[]{:S(2)}) copy-start(f32[16]{0:T(128)} %param.31) | copy-start | bytes 196
  7.2 52.5 %copy-start.97 = (f32[3,4,2048]{2,1,0:T(4,128)S(1)}, f32[3,4,2048]{2,1,0:T(4,128)}, u32[]{:S(2)}) copy-start(f32[3,4,2048]{2,1,0:T(4,128)} %param.32) | copy-start | bytes 294916
  7.3 202.1 %all-gather.17.cloned.1.call-start = ((), (), s32[]{:S(2)}) async-start(), calls=%async_computation.3 | async-start | bytes 34603008 | tf_op jit(solution)/shard_map/all_gather | solution.py:245
  10.2 542.9 %all-gather.31.cloned.1.call-start = ((), (), s32[]{:S(2)}) async-start(), calls=%async_computation.13 | async-start | bytes 17301504 | tf_op jit(solution)/shard_map/all_gather | solution.py:24
  55.1 164.4 %copy-start.114 = (f32[128]{0:T(128)}, f32[128]{0:T(128)S(1)}, u32[]{:S(2)}) copy-start(f32[128]{0:T(128)S(1)} %convert_element_type.228) | copy-start | bytes 1540
  58.2 161.3 %copy-start.94 = (pred[64,64]{1,0:T(8,128)(4,1)}, pred[64,64]{1,0:T(8,128)(4,1)S(1)}, u32[]{:S(2)}) copy-start(pred[64,64]{1,0:T(8,128)(4,1)S(1)} %get-tuple-element.770) | copy-start | bytes 12292
  58.9 350.4 %copy-start.75 = (f32[2,16,64]{2,1,0:T(8,128)}, f32[2,16,64]{2,1,0:T(8,128)S(1)}, u32[]{:S(2)}) copy-start(f32[2,16,64]{2,1,0:T(8,128)S(1)} %broadcast_multiply_fusion.5) | copy-start | bytes 24580
  59.0 177.9 %copy-start.77 = (f32[2,64,64]{2,1,0:T(8,128)}, f32[2,64,64]{2,1,0:T(8,128)S(1)}, u32[]{:S(2)}) copy-start(f32[2,64,64]{2,1,0:T(8,128)S(1)} %get-tuple-element.739) | copy-start | bytes 98308
  59.8 164.6 %copy-start.84 = (f32[3,2048]{1,0:T(4,128)}, f32[3,2048]{1,0:T(4,128)S(1)}, u32[]{:S(2)}) copy-start(f32[3,2048]{1,0:T(4,128)S(1)} %get-tuple-element.765) | copy-start | bytes 73732
  59.9 164.6 %copy-start.86 = (f32[3,2048]{1,0:T(4,128)}, f32[3,2048]{1,0:T(4,128)S(1)}, u32[]{:S(2)}) copy-start(f32[3,2048]{1,0:T(4,128)S(1)} %get-tuple-element.766) | copy-start | bytes 73732
  59.9 164.5 %copy-start.88 = (f32[3,2048]{1,0:T(4,128)}, f32[3,2048]{1,0:T(4,128)S(1)}, u32[]{:S(2)}) copy-start(f32[3,2048]{1,0:T(4,128)S(1)} %get-tuple-element.767) | copy-start | bytes 73732
  59.9 164.5 %copy-start.90 = (f32[3,2048]{1,0:T(4,128)}, f32[3,2048]{1,0:T(4,128)S(1)}, u32[]{:S(2)}) copy-start(f32[3,2048]{1,0:T(4,128)S(1)} %get-tuple-element.768) | copy-start | bytes 73732
  219.5 9.2 copy-start.49
  220.3 3.4 collective-permute-start
  231.8 170.9 %copy-start.56 = (f32[128,1,16,128]{3,2,0,1:T(8,128)}, f32[128,1,16,128]{3,2,0,1:T(8,128)S(1)}, u32[]{:S(2)}) copy-start(f32[128,1,16,128]{3,2,0,1:T(8,128)S(1)} %get-tuple-element.726) | copy-start | bytes 3145732
  234.8 166.4 %copy-start.51 = (f32[2,64,16,128]{3,2,1,0:T(8,128)}, f32[2,64,16,128]{3,2,1,0:T(8,128)S(1)}, u32[]{:S(2)}) copy-start(f32[2,64,16,128]{3,2,1,0:T(8,128)S(1)} %get-tuple-element.710) | copy-start | bytes 3145732
  234.8 174.5 %copy-start = (f32[2,64,16,128]{3,2,1,0:T(8,128)}, f32[2,64,16,128]{3,2,1,0:T(8,128)S(1)}, u32[]{:S(2)}) copy-start(f32[2,64,16,128]{3,2,1,0:T(8,128)S(1)} %get-tuple-element.711) | copy-start | bytes 3145732
  402.6 6.6 copy-start.14
  402.7 6.6 copy-start.83
  404.1 9.2 copy-start.19
  436.6 232.4 %all-gather.33.cloned.1.call-start = ((), (), s32[]{:S(2)}) async-start(), calls=%async_computation.14 | async-start | bytes 17301504 | tf_op jit(solution)/shard_map/all_gather | solution.py:24
  438.9 396.2 %all-gather.19.cloned.1.call-start = ((), (), s32[]{:S(2)}) async-start(), calls=%async_computation.4 | async-start | bytes 2621440 | tf_op jit(solution)/shard_map/all_gather | solution.py:281
  685.2 232.0 %copy-start.112 = (f32[128]{0:T(128)}, f32[128]{0:T(128)S(1)}, u32[]{:S(2)}) copy-start(f32[128]{0:T(128)S(1)} %fusion.211) | copy-start | bytes 1540
  687.1 172.0 %all-gather.21.cloned.1.call-start = ((), (), s32[]{:S(2)}) async-start(), calls=%async_computation.6 | async-start | bytes 2621440 | tf_op jit(solution)/shard_map/all_gather | solution.py:295
  687.7 227.5 %reduce-scatter.6.cloned.1.call-start = ((), (), s32[]{:S(2)}) async-start(), calls=%async_computation.7 | async-start | bytes 2621440 | tf_op jit(solution)/shard_map/reduce_scatter | solution.py:304
  835.1 8.4 copy-start.126
  869.7 6.5 copy-start.135
  869.7 6.5 copy-start.133
  876.2 7.5 copy-start.5
  883.7 149.7 %all-gather.35.cloned.1.call-start = ((), (), s32[]{:S(2)}) async-start(), calls=%async_computation.15 | async-start | bytes 17301504 | tf_op jit(solution)/shard_map/all_gather | solution.py:44
  886.7 263.1 %all-gather.37.cloned.1.call-start = ((), (), s32[]{:S(2)}) async-start(), calls=%async_computation.16 | async-start | bytes 17301504 | tf_op jit(solution)/shard_map/all_gather | solution.py:44
  886.9 9.0 copy-start.6
  886.9 9.0 copy-start.44
  895.9 19.4 copy-start.39
  919.6 7.5 copy-start.48
  931.7 493.4 %all-gather.23.cloned.1.call-start = ((), (), s32[]{:S(2)}) async-start(), calls=%async_computation.8 | async-start | bytes 2621440 | tf_op jit(solution)/shard_map/all_gather | solution.py:351
  932.5 496.4 %all-gather.27.cloned.1.call-start = ((), (), s32[]{:S(2)}) async-start(), calls=%async_computation.10 | async-start | bytes 2621440 | tf_op jit(solution)/shard_map/all_gather | solution.py:353
  933.9 7.2 copy-start.16
  936.7 495.1 %all-gather.29.cloned.1.call-start = ((), (), s32[]{:S(2)}) async-start(), calls=%async_computation.11 | async-start | bytes 2621440 | tf_op jit(solution)/shard_map/all_gather | solution.py:354
  948.1 6.5 copy-start.4
  960.2 488.0 %all-gather.25.cloned.1.call-start = ((), (), s32[]{:S(2)}) async-start(), calls=%async_computation.9 | async-start | bytes 7864320 | tf_op jit(solution)/shard_map/all_gather | solution.py:352
  1394.3 3.3 collective-permute-start.1
  1399.3 581.6 %all-reduce.20.cloned.1.call-start = ((), (), s32[]{:S(2)}) async-start(), calls=%async_computation.18 | async-start | bytes 34603008 | tf_op jit(solution)/shard_map/psum | solution.py:313
  1399.4 6.8 copy-start.134
  1416.5 640.5 %reduce-scatter.4.cloned.1.call-start = ((), (), s32[]{:S(2)}) async-start(), calls=%async_computation.5 | async-start | bytes 2621440 | tf_op jit(solution)/shard_map/reduce_scatter | solution.py:287
  1425.0 721.0 %all-reduce.18.cloned.1.call-start = ((), (), s32[]{:S(2)}) async-start(), calls=%async_computation.17 | async-start | bytes 524288 | tf_op jit(solution)/shard_map/psum | solution.py:378
  1437.9 860.5 %reduce-scatter.8.cloned.1.call-start = ((), (), s32[]{:S(2)}) async-start(), calls=%async_computation.12 | async-start | bytes 9437184 | tf_op jit(solution)/shard_map/reduce_scatter | solution.py:371
  1980.9 8.8 copy-start.65
  1980.9 14.0 slice-start
  1995.0 7.3 copy-start.64
  1995.0 7.3 copy-start.101
  1995.0 7.3 copy-start.120
  2002.3 14.6 copy-start.103
  2002.3 14.6 copy-start.118
  2002.3 54.7 %copy-start.125 = (f32[128]{0:T(128)S(1)}, f32[128]{0:T(128)}, u32[]{:S(2)}) copy-start(f32[128]{0:T(128)} %copy-done.124) | copy-start | bytes 1540
  2002.3 54.7 %copy-start.40 = (f32[128,2048]{1,0:T(8,128)S(1)}, f32[128,2048]{1,0:T(8,128)}, u32[]{:S(2)}) copy-start(f32[128,2048]{1,0:T(8,128)} %copy-done.38) | copy-start | bytes 3145732
  2002.3 54.7 %copy-start.66 = (bf16[128,2048]{1,0:T(8,128)(2,1)S(1)}, bf16[128,2048]{1,0:T(8,128)(2,1)}, u32[]{:S(2)}) copy-start(bf16[128,2048]{1,0:T(8,128)(2,1)} %param.25) | copy-start | bytes 1572868
  2002.3 54.7 %copy-start.93 = (f32[2048]{0:T(1024)S(1)}, f32[2048]{0:T(1024)}, u32[]{:S(2)}) copy-start(f32[2048]{0:T(1024)} %param.34) | copy-start | bytes 24580
  2002.4 54.7 %copy-start.113 = (f32[128]{0:T(128)S(1)}, f32[128]{0:T(128)}, u32[]{:S(2)}) copy-start(f32[128]{0:T(128)} %copy-done.112) | copy-start | bytes 1540
  2002.4 54.7 %copy-start.122 = (f32[128]{0:T(128)S(1)}, f32[128]{0:T(128)}, u32[]{:S(2)}) copy-start(f32[128]{0:T(128)} %copy-done.121) | copy-start | bytes 1540
  (101 other events, 383.8 us)
Sparse Core Ops, SparseCore 0:
  11.6 197.6 all-gather.16
  436.7 116.2 all-gather.30
  555.9 113.0 all-gather.32
  687.2 147.7 all-gather.18
  836.5 22.5 all-gather.20
  883.8 31.3 reduce-scatter.5
  918.5 114.8 all-gather.34
  1036.7 113.0 all-gather.36
  1152.0 20.7 all-gather.22
  1174.2 22.5 all-gather.26
  1198.5 22.5 all-gather.28
  1399.4 48.7 all-gather.24
  1454.1 526.7 all-reduce.19
  1983.9 30.3 reduce-scatter.3
  2020.8 125.2 all-reduce.17
  2150.0 148.3 reduce-scatter.7
where the time goes:
time: 2320 us; the launch traced here: 2310 us
  waiting for transfers between devices  1490 us (64%)
  matrix products  349 us (15%)
  other arithmetic  235 us (10%)
  local copies, waits for them, and re-layouts  123 us (5%)
  blocking collectives  84.7 us (4%)
    psum x1, waiting for transfers between devices, body(): lax.psum(grad_w_gate.astype(jnp.bfloat16), 'dev').astype(jnp.float32)  520 us
    all_gather x2, waiting for transfers between devices, entering(): lax.all_gather(a.astype(kind), axis)  218 us
    all_gather x2, waiting for transfers between devices, prefix(): lax.all_gather(part.astype(kind), axis)  190 us
    another operation x2, other arithmetic, span_terms(): jax.scipy.linalg.solve_triangular(system, jnp.broadcast_to(jnp.eye(SPAN,...  160 us
    all_gather x1, waiting for transfers between devices, body(): lax.all_gather(projection_weight, ('dev', 'ta'), axis=0, tiled=True)  149 us
    reduce_scatter x1, waiting for transfers between devices, body(): lax.psum_scatter(jnp.concatenate([inputs_term, output_term], axis=1).asty...  149 us
    all_gather x1, waiting for transfers between devices, body(): lax.all_gather(feed.astype(jnp.bfloat16), 'ta', axis=0, tiled=True)  147 us
    dot_general x38, matrix products, combine(): jnp.einsum('hde,hef->hdf', later[0], earlier[1], precision=HIGHEST_ACCURACY)  116 us
  transfers between devices with their start and end apart: 18, of which 14 were waited for; matrix products, arithmetic and copies ran while one was open for 18% of the time, Pallas kernels for 0%

commit v1 on v0

v1 whole, which is shorter than its diff:
```python
import jax
import jax.numpy as jnp
from jax import lax
from jax.sharding import PartitionSpec as P

HIGHEST = lax.Precision.HIGHEST
NORM_EPS = 1e-06
HEAD_EPS = 1e-05
UNIT_EPS = 1e-06
BOTH = ("dev", "ta")
BF = jnp.bfloat16
F32 = jnp.float32


def swap(x, axis, bit):
    return lax.ppermute(x, axis, [(i, i ^ bit) for i in range(lax.axis_size(axis))])


def gather_parts(x):
    parts = [x]
    for j in range(1, lax.axis_size("ta")):
        bit = j & -j
        parts.append(swap(parts[j ^ bit], "ta", bit))
    return parts


def in_order(parts, rank, axis):
    size = parts[0].shape[axis]
    shape = list(parts[0].shape)
    shape[axis] = size * len(parts)
    joined = jnp.zeros(shape, parts[0].dtype)
    for j, part in enumerate(parts):
        joined = lax.dynamic_update_slice_in_dim(joined, part, (rank ^ j) * size, axis)
    return joined


def exchange(blocks, rank):
    lanes = lax.axis_size("ta")
    parts = []
    for j in range(lanes):
        block = lax.dynamic_index_in_dim(blocks, rank ^ j, 0, False)
        parts.append(swap(block, "ta", j) if j else block)
    return parts


def scatter_sum(blocks, rank):
    lanes = lax.axis_size("ta")
    bit = 1
    while bit < lanes:
        pairs = blocks.reshape((blocks.shape[0] // 2, 2) + blocks.shape[1:])
        mine = (rank // bit) % 2
        kept = lax.dynamic_index_in_dim(pairs, mine, 1, False)
        sent = lax.dynamic_index_in_dim(pairs, 1 - mine, 1, False)
        arrived = swap(sent.astype(BF), "ta", bit)
        blocks = kept.astype(F32) + arrived.astype(F32)
        bit *= 2
    return blocks[0]


def ring_order(size):
    if size % 2:
        return list(range(size))
    return list(range(0, size, 2)) + list(range(size - 1, 0, -2))


class Ring:
    def __init__(self):
        self.size = lax.axis_size("dev")
        self.order = ring_order(self.size)
        self.spot = [self.order.index(i) for i in range(self.size)]
        self.place = lax.axis_index("dev")

    def move(self, x, step):
        n = self.size
        return lax.ppermute(x, "dev", [(self.order[p], self.order[(p + step) % n]) for p in range(n)])

    def at(self, distance):
        n = self.size
        table = jnp.array([self.order[(self.spot[i] + distance) % n] for i in range(n)], jnp.int32)
        return table[self.place]

    def gather(self, x):
        n = self.size
        half = x.shape[0] // 2
        joined = jnp.zeros((n,) + x.shape, x.dtype)
        joined = lax.dynamic_update_index_in_dim(joined, x, self.place, 0)
        onward, back = x, x
        for s in range(1, n // 2):
            onward, back = self.move(onward, 1), self.move(back, -1)
            joined = lax.dynamic_update_index_in_dim(joined, onward, self.at(-s), 0)
            joined = lax.dynamic_update_index_in_dim(joined, back, self.at(s), 0)
        far = jnp.concatenate([self.move(onward[:half], 1), self.move(back[half:], -1)], axis=0)
        return lax.dynamic_update_index_in_dim(joined, far, self.at(n // 2), 0)

    def scatter(self, blocks):
        n = self.size
        half = blocks.shape[1] // 2

        def block(distance):
            return lax.dynamic_index_in_dim(blocks, self.at(distance), 0, False)

        far = block(n // 2)
        ahead = self.move(far[:half], 1)
        behind = self.move(far[half:], -1)
        for s in range(n // 2 - 1, 0, -1):
            right, left = block(s).astype(F32), block(-s).astype(F32)
            if s == n // 2 - 1:
                right = jnp.concatenate([right[:half] + ahead.astype(F32), right[half:]], axis=0)
                left = jnp.concatenate([left[:half], left[half:] + behind.astype(F32)], axis=0)
            else:
                right, left = right + ahead.astype(F32), left + behind.astype(F32)
            ahead, behind = self.move(right.astype(BF), 1), self.move(left.astype(BF), -1)
        return block(0).astype(F32) + ahead.astype(F32) + behind.astype(F32)


def sum_over(x, axis):
    size = lax.axis_size(axis)
    bit = 1
    while bit < size:
        x = x + swap(x, axis, bit)
        bit *= 2
    return x


def shifted(x, distance):
    devices = range(lax.axis_size("dev"))
    return lax.ppermute(x, "dev", [(i - distance, i) for i in devices if i - distance in devices])


def rms_scale(values, gain):
    return values * lax.rsqrt(jnp.mean(values * values, axis=-1, keepdims=True) + NORM_EPS) * gain


def head_norm(heads_out, head_gain):
    scaled = (
        heads_out
        * lax.rsqrt(jnp.mean(heads_out * heads_out, axis=-1, keepdims=True) + HEAD_EPS)
        * head_gain
    )
    return scaled.reshape(heads_out.shape[0], -1)


def unit_rows(values):
    return values * lax.rsqrt(jnp.sum(values * values, axis=-1, keepdims=True) + UNIT_EPS)


def document_of(lengths, positions):
    starts = jnp.cumsum(lengths) - lengths
    above = (starts[None, :] <= positions[:, None]).astype(jnp.int32)
    return jnp.sum(above, axis=1) - 1


def contract_rows(left, right):
    return lax.dot_general(left, right, (((0,), (0,)), ((), ())), preferred_element_type=F32)


def contract_cols(left, right):
    return lax.dot_general(left, right, (((1,), (1,)), ((), ())), preferred_element_type=F32)


def dot(left, right):
    return jnp.dot(left, right, preferred_element_type=F32)


def mixer_inputs(extended, conv_weight, valid, beta_logit, beta_bias, live):
    width, heads = beta_logit.shape
    ksize = conv_weight.shape[1]
    summed = extended[0:width] * conv_weight[:, 0, :][None] * valid[:, 0, None, None]
    for offset in range(1, ksize):
        summed = (
            summed
            + extended[offset : offset + width]
            * conv_weight[:, offset, :][None]
            * valid[:, offset, None, None]
        )
    active = jax.nn.silu(summed).reshape(width, 3, heads, -1)
    depth = active.shape[3]
    queries = unit_rows(active[:, 0]) * depth ** (-0.5)
    keys = unit_rows(active[:, 1])
    values = active[:, 2]
    beta = jax.nn.sigmoid(beta_logit + beta_bias) * live[:, None]
    return (queries, keys, values, beta)


def mm(spec, a, b):
    return jnp.einsum(spec, a, b, precision=HIGHEST)


def inverse_of(lower):
    size = lower.shape[-1]
    row = jnp.arange(size)[:, None]
    col = jnp.arange(size)[None, :]
    found = jnp.eye(size, dtype=F32) - lower * ((row // 2 == col // 2)).astype(F32)
    block = 2
    while block < size:
        joint = (row // (2 * block) == col // (2 * block)) & (row // block != col // block)
        step = mm("...ts,...su->...tu", lower * joint.astype(F32), found)
        found = found - mm("...ts,...su->...tu", found, step)
        block *= 2
    return found


class Chunks:
    def __init__(self, queries, keys, values, beta, documents, previous):
        size = documents.shape[1]
        order = jnp.arange(size, dtype=jnp.int32)
        same = documents[:, :, None] == documents[:, None, :]
        self.q, self.k, self.v, self.beta = queries, keys, values, beta
        self.strict = (same & (order[:, None] > order[None, :])[None]).astype(F32)
        self.weak = (same & (order[:, None] >= order[None, :])[None]).astype(F32)
        self.cont = (documents == previous[:, None]).astype(F32)
        self.clos = (documents == documents[:, size - 1 :]).astype(F32)
        self.keep = self.cont[:, size - 1]
        k, q = keys, queries
        rate = beta[:, :, None, :]
        self.kk = mm("hctd,hcsd->hcts", k, k)
        self.qk = mm("hctd,hcsd->hcts", q, k)
        self.inv = inverse_of(self.kk * rate * self.strict)
        self.mix = self.qk * rate * self.weak
        self.wk = k * (beta * self.clos)[..., None]
        plain = mm("hcts,hcse->hcte", self.inv, values)
        reach = mm("hcts,hcsd->hctd", self.inv, k * self.cont[..., None])
        self.plain, self.reach = plain, reach
        self.read = q * self.cont[..., None] - mm("hcts,hcsd->hctd", self.mix, reach)
        self.direct = mm("hcts,hcse->hcte", self.mix, plain)
        eye = jnp.eye(k.shape[-1], dtype=F32)
        self.trans = self.keep[:, None, None] * eye - mm("hctd,hcte->hcde", self.wk, reach)
        self.fresh = mm("hctd,hcte->hcde", self.wk, plain)

    def whole(self):
        count = self.trans.shape[1]
        total, added = self.trans[:, 0], self.fresh[:, 0]
        for c in range(1, count):
            total = mm("hde,hef->hdf", self.trans[:, c], total)
            added = mm("hde,hef->hdf", self.trans[:, c], added) + self.fresh[:, c]
        return total, added

    def outputs(self, incoming):
        states = [incoming]
        for c in range(self.trans.shape[1] - 1):
            states.append(mm("hde,hef->hdf", self.trans[:, c], states[-1]) + self.fresh[:, c])
        self.states = jnp.stack(states, axis=1)
        return self.direct + mm("hctd,hcdf->hctf", self.read, self.states)

    def leak(self, grad_out):
        self.from_out = mm("hctd,hcte->hcde", self.read, grad_out)
        total = self.from_out[:, -1]
        for c in range(self.trans.shape[1] - 2, -1, -1):
            total = mm("hed,hef->hdf", self.trans[:, c], total) + self.from_out[:, c]
        return total

    def back(self, grad_out, leaving):
        grads = [leaving]
        for c in range(self.trans.shape[1] - 1, 0, -1):
            grads.append(mm("hed,hef->hdf", self.trans[:, c], grads[-1]) + self.from_out[:, c])
        ds = jnp.stack(grads[::-1], axis=1)
        q, k, beta, s = self.q, self.k, self.beta, self.states
        rate = beta[:, :, None, :]
        u = self.plain - mm("hctd,hcde->hcte", self.reach, s)
        kds = mm("hctd,hcde->hcte", k, ds)
        du = mm("hcts,hcte->hcse", self.mix, grad_out) + (beta * self.clos)[..., None] * kds
        dr = mm("hcts,hcte->hcse", self.inv, du)
        dp = mm("hcte,hcse->hcts", grad_out, u) * self.weak
        dl = -mm("hcte,hcse->hcts", dr, u) * self.strict
        dbeta = jnp.sum(dp * self.qk + dl * self.kk, axis=2) + self.clos * jnp.sum(kds * u, axis=-1)
        dqk = dp * rate
        da = dl * rate
        cont = self.cont[..., None]
        dq = cont * mm("hcte,hcde->hctd", grad_out, s) + mm("hcts,hcsd->hctd", dqk, k)
        dk = (
            mm("hcts,hctd->hcsd", dqk, q)
            + (beta * self.clos)[..., None] * mm("hcte,hcde->hctd", u, ds)
            - cont * mm("hcte,hcde->hctd", dr, s)
            + mm("hcts,hcsd->hctd", da, k)
            + mm("hcts,hctd->hcsd", da, k)
        )
        return dq, dk, dr, dbeta


def body(
    tokens,
    cotangent,
    lengths,
    pad_mask,
    attn_gain,
    projection_weight,
    w_beta,
    beta_bias,
    conv_weight,
    head_gain,
    mlp_gain,
    w_gate,
    w_up,
    w_down,
):
    width, model = tokens.shape
    heads = w_beta.shape[1]
    depth = head_gain.shape[0]
    ksize = conv_weight.shape[1]
    margin = ksize - 1
    lanes, blocks = lax.axis_size("ta"), lax.axis_size("dev")
    rank, place = lax.axis_index("ta"), lax.axis_index("dev")
    own_heads = heads // lanes
    cols = own_heads * depth
    rows = projection_weight.shape[0]
    group = lanes * width
    ring = Ring()

    positions = place * group + jnp.arange(group, dtype=jnp.int32)
    documents = document_of(lengths, positions)
    valid = jnp.stack(
        [
            (document_of(lengths, positions - margin + offset) == documents).astype(F32)
            for offset in range(ksize)
        ],
        axis=1,
    )
    previous = document_of(lengths, positions[::width] - 1)

    split = jnp.transpose(
        projection_weight[:, 0:3].reshape(rows, 3, lanes, cols), (2, 0, 1, 3)
    ).reshape(lanes, rows, 3 * cols)
    beta_split = jnp.transpose(w_beta.reshape(rows, lanes, own_heads), (1, 0, 2))
    own_rows = in_order(exchange(split, rank), rank, 0)
    own_beta = in_order(exchange(beta_split, rank), rank, 0)
    wqkv = ring.gather(own_rows).reshape(model, 3 * cols)
    wbeta = ring.gather(own_beta).reshape(model, own_heads)

    live_row = jnp.zeros((8, model), BF).at[0, 0:width].set(pad_mask.astype(BF))
    packed = in_order(gather_parts(jnp.concatenate([tokens, live_row], axis=0)[None]), rank, 0)
    halo = shifted(packed[lanes - 1, width - 8 :], 1)
    group_tokens = packed[:, :width].reshape(group, model).astype(F32)
    live = packed[:, width, 0:width].reshape(group).astype(F32)
    live_ext = jnp.concatenate([halo[8, width - 8 : width].astype(F32), live])
    normed = rms_scale(jnp.concatenate([halo[0:8].astype(F32), group_tokens], axis=0), attn_gain)
    normed = normed.astype(BF)
    normed_group = normed[8:]
    projected = dot(normed, wqkv) * live_ext[:, None]
    extended = projected[8 - margin :].reshape(group + margin, 3, cols)
    beta_logit = dot(normed_group, wbeta)

    own_conv = lax.dynamic_slice_in_dim(conv_weight, rank * cols, cols, 2)
    own_bias = lax.dynamic_slice_in_dim(beta_bias, rank * own_heads, own_heads, 0)

    def prepare(extended, conv_weight, beta_logit, beta_bias):
        return mixer_inputs(extended, conv_weight, valid, beta_logit, beta_bias, live)

    (queries, keys, values, beta), prepare_back = jax.vjp(
        prepare, extended, own_conv, beta_logit, own_bias
    )

    def by_chunk(x):
        return jnp.transpose(x.reshape(lanes, width, own_heads, depth), (2, 0, 1, 3))

    def by_token(x):
        return jnp.transpose(x, (1, 2, 0, 3)).reshape(group, own_heads, depth)

    chunks = Chunks(
        by_chunk(queries),
        by_chunk(keys),
        by_chunk(values),
        jnp.transpose(beta.reshape(lanes, width, own_heads), (2, 0, 1)),
        documents.reshape(lanes, width),
        previous,
    )
    whole_map, whole_add = chunks.whole()
    both = ring.gather(jnp.stack([whole_map, whole_add]).astype(BF))
    incoming = jnp.zeros((own_heads, depth, depth), F32)
    for i in range(blocks - 1):
        new = mm("hde,hef->hdf", both[i, 0].astype(F32), incoming) + both[i, 1].astype(F32)
        incoming = jnp.where(i < place, new, incoming)
    outputs = by_token(chunks.outputs(incoming))

    head_normed, head_back = jax.vjp(head_norm, outputs, head_gain)
    heads_low = in_order(gather_parts(head_normed.astype(BF)), rank, 1)
    w_out = lax.all_gather(projection_weight[:, 3], BOTH, axis=0, tiled=True)
    residual = group_tokens + dot(heads_low, w_out)
    feed_rows = rms_scale(residual, mlp_gain).astype(BF)
    own_residual = lax.dynamic_slice_in_dim(residual, rank * width, width, 0)
    own_feed = lax.dynamic_slice_in_dim(feed_rows, rank * width, width, 0)
    feed_all = lax.all_gather(own_feed, BOTH, axis=0, tiled=True)
    cot_all = lax.all_gather(cotangent, BOTH, axis=0, tiled=True)
    cot_group = lax.dynamic_slice_in_dim(cot_all, place * group, group, 0)

    def feed_forward(feed, grad_rows):
        gate = dot(feed, w_gate)
        lifted = dot(feed, w_up)
        sig = jax.nn.sigmoid(gate)
        swish = gate * sig
        hidden = (swish * lifted).astype(BF)
        grad_hidden = contract_cols(grad_rows, w_down)
        grad_gate = (grad_hidden * lifted * sig * (1.0 + gate * (1.0 - sig))).astype(BF)
        grad_lifted = (grad_hidden * swish).astype(BF)
        return hidden, grad_gate, grad_lifted

    hidden, grad_gate, grad_lifted = feed_forward(feed_rows, cot_group)
    partial_feed = contract_cols(grad_gate, w_gate) + contract_cols(grad_lifted, w_up)
    grad_feed = scatter_sum(partial_feed.astype(BF).reshape(lanes, width, model), rank)
    branch = scatter_sum(dot(hidden, w_down).astype(BF).reshape(lanes, width, model), rank)
    block_out = (own_residual + branch).astype(BF)

    hidden, grad_gate, grad_lifted = feed_forward(feed_all, cot_all)
    grad_w_down = contract_rows(hidden, cot_all)
    grad_w_gate = contract_rows(feed_all, grad_gate)
    grad_w_up = contract_rows(feed_all, grad_lifted)

    _, feed_back = jax.vjp(rms_scale, own_residual, mlp_gain)
    grad_from_feed, grad_mlp_gain = feed_back(grad_feed)
    grad_residual = cotangent.astype(F32) + grad_from_feed
    grad_mixed = grad_residual.astype(BF)
    grad_heads = contract_cols(grad_mixed, w_out).astype(BF)

    def to_heads(x):
        split = jnp.transpose(x.reshape(width, lanes, cols), (1, 0, 2))
        return in_order(exchange(split, rank), rank, 0)

    grad_heads = to_heads(grad_heads).astype(F32)
    mixed_cols = to_heads(grad_mixed)
    grad_outputs, grad_head_gain = head_back(grad_heads)
    grad_outputs = by_chunk(grad_outputs)
    leaks = ring.gather(chunks.leak(grad_outputs).astype(BF))
    leaving = jnp.zeros((own_heads, depth, depth), F32)
    for i in range(blocks - 1, 0, -1):
        new = mm("hed,hef->hdf", both[i, 0].astype(F32), leaving) + leaks[i].astype(F32)
        leaving = jnp.where(i > place, new, leaving)
    grad_q, grad_k, grad_v, grad_beta = chunks.back(grad_outputs, leaving)
    grad_extended, grad_conv, grad_logit, grad_bias = prepare_back(
        (
            by_token(grad_q),
            by_token(grad_k),
            by_token(grad_v),
            jnp.transpose(grad_beta, (1, 2, 0)).reshape(group, own_heads),
        )
    )
    spilled = shifted(grad_extended[:margin].astype(BF), -1).astype(F32)
    grad_masked = grad_extended[margin:] + jnp.concatenate(
        [jnp.zeros((group - margin, 3, cols), F32), spilled], axis=0
    )
    grad_projected = (grad_masked * live[:, None, None]).astype(BF).reshape(group, 3 * cols)
    grad_logit_low = grad_logit.astype(BF)
    partial_normed = contract_cols(grad_projected, wqkv) + contract_cols(grad_logit_low, wbeta)
    grad_normed = scatter_sum(partial_normed.astype(BF).reshape(lanes, width, model), rank)
    _, attention_back = jax.vjp(rms_scale, tokens.astype(F32), attn_gain)
    grad_from_norm, grad_attn_gain = attention_back(grad_normed)
    grad_tokens = grad_residual + grad_from_norm

    def weight_rows(partial):
        share = partial.shape[1]
        part = ring.scatter(partial.astype(BF).reshape(blocks, model // blocks, share))
        return exchange(part.astype(BF).reshape(lanes, rows, share), rank)

    qkv_parts = weight_rows(contract_rows(normed_group, grad_projected))
    out_parts = weight_rows(contract_rows(heads_low, mixed_cols))
    qkv_grad = in_order([p.astype(F32).reshape(rows, 3, cols) for p in qkv_parts], rank, 2)
    out_grad = in_order([p.astype(F32) for p in out_parts], rank, 1)
    grad_projection = jnp.concatenate([qkv_grad, out_grad[:, None]], axis=1)

    partial_wbeta = contract_rows(normed_group, grad_logit_low)
    sizes = [3 * ksize * cols, own_heads * model, own_heads]
    flat = jnp.concatenate([grad_conv.reshape(-1), partial_wbeta.T.reshape(-1), grad_bias])
    flat = jnp.pad(flat, (0, -flat.shape[0] % 1024)).reshape(-1, 128)
    flat = in_order(gather_parts(sum_over(flat, "dev")[None]), rank, 0).reshape(lanes, -1)
    conv_sum = flat[:, : sizes[0]].reshape(lanes, 3, ksize, cols)
    conv_sum = jnp.transpose(conv_sum, (1, 2, 0, 3)).reshape(3, ksize, lanes * cols)
    wbeta_sum = flat[:, sizes[0] : sizes[0] + sizes[1]].reshape(heads, model).T
    grad_w_beta = lax.dynamic_slice_in_dim(wbeta_sum, (place * lanes + rank) * rows, rows, 0)
    bias_sum = flat[:, sizes[0] + sizes[1] : sum(sizes)].reshape(heads)

    gains = jnp.concatenate([grad_mlp_gain, grad_head_gain, grad_attn_gain])
    gains = jnp.pad(gains, (0, -gains.shape[0] % 1024)).reshape(-1, 128)
    gains = sum_over(sum_over(gains, "dev"), "ta").reshape(-1)
    return (
        block_out,
        grad_tokens,
        gains[model + depth : 2 * model + depth],
        grad_projection,
        grad_w_beta,
        bias_sum,
        conv_sum,
        gains[model : model + depth],
        gains[:model],
        grad_w_gate,
        grad_w_up,
        grad_w_down,
    )


def solution(mesh):
    rows = P(BOTH, None)
    three = P(BOTH, None, None)
    return jax.shard_map(
        body,
        mesh=mesh,
        in_specs=(
            rows,
            rows,
            P(),
            P(BOTH),
            P(),
            three,
            rows,
            P(),
            P(),
            P(),
            P(),
            P(None, "ta"),
            P(None, "ta"),
            P("ta", None),
        ),
        out_specs=(
            rows,
            rows,
            P(),
            three,
            rows,
            P(),
            P(),
            P(),
            P(),
            P(None, "ta"),
            P(None, "ta"),
            P("ta", None),
        ),
        check_vma=False,
    )
```

time: 2320 us -> 960 us (0.41)
  waiting for transfers between devices: 1490 us -> 222 us
  other arithmetic: 235 us -> 68.9 us
  starting transfers between devices: 5.85 us -> 96.4 us
  blocking collectives: 84.7 us -> 0 us
  local copies, waits for them, and re-layouts: 123 us -> 156 us
  matrix products: 349 us -> 375 us
    all_gather x11 -> x3, waiting for transfers between devices: 722 us -> 0.01 us  [the longest x1 0.01 us: body(): cot_all = lax.all_gather(cotangent, BOTH, axis=0, tiled=True)]
    psum x2 -> x0, waiting for transfers between devices: 606 us -> none  [the longest x1 520 us: body(): lax.psum(grad_w_gate.astype(jnp.bfloat16), 'dev').astype(jnp.float32)]
    ppermute x2 -> x91, waiting for transfers between devices: 2.41 us -> 222 us  [the longest x48 130 us: move(): lax.ppermute(x, 'dev', [(self.order[p], self.order[(p + step) % n]) for p...]
    reduce_scatter x3 -> x0, waiting for transfers between devices: 164 us -> none  [the longest x1 149 us: body(): lax.psum_scatter(jnp.concatenate([inputs_term, output_term], axis=1).asty...]
    another operation x3 -> x5, other arithmetic: 160 us -> 3.23 us  [the longest x2 160 us: span_terms(): jax.scipy.linalg.solve_triangular(system, jnp.broadcast_to(jnp.eye(SPAN,...]
    dot_general x85 -> x72, matrix products: 289 us -> 184 us  [the longest x8 95.8 us: dot(): return jnp.dot(left, right, preferred_element_type=F32)]
    dot_general x5 -> x6, matrix products: 22.1 us -> 123 us  [contract_rows(): lax.dot_general(left, right, (((0,), (0,)), ((), ())), preferred_element_...]
    ppermute x2 -> x91, starting transfers between devices: 4.19 us -> 96.3 us  [the longest x48 59 us: move(): lax.ppermute(x, 'dev', [(self.order[p], self.order[(p + step) % n]) for p...]
  transfers between devices with their start and end apart: 18 -> 94, of which waited for: 14 -> 39; matrix products, arithmetic and copies ran while one was open for 18% -> 43% of each run, Pallas kernels for 0% -> 0%
where the time goes in v1:
time: 960 us; the launch traced here: 950 us
  matrix products  375 us (39%)
  waiting for transfers between devices  222 us (23%)
  local copies, waits for them, and re-layouts  156 us (16%)
  starting transfers between devices  96.4 us (10%)
  other arithmetic  68.9 us (7%)
  between operations  31.4 us (3%)
    ppermute x48, waiting for transfers between devices, move(): lax.ppermute(x, 'dev', [(self.order[p], self.order[(p + step) % n]) for p...  130 us
    dot_general x6, matrix products, contract_rows(): lax.dot_general(left, right, (((0,), (0,)), ((), ())), preferred_element_...  123 us
    dot_general x8, matrix products, dot(): return jnp.dot(left, right, preferred_element_type=F32)  95.8 us
    dot_general x64, matrix products, mm(): return jnp.einsum(spec, a, b, precision=HIGHEST)  88 us
    ppermute x41, waiting for transfers between devices, swap(): lax.ppermute(x, axis, [(i, i ^ bit) for i in range(lax.axis_size(axis))])  72.2 us
    dot_general x7, matrix products, contract_cols(): lax.dot_general(left, right, (((1,), (1,)), ((), ())), preferred_element_...  67.8 us
    ppermute x48, starting transfers between devices, move(): lax.ppermute(x, 'dev', [(self.order[p], self.order[(p + step) % n]) for p...  59 us
    ppermute x41, starting transfers between devices, swap(): lax.ppermute(x, axis, [(i, i ^ bit) for i in range(lax.axis_size(axis))])  33.7 us
  transfers between devices with their start and end apart: 94, of which 39 were waited for; matrix products, arithmetic and copies ran while one was open for 43% of the time, Pallas kernels for 0%

profile of v1, /device:TPU:0, one launch (start us, length us, event | category | flops | bytes accessed | tf_op | source)
XLA Modules:
  0.0 950.1 jit_solution(268494935833224280)
XLA Ops:
  73.8 14.4 %collective-permute-done.5 = bf16[64,1536]{1,0:T(8,128)(2,1)S(1)} collective-permute-done((bf16[64,1536]{1,0:T(8,128)(2,1)S(1)}, bf16[64,1536]{1,0:T(8,128)(2,1)S(1)}, u32[]{:S(2)}, u32[]{:S(2)}) %collective-permute-start.5) | collective-permute-done | bytes 196640 | tf_op jit(solution)/shard_map/ppermute | solution.py:16
  94.6 19.9 %collective-permute-done.8 = bf16[256,1536]{1,0:T(8,128)(2,1)} collective-permute-done((bf16[256,1536]{1,0:T(8,128)(2,1)}, bf16[256,1536]{1,0:T(8,128)(2,1)}, u32[]{:S(2)}, u32[]{:S(2)}) %collective-permute-start.8) | collective-permute-done | bytes 786464 | tf_op jit(solution)/shard_map/ppermute | solution.py:75
  122.4 14.5 %collective-permute-done.3 = bf16[16,2048]{1,0:T(8,128)(2,1)S(1)} collective-permute-done((bf16[16,2048]{1,0:T(8,128)(2,1)S(1)}, bf16[16,2048]{1,0:T(8,128)(2,1)S(1)}, u32[]{:S(2)}, u32[]{:S(2)}) %collective-permute-start.3) | collective-permute-done | bytes 65568 | tf_op jit(solution)/shard_map/ppermute | solution.py:127
  139.4 5.8 collective-permute-done.10
  145.2 3.4 collective-permute-start.12
  154.8 32.8 %collective-permute-done.12 = bf16[256,1536]{1,0:T(8,128)(2,1)S(1)} collective-permute-done((bf16[256,1536]{1,0:T(8,128)(2,1)}, bf16[256,1536]{1,0:T(8,128)(2,1)S(1)}, u32[]{:S(2)}, u32[]{:S(2)}) %collective-permute-start.12) | collective-permute-done | bytes 786464 | tf_op jit(solution)/shard_map/ppermute | solution.py:75
  191.9 13.9 %collective-permute-done.14 = bf16[128,1536]{1,0:T(8,128)(2,1)S(1)} collective-permute-done((bf16[128,1536]{1,0:T(8,128)(2,1)S(1)}, bf16[128,1536]{1,0:T(8,128)(2,1)S(1)}, u32[]{:S(2)}, u32[]{:S(2)}) %collective-permute-start.14) | collective-permute-done | bytes 393248 | tf_op jit(solution)/shard_map/ppermute | solution.py:75
  206.7 5.7 convolution_multiply_fusion
  212.5 4.2 fusion.258
  217.1 5.3 slice.388
  222.4 4.9 slice.397
  227.4 4.9 slice.394
  234.6 7.1 divide_multiply_fusion
  245.3 3.0 fusion.259
  272.9 2.7 fusion.103
  290.9 4.4 collective-permute-start.29
  297.3 2.8 collective-permute-done.29
  303.0 3.5 collective-permute-done.31
  311.5 2.7 collective-permute-done.32
  317.6 2.9 multiply_reduce_fusion.11
  333.5 3.7 copy.927
  337.2 3.5 copy.930
  340.8 3.6 copy.929
  344.4 3.5 copy.928
  348.4 4.2 convolution_subtract_fusion.6
  357.2 9.2 multiply_reduce_fusion.1
  368.6 7.3 fusion.260
  375.9 3.4 fusion.261
  379.4 3.9 convolution_convert_fusion.2
  385.8 6.6 fusion.29
  392.4 7.1 fusion.42
  399.6 5.7 add_convert_fusion.1
  417.2 33.9 %fusion.263 = f32[4096,1408]{1,0:T(8,128)} fusion(bf16[4096,2048]{1,0:T(8,128)(2,1)} %all-gather.5.cloned.1.call-done, bf16[1408,2048]{1,0:T(8,128)(2,1)} %param.73), kind=kOutput, calls=%fused_computation.633 | convolution fusion | flops 23622320128 | bytes 45613056 | tf_op jit(solution)/shard_map/dot_general | solution.py:158
  453.7 7.1 fusion.26
  472.7 7.6 collective-permute-done.42
  480.9 4.1 collective-permute-done.43
  503.1 3.0 convolution_convert_fusion.1
  512.1 3.1 convolution_bitcast_fusion.3
  524.2 10.0 %collective-permute-done.46 = bf16[4,128,128]{2,1,0:T(8,128)(2,1)S(1)} collective-permute-done((bf16[4,128,128]{2,1,0:T(8,128)(2,1)S(1)}, bf16[4,128,128]{2,1,0:T(8,128)(2,1)S(1)}, u32[]{:S(2)}, u32[]{:S(2)}) %collective-permute-start.46) | collective-permute-done | bytes 131104 | tf_op jit(solution)/shard_map/ppermute | solution.py:75
  537.3 3.5 collective-permute-done.48
  556.7 3.3 multiply_reduce_fusion.7
  562.6 3.5 convolution_add_fusion.1
  581.1 3.7 copy.940
  589.3 5.2 reshape.1644
  594.6 6.1 multiply_reduce_fusion.5
  600.9 6.8 broadcast_multiply_fusion
  608.6 3.1 pad_add_fusion
  614.3 2.7 collective-permute-start.85
  617.0 5.7 collective-permute-done.52
  623.7 6.7 add_convert_fusion
  630.5 3.8 convolution_convert_fusion
  666.4 5.4 collective-permute-done.81
  675.3 3.4 collective-permute-done.83
  685.2 9.6 %collective-permute-done.54 = bf16[1,128,2048]{2,1,0:T(8,128)(2,1)S(1)} collective-permute-done((bf16[1,128,2048]{2,1,0:T(8,128)(2,1)S(1)}, bf16[1,128,2048]{2,1,0:T(8,128)(2,1)S(1)}, u32[]{:S(2)}, u32[]{:S(2)}) %collective-permute-start.54) | collective-permute-done | bytes 524320 | tf_op jit(solution)/shard_map/ppermute | solution.py:16
  697.2 4.5 collective-permute-done.62
  704.3 14.8 %collective-permute-done.56 = f32[40,128]{1,0:T(8,128)S(1)} collective-permute-done((f32[40,128]{1,0:T(8,128)S(1)}, f32[40,128]{1,0:T(8,128)S(1)}, u32[]{:S(2)}, u32[]{:S(2)}) %collective-permute-start.56) | collective-permute-done | bytes 20512 | tf_op jit(solution)/shard_map/ppermute | solution.py:16
  719.7 4.1 collective-permute-done.57
  730.7 13.1 %collective-permute-done.63 = bf16[256,1536]{1,0:T(8,128)(2,1)S(1)} collective-permute-done((bf16[256,1536]{1,0:T(8,128)(2,1)S(1)}, bf16[256,1536]{1,0:T(8,128)(2,1)S(1)}, u32[]{:S(2)}, u32[]{:S(2)}) %collective-permute-start.63) | collective-permute-done | bytes 786464 | tf_op jit(solution)/shard_map/ppermute | solution.py:75
  749.8 6.7 collective-permute-done.69
  763.6 33.3 %fusion.265 = f32[4096,1408]{1,0:T(8,128)} fusion(bf16[4096,2048]{1,0:T(8,128)(2,1)} %all-gather.7.cloned.1.call-done, bf16[2048,1408]{1,0:T(8,128)(2,1)} %param.71), kind=kOutput, calls=%fused_computation.635 | convolution fusion | flops 23622320128 | bytes 45613056 | tf_op jit(solution)/shard_map/dot_general | solution.py:162
  796.8 31.6 %fusion.264 = f32[4096,1408]{1,0:T(8,128)} fusion(bf16[4096,2048]{1,0:T(8,128)(2,1)S(1)} %copy-done.133, bf16[2048,1408]{1,0:T(8,128)(2,1)} %param.72), kind=kOutput, calls=%fused_computation.634 | convolution fusion | flops 23622320128 | bytes 45613056 | tf_op jit(solution)/shard_map/dot_general | solution.py:162
  828.4 36.6 %fusion.2 = f32[1408,2048]{1,0:T(8,128)} fusion(bf16[4096,2048]{1,0:T(8,128)(2,1)} %all-gather.5.cloned.1.call-done, f32[4096,1408]{1,0:T(8,128)} %fusion.264, f32[4096,1408]{1,0:T(8,128)} %fusion.265), kind=kOutput, calls=%fused_computation.6 | convolution fusion | flops 23656923136 | bytes 74448896 | tf_op jit(solution)/shard_map/dot_general | solution.py:154
  865.0 40.1 %fusion.3 = f32[2048,1408]{1,0:T(8,128)} fusion(bf16[4096,2048]{1,0:T(8,128)(2,1)} %all-gather.7.cloned.1.call-done, f32[4096,1408]{1,0:T(8,128)} %fusion.265, f32[4096,1408]{1,0:T(8,128)} %fusion.263, f32[4096,1408]{1,0:T(8,128)} %fusion.264), kind=kOutput, calls=%fused_computation.7 | convolution fusion | flops 23679991808 | bytes 97517568 | tf_op jit(solution)/shard_map/dot_general | solution.py:154
  905.1 37.9 %fusion.1 = f32[2048,1408]{1,0:T(8,128)} fusion(bf16[4096,2048]{1,0:T(8,128)(2,1)} %all-gather.7.cloned.1.call-done, f32[4096,1408]{1,0:T(8,128)} %fusion.263, f32[4096,1408]{1,0:T(8,128)} %fusion.265), kind=kOutput, calls=%fused_computation.5 | convolution fusion | flops 23656923136 | bytes 74448896 | tf_op jit(solution)/shard_map/dot_general | solution.py:154
  (802 shorter events, 333.7 us)
Async XLA Ops:
  7.2 350.0 %all-gather.9.cloned.1.call-start = ((), (), s32[]{:S(2)}) async-start(), calls=%async_computation.2 | async-start | bytes 8650752 | tf_op jit(solution)/shard_map/all_gather | solution.py:376
  10.0 375.7 %all-gather.5.cloned.1.call-start = ((), (), s32[]{:S(2)}) async-start(), calls=%async_computation | async-start | bytes 17301504 | tf_op jit(solution)/shard_map/all_gather | solution.py:382
  12.6 79.7 %collective-permute-start = (bf16[1,136,2048]{2,1,0:T(8,128)(2,1)}, bf16[1,136,2048]{2,1,0:T(8,128)(2,1)}, u32[]{:S(2)}, u32[]{:S(2)}) collective-permute-start(bf16[1,136,2048]{2,1,0:T(8,128)(2,1)} %fusion.147), channel_id=1, source_target_pairs={{0,1},{1,0},{2,3},{3,2},{4,5},{5,4},{6,7},{7,6},{8,9},{9,8},{10,11... | collective-permute-start | bytes 1671176 | tf_op jit(solution)/shard_map/ppermute | solution.py:16
  13.1 79.2 %collective-permute-start.1 = (bf16[1,136,2048]{2,1,0:T(8,128)(2,1)}, bf16[1,136,2048]{2,1,0:T(8,128)(2,1)}, u32[]{:S(2)}, u32[]{:S(2)}) collective-permute-start(bf16[1,136,2048]{2,1,0:T(8,128)(2,1)} %fusion.147), channel_id=1, source_target_pairs={{0,2},{1,3},{2,0},{3,1},{4,6},{5,7},{6,4},{7,5},{8,10},{9,11},{10,... | collective-permute-start | bytes 1671176 | tf_op jit(solution)/shard_map/ppermute | solution.py:16
  16.2 15.7 %collective-permute-start.17 = (bf16[64,4]{0,1:T(4,128)(2,1)}, bf16[64,4]{0,1:T(4,128)(2,1)}, u32[]{:S(2)}, u32[]{:S(2)}) collective-permute-start(bf16[64,4]{0,1:T(4,128)(2,1)} %get-tuple-element.116), channel_id=1, source_target_pairs={{0,3},{1,2},{2,1},{3,0},{4,7},{5,6},{6,5},{7,4},{8,11},{9,10},{10,... | collective-permute-start | bytes 1544 | tf_op jit(solution)/shard_map/ppermute | solution.py:16
  16.3 14.8 %collective-permute-start.16 = (bf16[64,4]{0,1:T(4,128)(2,1)}, bf16[64,4]{0,1:T(4,128)(2,1)}, u32[]{:S(2)}, u32[]{:S(2)}) collective-permute-start(bf16[64,4]{0,1:T(4,128)(2,1)} %get-tuple-element.117), channel_id=1, source_target_pairs={{0,2},{1,3},{2,0},{3,1},{4,6},{5,7},{6,4},{7,5},{8,10},{9,11},{10,... | collective-permute-start | bytes 1544 | tf_op jit(solution)/shard_map/ppermute | solution.py:16
  18.1 10.6 %collective-permute-start.15 = (bf16[64,4]{0,1:T(4,128)(2,1)}, bf16[64,4]{0,1:T(4,128)(2,1)}, u32[]{:S(2)}, u32[]{:S(2)}) collective-permute-start(bf16[64,4]{0,1:T(4,128)(2,1)} %get-tuple-element.118), channel_id=1, source_target_pairs={{0,1},{1,0},{2,3},{3,2},{4,5},{5,4},{6,7},{7,6},{8,9},{9,8},{10,11... | collective-permute-start | bytes 1544 | tf_op jit(solution)/shard_map/ppermute | solution.py:16
  18.1 745.5 %all-gather.7.cloned.1.call-start = ((), (), s32[]{:S(2)}) async-start(), calls=%async_computation.1 | async-start | bytes 17301504 | tf_op jit(solution)/shard_map/all_gather | solution.py:381
  28.7 43.5 %collective-permute-start.4 = (bf16[64,1536]{1,0:T(8,128)(2,1)}, bf16[64,1536]{1,0:T(8,128)(2,1)}, u32[]{:S(2)}, u32[]{:S(2)}) collective-permute-start(bf16[64,1536]{1,0:T(8,128)(2,1)} %get-tuple-element.93), channel_id=1, source_target_pairs={{0,1},{1,0},{2,3},{3,2},{4,5},{5,4},{6,7},{7,6},{8,9},{9,8},{10,11... | collective-permute-start | bytes 589832 | tf_op jit(solution)/shard_map/ppermute | solution.py:16
  36.4 11.8 %collective-permute-start.21 = (bf16[256,4]{0,1:T(4,128)(2,1)S(1)}, bf16[256,4]{0,1:T(4,128)(2,1)S(1)}, u32[]{:S(2)}, u32[]{:S(2)}) collective-permute-start(bf16[256,4]{0,1:T(4,128)(2,1)S(1)} %collective-permute-done.19), channel_id=1, source_target_pairs={{0,4},{8,0},{16,8},{24,16},{28,24},{20,28},{12,20},{4,12},{1,5},{9... | collective-permute-start | bytes 6152 | tf_op jit(solution)/shard_map/ppermute | solution.py:75
  38.2 11.8 %collective-permute-start.20 = (bf16[256,4]{0,1:T(4,128)(2,1)S(1)}, bf16[256,4]{0,1:T(4,128)(2,1)}, u32[]{:S(2)}, u32[]{:S(2)}) collective-permute-start(bf16[256,4]{0,1:T(4,128)(2,1)S(1)} %collective-permute-done.18), channel_id=1, source_target_pairs={{0,8},{8,16},{16,24},{24,28},{28,20},{20,12},{12,4},{4,0},{1,9},{9... | collective-permute-start | bytes 6152 | tf_op jit(solution)/shard_map/ppermute | solution.py:75
  48.3 16.9 %collective-permute-start.23 = (bf16[256,4]{0,1:T(4,128)(2,1)S(1)}, bf16[256,4]{0,1:T(4,128)(2,1)S(1)}, u32[]{:S(2)}, u32[]{:S(2)}) collective-permute-start(bf16[256,4]{0,1:T(4,128)(2,1)S(1)} %collective-permute-done.21), channel_id=1, source_target_pairs={{0,4},{8,0},{16,8},{24,16},{28,24},{20,28},{12,20},{4,12},{1,5},{9... | collective-permute-start | bytes 6152 | tf_op jit(solution)/shard_map/ppermute | solution.py:75
  50.0 17.0 %collective-permute-start.22 = (bf16[256,4]{0,1:T(4,128)(2,1)}, bf16[256,4]{0,1:T(4,128)(2,1)S(1)}, u32[]{:S(2)}, u32[]{:S(2)}) collective-permute-start(bf16[256,4]{0,1:T(4,128)(2,1)} %collective-permute-done.20), channel_id=1, source_target_pairs={{0,8},{8,16},{16,24},{24,28},{28,20},{20,12},{12,4},{4,0},{1,9},{9... | collective-permute-start | bytes 6152 | tf_op jit(solution)/shard_map/ppermute | solution.py:75
  68.8 20.1 %collective-permute-start.6 = (bf16[64,1536]{1,0:T(8,128)(2,1)S(1)}, bf16[64,1536]{1,0:T(8,128)(2,1)S(1)}, u32[]{:S(2)}, u32[]{:S(2)}) collective-permute-start(bf16[64,1536]{1,0:T(8,128)(2,1)S(1)} %get-tuple-element.91), channel_id=1, source_target_pairs={{0,3},{1,2},{2,1},{3,0},{4,7},{5,6},{6,5},{7,4},{8,11},{9,10},{10,... | collective-permute-start | bytes 589832 | tf_op jit(solution)/shard_map/ppermute | solution.py:16
  70.5 17.7 %collective-permute-start.5 = (bf16[64,1536]{1,0:T(8,128)(2,1)S(1)}, bf16[64,1536]{1,0:T(8,128)(2,1)S(1)}, u32[]{:S(2)}, u32[]{:S(2)}) collective-permute-start(bf16[64,1536]{1,0:T(8,128)(2,1)S(1)} %get-tuple-element.92), channel_id=1, source_target_pairs={{0,2},{1,3},{2,0},{3,1},{4,6},{5,7},{6,4},{7,5},{8,10},{9,11},{10,... | collective-permute-start | bytes 589832 | tf_op jit(solution)/shard_map/ppermute | solution.py:16
  89.6 24.8 %collective-permute-start.8 = (bf16[256,1536]{1,0:T(8,128)(2,1)}, bf16[256,1536]{1,0:T(8,128)(2,1)}, u32[]{:S(2)}, u32[]{:S(2)}) collective-permute-start(bf16[256,1536]{1,0:T(8,128)(2,1)} %constant_dynamic-update-slice_fusion.18), channel_id=1, source_target_pairs={{0,4},{8,0},{16,8},{24,16},{28,24},{20,28},{12,20},{4,12},{1,5},{9... | collective-permute-start | bytes 2359304 | tf_op jit(solution)/shard_map/ppermute | solution.py:75
  91.1 23.4 %collective-permute-start.7 = (bf16[256,1536]{1,0:T(8,128)(2,1)}, bf16[256,1536]{1,0:T(8,128)(2,1)}, u32[]{:S(2)}, u32[]{:S(2)}) collective-permute-start(bf16[256,1536]{1,0:T(8,128)(2,1)} %constant_dynamic-update-slice_fusion.18), channel_id=1, source_target_pairs={{0,8},{8,16},{16,24},{24,28},{28,20},{20,12},{12,4},{4,0},{1,9},{9... | collective-permute-start | bytes 2359304 | tf_op jit(solution)/shard_map/ppermute | solution.py:75
  92.3 26.7 %collective-permute-start.2 = (bf16[1,136,2048]{2,1,0:T(8,128)(2,1)}, bf16[1,136,2048]{2,1,0:T(8,128)(2,1)S(1)}, u32[]{:S(2)}, u32[]{:S(2)}) collective-permute-start(bf16[1,136,2048]{2,1,0:T(8,128)(2,1)} %collective-permute-done.1), channel_id=1, source_target_pairs={{0,1},{1,0},{2,3},{3,2},{4,5},{5,4},{6,7},{7,6},{8,9},{9,8},{10,11... | collective-permute-start | bytes 1671176 | tf_op jit(solution)/shard_map/ppermute | solution.py:16
  114.5 30.8 %collective-permute-start.10 = (bf16[256,1536]{1,0:T(8,128)(2,1)}, bf16[256,1536]{1,0:T(8,128)(2,1)}, u32[]{:S(2)}, u32[]{:S(2)}) collective-permute-start(bf16[256,1536]{1,0:T(8,128)(2,1)} %collective-permute-done.8), channel_id=1, source_target_pairs={{0,4},{8,0},{16,8},{24,16},{28,24},{20,28},{12,20},{4,12},{1,5},{9... | collective-permute-start | bytes 2359304 | tf_op jit(solution)/shard_map/ppermute | solution.py:75
  114.5 34.2 %collective-permute-start.9 = (bf16[256,1536]{1,0:T(8,128)(2,1)}, bf16[256,1536]{1,0:T(8,128)(2,1)}, u32[]{:S(2)}, u32[]{:S(2)}) collective-permute-start(bf16[256,1536]{1,0:T(8,128)(2,1)} %collective-permute-done.7), channel_id=1, source_target_pairs={{0,8},{8,16},{16,24},{24,28},{28,20},{20,12},{12,4},{4,0},{1,9},{9... | collective-permute-start | bytes 2359304 | tf_op jit(solution)/shard_map/ppermute | solution.py:75
  119.0 17.9 %collective-permute-start.3 = (bf16[16,2048]{1,0:T(8,128)(2,1)S(1)}, bf16[16,2048]{1,0:T(8,128)(2,1)S(1)}, u32[]{:S(2)}, u32[]{:S(2)}) collective-permute-start(bf16[16,2048]{1,0:T(8,128)(2,1)S(1)} %slice_bitcast_fusion.66), channel_id=1, source_target_pairs={{0,4},{4,8},{8,12},{12,16},{16,20},{20,24},{24,28},{1,5},{5,9},{9,... | collective-permute-start | bytes 196616 | tf_op jit(solution)/shard_map/ppermute | solution.py:127
  145.2 42.3 %collective-permute-start.12 = (bf16[256,1536]{1,0:T(8,128)(2,1)}, bf16[256,1536]{1,0:T(8,128)(2,1)S(1)}, u32[]{:S(2)}, u32[]{:S(2)}) collective-permute-start(bf16[256,1536]{1,0:T(8,128)(2,1)} %collective-permute-done.10), channel_id=1, source_target_pairs={{0,4},{8,0},{16,8},{24,16},{28,24},{20,28},{12,20},{4,12},{1,5},{9... | collective-permute-start | bytes 2359304 | tf_op jit(solution)/shard_map/ppermute | solution.py:75
  148.7 39.0 %collective-permute-start.11 = (bf16[256,1536]{1,0:T(8,128)(2,1)}, bf16[256,1536]{1,0:T(8,128)(2,1)S(1)}, u32[]{:S(2)}, u32[]{:S(2)}) collective-permute-start(bf16[256,1536]{1,0:T(8,128)(2,1)} %collective-permute-done.9), channel_id=1, source_target_pairs={{0,8},{8,16},{16,24},{24,28},{28,20},{20,12},{12,4},{4,0},{1,9},{9... | collective-permute-start | bytes 2359304 | tf_op jit(solution)/shard_map/ppermute | solution.py:75
  187.6 18.2 %collective-permute-start.14 = (bf16[128,1536]{1,0:T(8,128)(2,1)S(1)}, bf16[128,1536]{1,0:T(8,128)(2,1)S(1)}, u32[]{:S(2)}, u32[]{:S(2)}) collective-permute-start(bf16[128,1536]{1,0:T(8,128)(2,1)S(1)} %slice.498), channel_id=1, source_target_pairs={{0,4},{8,0},{16,8},{24,16},{28,24},{20,28},{12,20},{4,12},{1,5},{9... | collective-permute-start | bytes 1179656 | tf_op jit(solution)/shard_map/ppermute | solution.py:75
  187.7 18.1 %collective-permute-start.13 = (bf16[128,1536]{1,0:T(8,128)(2,1)S(1)}, bf16[128,1536]{1,0:T(8,128)(2,1)S(1)}, u32[]{:S(2)}, u32[]{:S(2)}) collective-permute-start(bf16[128,1536]{1,0:T(8,128)(2,1)S(1)} %slice.497), channel_id=1, source_target_pairs={{0,8},{8,16},{16,24},{24,28},{28,20},{20,12},{12,4},{4,0},{1,9},{9... | collective-permute-start | bytes 1179656 | tf_op jit(solution)/shard_map/ppermute | solution.py:75
  280.1 10.8 %collective-permute-start.27 = (bf16[2,4,128,128]{3,2,1,0:T(8,128)(2,1)}, bf16[2,4,128,128]{3,2,1,0:T(8,128)(2,1)}, u32[]{:S(2)}, u32[]{:S(2)}) collective-permute-start(bf16[2,4,128,128]{3,2,1,0:T(8,128)(2,1)} %pad_maximum_fusion.6), channel_id=1, source_target_pairs={{0,4},{8,0},{16,8},{24,16},{28,24},{20,28},{12,20},{4,12},{1,5},{9... | collective-permute-start | bytes 786440 | tf_op jit(solution)/shard_map/ppermute | solution.py:75
  282.7 12.6 %collective-permute-start.26 = (bf16[2,4,128,128]{3,2,1,0:T(8,128)(2,1)}, bf16[2,4,128,128]{3,2,1,0:T(8,128)(2,1)}, u32[]{:S(2)}, u32[]{:S(2)}) collective-permute-start(bf16[2,4,128,128]{3,2,1,0:T(8,128)(2,1)} %pad_maximum_fusion.6), channel_id=1, source_target_pairs={{0,8},{8,16},{16,24},{24,28},{28,20},{20,12},{12,4},{4,0},{1,9},{9... | collective-permute-start | bytes 786440 | tf_op jit(solution)/shard_map/ppermute | solution.py:75
  328.6 19.3 %collective-permute-start.35 = (bf16[512,512]{1,0:T(8,128)(2,1)}, bf16[512,512]{1,0:T(8,128)(2,1)}, u32[]{:S(2)}, u32[]{:S(2)}) collective-permute-start(bf16[512,512]{1,0:T(8,128)(2,1)} %get-tuple-element.57), channel_id=1, source_target_pairs={{0,2},{1,3},{2,0},{3,1},{4,6},{5,7},{6,4},{7,5},{8,10},{9,11},{10,... | collective-permute-start | bytes 1572872 | tf_op jit(solution)/shard_map/ppermute | solution.py:16
  333.5 19.2 %collective-permute-start.34 = (bf16[512,512]{1,0:T(8,128)(2,1)}, bf16[512,512]{1,0:T(8,128)(2,1)}, u32[]{:S(2)}, u32[]{:S(2)}) collective-permute-start(bf16[512,512]{1,0:T(8,128)(2,1)} %get-tuple-element.57), channel_id=1, source_target_pairs={{0,1},{1,0},{2,3},{3,2},{4,5},{5,4},{6,7},{7,6},{8,9},{9,8},{10,11... | collective-permute-start | bytes 1572872 | tf_op jit(solution)/shard_map/ppermute | solution.py:16
  385.8 25.9 %collective-permute-start.37 = (bf16[2,128,2048]{2,1,0:T(8,128)(2,1)}, bf16[2,128,2048]{2,1,0:T(8,128)(2,1)S(1)}, u32[]{:S(2)}, u32[]{:S(2)}) collective-permute-start(bf16[2,128,2048]{2,1,0:T(8,128)(2,1)} %dynamic-slice_bitcast_fusion.2), channel_id=1, source_target_pairs={{0,1},{1,0},{2,3},{3,2},{4,5},{5,4},{6,7},{7,6},{8,9},{9,8},{10,11... | collective-permute-start | bytes 3145736 | tf_op jit(solution)/shard_map/ppermute | solution.py:16
  413.4 38.2 %collective-permute-start.38 = (bf16[1,128,2048]{2,1,0:T(8,128)(2,1)S(1)}, bf16[1,128,2048]{2,1,0:T(8,128)(2,1)S(1)}, u32[]{:S(2)}, u32[]{:S(2)}) collective-permute-start(bf16[1,128,2048]{2,1,0:T(8,128)(2,1)S(1)} %dynamic-slice_convert_fusion.2), channel_id=1, source_target_pairs={{0,2},{1,3},{2,0},{3,1},{4,6},{5,7},{6,4},{7,5},{8,10},{9,11},{10,... | collective-permute-start | bytes 1572872 | tf_op jit(solution)/shard_map/ppermute | solution.py:16
  415.8 35.3 %collective-permute-start.40 = (bf16[1,128,2048]{2,1,0:T(8,128)(2,1)S(1)}, bf16[1,128,2048]{2,1,0:T(8,128)(2,1)S(1)}, u32[]{:S(2)}, u32[]{:S(2)}) collective-permute-start(bf16[1,128,2048]{2,1,0:T(8,128)(2,1)S(1)} %dynamic-slice_convert_fusion.1), channel_id=1, source_target_pairs={{0,2},{1,3},{2,0},{3,1},{4,6},{5,7},{6,4},{7,5},{8,10},{9,11},{10,... | collective-permute-start | bytes 1572872 | tf_op jit(solution)/shard_map/ppermute | solution.py:16
  465.4 35.0 %collective-permute-start.71 = (bf16[128,512]{1,0:T(8,128)(2,1)}, bf16[128,512]{1,0:T(8,128)(2,1)}, u32[]{:S(2)}, u32[]{:S(2)}) collective-permute-start(bf16[128,512]{1,0:T(8,128)(2,1)} %bitcast.758), channel_id=1, source_target_pairs={{0,1},{1,0},{2,3},{3,2},{4,5},{5,4},{6,7},{7,6},{8,9},{9,8},{10,11... | collective-permute-start | bytes 393224 | tf_op jit(solution)/shard_map/ppermute | solution.py:16
  465.4 35.9 %collective-permute-start.72 = (bf16[128,512]{1,0:T(8,128)(2,1)}, bf16[128,512]{1,0:T(8,128)(2,1)}, u32[]{:S(2)}, u32[]{:S(2)}) collective-permute-start(bf16[128,512]{1,0:T(8,128)(2,1)} %bitcast.757), channel_id=1, source_target_pairs={{0,2},{1,3},{2,0},{3,1},{4,6},{5,7},{6,4},{7,5},{8,10},{9,11},{10,... | collective-permute-start | bytes 393224 | tf_op jit(solution)/shard_map/ppermute | solution.py:16
  466.5 35.6 %collective-permute-start.73 = (bf16[128,512]{1,0:T(8,128)(2,1)}, bf16[128,512]{1,0:T(8,128)(2,1)}, u32[]{:S(2)}, u32[]{:S(2)}) collective-permute-start(bf16[128,512]{1,0:T(8,128)(2,1)} %bitcast.756), channel_id=1, source_target_pairs={{0,3},{1,2},{2,1},{3,0},{4,7},{5,6},{6,5},{7,4},{8,11},{9,10},{10,... | collective-permute-start | bytes 393224 | tf_op jit(solution)/shard_map/ppermute | solution.py:16
  468.7 11.6 %collective-permute-start.42 = (bf16[128,512]{1,0:T(8,128)(2,1)S(1)}, bf16[128,512]{1,0:T(8,128)(2,1)S(1)}, u32[]{:S(2)}, u32[]{:S(2)}) collective-permute-start(bf16[128,512]{1,0:T(8,128)(2,1)S(1)} %bitcast.867), channel_id=1, source_target_pairs={{0,2},{1,3},{2,0},{3,1},{4,6},{5,7},{6,4},{7,5},{8,10},{9,11},{10,... | collective-permute-start | bytes 393224 | tf_op jit(solution)/shard_map/ppermute | solution.py:16
  471.5 13.5 %collective-permute-start.43 = (bf16[128,512]{1,0:T(8,128)(2,1)S(1)}, bf16[128,512]{1,0:T(8,128)(2,1)S(1)}, u32[]{:S(2)}, u32[]{:S(2)}) collective-permute-start(bf16[128,512]{1,0:T(8,128)(2,1)S(1)} %bitcast.869), channel_id=1, source_target_pairs={{0,3},{1,2},{2,1},{3,0},{4,7},{5,6},{6,5},{7,4},{8,11},{9,10},{10,... | collective-permute-start | bytes 393224 | tf_op jit(solution)/shard_map/ppermute | solution.py:16
  498.1 24.1 %collective-permute-start.44 = (bf16[4,128,128]{2,1,0:T(8,128)(2,1)S(1)}, bf16[4,128,128]{2,1,0:T(8,128)(2,1)S(1)}, u32[]{:S(2)}, u32[]{:S(2)}) collective-permute-start(bf16[4,128,128]{2,1,0:T(8,128)(2,1)S(1)} %get-tuple-element.141), channel_id=1, source_target_pairs={{0,8},{8,16},{16,24},{24,28},{28,20},{20,12},{12,4},{4,0},{1,9},{9... | collective-permute-start | bytes 393224 | tf_op jit(solution)/shard_map/ppermute | solution.py:75
  498.1 24.2 %collective-permute-start.45 = (bf16[4,128,128]{2,1,0:T(8,128)(2,1)S(1)}, bf16[4,128,128]{2,1,0:T(8,128)(2,1)S(1)}, u32[]{:S(2)}, u32[]{:S(2)}) collective-permute-start(bf16[4,128,128]{2,1,0:T(8,128)(2,1)S(1)} %get-tuple-element.141), channel_id=1, source_target_pairs={{0,4},{8,0},{16,8},{24,16},{28,24},{20,28},{12,20},{4,12},{1,5},{9... | collective-permute-start | bytes 393224 | tf_op jit(solution)/shard_map/ppermute | solution.py:75
  506.2 13.0 %collective-permute-start.74 = (bf16[128,512]{1,0:T(8,128)(2,1)S(1)}, bf16[128,512]{1,0:T(8,128)(2,1)S(1)}, u32[]{:S(2)}, u32[]{:S(2)}) collective-permute-start(bf16[128,512]{1,0:T(8,128)(2,1)S(1)} %get-tuple-element.83), channel_id=1, source_target_pairs={{0,8},{8,16},{16,24},{24,28},{28,20},{20,12},{12,4},{4,0},{1,9},{9... | collective-permute-start | bytes 393224 | tf_op jit(solution)/shard_map/ppermute | solution.py:75
  506.4 12.9 %collective-permute-start.78 = (bf16[128,512]{1,0:T(8,128)(2,1)S(1)}, bf16[128,512]{1,0:T(8,128)(2,1)S(1)}, u32[]{:S(2)}, u32[]{:S(2)}) collective-permute-start(bf16[128,512]{1,0:T(8,128)(2,1)S(1)} %get-tuple-element.85), channel_id=1, source_target_pairs={{0,4},{8,0},{16,8},{24,16},{28,24},{20,28},{12,20},{4,12},{1,5},{9... | collective-permute-start | bytes 393224 | tf_op jit(solution)/shard_map/ppermute | solution.py:75
  520.1 126.2 %collective-permute-start.79 = (bf16[256,512]{1,0:T(8,128)(2,1)}, bf16[256,512]{1,0:T(8,128)(2,1)}, u32[]{:S(2)}, u32[]{:S(2)}) collective-permute-start(bf16[256,512]{1,0:T(8,128)(2,1)} %pad_maximum_fusion.8), channel_id=1, source_target_pairs={{0,4},{8,0},{16,8},{24,16},{28,24},{20,28},{12,20},{4,12},{1,5},{9... | collective-permute-start | bytes 786440 | tf_op jit(solution)/shard_map/ppermute | solution.py:75
  521.9 21.0 %collective-permute-start.75 = (bf16[256,512]{1,0:T(8,128)(2,1)S(1)}, bf16[256,512]{1,0:T(8,128)(2,1)S(1)}, u32[]{:S(2)}, u32[]{:S(2)}) collective-permute-start(bf16[256,512]{1,0:T(8,128)(2,1)S(1)} %pad_maximum_fusion.7), channel_id=1, source_target_pairs={{0,8},{8,16},{16,24},{24,28},{28,20},{20,12},{12,4},{4,0},{1,9},{9... | collective-permute-start | bytes 786440 | tf_op jit(solution)/shard_map/ppermute | solution.py:75
  522.2 12.1 %collective-permute-start.46 = (bf16[4,128,128]{2,1,0:T(8,128)(2,1)S(1)}, bf16[4,128,128]{2,1,0:T(8,128)(2,1)S(1)}, u32[]{:S(2)}, u32[]{:S(2)}) collective-permute-start(bf16[4,128,128]{2,1,0:T(8,128)(2,1)S(1)} %collective-permute-done.44), channel_id=1, source_target_pairs={{0,8},{8,16},{16,24},{24,28},{28,20},{20,12},{12,4},{4,0},{1,9},{9... | collective-permute-start | bytes 393224 | tf_op jit(solution)/shard_map/ppermute | solution.py:75
  522.3 14.4 %collective-permute-start.47 = (bf16[4,128,128]{2,1,0:T(8,128)(2,1)S(1)}, bf16[4,128,128]{2,1,0:T(8,128)(2,1)S(1)}, u32[]{:S(2)}, u32[]{:S(2)}) collective-permute-start(bf16[4,128,128]{2,1,0:T(8,128)(2,1)S(1)} %collective-permute-done.45), channel_id=1, source_target_pairs={{0,4},{8,0},{16,8},{24,16},{28,24},{20,28},{12,20},{4,12},{1,5},{9... | collective-permute-start | bytes 393224 | tf_op jit(solution)/shard_map/ppermute | solution.py:75
  543.8 102.6 %collective-permute-start.76 = (bf16[256,512]{1,0:T(8,128)(2,1)}, bf16[256,512]{1,0:T(8,128)(2,1)}, u32[]{:S(2)}, u32[]{:S(2)}) collective-permute-start(bf16[256,512]{1,0:T(8,128)(2,1)} %fusion.159), channel_id=1, source_target_pairs={{0,8},{8,16},{16,24},{24,28},{28,20},{20,12},{12,4},{4,0},{1,9},{9... | collective-permute-start | bytes 786440 | tf_op jit(solution)/shard_map/ppermute | solution.py:75
  611.8 10.9 %collective-permute-start.52 = (bf16[3,3,512]{0,2,1:T(8,128)(2,1)S(1)}, bf16[3,3,512]{0,2,1:T(8,128)(2,1)S(1)}, u32[]{:S(2)}, u32[]{:S(2)}) collective-permute-start(bf16[3,3,512]{0,2,1:T(8,128)(2,1)S(1)} %slice.724), channel_id=1, source_target_pairs={{4,0},{8,4},{12,8},{16,12},{20,16},{24,20},{28,24},{5,1},{9,5},{13... | collective-permute-start | bytes 27656 | tf_op jit(solution)/shard_map/ppermute | solution.py:127
  614.3 20.0 %collective-permute-start.85 = (f32[120,128]{1,0:T(8,128)S(1)}, f32[120,128]{1,0:T(8,128)S(1)}, u32[]{:S(2)}, u32[]{:S(2)}) collective-permute-start(f32[120,128]{1,0:T(8,128)S(1)} %fusion.214), channel_id=1, source_target_pairs={{0,4},{4,0},{8,12},{12,8},{16,20},{20,16},{24,28},{28,24},{1,5},{5... | collective-permute-start | bytes 184328 | tf_op jit(solution)/shard_map/ppermute | solution.py:16
  637.3 41.7 %collective-permute-start.53 = (bf16[2,128,2048]{2,1,0:T(8,128)(2,1)}, bf16[2,128,2048]{2,1,0:T(8,128)(2,1)}, u32[]{:S(2)}, u32[]{:S(2)}) collective-permute-start(bf16[2,128,2048]{2,1,0:T(8,128)(2,1)} %dynamic-slice_bitcast_fusion), channel_id=1, source_target_pairs={{0,1},{1,0},{2,3},{3,2},{4,5},{5,4},{6,7},{7,6},{8,9},{9,8},{10,11... | collective-permute-start | bytes 3145736 | tf_op jit(solution)/shard_map/ppermute | solution.py:16
  641.3 16.6 %collective-permute-start.60 = (bf16[128,1536]{1,0:T(8,128)(2,1)}, bf16[128,1536]{1,0:T(8,128)(2,1)S(1)}, u32[]{:S(2)}, u32[]{:S(2)}) collective-permute-start(bf16[128,1536]{1,0:T(8,128)(2,1)} %get-tuple-element.62), channel_id=1, source_target_pairs={{0,8},{8,16},{16,24},{24,28},{28,20},{20,12},{12,4},{4,0},{1,9},{9... | collective-permute-start | bytes 1179656 | tf_op jit(solution)/shard_map/ppermute | solution.py:75
  643.8 14.1 %collective-permute-start.64 = (bf16[128,1536]{1,0:T(8,128)(2,1)}, bf16[128,1536]{1,0:T(8,128)(2,1)}, u32[]{:S(2)}, u32[]{:S(2)}) collective-permute-start(bf16[128,1536]{1,0:T(8,128)(2,1)} %get-tuple-element.64), channel_id=1, source_target_pairs={{0,4},{8,0},{16,8},{24,16},{28,24},{20,28},{12,20},{4,12},{1,5},{9... | collective-permute-start | bytes 1179656 | tf_op jit(solution)/shard_map/ppermute | solution.py:75
  651.0 15.4 %collective-permute-start.77 = (bf16[256,512]{1,0:T(8,128)(2,1)}, bf16[256,512]{1,0:T(8,128)(2,1)}, u32[]{:S(2)}, u32[]{:S(2)}) collective-permute-start(bf16[256,512]{1,0:T(8,128)(2,1)} %get-tuple-element.79), channel_id=1, source_target_pairs={{0,8},{8,16},{16,24},{24,28},{28,20},{20,12},{12,4},{4,0},{1,9},{9... | collective-permute-start | bytes 786440 | tf_op jit(solution)/shard_map/ppermute | solution.py:75
  662.5 9.3 collective-permute-start.81
  664.2 33.0 %collective-permute-start.65 = (bf16[256,1536]{1,0:T(8,128)(2,1)S(1)}, bf16[256,1536]{1,0:T(8,128)(2,1)S(1)}, u32[]{:S(2)}, u32[]{:S(2)}) collective-permute-start(bf16[256,1536]{1,0:T(8,128)(2,1)S(1)} %pad_maximum_fusion.5), channel_id=1, source_target_pairs={{0,4},{8,0},{16,8},{24,16},{28,24},{20,28},{12,20},{4,12},{1,5},{9... | collective-permute-start | bytes 2359304 | tf_op jit(solution)/shard_map/ppermute | solution.py:75
  665.6 18.3 %collective-permute-start.61 = (bf16[256,1536]{1,0:T(8,128)(2,1)S(1)}, bf16[256,1536]{1,0:T(8,128)(2,1)S(1)}, u32[]{:S(2)}, u32[]{:S(2)}) collective-permute-start(bf16[256,1536]{1,0:T(8,128)(2,1)S(1)} %pad_maximum_fusion.4), channel_id=1, source_target_pairs={{0,8},{8,16},{16,24},{24,28},{28,20},{20,12},{12,4},{4,0},{1,9},{9... | collective-permute-start | bytes 2359304 | tf_op jit(solution)/shard_map/ppermute | solution.py:75
  673.0 31.4 %collective-permute-start.84 = (bf16[64,512]{1,0:T(8,128)(2,1)S(1)}, bf16[64,512]{1,0:T(8,128)(2,1)S(1)}, u32[]{:S(2)}, u32[]{:S(2)}) collective-permute-start(bf16[64,512]{1,0:T(8,128)(2,1)S(1)} %get-tuple-element.102), channel_id=1, source_target_pairs={{0,3},{1,2},{2,1},{3,0},{4,7},{5,6},{6,5},{7,4},{8,11},{9,10},{10,... | collective-permute-start | bytes 196616 | tf_op jit(solution)/shard_map/ppermute | solution.py:16
  680.7 14.2 %collective-permute-start.54 = (bf16[1,128,2048]{2,1,0:T(8,128)(2,1)S(1)}, bf16[1,128,2048]{2,1,0:T(8,128)(2,1)S(1)}, u32[]{:S(2)}, u32[]{:S(2)}) collective-permute-start(bf16[1,128,2048]{2,1,0:T(8,128)(2,1)S(1)} %dynamic-slice_convert_fusion), channel_id=1, source_target_pairs={{0,2},{1,3},{2,0},{3,1},{4,6},{5,7},{6,4},{7,5},{8,10},{9,11},{10,... | collective-permute-start | bytes 1572872 | tf_op jit(solution)/shard_map/ppermute | solution.py:16
  684.1 17.7 %collective-permute-start.62 = (bf16[256,1536]{1,0:T(8,128)(2,1)S(1)}, bf16[256,1536]{1,0:T(8,128)(2,1)S(1)}, u32[]{:S(2)}, u32[]{:S(2)}) collective-permute-start(bf16[256,1536]{1,0:T(8,128)(2,1)S(1)} %fusion.38), channel_id=1, source_target_pairs={{0,8},{8,16},{16,24},{24,28},{28,20},{20,12},{12,4},{4,0},{1,9},{9... | collective-permute-start | bytes 2359304 | tf_op jit(solution)/shard_map/ppermute | solution.py:75
  702.2 21.8 %collective-permute-start.66 = (bf16[256,1536]{1,0:T(8,128)(2,1)S(1)}, bf16[256,1536]{1,0:T(8,128)(2,1)S(1)}, u32[]{:S(2)}, u32[]{:S(2)}) collective-permute-start(bf16[256,1536]{1,0:T(8,128)(2,1)S(1)} %get-tuple-element.59), channel_id=1, source_target_pairs={{0,4},{8,0},{16,8},{24,16},{28,24},{20,28},{12,20},{4,12},{1,5},{9... | collective-permute-start | bytes 2359304 | tf_op jit(solution)/shard_map/ppermute | solution.py:75
  703.3 15.8 %collective-permute-start.56 = (f32[40,128]{1,0:T(8,128)S(1)}, f32[40,128]{1,0:T(8,128)S(1)}, u32[]{:S(2)}, u32[]{:S(2)}) collective-permute-start(f32[40,128]{1,0:T(8,128)S(1)} %fusion.247), channel_id=1, source_target_pairs={{0,8},{4,12},{8,0},{12,4},{16,24},{20,28},{24,16},{28,20},{1,9},{5... | collective-permute-start | bytes 61448 | tf_op jit(solution)/shard_map/ppermute | solution.py:16
  723.9 20.0 %collective-permute-start.63 = (bf16[256,1536]{1,0:T(8,128)(2,1)S(1)}, bf16[256,1536]{1,0:T(8,128)(2,1)S(1)}, u32[]{:S(2)}, u32[]{:S(2)}) collective-permute-start(bf16[256,1536]{1,0:T(8,128)(2,1)S(1)} %get-tuple-element.58), channel_id=1, source_target_pairs={{0,8},{8,16},{16,24},{24,28},{28,20},{20,12},{12,4},{4,0},{1,9},{9... | collective-permute-start | bytes 2359304 | tf_op jit(solution)/shard_map/ppermute | solution.py:75
  724.2 19.9 %collective-permute-start.67 = (bf16[256,1536]{1,0:T(8,128)(2,1)S(1)}, bf16[256,1536]{1,0:T(8,128)(2,1)S(1)}, u32[]{:S(2)}, u32[]{:S(2)}) collective-permute-start(bf16[256,1536]{1,0:T(8,128)(2,1)S(1)} %fusion.37), channel_id=1, source_target_pairs={{0,4},{8,0},{16,8},{24,16},{28,24},{20,28},{12,20},{4,12},{1,5},{9... | collective-permute-start | bytes 2359304 | tf_op jit(solution)/shard_map/ppermute | solution.py:75
  745.3 12.4 %collective-permute-start.70 = (bf16[64,1536]{1,0:T(8,128)(2,1)}, bf16[64,1536]{1,0:T(8,128)(2,1)S(1)}, u32[]{:S(2)}, u32[]{:S(2)}) collective-permute-start(bf16[64,1536]{1,0:T(8,128)(2,1)} %get-tuple-element.87), channel_id=1, source_target_pairs={{0,3},{1,2},{2,1},{3,0},{4,7},{5,6},{6,5},{7,4},{8,11},{9,10},{10,... | collective-permute-start | bytes 589832 | tf_op jit(solution)/shard_map/ppermute | solution.py:16
  745.7 10.8 %collective-permute-start.69 = (bf16[64,1536]{1,0:T(8,128)(2,1)}, bf16[64,1536]{1,0:T(8,128)(2,1)S(1)}, u32[]{:S(2)}, u32[]{:S(2)}) collective-permute-start(bf16[64,1536]{1,0:T(8,128)(2,1)} %get-tuple-element.88), channel_id=1, source_target_pairs={{0,2},{1,3},{2,0},{3,1},{4,6},{5,7},{6,4},{7,5},{8,10},{9,11},{10,... | collective-permute-start | bytes 589832 | tf_op jit(solution)/shard_map/ppermute | solution.py:16
  (178 other events, 2037.5 us)
Sparse Core Ops, SparseCore 0:
  10.9 92.1 all-gather.8
  106.0 140.5 all-gather.4
  410.3 121.6 all-gather.6

commit v2 on v1

v2 whole, which is shorter than its diff:
```python
import functools

import jax
import jax.numpy as jnp
from jax import lax
from jax.experimental import pallas as pl
from jax.experimental.pallas import tpu as pltpu
from jax.sharding import PartitionSpec as P

NORM_EPS = 1e-06
HEAD_EPS = 1e-05
UNIT_EPS = 1e-06
BOTH = ("dev", "ta")
BF = jnp.bfloat16
F32 = jnp.float32


def swap(x, axis, bit):
    return lax.ppermute(x, axis, [(i, i ^ bit) for i in range(lax.axis_size(axis))])


def gather_parts(x):
    parts = [x]
    for j in range(1, lax.axis_size("ta")):
        bit = j & -j
        parts.append(swap(parts[j ^ bit], "ta", bit))
    return parts


def in_order(parts, rank, axis):
    size = parts[0].shape[axis]
    shape = list(parts[0].shape)
    shape[axis] = size * len(parts)
    joined = jnp.zeros(shape, parts[0].dtype)
    for j, part in enumerate(parts):
        joined = lax.dynamic_update_slice_in_dim(joined, part, (rank ^ j) * size, axis)
    return joined


def exchange(blocks, rank):
    lanes = lax.axis_size("ta")
    parts = []
    for j in range(lanes):
        block = lax.dynamic_index_in_dim(blocks, rank ^ j, 0, False)
        parts.append(swap(block, "ta", j) if j else block)
    return parts


def scatter_sum(blocks, rank, beside=None):
    lanes = lax.axis_size("ta")
    made = None
    bit = 1
    while bit < lanes:
        pairs = blocks.reshape((blocks.shape[0] // 2, 2) + blocks.shape[1:])
        mine = (rank // bit) % 2
        kept = lax.dynamic_index_in_dim(pairs, mine, 1, False)
        sent = lax.dynamic_index_in_dim(pairs, 1 - mine, 1, False).astype(BF)
        arrived = swap(sent, "ta", bit)
        bit *= 2
        if beside and bit == lanes:
            made = beside(sent)
            arrived = gate(arrived, made[0])
        blocks = kept.astype(F32) + arrived.astype(F32)
    return (blocks[0], made) if beside else blocks[0]


def ring_order(size):
    if size % 2:
        return list(range(size))
    return list(range(0, size, 2)) + list(range(size - 1, 0, -2))


class Ring:
    def __init__(self):
        self.size = lax.axis_size("dev")
        self.order = ring_order(self.size)
        self.spot = [self.order.index(i) for i in range(self.size)]
        self.place = lax.axis_index("dev")

    def move(self, x, step):
        n = self.size
        return lax.ppermute(x, "dev", [(self.order[p], self.order[(p + step) % n]) for p in range(n)])

    def at(self, distance):
        n = self.size
        table = jnp.array([self.order[(self.spot[i] + distance) % n] for i in range(n)], jnp.int32)
        return table[self.place]

    def gather(self, x):
        last = self.size // 2
        half = x.shape[0] // 2
        joined = jnp.zeros((self.size,) + x.shape, x.dtype)

        def put_at(joined, part, distance):
            return lax.dynamic_update_index_in_dim(joined, part, self.at(distance), 0)

        joined = put_at(joined, x, 0)
        onward, back = x, x
        for s in range(1, last):
            onward, back = self.move(onward, 1), self.move(back, -1)
            joined = put_at(put_at(joined, onward, -s), back, s)
        far = [self.move(onward[:half], 1), self.move(back[half:], -1)]
        return put_at(joined, jnp.concatenate(far, axis=0), last)

    def scatter(self, blocks, beside=()):
        last = self.size // 2
        half = blocks.shape[1] // 2
        beside = list(beside) + [None] * last

        def block(distance):
            return lax.dynamic_index_in_dim(blocks, self.at(distance), 0, False)

        far = block(last)
        right, left = far[:half], far[half:]
        for s in range(last - 1, -1, -1):
            ahead, behind = self.move(right, 1), self.move(left, -1)
            if beside[last - 1 - s]:
                token = beside[last - 1 - s](right)
                ahead, behind = gate(ahead, token), gate(behind, token)
            ahead, behind = ahead.astype(F32), behind.astype(F32)
            if s:
                right, left = block(s).astype(F32), block(-s).astype(F32)
                if s == last - 1:
                    right = jnp.concatenate([right[:half] + ahead, right[half:]], axis=0)
                    left = jnp.concatenate([left[:half], left[half:] + behind], axis=0)
                else:
                    right, left = right + ahead, left + behind
                right, left = right.astype(BF), left.astype(BF)
        return block(0).astype(F32) + ahead + behind


def gather_dev(x):
    place = lax.axis_index("dev")
    held = x[None]
    bit = 1
    while bit < lax.axis_size("dev"):
        other = swap(held, "dev", bit)
        upper = (place // bit) % 2 == 1
        held = jnp.concatenate([jnp.where(upper, other, held), jnp.where(upper, held, other)], axis=0)
        bit *= 2
    return held


def sum_over(x, axis):
    size = lax.axis_size(axis)
    bit = 1
    while bit < size:
        x = x + swap(x, axis, bit)
        bit *= 2
    return x


def gate(x, *deps):
    return pl.pallas_call(
        lambda *refs: None,
        name="gate",
        out_shape=jax.ShapeDtypeStruct(x.shape, x.dtype),
        in_specs=[pl.BlockSpec(memory_space=pl.ANY)] * (1 + len(deps)),
        out_specs=pl.BlockSpec(memory_space=pl.ANY),
        input_output_aliases={0: 0},
    )(x, *deps)


def shifted(x, distance):
    devices = range(lax.axis_size("dev"))
    return lax.ppermute(x, "dev", [(i - distance, i) for i in devices if i - distance in devices])


def rms_scale(values, gain):
    return values * lax.rsqrt(jnp.mean(values * values, axis=-1, keepdims=True) + NORM_EPS) * gain


def document_of(lengths, positions):
    starts = jnp.cumsum(lengths) - lengths
    above = (starts[None, :] <= positions[:, None]).astype(jnp.int32)
    return jnp.sum(above, axis=1) - 1


def contract_rows(left, right):
    return lax.dot_general(left, right, (((0,), (0,)), ((), ())), preferred_element_type=F32)


def contract_cols(left, right):
    return lax.dot_general(left, right, (((1,), (1,)), ((), ())), preferred_element_type=F32)


def dot(left, right):
    return jnp.dot(left, right, preferred_element_type=F32)


PAD = 8
VMEM_LIMIT = 48 * 1024 * 1024
FFN_VMEM = 56 * 1024 * 1024


def dims(a, b, ca, cb):
    return lax.dot_general(a, b, (((ca,), (cb,)), ((), ())), preferred_element_type=F32)


def d1(a, b, ca=1, cb=0):
    return dims(a.astype(BF), b.astype(BF), ca, cb)


def parts_of(a):
    high = a.astype(BF)
    return high, (a - high.astype(F32)).astype(BF)


def d3(a, b, ca=1, cb=0):
    ah, al = parts_of(a)
    bh, bl = parts_of(b)
    return dims(ah, bh, ca, cb) + (dims(ah, bl, ca, cb) + dims(al, bh, ca, cb))


def iotas(size):
    return (
        lax.broadcasted_iota(jnp.int32, (size, size), 0),
        lax.broadcasted_iota(jnp.int32, (size, size), 1),
    )


def inverses_of(lowers):
    size = lowers[0].shape[0]
    row, col = iotas(size)
    eye = (row == col).astype(F32)
    pair = (row // 2 == col // 2).astype(F32)
    found = [eye - low * pair for low in lowers]
    block = 2
    while block < size:
        joint = ((row // (2 * block) == col // (2 * block)) & (row // block != col // block)).astype(F32)
        steps = [d3(low * joint, x) for low, x in zip(lowers, found)]
        found = [x - d3(x, s) for x, s in zip(found, steps)]
        block *= 2
    return found


def unit_of(active):
    scale = lax.rsqrt(jnp.sum(active * active, axis=-1, keepdims=True) + UNIT_EPS)
    return active * scale, scale


def masks_of(aux, row, at, size):
    doc, doc_row = aux[at, 6:7], row[6:7, at]
    r, c = iotas(size)
    same = doc == doc_row
    weak = (same & (r >= c)).astype(F32)
    strict = (same & (r > c)).astype(F32)
    return weak, strict


def forward_kernel(size, xq, xk, xv, conv, aux_ref, row_ref, yq, yk, yv, inv, plain, reach, read, direct, trans, fresh, whole):
    count = inv.shape[1]
    depth = xq.shape[1]
    ksize = conv.shape[1]
    aux, row = aux_ref.at[0], row_ref.at[0]
    r, c = iotas(depth)
    eye = (r == c).astype(F32)
    spans = [slice(n * size, (n + 1) * size) for n in range(count)]
    saved = []
    lowers = []
    for n, at in enumerate(spans):
        active = []
        for i, (x, y) in enumerate(((xq, yq), (xk, yk), (xv, yv))):
            first = PAD - (ksize - 1) + n * size
            summed = x[first + ksize - 1 : first + ksize - 1 + size, :] * conv[i, ksize - 1 : ksize, :]
            for j in range(ksize - 1):
                summed = summed + x[first + j : first + j + size, :] * conv[i, j : j + 1, :] * aux[at, j : j + 1]
            y[at, :] = summed
            active.append(summed * jax.nn.sigmoid(summed))
        q = unit_of(active[0])[0] * depth ** (-0.5)
        k = unit_of(active[1])[0]
        weak, strict = masks_of(aux, row, at, size)
        rate = row[7:8, at]
        products = d3(jnp.concatenate([q, k], axis=0), k, 1, 1)
        lowers.append(products[size:] * rate * strict)
        saved.append((q, k, active[2], products[:size] * rate * weak))
    inverses = inverses_of(lowers)
    total = added = None
    for n, at in enumerate(spans):
        q, k, v, mix = saved[n]
        cont, clos, beta = aux[at, 3:4], aux[at, 4:5], aux[at, 7:8]
        both = d3(inverses[n], jnp.concatenate([v, k * cont], axis=1))
        spread = d3(mix, both)
        inv[0, n] = inverses[n]
        plain[0, at, :] = both[:, :depth]
        reach[0, at, :] = both[:, depth:]
        direct[0, at, :] = spread[:, :depth]
        read[0, at, :] = q * cont - spread[:, depth:]
        gained = d3(k * (beta * clos), both, 0, 0)
        map_n = aux[(n + 1) * size - 1 : (n + 1) * size, 3:4] * eye - gained[:, depth:]
        add_n = gained[:, :depth]
        trans[0, n] = map_n
        fresh[0, n] = add_n
        if n == 0:
            total, added = map_n, add_n
        else:
            new = d3(map_n, jnp.concatenate([added, total], axis=1))
            total, added = new[:, depth:], new[:, :depth] + add_n
    whole[0, 0] = total.astype(BF)
    whole[0, 1] = added.astype(BF)


def read_kernel(size, place, both, trans, fresh, read, direct, gain, states, outputs, normed):
    heads, count = trans.shape[0], trans.shape[1]
    depth = trans.shape[-1]

    def earlier(i, carry):
        return tuple(
            d3(both[i, h, 0].astype(F32), carry[h]) + both[i, h, 1].astype(F32) for h in range(heads)
        )

    carry = lax.fori_loop(0, place[0], earlier, tuple(jnp.zeros((depth, depth), F32) for _ in range(heads)))
    carry = list(carry)
    for n in range(count):
        at = slice(n * size, (n + 1) * size)
        for h in range(heads):
            state = carry[h]
            states[h, n] = state
            out = direct[h, at, :] + d3(read[h, at, :], state)
            cols = slice(h * depth, (h + 1) * depth)
            outputs[at, cols] = out
            scale = lax.rsqrt(jnp.mean(out * out, axis=-1, keepdims=True) + HEAD_EPS)
            normed[at, cols] = (out * scale * gain[...]).astype(BF)
            if n < count - 1:
                carry[h] = d3(trans[h, n], state) + fresh[h, n]


def leak_kernel(size, grads, outputs, gain, read, trans, grad_out, from_out, leak, grad_gain):
    heads, count = trans.shape[0], trans.shape[1]
    depth = trans.shape[-1]
    gained = jnp.zeros((1, depth), F32)
    totals = [None] * heads
    for n in range(count - 1, -1, -1):
        at = slice(n * size, (n + 1) * size)
        for h in range(heads):
            cols = slice(h * depth, (h + 1) * depth)
            out, grad = outputs[at, cols], grads[at, cols].astype(F32)
            scale = lax.rsqrt(jnp.mean(out * out, axis=-1, keepdims=True) + HEAD_EPS)
            unit = out * scale
            gained = gained + jnp.sum(grad * unit, axis=0, keepdims=True)
            grad = grad * gain[...]
            grad = scale * (grad - unit * jnp.mean(grad * unit, axis=-1, keepdims=True))
            grad_out[h, at, :] = grad
            term = d3(read[h, at, :], grad, 0, 0)
            from_out[h, n] = term
            totals[h] = term if n == count - 1 else d3(trans[h, n], totals[h], 0, 0) + term
    for h in range(heads):
        leak[h] = totals[h].astype(BF)
    grad_gain[...] = gained


def chain_kernel(place, both, leaks, trans, from_out, grads):
    heads, count = trans.shape[0], trans.shape[1]
    depth = trans.shape[-1]
    devices = both.shape[0]

    def later(i, carry):
        at = devices - 1 - i
        return tuple(
            d3(both[at, h, 0].astype(F32), carry[h], 0, 0) + leaks[at, h].astype(F32) for h in range(heads)
        )

    zero = tuple(jnp.zeros((depth, depth), F32) for _ in range(heads))
    carry = list(lax.fori_loop(0, devices - 1 - place[0], later, zero))
    for n in range(count - 1, -1, -1):
        for h in range(heads):
            grads[h, n] = carry[h]
            if n:
                carry[h] = d3(trans[h, n], carry[h], 0, 0) + from_out[h, n]


def backward_kernel(size, xq, xk, xv, yq, yk, yv, conv, aux_ref, row_ref, inv, plain, reach, states, grads, grad_out,
                    gq, gk, gv, tail, spill, grad_conv, grad_beta, zs):
    count = inv.shape[1]
    depth = xq.shape[1]
    ksize = conv.shape[1]
    aux, row = aux_ref.at[0], row_ref.at[0]
    length = count * size
    scale_q = depth ** (-0.5)
    for n in range(count):
        at = slice(n * size, (n + 1) * size)
        cont, clos, beta = aux[at, 3:4], aux[at, 4:5], aux[at, 7:8]
        weak, strict = masks_of(aux, row, at, size)
        rate = row[7:8, at]
        ys = [yq[at, :], yk[at, :], yv[at, :]]
        sigs = [jax.nn.sigmoid(y) for y in ys]
        uq, rq = unit_of(ys[0] * sigs[0])
        k, rk = unit_of(ys[1] * sigs[1])
        q = uq * scale_q
        products = d1(jnp.concatenate([q, k], axis=0), k, 1, 1)
        qk, kk = products[:size], products[size:]
        mix = qk * rate * weak
        state, grad_state, dout = states[0, n], grads[0, n], grad_out[0, at, :]
        u = plain[0, at, :] - d1(reach[0, at, :], state)
        kds = d1(k, grad_state)
        written = beta * clos
        du = d1(mix, dout, 0, 0) + written * kds
        dr = d1(inv[0, n], du, 0, 0)
        pair = jnp.concatenate([dout, dr], axis=0)
        outer = d1(pair, u, 1, 1)
        through = d1(pair, state, 1, 1)
        dp = outer[:size] * weak
        dl = -outer[size:] * strict
        per_key = jnp.sum(dp * qk + dl * kk, axis=0, keepdims=True)
        per_state = jnp.sum((kds * u).T, axis=0, keepdims=True)
        grad_beta[0, :, at] = per_key + row[4:5, at] * per_state
        dqk = dp * rate
        da = dl * rate
        dq = cont * through[:size] + d1(dqk, k)
        dk = d1(dqk, q, 0, 0) + written * d1(u, grad_state, 1, 1) - cont * through[size:] + d1(da + da.T, k)
        dq = dq * scale_q
        acts = [
            rq * (dq - uq * jnp.sum(uq * dq, axis=-1, keepdims=True)),
            rk * (dk - k * jnp.sum(k * dk, axis=-1, keepdims=True)),
            dr,
        ]
        for i, x in enumerate((xq, xk, xv)):
            dy = acts[i] * sigs[i] * (1.0 + ys[i] * (1.0 - sigs[i]))
            first = PAD - (ksize - 1) + n * size
            for j in range(ksize):
                dv = dy if j == ksize - 1 else dy * aux[at, j : j + 1]
                term = jnp.sum(dv * x[first + j : first + j + size, :], axis=0, keepdims=True)
                before = jnp.zeros_like(term) if n == 0 else grad_conv[i, j : j + 1, :]
                grad_conv[i, j : j + 1, :] = before + term
                zs[i, j, PAD + n * size : PAD + (n + 1) * size, :] = dv * conv[i, j : j + 1, :]
    for i, g in enumerate((gq, gk, gv)):
        for j in range(ksize):
            zs[i, j, 0:PAD, :] = jnp.zeros((PAD, depth), F32)
            zs[i, j, PAD + length : 2 * PAD + length, :] = jnp.zeros((PAD, depth), F32)

        def shifted_sum(first, rows):
            return sum(zs[i, j, first + ksize - 1 - j : first + ksize - 1 - j + rows, :] for j in range(ksize))

        for n in range(count):
            at = slice(n * size, (n + 1) * size)
            g[at, :] = (shifted_sum(PAD + n * size, size) * aux[at, 5:6]).astype(BF)
        tail[i] = shifted_sum(length, PAD)
        spill[i] = shifted_sum(0, PAD)


def vmem_call(name, kernel, out_shape, inputs, flops, deps=()):
    return pl.pallas_call(
        lambda *refs: kernel(*refs[: len(inputs)], *refs[len(inputs) + len(deps) :]),
        name=name,
        out_shape=out_shape,
        in_specs=[
            pl.BlockSpec(memory_space=pltpu.SMEM if x.dtype == jnp.int32 else pltpu.VMEM) for x in inputs
        ]
        + [pl.BlockSpec(memory_space=pl.ANY)] * len(deps),
        out_specs=[pl.BlockSpec(memory_space=pltpu.VMEM)] * len(out_shape),
        cost_estimate=cost(flops, inputs, out_shape),
        compiler_params=pltpu.CompilerParams(vmem_limit_bytes=VMEM_LIMIT),
    )(*inputs, *deps)


def cost(flops, inputs, outputs):
    moved = sum(x.size * x.dtype.itemsize for x in list(inputs) + list(outputs))
    return pl.CostEstimate(flops=int(flops), bytes_accessed=int(moved), transcendentals=0)


def shape(dims, dtype=F32):
    return jax.ShapeDtypeStruct(dims, dtype)


class Mixer:
    def __init__(self, projected, own_conv, aux, row, size):
        self.size = size
        self.heads, self.length = aux.shape[0], aux.shape[1]
        self.depth = own_conv.shape[2] // self.heads
        self.count = self.length // size
        self.projected, self.conv, self.aux, self.row = projected, own_conv, aux, row
        heads, length, depth, count = self.heads, self.length, self.depth, self.count
        ksize = own_conv.shape[1]
        self.token_specs = [
            pl.BlockSpec((length + PAD, depth), lambda h, i=i: (0, i * heads + h)) for i in range(3)
        ]
        self.head_cols = pl.BlockSpec((length, depth), lambda h: (0, h))
        self.conv_spec = pl.BlockSpec((3, ksize, depth), lambda h: (0, 0, h))
        self.aux_specs = [
            pl.BlockSpec((1, length, 8), lambda h: (h, 0, 0)),
            pl.BlockSpec((1, 8, length), lambda h: (h, 0, 0)),
        ]
        self.chunk_spec = pl.BlockSpec((1, count, depth, depth), lambda h: (h, 0, 0, 0))
        self.inv_spec = pl.BlockSpec((1, count, size, size), lambda h: (h, 0, 0, 0))
        self.rows_spec = pl.BlockSpec((1, length, depth), lambda h: (h, 0, 0))
        self.flops = 2 * heads * count * size * depth * depth
        inputs = [projected] * 3 + [own_conv, aux, row]
        square = shape((heads, count, depth, depth))
        tokens = shape((heads, length, depth))
        out_shape = (
            [shape((length, heads * depth))] * 3
            + [shape((heads, count, size, size))]
            + [tokens] * 4
            + [square] * 2
            + [shape((heads, 2, depth, depth), BF)]
        )
        (
            self.yq, self.yk, self.yv, self.inv, self.plain, self.reach, self.read, self.direct,
            self.trans, self.fresh, self.whole,
        ) = pl.pallas_call(
            functools.partial(forward_kernel, size),
            name="mixer_forward",
            out_shape=out_shape,
            grid=(heads,),
            in_specs=self.token_specs + [self.conv_spec] + self.aux_specs,
            out_specs=[self.head_cols] * 3
            + [self.inv_spec]
            + [self.rows_spec] * 4
            + [self.chunk_spec] * 2
            + [pl.BlockSpec((1, 2, depth, depth), lambda h: (h, 0, 0, 0))],
            cost_estimate=cost(60 * self.flops, inputs, out_shape),
            compiler_params=pltpu.CompilerParams(vmem_limit_bytes=VMEM_LIMIT),
        )(*inputs)

    def outputs(self, place, both, head_gain):
        heads, length, depth, count = self.heads, self.length, self.depth, self.count
        self.place, self.both, self.gain = place, both, head_gain
        self.states, self.out, normed = vmem_call(
            "mixer_read",
            functools.partial(read_kernel, self.size),
            [
                shape((heads, count, depth, depth)),
                shape((length, heads * depth)),
                shape((length, heads * depth), BF),
            ],
            [place, both, self.trans, self.fresh, self.read, self.direct, head_gain],
            12 * self.flops,
        )
        return normed

    def leak(self, grads, deps=()):
        heads, length, depth, count = self.heads, self.length, self.depth, self.count
        self.grad_out, self.from_out, leak, grad_gain = vmem_call(
            "mixer_leak",
            functools.partial(leak_kernel, self.size),
            [
                shape((heads, length, depth)),
                shape((heads, count, depth, depth)),
                shape((heads, depth, depth), BF),
                shape((1, depth)),
            ],
            [grads, self.out, self.gain, self.read, self.trans],
            6 * self.flops,
            deps,
        )
        return leak, grad_gain

    def back(self, leaks):
        heads, length, depth, count = self.heads, self.length, self.depth, self.count
        ksize = self.conv.shape[1]
        (grads,) = vmem_call(
            "mixer_chain",
            chain_kernel,
            [shape((heads, count, depth, depth))],
            [self.place, self.both, leaks, self.trans, self.from_out],
            6 * self.flops,
        )
        inputs = [self.projected] * 3 + [self.yq, self.yk, self.yv, self.conv, self.aux, self.row]
        inputs += [self.inv, self.plain, self.reach, self.states, grads, self.grad_out]
        edge = shape((3, PAD, heads * depth))
        out_shape = [shape((length, heads * depth), BF)] * 3 + [edge] * 2
        out_shape += [shape((3, ksize, heads * depth)), shape((heads, 1, length))]
        edge_spec = pl.BlockSpec((3, PAD, depth), lambda h: (0, 0, h))
        return pl.pallas_call(
            functools.partial(backward_kernel, self.size),
            name="mixer_backward",
            out_shape=out_shape,
            grid=(heads,),
            in_specs=self.token_specs
            + [self.head_cols] * 3
            + [self.conv_spec]
            + self.aux_specs
            + [self.inv_spec, self.rows_spec, self.rows_spec, self.chunk_spec, self.chunk_spec, self.rows_spec],
            out_specs=[self.head_cols] * 3
            + [edge_spec] * 2
            + [self.conv_spec, pl.BlockSpec((1, 1, length), lambda h: (h, 0, 0))],
            scratch_shapes=[pltpu.VMEM((3, ksize, length + 2 * PAD, depth), F32)],
            cost_estimate=cost(30 * self.flops, inputs, out_shape),
            compiler_params=pltpu.CompilerParams(vmem_limit_bytes=VMEM_LIMIT),
        )(*inputs)


ANY = pl.BlockSpec(memory_space=pl.ANY)
TOKEN = shape((8, 128))


def resident(x):
    return pl.BlockSpec(x.shape, lambda *_: (0,) * x.ndim, pipeline_mode=pl.Buffered(1))


def activations(gate, lifted, grad_hidden):
    sig = jax.nn.sigmoid(gate)
    swish = gate * sig
    return (
        (swish * lifted).astype(BF),
        (grad_hidden * lifted * sig * (1.0 + gate * (1.0 - sig))).astype(BF),
        (grad_hidden * swish).astype(BF),
    )


def chunks_of(size, chunk=256):
    return [slice(at, min(at + chunk, size)) for at in range(0, size, chunk)]


def params(flops, moved):
    return dict(
        cost_estimate=pl.CostEstimate(flops=int(flops), bytes_accessed=int(moved), transcendentals=0),
        compiler_params=pltpu.CompilerParams(vmem_limit_bytes=FFN_VMEM),
    )


TOKEN_SPEC = pl.BlockSpec((8, 128), lambda *_: (0, 0))


def own_kernel(groups, feed, cot, wg, wu, wd, hidden, grad_gate, grad_lifted, grad_feed, branch):
    units, model = wd.shape
    for cut in chunks_of(units):
        gated = jnp.dot(feed[...], wg[:, cut], preferred_element_type=F32)
        lifted = jnp.dot(feed[...], wu[:, cut], preferred_element_type=F32)
        grad_hidden = dims(cot[...], wd[cut, :], 1, 1)
        hidden[:, cut], grad_gate[:, cut], grad_lifted[:, cut] = activations(gated, lifted, grad_hidden)
    for cut in chunks_of(model):
        total = dims(grad_gate[...], wg[cut, :], 1, 1) + dims(grad_lifted[...], wu[cut, :], 1, 1)
        grad_feed[:, cut] = total.astype(BF)
        branch[:, cut] = jnp.dot(hidden[...], wd[:, cut], preferred_element_type=F32).astype(BF)


def hidden_kernel(groups, cot, wd, *refs):
    out, token = refs[-2:]
    out[...] = dims(cot[...], wd[...], 1, 1).astype(BF)
    token[...] = jnp.zeros_like(token)


def rows_kernel(groups, feed, grad_hidden, wg, wu, *refs):
    hidden, grad_gate, grad_lifted, token = refs[-4:]
    for cut in chunks_of(wg.shape[1]):
        gated = jnp.dot(feed[...], wg[:, cut], preferred_element_type=F32)
        lifted = jnp.dot(feed[...], wu[:, cut], preferred_element_type=F32)
        hidden[:, cut], grad_gate[:, cut], grad_lifted[:, cut] = activations(
            gated, lifted, grad_hidden[:, cut].astype(F32)
        )
    token[...] = jnp.zeros_like(token)


def by_group(name, kernel, groups, size, inputs, weights, outs, held, deps, products):
    tokens = inputs[0].shape[0]
    count = groups.shape[0]
    picked = lambda width: pl.BlockSpec((size, width), lambda i, g: (g[i], 0))
    first = 1 + len(inputs) + len(weights) + len(deps)
    return pl.pallas_call(
        kernel,
        name=name,
        out_shape=[shape((tokens, width), BF) for width in outs] + [TOKEN],
        grid_spec=pltpu.PrefetchScalarGridSpec(
            num_scalar_prefetch=1,
            grid=(count,),
            in_specs=[picked(x.shape[1]) for x in inputs]
            + [resident(w) for w in weights]
            + [ANY] * (len(deps) + len(held)),
            out_specs=[picked(width) for width in outs] + [TOKEN_SPEC],
        ),
        input_output_aliases={first + n: n for n in range(len(held))},
        **params(
            2 * count * size * weights[0].size * products,
            sum(w.size for w in weights) * 2 + count * size * 2 * (sum(outs) + sum(x.shape[1] for x in inputs)),
        ),
    )(groups, *inputs, *weights, *deps, *held)


def feed_own(place, feed, cot, weights, tokens):
    rows, model = feed.shape
    units = weights[0].shape[1]
    block = 256
    count = rows // block
    wide = pl.BlockSpec((block, units), lambda i, g: (g[0] * count + i, 0))
    here = pl.BlockSpec((block, model), lambda i, g: (i, 0))
    return pl.pallas_call(
        own_kernel,
        name="feed_own",
        out_shape=[shape((tokens, units), BF)] * 3 + [shape((rows, model), BF)] * 2,
        grid_spec=pltpu.PrefetchScalarGridSpec(
            num_scalar_prefetch=1,
            grid=(count,),
            in_specs=[here] * 2 + [resident(w) for w in weights],
            out_specs=[wide] * 3 + [here] * 2,
        ),
        **params(12 * rows * model * units, 6 * model * units + rows * (3 * units + 4 * model) * 2),
    )(place, feed, cot, *weights)


GRAD_COLS = 256


def grad_kernel(transposed, left, right, *refs):
    out, token = refs[-2:]
    term = dims(left[...], right[...], 0, 0)
    out[...] = term.T if transposed else term
    token[...] = jnp.zeros_like(token)


def weight_grad(part, parts, left, right, held, deps, transposed):
    rows, model = left.shape
    units = right.shape[1]
    count = model // GRAD_COLS // parts
    if transposed:
        out_spec = pl.BlockSpec((units, GRAD_COLS), lambda m: (0, part * count + m))
    else:
        out_spec = pl.BlockSpec((GRAD_COLS, units), lambda m: (part * count + m, 0))
    return pl.pallas_call(
        functools.partial(grad_kernel, transposed),
        name="weight_grad",
        out_shape=[shape((units, model) if transposed else (model, units)), TOKEN],
        grid=(count,),
        in_specs=[pl.BlockSpec((rows, GRAD_COLS), lambda m: (0, part * count + m)), resident(right)]
        + [ANY] * (len(deps) + len(held)),
        out_specs=[out_spec, pl.BlockSpec((8, 128), lambda m: (0, 0))],
        input_output_aliases={2 + len(deps) + n: n for n in range(len(held))},
        **params(
            2 * rows * count * GRAD_COLS * units,
            2 * rows * (units + count * GRAD_COLS) + 4 * count * GRAD_COLS * units,
        ),
    )(left, right, *deps, *held)


def body(
    tokens,
    cotangent,
    lengths,
    pad_mask,
    attn_gain,
    projection_weight,
    w_beta,
    beta_bias,
    conv_weight,
    head_gain,
    mlp_gain,
    w_gate,
    w_up,
    w_down,
):
    width, model = tokens.shape
    heads = w_beta.shape[1]
    depth = head_gain.shape[0]
    ksize = conv_weight.shape[1]
    margin = ksize - 1
    lanes, blocks = lax.axis_size("ta"), lax.axis_size("dev")
    rank, place = lax.axis_index("ta"), lax.axis_index("dev")
    own_heads = heads // lanes
    cols = own_heads * depth
    rows = projection_weight.shape[0]
    group = lanes * width
    ring = Ring()

    positions = place * group + jnp.arange(group, dtype=jnp.int32)
    documents = document_of(lengths, positions)
    valid = jnp.stack(
        [
            (document_of(lengths, positions - margin + offset) == documents).astype(F32)
            for offset in range(ksize)
        ],
        axis=1,
    )
    previous = document_of(lengths, positions[::width] - 1)

    extra = jnp.zeros((8, model), BF).at[0, 0:width].set(pad_mask.astype(BF))
    extra = extra.at[1, 0 : rows * heads].set(w_beta.reshape(-1))
    packed = in_order(gather_parts(jnp.concatenate([tokens, extra], axis=0)[None]), rank, 0)
    cot_group = in_order(gather_parts(cotangent), rank, 0)

    split = jnp.transpose(projection_weight.reshape(rows, 4, lanes, cols), (2, 0, 1, 3))
    own_rows = in_order(exchange(split.reshape(lanes, rows, 4 * cols), rank), rank, 0)
    w_all = ring.gather(own_rows).reshape(model, 4 * cols)
    w_out = in_order(gather_parts(w_all[:, 3 * cols :]), rank, 1)
    beta_rows = packed[:, width + 1, 0 : rows * heads].reshape(lanes * rows * heads // 128, 128)
    wbeta = gather_dev(beta_rows).reshape(model, lanes, own_heads)
    wbeta = lax.dynamic_index_in_dim(wbeta, rank, 1, False)
    cot_all = lax.all_gather(gate(cotangent, w_all), BOTH, axis=0, tiled=True)

    halo = shifted(packed[lanes - 1, width - 8 :], 1)
    group_tokens = packed[:, :width].reshape(group, model).astype(F32)
    live = packed[:, width, 0:width].reshape(group).astype(F32)
    live_ext = jnp.concatenate([halo[8, width - 8 : width].astype(F32), live])
    normed = rms_scale(jnp.concatenate([halo[0:8].astype(F32), group_tokens], axis=0), attn_gain)
    normed = normed.astype(BF)
    normed_group = normed[8:]
    projected = dot(normed, w_all) * live_ext[:, None]
    beta_logit = dot(normed_group, wbeta)

    own_conv = lax.dynamic_slice_in_dim(conv_weight, rank * cols, cols, 2)
    own_bias = lax.dynamic_slice_in_dim(beta_bias, rank * own_heads, own_heads, 0)
    sig_beta = jax.nn.sigmoid(beta_logit + own_bias)
    beta = sig_beta * live[:, None]
    chunk_docs = documents.reshape(lanes, width)
    continuing = (chunk_docs == previous[:, None]).reshape(group).astype(F32)
    closing = (chunk_docs == chunk_docs[:, width - 1 :]).reshape(group).astype(F32)
    shared = jnp.stack(
        [valid[:, j] for j in range(margin)] + [continuing, closing, live, documents.astype(F32)], axis=0
    )
    row = jnp.concatenate(
        [jnp.broadcast_to(shared, (own_heads,) + shared.shape), beta.T[:, None]], axis=1
    )
    mixer = Mixer(projected, own_conv, jnp.transpose(row, (0, 2, 1)), row, width)
    both = ring.gather(mixer.whole)
    at_place = place.astype(jnp.int32).reshape(1)
    head_normed = mixer.outputs(at_place, both, head_gain[None])
    heads_low = in_order(gather_parts(head_normed), rank, 1)
    residual = group_tokens + dot(heads_low, w_out)
    feed_rows = rms_scale(residual, mlp_gain).astype(BF)
    own_residual = lax.dynamic_slice_in_dim(residual, rank * width, width, 0)

    own_feed = lax.dynamic_slice_in_dim(feed_rows, rank * width, width, 0)
    feed_all = lax.all_gather(own_feed, BOTH, axis=0, tiled=True)

    weights = [w_gate, w_up, w_down]
    units = w_gate.shape[1]
    *arrays, partial_feed, partial_branch = feed_own(at_place, feed_rows, cot_group, weights, blocks * group)
    others = lax.rem(place + 1 + jnp.arange(blocks - 1, dtype=jnp.int32), blocks)
    grad_feed, (token, grad_hidden) = scatter_sum(
        partial_feed.reshape(lanes, width, model), rank,
        lambda sent: by_group(
            "feed_hidden", hidden_kernel, others, group, [cot_all], [w_down], [units], [], [sent], 1
        )[::-1],
    )
    row_parts = [others[: (blocks - 1) // 2], others[(blocks - 1) // 2 :]]

    def fill_rows(deps):
        *arrays[:], token = by_group(
            "feed_rows", rows_kernel, row_parts.pop(0), group, [feed_all, grad_hidden], weights[:2],
            [units] * 3, list(arrays), deps, 2,
        )
        return token

    grad_parts = [(which, part) for which in range(3) for part in range(2)]
    ffn_grads = [[], [], []]

    def fill_grads(*deps):
        which, part = grad_parts.pop(0)
        left = cot_all if which == 2 else feed_all
        hidden, grad_gate, grad_lifted = arrays
        right = (grad_gate, grad_lifted, hidden)[which]
        out, token = weight_grad(part, 2, left, right, ffn_grads[which], deps, which == 2)
        ffn_grads[which] = [out]
        return token

    _, feed_back = jax.vjp(rms_scale, own_residual, mlp_gain)
    grad_from_feed, grad_mlp_gain = feed_back(grad_feed)
    grad_residual = cotangent.astype(F32) + grad_from_feed
    grad_mixed = grad_residual.astype(BF)

    parts, sent = [], []
    for j in range(lanes):
        at = (rank ^ j) * cols
        heads_part = contract_cols(grad_mixed, lax.dynamic_slice_in_dim(w_out, at, cols, 0)).astype(BF)
        mixed_part = lax.dynamic_slice_in_dim(grad_mixed, at, cols, 1)
        sent.append(jnp.concatenate([heads_part, mixed_part], axis=1))
        parts.append(swap(sent[j], "ta", j) if j else sent[j])
    by_heads = in_order(parts, rank, 0)
    mixed_cols = by_heads[:, cols:]
    leak, grad_head_gain = mixer.leak(by_heads)
    grad_head_gain = grad_head_gain[0]
    leaks = ring.gather(leak)
    grad_q, grad_k, grad_v, tail, spill, grad_conv, grad_beta = mixer.back(leaks)
    arrived = shifted(spill.astype(BF), -1).astype(F32)
    last = ((tail + arrived) * live[None, group - PAD :, None]).astype(BF)
    grad_projected = jnp.concatenate([grad_q, grad_k, grad_v], axis=1)
    last = jnp.transpose(last, (1, 0, 2)).reshape(PAD, 3 * cols)
    grad_projected = lax.dynamic_update_slice(grad_projected, last, (group - PAD, 0))
    grad_logit = grad_beta[:, 0].T * beta * (1.0 - sig_beta)
    grad_bias = jnp.sum(grad_logit, axis=0)
    grad_logit_low = grad_logit.astype(BF)

    def weight_rows(partial, beside):
        share = partial.shape[1]
        part = ring.scatter(partial.reshape(blocks, model // blocks, share), beside)
        return exchange(part.astype(BF).reshape(lanes, rows, share), rank)

    w_partial = jnp.concatenate(
        [contract_rows(normed_group, grad_projected).astype(BF), contract_rows(heads_low, mixed_cols).astype(BF)],
        axis=1,
    )
    w_parts = weight_rows(
        w_partial, [lambda x: fill_rows([x]), lambda x: fill_rows([x]), fill_grads, fill_grads]
    )
    grad_projection = in_order([p.astype(F32).reshape(rows, 4, cols) for p in w_parts], rank, 2)

    partial_normed = contract_cols(grad_projected, w_all[:, : 3 * cols]) + contract_cols(grad_logit_low, wbeta)
    scale = lax.rsqrt(jnp.mean(group_tokens * group_tokens, axis=-1, keepdims=True) + NORM_EPS)
    grad_attn_gain = jnp.sum(partial_normed * (group_tokens * scale), axis=0)
    both_sums = jnp.stack([partial_normed.astype(BF), partial_branch]).reshape(2, lanes, width, model)
    both_sums = scatter_sum(jnp.transpose(both_sums, (1, 0, 2, 3)), rank)
    grad_normed, branch = both_sums[0], both_sums[1]
    block_out = (own_residual + branch).astype(BF)
    _, attention_back = jax.vjp(lambda x: rms_scale(x, attn_gain), tokens.astype(F32))
    grad_tokens = grad_residual + attention_back(grad_normed)[0]

    partial_wbeta = contract_rows(normed_group, grad_logit_low)
    gains = jnp.concatenate([grad_mlp_gain, grad_head_gain, grad_attn_gain])
    pieces = [grad_conv.reshape(-1), partial_wbeta.T.reshape(-1), grad_bias, gains]
    ends = [0]
    for piece in pieces:
        ends.append(ends[-1] + piece.shape[0])
    flat = jnp.concatenate(pieces)
    flat = jnp.pad(flat, (0, -flat.shape[0] % 1024)).reshape(-1, 128)
    flat = in_order(gather_parts(sum_over(flat, "dev")[None]), rank, 0).reshape(lanes, -1)
    conv_sum, wbeta_sum, bias_sum, gains = (flat[:, a:b] for a, b in zip(ends, ends[1:]))
    conv_sum = jnp.transpose(conv_sum.reshape(lanes, 3, ksize, cols), (1, 2, 0, 3))
    conv_sum = conv_sum.reshape(3, ksize, lanes * cols)
    wbeta_sum = lax.dynamic_slice_in_dim(
        wbeta_sum.reshape(heads, model), (place * lanes + rank) * rows, rows, 1
    )
    grad_w_beta = wbeta_sum.T
    bias_sum = bias_sum.reshape(heads)
    gains = jnp.sum(gains, axis=0)

    while grad_parts:
        fill_grads(w_partial)
    (grad_w_gate,), (grad_w_up,), (grad_w_down,) = ffn_grads
    return (
        block_out,
        grad_tokens,
        gains[model + depth : 2 * model + depth],
        grad_projection,
        grad_w_beta,
        bias_sum,
        conv_sum,
        gains[model : model + depth],
        gains[:model],
        grad_w_gate,
        grad_w_up,
        grad_w_down,
    )


def solution(mesh):
    rows = P(BOTH, None)
    three = P(BOTH, None, None)
    return jax.shard_map(
        body,
        mesh=mesh,
        in_specs=(
            rows,
            rows,
            P(),
            P(BOTH),
            P(),
            three,
            rows,
            P(),
            P(),
            P(),
            P(),
            P(None, "ta"),
            P(None, "ta"),
            P("ta", None),
        ),
        out_specs=(
            rows,
            rows,
            P(),
            three,
            rows,
            P(),
            P(),
            P(),
            P(),
            P(None, "ta"),
            P(None, "ta"),
            P("ta", None),
        ),
        check_vma=False,
    )
```

time: 960 us -> 801 us (0.83)
  matrix products: 375 us -> 46.9 us
  Pallas kernels: 0 us -> 302 us
  local copies, waits for them, and re-layouts: 156 us -> 107 us
  waiting for transfers between devices: 222 us -> 186 us
  starting transfers between devices: 96.4 us -> 72.3 us
  other arithmetic: 68.9 us -> 49.9 us
    pallas_call x0 -> x25, Pallas kernels: none -> 302 us  [the longest x6 121 us: weight_grad(): pl.pallas_call(functools.partial(grad_kernel, transposed), name='weight_g...]
    dot_general x6 -> x3, matrix products: 123 us -> 8.77 us  [contract_rows(): lax.dot_general(left, right, (((0,), (0,)), ((), ())), preferred_element_...]
    dot_general x64 -> x0, matrix products: 88 us -> none  [mm(): return jnp.einsum(spec, a, b, precision=HIGHEST)]
    dot_general x8 -> x3, matrix products: 95.8 us -> 20.2 us  [dot(): return jnp.dot(left, right, preferred_element_type=F32)]
    dot_general x7 -> x6, matrix products: 67.8 us -> 18 us  [contract_cols(): lax.dot_general(left, right, (((1,), (1,)), ((), ())), preferred_element_...]
    ppermute x48 -> x32, waiting for transfers between devices: 130 us -> 89.4 us  [move(): lax.ppermute(x, 'dev', [(self.order[p], self.order[(p + step) % n]) for p...]
    slice x29 -> x15, local copies, waits for them, and re-layouts: 44.4 us -> 6.86 us  [the longest x1 3.29 us: body(): w_out = in_order(gather_parts(w_all[:, 3 * cols:]), rank, 1)]
    ppermute x41 -> x34, waiting for transfers between devices: 72.2 us -> 94 us  [swap(): lax.ppermute(x, axis, [(i, i ^ bit) for i in range(lax.axis_size(axis))])]
  transfers between devices with their start and end apart: 94 -> 70, of which waited for: 39 -> 29; matrix products, arithmetic and copies ran while one was open for 43% -> 21% of each run, Pallas kernels for 0% -> 38%
where the time goes in v2:
time: 801 us; the launch traced here: 794 us
  Pallas kernels  302 us (38%)
  waiting for transfers between devices  186 us (23%)
  local copies, waits for them, and re-layouts  107 us (13%)
  starting transfers between devices  72.3 us (9%)
  other arithmetic  49.9 us (6%)
  matrix products  46.9 us (6%)
  between operations  29.7 us (4%)
    pallas_call x6, Pallas kernels, weight_grad(): pl.pallas_call(functools.partial(grad_kernel, transposed), name='weight_g...  121 us
    pallas_call x3, Pallas kernels, by_group(): pl.pallas_call(kernel, name=name, out_shape=[shape((tokens, width), BF) f...  99.3 us
    ppermute x34, waiting for transfers between devices, swap(): lax.ppermute(x, axis, [(i, i ^ bit) for i in range(lax.axis_size(axis))])  94 us
    ppermute x32, waiting for transfers between devices, move(): lax.ppermute(x, 'dev', [(self.order[p], self.order[(p + step) % n]) for p...  89.4 us
    ppermute x32, starting transfers between devices, move(): lax.ppermute(x, 'dev', [(self.order[p], self.order[(p + step) % n]) for p...  38.7 us
    pallas_call x1, Pallas kernels, feed_own(): pl.pallas_call(own_kernel, name='feed_own', out_shape=[shape((tokens, uni...  29.5 us
    ppermute x34, starting transfers between devices, swap(): lax.ppermute(x, axis, [(i, i ^ bit) for i in range(lax.axis_size(axis))])  29 us
    dynamic_update_slice x28, local copies, waits for them, and re-layouts, in_order(): lax.dynamic_update_slice_in_dim(joined, part, (rank ^ j) * size, axis)  24.8 us
  transfers between devices with their start and end apart: 70, of which 29 were waited for; matrix products, arithmetic and copies ran while one was open for 21% of the time, Pallas kernels for 38%

profile of v2, /device:TPU:0, one launch (start us, length us, event | category | flops | bytes accessed | tf_op | source)
XLA Modules:
  0.0 794.2 jit_solution(4438093477087476959)
XLA Ops:
  11.0 2.5 collective-permute-start.5
  14.8 6.0 collective-permute-done.5
  21.8 4.3 collective-permute-done.6
  29.1 23.3 %collective-permute-done.7 = bf16[256,2048]{1,0:T(8,128)(2,1)} collective-permute-done((bf16[256,2048]{1,0:T(8,128)(2,1)S(1)}, bf16[256,2048]{1,0:T(8,128)(2,1)}, u32[]{:S(2)}, u32[]{:S(2)}) %collective-permute-start.7) | collective-permute-done | bytes 1048608 | tf_op jit(solution)/shard_map/ppermute | solution.py:82
  73.0 4.5 broadcast_in_dim.151
  88.5 17.8 %collective-permute-done.12 = bf16[256,2048]{1,0:T(8,128)(2,1)S(1)} collective-permute-done((bf16[256,2048]{1,0:T(8,128)(2,1)}, bf16[256,2048]{1,0:T(8,128)(2,1)S(1)}, u32[]{:S(2)}, u32[]{:S(2)}) %collective-permute-start.12) | collective-permute-done | bytes 1048608 | tf_op jit(solution)/shard_map/ppermute | solution.py:82
  110.7 7.3 collective-permute-done.14
  124.3 16.0 %collective-permute-done.1 = bf16[1,136,2048]{2,1,0:T(8,128)(2,1)} collective-permute-done((bf16[1,136,2048]{2,1,0:T(8,128)(2,1)}, bf16[1,136,2048]{2,1,0:T(8,128)(2,1)}, u32[]{:S(2)}, u32[]{:S(2)}) %collective-permute-start.1) | collective-permute-done | bytes 557088 | tf_op jit(solution)/shard_map/ppermute | solution.py:19
  144.4 2.5 slice_convert_fusion
  150.8 2.6 collective-permute-start.17
  153.4 3.2 collective-permute-start.3
  156.8 4.5 reshape.466
  165.6 2.7 multiply_reduce_fusion
  172.7 3.3 fusion.94
  177.5 11.9 %convolution_multiply_fusion.xq.xk.xv = f32[520,2048]{1,0:T(8,128)} fusion(bf16[520,2048]{1,0:T(8,128)(2,1)S(1)} %multiply_convert_fusion, bf16[2048,2048]{1,0:T(8,128)(2,1)} %bitcast.25.refs_1_, f32[520]{0:T(1024)S(1)} %pad_maximum_fusion.13), kind=kOutput, calls=%fused_computation.13 | convolution fusion | flops 4363141120 | bytes 14780448 | tf_op jit(solution)/shard_map/dot_general | solution.py:188
  189.5 24.3 %mixer_forward.1 = (f32[512,512]{1,0:T(8,128)S(1)}, f32[512,512]{1,0:T(8,128)S(1)}, f32[512,512]{1,0:T(8,128)S(1)}, f32[4,4,128,128]{3,2,1,0:T(8,128)S(1)}, f32[...) custom-call(f32[520,2048]{1,0:T(8,128)} %convolution_multiply_fusion, ...), custom_call_target="tpu_custom_call" | custom-call | flops 4026531840 | bytes 23683072 | tf_op jit(solution)/shard_map/mixer_forward/pallas_call | solution.py:500
  216.5 7.8 collective-permute-done.18
  226.4 5.6 collective-permute-done.20
  234.5 9.3 %collective-permute-done.23 = bf16[4,2,128,128]{3,2,1,0:T(8,128)(2,1)S(1)} collective-permute-done((bf16[4,2,128,128]{3,2,1,0:T(8,128)(2,1)S(1)}, bf16[4,2,128,128]{3,2,1,0:T(8,128)(2,1)S(1)}, u32[]{:S(2)}, u32[]{:S(2)}) %collective-permute-start.23) | collective-permute-done | bytes 262176 | tf_op jit(solution)/shard_map/ppermute | solution.py:82
  246.3 5.4 collective-permute-done.30
  253.1 3.8 mixer_read.1
  260.7 12.7 %collective-permute-done.27 = bf16[512,512]{1,0:T(8,128)(2,1)S(1)} collective-permute-done((bf16[512,512]{1,0:T(8,128)(2,1)}, bf16[512,512]{1,0:T(8,128)(2,1)S(1)}, u32[]{:S(2)}, u32[]{:S(2)}) %collective-permute-start.27) | collective-permute-done | bytes 524320 | tf_op jit(solution)/shard_map/ppermute | solution.py:19
  277.1 3.9 constant_dynamic-update-slice_fusion.15
  281.0 3.2 constant_dynamic-update-slice_fusion.14
  284.1 3.2 constant_dynamic-update-slice_fusion.13
  287.4 7.5 multiply_reduce_fusion.3
  301.1 12.4 %collective-permute-done.33 = bf16[128,2048]{1,0:T(8,128)(2,1)S(1)} collective-permute-done((bf16[128,2048]{1,0:T(8,128)(2,1)S(1)}, bf16[128,2048]{1,0:T(8,128)(2,1)S(1)}, u32[]{:S(2)}, u32[]{:S(2)}) %collective-permute-start.33) | collective-permute-done | bytes 524320 | tf_op jit(solution)/shard_map/ppermute | solution.py:19
  320.6 29.5 %feed_own.1 = (bf16[4096,1408]{1,0:T(8,128)(2,1)}, bf16[4096,1408]{1,0:T(8,128)(2,1)}, bf16[4096,1408]{1,0:T(8,128)(2,1)}, bf16[512,2048]{1,0:T(8,128)(2,1)}, bf16[512,2048]{1,0:T(8,128)(2,1)}) custom-call(s32[1]{0:T(128)} %bitcast.3.refs_0_.groups, bf16[512,2048]{1,0:T(8,128)(2,1)} %copy-done.47, bf16[512,2048]{1,0:T(8,128)(2,1)} %constant_dynamic-update-slice_fusion.9.cot, ...), custom_call_target="tpu_custom_call" | custom-call | flops 17716740096 | bytes 30015488 | tf_op jit(solution)/shard_map/feed_own/pallas_call | solution.py:677
  362.9 29.3 %feed_hidden.1 = (bf16[4096,1408]{1,0:T(8,128)(2,1)}, f32[8,128]{1,0:T(8,128)}) custom-call(s32[7]{0:T(128)} %copy-done.63, bf16[4096,2048]{1,0:T(8,128)(2,1)} %all-gather.3.cloned.1.call-done.cot.left, bf16[1408,2048]{1,0:T(8,128)(2,1)} %wd.3, bf16[1,128,2048]{2,1,0:T(8,128)(2,1)} %dynamic-slice_convert_fusion.1.refs_0_), custom_call_target="tpu_custom_call" | custom-call | flops 20669530112 | bytes 30539776 | tf_op jit(solution)/shard_map/feed_hidden/pallas_call | solution.py:650
  395.5 2.7 fusion.92
  398.2 2.5 fusion.27
  400.8 2.4 fusion.24
  403.2 2.4 fusion.30
  405.7 2.8 fusion.33
  410.6 7.1 collective-permute-done.38
  417.7 4.5 collective-permute-done.39
  422.2 3.6 mixer_leak.1
  425.9 2.4 collective-permute-start.40
  430.0 3.7 collective-permute-done.40
  435.8 3.2 collective-permute-done.42
  438.9 5.6 collective-permute-start.44
  445.8 4.9 collective-permute-done.45
  455.1 4.7 mixer_chain.1.grads
  460.8 16.5 %mixer_backward.1 = (bf16[512,512]{1,0:T(8,128)(2,1)S(1)}, bf16[512,512]{1,0:T(8,128)(2,1)S(1)}, bf16[512,512]{1,0:T(8,128)(2,1)S(1)}, f32[3,8,512]{2,1,0:T(8,12...) custom-call(f32[520,2048]{1,0:T(8,128)} %convolution_multiply_fusion.xq.xk.xv, ...), custom_call_target="tpu_custom_call" | custom-call | flops 2013265920 | bytes 24076288 | tf_op jit(solution)/shard_map/mixer_backward/pallas_call | solution.py:564
  483.2 7.1 multiply_reduce_fusion.1
  495.5 2.6 convolution_convert_fusion.1
  500.6 5.7 convolution_convert_fusion
  508.3 7.3 pad_maximum_fusion.refs_0_
  516.1 3.0 convert_add_fusion
  522.2 2.5 dynamic-slice_bitcast_fusion.5
  531.4 14.6 %collective-permute-done.50 = bf16[1,2,128,2048]{3,2,1,0:T(8,128)(2,1)} collective-permute-done((bf16[1,2,128,2048]{3,2,1,0:T(8,128)(2,1)}, bf16[1,2,128,2048]{3,2,1,0:T(8,128)(2,1)}, u32[]{:S(2)}, u32[]{:S(2)}) %collective-permute-start.50) | collective-permute-done | bytes 1048608 | tf_op jit(solution)/shard_map/ppermute | solution.py:19
  548.5 2.8 fusion.57
  551.3 31.1 %feed_rows.2 = (bf16[4096,1408]{1,0:T(8,128)(2,1)}, bf16[4096,1408]{1,0:T(8,128)(2,1)}, bf16[4096,1408]{1,0:T(8,128)(2,1)}, f32[8,128]{1,0:T(8,128)}) custom-call(s32[3]{0:T(128)} %bitcast.298, bf16[4096,2048]{1,0:T(8,128)(2,1)} %all-gather.5.cloned.1.call-done.feed.left, ...), custom_call_target="tpu_custom_call", output_to_operand_aliasing={{0}: (6, {}), {1}: (7, {}), {2}: (8, {})} | custom-call | flops 17716740096 | bytes 35127296 | tf_op jit(solution)/shard_map/feed_rows/pallas_call | solution.py:650
  589.1 38.9 %feed_rows.3 = (bf16[4096,1408]{1,0:T(8,128)(2,1)}, bf16[4096,1408]{1,0:T(8,128)(2,1)}, bf16[4096,1408]{1,0:T(8,128)(2,1)}, f32[8,128]{1,0:T(8,128)}) custom-call(s32[4]{0:T(128)} %slice.202.groups, bf16[4096,2048]{1,0:T(8,128)(2,1)} %all-gather.5.cloned.1.call-done.feed.left, ...), custom_call_target="tpu_custom_call", output_to_operand_aliasing={{0}: (6, {}), {1}: (7, {}), {2}: (8, {})} | custom-call | flops 23622320128 | bytes 42991616 | tf_op jit(solution)/shard_map/feed_rows/pallas_call | solution.py:650
  628.0 19.9 %weight_grad.8 = (f32[2048,1408]{1,0:T(8,128)}, f32[8,128]{1,0:T(8,128)}) custom-call(bf16[4096,2048]{1,0:T(8,128)(2,1)} %all-gather.5.cloned.1.call-done.feed.left, bf16[4096,1408]{1,0:T(8,128)(2,1)} %get-tuple-element.126.right, bf16[2048,2048]{1,0:T(8,128)(2,1)} %pad_maximum_fusion.refs_0_), custom_call_target="tpu_custom_call" | custom-call | flops 11811160064 | bytes 25690112 | tf_op jit(solution)/shard_map/weight_grad/pallas_call | solution.py:709
  647.9 19.9 %weight_grad.9 = (f32[2048,1408]{1,0:T(8,128)}, f32[8,128]{1,0:T(8,128)}) custom-call(bf16[4096,2048]{1,0:T(8,128)(2,1)} %all-gather.5.cloned.1.call-done.feed.left, bf16[4096,1408]{1,0:T(8,128)(2,1)} %get-tuple-element.126.right, bf16[2048,2048]{1,0:T(8,128)(2,1)} %pad_maximum_fusion.refs_0_, ...), custom_call_target="tpu_custom_call", output_to_operand_aliasing={{0}: (3, {})} | custom-call | flops 11811160064 | bytes 25690112 | tf_op jit(solution)/shard_map/weight_grad/pallas_call | solution.py:709
  668.8 2.9 fusion.7.refs_0_
  673.3 20.1 %weight_grad.6 = (f32[2048,1408]{1,0:T(8,128)}, f32[8,128]{1,0:T(8,128)}) custom-call(bf16[4096,2048]{1,0:T(8,128)(2,1)} %all-gather.5.cloned.1.call-done.feed.left, bf16[4096,1408]{1,0:T(8,128)(2,1)} %get-tuple-element.121.right, bf16[256,2048]{1,0:T(8,128)(2,1)} %fusion.7.refs_0_), custom_call_target="tpu_custom_call" | custom-call | flops 11811160064 | bytes 25690112 | tf_op jit(solution)/shard_map/weight_grad/pallas_call | solution.py:709
  693.4 2.4 collective-permute-done.59.refs_0_
  696.8 3.6 fusion.8
  701.6 20.3 %weight_grad.10 = (f32[1408,2048]{1,0:T(8,128)}, f32[8,128]{1,0:T(8,128)}) custom-call(bf16[4096,2048]{1,0:T(8,128)(2,1)} %all-gather.3.cloned.1.call-done.cot.left, bf16[4096,1408]{1,0:T(8,128)(2,1)} %get-tuple-element.129.right, bf16[2048,2048]{1,0:T(8,128)(2,1)} %pad_maximum_fusion.refs_0_), custom_call_target="tpu_custom_call" | custom-call | flops 11811160064 | bytes 25690112 | tf_op jit(solution)/shard_map/weight_grad/pallas_call | solution.py:709
  727.6 20.1 %weight_grad.7 = (f32[2048,1408]{1,0:T(8,128)}, f32[8,128]{1,0:T(8,128)}) custom-call(bf16[4096,2048]{1,0:T(8,128)(2,1)} %all-gather.5.cloned.1.call-done.feed.left, bf16[4096,1408]{1,0:T(8,128)(2,1)} %get-tuple-element.121.right, bf16[256,2048]{1,0:T(8,128)(2,1)} %get-tuple-element.146.refs_0_, ...), custom_call_target="tpu_custom_call", output_to_operand_aliasing={{0}: (3, {})} | custom-call | flops 11811160064 | bytes 25690112 | tf_op jit(solution)/shard_map/weight_grad/pallas_call | solution.py:709
  754.9 20.3 %weight_grad.11 = (f32[1408,2048]{1,0:T(8,128)}, f32[8,128]{1,0:T(8,128)}) custom-call(bf16[4096,2048]{1,0:T(8,128)(2,1)} %all-gather.3.cloned.1.call-done.cot.left, bf16[4096,1408]{1,0:T(8,128)(2,1)} %get-tuple-element.129.right, bf16[2048,2048]{1,0:T(8,128)(2,1)} %pad_maximum_fusion.refs_0_, ...), custom_call_target="tpu_custom_call", output_to_operand_aliasing={{0}: (3, {})} | custom-call | flops 11811160064 | bytes 25690112 | tf_op jit(solution)/shard_map/weight_grad/pallas_call | solution.py:709
  777.5 6.7 collective-permute-done.67
  (463 shorter events, 173.3 us)
Async XLA Ops:
  7.2 355.7 %all-gather.3.cloned.1.call-start = ((), (), s32[]{:S(2)}) async-start(), calls=%async_computation | async-start | bytes 17301504 | tf_op jit(solution)/shard_map/all_gather | solution.py:777
  11.0 9.8 %collective-permute-start.5 = (bf16[64,2048]{1,0:T(8,128)(2,1)S(1)}, bf16[64,2048]{1,0:T(8,128)(2,1)}, u32[]{:S(2)}, u32[]{:S(2)}) collective-permute-start(bf16[64,2048]{1,0:T(8,128)(2,1)S(1)} %get-tuple-element.167), channel_id=1, source_target_pairs={{0,2},{1,3},{2,0},{3,1},{4,6},{5,7},{6,4},{7,5},{8,10},{9,11},{10,... | collective-permute-start | bytes 786440 | tf_op jit(solution)/shard_map/ppermute | solution.py:19
  13.5 12.5 %collective-permute-start.6 = (bf16[64,2048]{1,0:T(8,128)(2,1)S(1)}, bf16[64,2048]{1,0:T(8,128)(2,1)}, u32[]{:S(2)}, u32[]{:S(2)}) collective-permute-start(bf16[64,2048]{1,0:T(8,128)(2,1)S(1)} %get-tuple-element.166), channel_id=1, source_target_pairs={{0,3},{1,2},{2,1},{3,0},{4,7},{5,6},{6,5},{7,4},{8,11},{9,10},{10,... | collective-permute-start | bytes 786440 | tf_op jit(solution)/shard_map/ppermute | solution.py:19
  27.0 25.3 %collective-permute-start.7 = (bf16[256,2048]{1,0:T(8,128)(2,1)S(1)}, bf16[256,2048]{1,0:T(8,128)(2,1)}, u32[]{:S(2)}, u32[]{:S(2)}) collective-permute-start(bf16[256,2048]{1,0:T(8,128)(2,1)S(1)} %constant_dynamic-update-slice_fusion.24), channel_id=1, source_target_pairs={{0,8},{8,16},{16,24},{24,28},{28,20},{20,12},{12,4},{4,0},{1,9},{9... | collective-permute-start | bytes 3145736 | tf_op jit(solution)/shard_map/ppermute | solution.py:82
  28.7 25.4 %collective-permute-start.8 = (bf16[256,2048]{1,0:T(8,128)(2,1)S(1)}, bf16[256,2048]{1,0:T(8,128)(2,1)}, u32[]{:S(2)}, u32[]{:S(2)}) collective-permute-start(bf16[256,2048]{1,0:T(8,128)(2,1)S(1)} %constant_dynamic-update-slice_fusion.24), channel_id=1, source_target_pairs={{0,4},{8,0},{16,8},{24,16},{28,24},{20,28},{12,20},{4,12},{1,5},{9... | collective-permute-start | bytes 3145736 | tf_op jit(solution)/shard_map/ppermute | solution.py:82
  52.4 28.5 %collective-permute-start.9 = (bf16[256,2048]{1,0:T(8,128)(2,1)}, bf16[256,2048]{1,0:T(8,128)(2,1)S(1)}, u32[]{:S(2)}, u32[]{:S(2)}) collective-permute-start(bf16[256,2048]{1,0:T(8,128)(2,1)} %collective-permute-done.7), channel_id=1, source_target_pairs={{0,8},{8,16},{16,24},{24,28},{28,20},{20,12},{12,4},{4,0},{1,9},{9... | collective-permute-start | bytes 3145736 | tf_op jit(solution)/shard_map/ppermute | solution.py:82
  54.1 28.5 %collective-permute-start.10 = (bf16[256,2048]{1,0:T(8,128)(2,1)}, bf16[256,2048]{1,0:T(8,128)(2,1)}, u32[]{:S(2)}, u32[]{:S(2)}) collective-permute-start(bf16[256,2048]{1,0:T(8,128)(2,1)} %collective-permute-done.8), channel_id=1, source_target_pairs={{0,4},{8,0},{16,8},{24,16},{28,24},{20,28},{12,20},{4,12},{1,5},{9... | collective-permute-start | bytes 3145736 | tf_op jit(solution)/shard_map/ppermute | solution.py:82
  80.8 25.9 %collective-permute-start.11 = (bf16[256,2048]{1,0:T(8,128)(2,1)S(1)}, bf16[256,2048]{1,0:T(8,128)(2,1)S(1)}, u32[]{:S(2)}, u32[]{:S(2)}) collective-permute-start(bf16[256,2048]{1,0:T(8,128)(2,1)S(1)} %collective-permute-done.9), channel_id=1, source_target_pairs={{0,8},{8,16},{16,24},{24,28},{28,20},{20,12},{12,4},{4,0},{1,9},{9... | collective-permute-start | bytes 3145736 | tf_op jit(solution)/shard_map/ppermute | solution.py:82
  82.5 23.8 %collective-permute-start.12 = (bf16[256,2048]{1,0:T(8,128)(2,1)}, bf16[256,2048]{1,0:T(8,128)(2,1)S(1)}, u32[]{:S(2)}, u32[]{:S(2)}) collective-permute-start(bf16[256,2048]{1,0:T(8,128)(2,1)} %collective-permute-done.10), channel_id=1, source_target_pairs={{0,4},{8,0},{16,8},{24,16},{28,24},{20,28},{12,20},{4,12},{1,5},{9... | collective-permute-start | bytes 3145736 | tf_op jit(solution)/shard_map/ppermute | solution.py:82
  106.4 11.5 %collective-permute-start.14 = (bf16[128,2048]{1,0:T(8,128)(2,1)S(1)}, bf16[128,2048]{1,0:T(8,128)(2,1)S(1)}, u32[]{:S(2)}, u32[]{:S(2)}) collective-permute-start(bf16[128,2048]{1,0:T(8,128)(2,1)S(1)} %slice.221), channel_id=1, source_target_pairs={{0,4},{8,0},{16,8},{24,16},{28,24},{20,28},{12,20},{4,12},{1,5},{9... | collective-permute-start | bytes 1572872 | tf_op jit(solution)/shard_map/ppermute | solution.py:82
  106.8 11.2 %collective-permute-start.13 = (bf16[128,2048]{1,0:T(8,128)(2,1)S(1)}, bf16[128,2048]{1,0:T(8,128)(2,1)S(1)}, u32[]{:S(2)}, u32[]{:S(2)}) collective-permute-start(bf16[128,2048]{1,0:T(8,128)(2,1)S(1)} %slice.220), channel_id=1, source_target_pairs={{0,8},{8,16},{16,24},{24,28},{28,20},{20,12},{12,4},{4,0},{1,9},{9... | collective-permute-start | bytes 1572872 | tf_op jit(solution)/shard_map/ppermute | solution.py:82
  119.1 432.2 %all-gather.5.cloned.1.call-start = ((), (), s32[]{:S(2)}) async-start(), calls=%async_computation.1 | async-start | bytes 17301504 | tf_op jit(solution)/shard_map/all_gather | solution.py:812
  121.2 19.1 %collective-permute-start = (bf16[1,136,2048]{2,1,0:T(8,128)(2,1)}, bf16[1,136,2048]{2,1,0:T(8,128)(2,1)}, u32[]{:S(2)}, u32[]{:S(2)}) collective-permute-start(bf16[1,136,2048]{2,1,0:T(8,128)(2,1)} %maximum_bitcast_fusion.1), channel_id=1, source_target_pairs={{0,1},{1,0},{2,3},{3,2},{4,5},{5,4},{6,7},{7,6},{8,9},{9,8},{10,11... | collective-permute-start | bytes 1671176 | tf_op jit(solution)/shard_map/ppermute | solution.py:19
  121.2 19.1 %collective-permute-start.1 = (bf16[1,136,2048]{2,1,0:T(8,128)(2,1)}, bf16[1,136,2048]{2,1,0:T(8,128)(2,1)}, u32[]{:S(2)}, u32[]{:S(2)}) collective-permute-start(bf16[1,136,2048]{2,1,0:T(8,128)(2,1)} %maximum_bitcast_fusion.1), channel_id=1, source_target_pairs={{0,2},{1,3},{2,0},{3,1},{4,6},{5,7},{6,4},{7,5},{8,10},{9,11},{10,... | collective-permute-start | bytes 1671176 | tf_op jit(solution)/shard_map/ppermute | solution.py:19
  150.8 5.9 collective-permute-start.17
  153.4 12.1 %collective-permute-start.3 = (bf16[16,2048]{1,0:T(8,128)(2,1)S(1)}, bf16[16,2048]{1,0:T(8,128)(2,1)S(1)}, u32[]{:S(2)}, u32[]{:S(2)}) collective-permute-start(bf16[16,2048]{1,0:T(8,128)(2,1)S(1)} %slice_bitcast_fusion.2), channel_id=1, source_target_pairs={{0,4},{4,8},{8,12},{12,16},{16,20},{20,24},{24,28},{1,5},{5,9},{9,... | collective-permute-start | bytes 196616 | tf_op jit(solution)/shard_map/ppermute | solution.py:166
  176.0 75.6 %collective-permute-start.30 = (bf16[2048,512]{1,0:T(8,128)(2,1)}, bf16[2048,512]{1,0:T(8,128)(2,1)}, u32[]{:S(2)}, u32[]{:S(2)}) collective-permute-start(bf16[2048,512]{1,0:T(8,128)(2,1)} %get-tuple-element.154), channel_id=1, source_target_pairs={{0,2},{1,3},{2,0},{3,1},{4,6},{5,7},{6,4},{7,5},{8,10},{9,11},{10,... | collective-permute-start | bytes 6291464 | tf_op jit(solution)/shard_map/ppermute | solution.py:19
  213.8 10.5 %collective-permute-start.18 = (bf16[4,2,128,128]{3,2,1,0:T(8,128)(2,1)S(1)}, bf16[4,2,128,128]{3,2,1,0:T(8,128)(2,1)S(1)}, u32[]{:S(2)}, u32[]{:S(2)}) collective-permute-start(bf16[4,2,128,128]{3,2,1,0:T(8,128)(2,1)S(1)} %get-tuple-element.84), channel_id=1, source_target_pairs={{0,8},{8,16},{16,24},{24,28},{28,20},{20,12},{12,4},{4,0},{1,9},{9... | collective-permute-start | bytes 786440 | tf_op jit(solution)/shard_map/ppermute | solution.py:82
  215.7 8.6 %collective-permute-start.19 = (bf16[4,2,128,128]{3,2,1,0:T(8,128)(2,1)S(1)}, bf16[4,2,128,128]{3,2,1,0:T(8,128)(2,1)S(1)}, u32[]{:S(2)}, u32[]{:S(2)}) collective-permute-start(bf16[4,2,128,128]{3,2,1,0:T(8,128)(2,1)S(1)} %get-tuple-element.84), channel_id=1, source_target_pairs={{0,4},{8,0},{16,8},{24,16},{28,24},{20,28},{12,20},{4,12},{1,5},{9... | collective-permute-start | bytes 786440 | tf_op jit(solution)/shard_map/ppermute | solution.py:82
  215.9 61.1 %collective-permute-start.29 = (bf16[2048,512]{1,0:T(8,128)(2,1)}, bf16[2048,512]{1,0:T(8,128)(2,1)}, u32[]{:S(2)}, u32[]{:S(2)}) collective-permute-start(bf16[2048,512]{1,0:T(8,128)(2,1)} %get-tuple-element.154), channel_id=1, source_target_pairs={{0,1},{1,0},{2,3},{3,2},{4,5},{5,4},{6,7},{7,6},{8,9},{9,8},{10,11... | collective-permute-start | bytes 6291464 | tf_op jit(solution)/shard_map/ppermute | solution.py:19
  224.3 7.7 collective-permute-start.20
  224.3 10.0 %collective-permute-start.21 = (bf16[4,2,128,128]{3,2,1,0:T(8,128)(2,1)S(1)}, bf16[4,2,128,128]{3,2,1,0:T(8,128)(2,1)S(1)}, u32[]{:S(2)}, u32[]{:S(2)}) collective-permute-start(bf16[4,2,128,128]{3,2,1,0:T(8,128)(2,1)S(1)} %collective-permute-done.19), channel_id=1, source_target_pairs={{0,4},{8,0},{16,8},{24,16},{28,24},{20,28},{12,20},{4,12},{1,5},{9... | collective-permute-start | bytes 786440 | tf_op jit(solution)/shard_map/ppermute | solution.py:82
  232.0 11.9 %collective-permute-start.22 = (bf16[4,2,128,128]{3,2,1,0:T(8,128)(2,1)S(1)}, bf16[4,2,128,128]{3,2,1,0:T(8,128)(2,1)S(1)}, u32[]{:S(2)}, u32[]{:S(2)}) collective-permute-start(bf16[4,2,128,128]{3,2,1,0:T(8,128)(2,1)S(1)} %collective-permute-done.20), channel_id=1, source_target_pairs={{0,8},{8,16},{16,24},{24,28},{28,20},{20,12},{12,4},{4,0},{1,9},{9... | collective-permute-start | bytes 786440 | tf_op jit(solution)/shard_map/ppermute | solution.py:82
  234.4 9.4 %collective-permute-start.23 = (bf16[4,2,128,128]{3,2,1,0:T(8,128)(2,1)S(1)}, bf16[4,2,128,128]{3,2,1,0:T(8,128)(2,1)S(1)}, u32[]{:S(2)}, u32[]{:S(2)}) collective-permute-start(bf16[4,2,128,128]{3,2,1,0:T(8,128)(2,1)S(1)} %collective-permute-done.21), channel_id=1, source_target_pairs={{0,4},{8,0},{16,8},{24,16},{28,24},{20,28},{12,20},{4,12},{1,5},{9... | collective-permute-start | bytes 786440 | tf_op jit(solution)/shard_map/ppermute | solution.py:82
  243.8 7.9 collective-permute-start.25
  243.9 7.9 collective-permute-start.24
  251.7 32.5 %collective-permute-start.31 = (bf16[2048,512]{1,0:T(8,128)(2,1)}, bf16[2048,512]{1,0:T(8,128)(2,1)}, u32[]{:S(2)}, u32[]{:S(2)}) collective-permute-start(bf16[2048,512]{1,0:T(8,128)(2,1)} %collective-permute-done.30), channel_id=1, source_target_pairs={{0,1},{1,0},{2,3},{3,2},{4,5},{5,4},{6,7},{7,6},{8,9},{9,8},{10,11... | collective-permute-start | bytes 6291464 | tf_op jit(solution)/shard_map/ppermute | solution.py:19
  258.8 14.5 %collective-permute-start.27 = (bf16[512,512]{1,0:T(8,128)(2,1)}, bf16[512,512]{1,0:T(8,128)(2,1)S(1)}, u32[]{:S(2)}, u32[]{:S(2)}) collective-permute-start(bf16[512,512]{1,0:T(8,128)(2,1)} %get-tuple-element.89), channel_id=1, source_target_pairs={{0,2},{1,3},{2,0},{3,1},{4,6},{5,7},{6,4},{7,5},{8,10},{9,11},{10,... | collective-permute-start | bytes 1572872 | tf_op jit(solution)/shard_map/ppermute | solution.py:19
  260.5 14.3 %collective-permute-start.26 = (bf16[512,512]{1,0:T(8,128)(2,1)}, bf16[512,512]{1,0:T(8,128)(2,1)}, u32[]{:S(2)}, u32[]{:S(2)}) collective-permute-start(bf16[512,512]{1,0:T(8,128)(2,1)} %get-tuple-element.89), channel_id=1, source_target_pairs={{0,1},{1,0},{2,3},{3,2},{4,5},{5,4},{6,7},{7,6},{8,9},{9,8},{10,11... | collective-permute-start | bytes 1572872 | tf_op jit(solution)/shard_map/ppermute | solution.py:19
  299.2 14.4 %collective-permute-start.33 = (bf16[128,2048]{1,0:T(8,128)(2,1)S(1)}, bf16[128,2048]{1,0:T(8,128)(2,1)S(1)}, u32[]{:S(2)}, u32[]{:S(2)}) collective-permute-start(bf16[128,2048]{1,0:T(8,128)(2,1)S(1)} %copy-done.35), channel_id=1, source_target_pairs={{0,2},{1,3},{2,0},{3,1},{4,6},{5,7},{6,4},{7,5},{8,10},{9,11},{10,... | collective-permute-start | bytes 1572872 | tf_op jit(solution)/shard_map/ppermute | solution.py:19
  300.8 15.1 %collective-permute-start.32 = (bf16[128,2048]{1,0:T(8,128)(2,1)S(1)}, bf16[128,2048]{1,0:T(8,128)(2,1)}, u32[]{:S(2)}, u32[]{:S(2)}) collective-permute-start(bf16[128,2048]{1,0:T(8,128)(2,1)S(1)} %copy-done.35), channel_id=1, source_target_pairs={{0,1},{1,0},{2,3},{3,2},{4,5},{5,4},{6,7},{7,6},{8,9},{9,8},{10,11... | collective-permute-start | bytes 1572872 | tf_op jit(solution)/shard_map/ppermute | solution.py:19
  313.6 5.2 collective-permute-start.34
  352.5 4.8 collective-permute-start.35
  361.2 31.0 %collective-permute-start.36 = (bf16[1,128,2048]{2,1,0:T(8,128)(2,1)}, bf16[1,128,2048]{2,1,0:T(8,128)(2,1)S(1)}, u32[]{:S(2)}, u32[]{:S(2)}) collective-permute-start(bf16[1,128,2048]{2,1,0:T(8,128)(2,1)} %dynamic-slice_convert_fusion.1.refs_0_), channel_id=1, source_target_pairs={{0,2},{1,3},{2,0},{3,1},{4,6},{5,7},{6,4},{7,5},{8,10},{9,11},{10,... | collective-permute-start | bytes 1572872 | tf_op jit(solution)/shard_map/ppermute | solution.py:19
  400.7 9.8 %collective-permute-start.37 = (bf16[128,1024]{1,0:T(8,128)(2,1)S(1)}, bf16[128,1024]{1,0:T(8,128)(2,1)S(1)}, u32[]{:S(2)}, u32[]{:S(2)}) collective-permute-start(bf16[128,1024]{1,0:T(8,128)(2,1)S(1)} %pad_maximum_fusion.6), channel_id=1, source_target_pairs={{0,1},{1,0},{2,3},{3,2},{4,5},{5,4},{6,7},{7,6},{8,9},{9,8},{10,11... | collective-permute-start | bytes 786440 | tf_op jit(solution)/shard_map/ppermute | solution.py:19
  408.5 9.2 %collective-permute-start.38 = (bf16[128,1024]{1,0:T(8,128)(2,1)S(1)}, bf16[128,1024]{1,0:T(8,128)(2,1)S(1)}, u32[]{:S(2)}, u32[]{:S(2)}) collective-permute-start(bf16[128,1024]{1,0:T(8,128)(2,1)S(1)} %pad_maximum_fusion.7), channel_id=1, source_target_pairs={{0,2},{1,3},{2,0},{3,1},{4,6},{5,7},{6,4},{7,5},{8,10},{9,11},{10,... | collective-permute-start | bytes 786440 | tf_op jit(solution)/shard_map/ppermute | solution.py:19
  408.6 13.6 %collective-permute-start.39 = (bf16[128,1024]{1,0:T(8,128)(2,1)S(1)}, bf16[128,1024]{1,0:T(8,128)(2,1)S(1)}, u32[]{:S(2)}, u32[]{:S(2)}) collective-permute-start(bf16[128,1024]{1,0:T(8,128)(2,1)S(1)} %pad_maximum_fusion.8), channel_id=1, source_target_pairs={{0,3},{1,2},{2,1},{3,0},{4,7},{5,6},{6,5},{7,4},{8,11},{9,10},{10,... | collective-permute-start | bytes 786440 | tf_op jit(solution)/shard_map/ppermute | solution.py:19
  425.9 7.8 collective-permute-start.40
  428.3 6.1 collective-permute-start.41
  433.7 5.2 collective-permute-start.42
  434.4 11.4 %collective-permute-start.43 = (bf16[4,128,128]{2,1,0:T(8,128)(2,1)S(1)}, bf16[4,128,128]{2,1,0:T(8,128)(2,1)S(1)}, u32[]{:S(2)}, u32[]{:S(2)}) collective-permute-start(bf16[4,128,128]{2,1,0:T(8,128)(2,1)S(1)} %collective-permute-done.41), channel_id=1, source_target_pairs={{0,4},{8,0},{16,8},{24,16},{28,24},{20,28},{12,20},{4,12},{1,5},{9... | collective-permute-start | bytes 393224 | tf_op jit(solution)/shard_map/ppermute | solution.py:82
  438.9 11.8 %collective-permute-start.44 = (bf16[4,128,128]{2,1,0:T(8,128)(2,1)S(1)}, bf16[4,128,128]{2,1,0:T(8,128)(2,1)S(1)}, u32[]{:S(2)}, u32[]{:S(2)}) collective-permute-start(bf16[4,128,128]{2,1,0:T(8,128)(2,1)S(1)} %collective-permute-done.42), channel_id=1, source_target_pairs={{0,8},{8,16},{16,24},{24,28},{28,20},{20,12},{12,4},{4,0},{1,9},{9... | collective-permute-start | bytes 393224 | tf_op jit(solution)/shard_map/ppermute | solution.py:82
  445.7 5.0 collective-permute-start.45
  450.7 4.3 collective-permute-start.47
  450.7 4.3 collective-permute-start.46
  477.3 5.7 collective-permute-start.48
  494.1 22.0 %collective-permute-start.49 = (bf16[2,2,128,2048]{3,2,1,0:T(8,128)(2,1)}, bf16[2,2,128,2048]{3,2,1,0:T(8,128)(2,1)}, u32[]{:S(2)}, u32[]{:S(2)}) collective-permute-start(bf16[2,2,128,2048]{3,2,1,0:T(8,128)(2,1)} %dynamic-slice_bitcast_fusion), channel_id=1, source_target_pairs={{0,1},{1,0},{2,3},{3,2},{4,5},{5,4},{6,7},{7,6},{8,9},{9,8},{10,11... | collective-permute-start | bytes 6291464 | tf_op jit(solution)/shard_map/ppermute | solution.py:19
  494.2 4.8 collective-permute-start.51
  499.1 7.2 collective-permute-start.52
  506.3 9.3 %collective-permute-start.53 = (f32[152,128]{1,0:T(8,128)S(1)}, f32[152,128]{1,0:T(8,128)S(1)}, u32[]{:S(2)}, u32[]{:S(2)}) collective-permute-start(f32[152,128]{1,0:T(8,128)S(1)} %fusion.109), channel_id=1, source_target_pairs={{0,16},{4,20},{8,24},{12,28},{16,0},{20,4},{24,8},{28,12},{1,17},{... | collective-permute-start | bytes 233480 | tf_op jit(solution)/shard_map/ppermute | solution.py:19
  515.7 11.0 %collective-permute-start.54 = (f32[1,152,128]{2,1,0:T(8,128)S(1)}, f32[1,152,128]{2,1,0:T(8,128)S(1)}, u32[]{:S(2)}, u32[]{:S(2)}) collective-permute-start(f32[1,152,128]{2,1,0:T(8,128)S(1)} %get-tuple-element.141), channel_id=1, source_target_pairs={{0,1},{1,0},{2,3},{3,2},{4,5},{5,4},{6,7},{7,6},{8,9},{9,8},{10,11... | collective-permute-start | bytes 233480 | tf_op jit(solution)/shard_map/ppermute | solution.py:19
  515.8 10.9 %collective-permute-start.55 = (f32[1,152,128]{2,1,0:T(8,128)S(1)}, f32[1,152,128]{2,1,0:T(8,128)S(1)}, u32[]{:S(2)}, u32[]{:S(2)}) collective-permute-start(f32[1,152,128]{2,1,0:T(8,128)S(1)} %get-tuple-element.141), channel_id=1, source_target_pairs={{0,2},{1,3},{2,0},{3,1},{4,6},{5,7},{6,4},{7,5},{8,10},{9,11},{10,... | collective-permute-start | bytes 233480 | tf_op jit(solution)/shard_map/ppermute | solution.py:19
  520.4 25.6 %collective-permute-start.50 = (bf16[1,2,128,2048]{3,2,1,0:T(8,128)(2,1)}, bf16[1,2,128,2048]{3,2,1,0:T(8,128)(2,1)}, u32[]{:S(2)}, u32[]{:S(2)}) collective-permute-start(bf16[1,2,128,2048]{3,2,1,0:T(8,128)(2,1)} %dynamic-slice_convert_fusion), channel_id=1, source_target_pairs={{0,2},{1,3},{2,0},{3,1},{4,6},{5,7},{6,4},{7,5},{8,10},{9,11},{10,... | collective-permute-start | bytes 3145736 | tf_op jit(solution)/shard_map/ppermute | solution.py:19
  524.7 57.7 %collective-permute-start.57 = (bf16[128,2048]{1,0:T(8,128)(2,1)S(1)}, bf16[128,2048]{1,0:T(8,128)(2,1)S(1)}, u32[]{:S(2)}, u32[]{:S(2)}) collective-permute-start(bf16[128,2048]{1,0:T(8,128)(2,1)S(1)} %get-tuple-element.152.refs_0_), channel_id=1, source_target_pairs={{0,8},{8,16},{16,24},{24,28},{28,20},{20,12},{12,4},{4,0},{1,9},{9... | collective-permute-start | bytes 1572872 | tf_op jit(solution)/shard_map/ppermute | solution.py:82
  525.3 57.9 %collective-permute-start.61 = (bf16[128,2048]{1,0:T(8,128)(2,1)}, bf16[128,2048]{1,0:T(8,128)(2,1)S(1)}, u32[]{:S(2)}, u32[]{:S(2)}) collective-permute-start(bf16[128,2048]{1,0:T(8,128)(2,1)} %get-tuple-element.153), channel_id=1, source_target_pairs={{0,4},{8,0},{16,8},{24,16},{28,24},{20,28},{12,20},{4,12},{1,5},{9... | collective-permute-start | bytes 1572872 | tf_op jit(solution)/shard_map/ppermute | solution.py:82
  586.0 81.8 %collective-permute-start.58 = (bf16[256,2048]{1,0:T(8,128)(2,1)S(1)}, bf16[256,2048]{1,0:T(8,128)(2,1)S(1)}, u32[]{:S(2)}, u32[]{:S(2)}) collective-permute-start(bf16[256,2048]{1,0:T(8,128)(2,1)S(1)} %pad_maximum_fusion.4.refs_0_), channel_id=1, source_target_pairs={{0,8},{8,16},{16,24},{24,28},{28,20},{20,12},{12,4},{4,0},{1,9},{9... | collective-permute-start | bytes 3145736 | tf_op jit(solution)/shard_map/ppermute | solution.py:82
  587.7 84.6 %collective-permute-start.62 = (bf16[256,2048]{1,0:T(8,128)(2,1)}, bf16[256,2048]{1,0:T(8,128)(2,1)S(1)}, u32[]{:S(2)}, u32[]{:S(2)}) collective-permute-start(bf16[256,2048]{1,0:T(8,128)(2,1)} %pad_maximum_fusion.5), channel_id=1, source_target_pairs={{0,4},{8,0},{16,8},{24,16},{28,24},{20,28},{12,20},{4,12},{1,5},{9... | collective-permute-start | bytes 3145736 | tf_op jit(solution)/shard_map/ppermute | solution.py:82
  671.7 24.1 %collective-permute-start.59 = (bf16[256,2048]{1,0:T(8,128)(2,1)}, bf16[256,2048]{1,0:T(8,128)(2,1)S(1)}, u32[]{:S(2)}, u32[]{:S(2)}) collective-permute-start(bf16[256,2048]{1,0:T(8,128)(2,1)} %fusion.7.refs_0_), channel_id=1, source_target_pairs={{0,8},{8,16},{16,24},{24,28},{28,20},{20,12},{12,4},{4,0},{1,9},{9... | collective-permute-start | bytes 3145736 | tf_op jit(solution)/shard_map/ppermute | solution.py:82
  700.4 23.0 %collective-permute-start.63 = (bf16[256,2048]{1,0:T(8,128)(2,1)S(1)}, bf16[256,2048]{1,0:T(8,128)(2,1)S(1)}, u32[]{:S(2)}, u32[]{:S(2)}) collective-permute-start(bf16[256,2048]{1,0:T(8,128)(2,1)S(1)} %get-tuple-element.147), channel_id=1, source_target_pairs={{0,4},{8,0},{16,8},{24,16},{28,24},{20,28},{12,20},{4,12},{1,5},{9... | collective-permute-start | bytes 3145736 | tf_op jit(solution)/shard_map/ppermute | solution.py:82
  721.9 25.8 %collective-permute-start.60 = (bf16[256,2048]{1,0:T(8,128)(2,1)}, bf16[256,2048]{1,0:T(8,128)(2,1)S(1)}, u32[]{:S(2)}, u32[]{:S(2)}) collective-permute-start(bf16[256,2048]{1,0:T(8,128)(2,1)} %get-tuple-element.146.refs_0_), channel_id=1, source_target_pairs={{0,8},{8,16},{16,24},{24,28},{28,20},{20,12},{12,4},{4,0},{1,9},{9... | collective-permute-start | bytes 3145736 | tf_op jit(solution)/shard_map/ppermute | solution.py:82
  726.3 22.4 %collective-permute-start.64 = (bf16[256,2048]{1,0:T(8,128)(2,1)S(1)}, bf16[256,2048]{1,0:T(8,128)(2,1)S(1)}, u32[]{:S(2)}, u32[]{:S(2)}) collective-permute-start(bf16[256,2048]{1,0:T(8,128)(2,1)S(1)} %fusion.6), channel_id=1, source_target_pairs={{0,4},{8,0},{16,8},{24,16},{28,24},{20,28},{12,20},{4,12},{1,5},{9... | collective-permute-start | bytes 3145736 | tf_op jit(solution)/shard_map/ppermute | solution.py:82
  753.3 23.2 %collective-permute-start.65 = (bf16[64,2048]{1,0:T(8,128)(2,1)}, bf16[64,2048]{1,0:T(8,128)(2,1)S(1)}, u32[]{:S(2)}, u32[]{:S(2)}) collective-permute-start(bf16[64,2048]{1,0:T(8,128)(2,1)} %get-tuple-element.164), channel_id=1, source_target_pairs={{0,1},{1,0},{2,3},{3,2},{4,5},{5,4},{6,7},{7,6},{8,9},{9,8},{10,11... | collective-permute-start | bytes 786440 | tf_op jit(solution)/shard_map/ppermute | solution.py:19
  753.3 23.6 %collective-permute-start.66 = (bf16[64,2048]{1,0:T(8,128)(2,1)S(1)}, bf16[64,2048]{1,0:T(8,128)(2,1)S(1)}, u32[]{:S(2)}, u32[]{:S(2)}) collective-permute-start(bf16[64,2048]{1,0:T(8,128)(2,1)S(1)} %get-tuple-element.163), channel_id=1, source_target_pairs={{0,2},{1,3},{2,0},{3,1},{4,6},{5,7},{6,4},{7,5},{8,10},{9,11},{10,... | collective-permute-start | bytes 786440 | tf_op jit(solution)/shard_map/ppermute | solution.py:19
  775.6 8.7 %collective-permute-start.67 = (bf16[64,2048]{1,0:T(8,128)(2,1)}, bf16[64,2048]{1,0:T(8,128)(2,1)}, u32[]{:S(2)}, u32[]{:S(2)}) collective-permute-start(bf16[64,2048]{1,0:T(8,128)(2,1)} %get-tuple-element.162), channel_id=1, source_target_pairs={{0,3},{1,2},{2,1},{3,0},{4,7},{5,6},{6,5},{7,4},{8,11},{9,10},{10,... | collective-permute-start | bytes 786440 | tf_op jit(solution)/shard_map/ppermute | solution.py:19
  (80 other events, 1111.3 us)
Sparse Core Ops, SparseCore 0:
  119.3 150.1 all-gather.2
  299.3 127.2 all-gather.4

commit v3 on v2

v3 whole, which is shorter than its diff:
```python
import functools

import jax
import jax.numpy as jnp
from jax import lax
from jax.experimental import pallas as pl
from jax.experimental.pallas import tpu as pltpu
from jax.sharding import PartitionSpec as P

NORM_EPS = 1e-06
HEAD_EPS = 1e-05
UNIT_EPS = 1e-06
BOTH = ("dev", "ta")
BF = jnp.bfloat16
F32 = jnp.float32


def swap(x, axis, bit):
    return lax.ppermute(x, axis, [(i, i ^ bit) for i in range(lax.axis_size(axis))])


def gather_parts(x, *waits):
    parts = [x]
    for j in range(1, lax.axis_size("ta")):
        bit = j & -j
        if waits and j == 2 * bit + bit:
            parts[j ^ bit] = gate(parts[j ^ bit], *waits)
        parts.append(swap(parts[j ^ bit], "ta", bit))
    return parts


def gate(x, *deps):
    return pl.pallas_call(
        lambda *refs: None,
        name="gate",
        out_shape=jax.ShapeDtypeStruct(x.shape, x.dtype),
        in_specs=[pl.BlockSpec(memory_space=pl.ANY)] * (1 + len(deps)),
        out_specs=pl.BlockSpec(memory_space=pl.ANY),
        input_output_aliases={0: 0},
    )(x, *deps)


class Ring:
    def __init__(self):
        n = self.size = lax.axis_size("dev")
        self.last = n // 2
        self.order = list(range(0, n, 2)) + list(range(n - 1, 0, -2))
        self.place = lax.axis_index("dev")
        self.spot = self.spot_of(self.place)
        distances = [0] + [d for s in range(1, self.last) for d in (-s, s)] + [self.last]
        spots = lax.rem(self.spot + n + jnp.array(distances, jnp.int32), n)
        self.slots = jnp.where(2 * spots < n, 2 * spots, 2 * (n - 1 - spots) + 1)
        away = lax.rem(self.spot_of(jnp.arange(n, dtype=jnp.int32)) + n - self.spot, n)
        slot = jnp.where(away < self.last, 2 * away, 2 * (n - away) - 1)
        self.slot_of = jnp.where(away == self.last, n - 1, slot)

    def spot_of(self, index):
        return jnp.where(index % 2 == 0, index // 2, self.size - 1 - index // 2)

    def move(self, x, step):
        n = self.size
        return lax.ppermute(x, "dev", [(self.order[p], self.order[(p + step) % n]) for p in range(n)])

    def collect(self, x, waits=()):
        half = x.shape[0] // 2
        found = [x]
        onward, back = x, x
        for s in range(1, self.last):
            onward, back = self.move(onward, 1), self.move(back, -1)
            if len(waits) >= s and waits[s - 1]:
                onward, back = gate(onward, *waits[s - 1]), gate(back, *waits[s - 1])
            found += [onward, back]
        far = [self.move(onward[:half], 1), self.move(back[half:], -1)]
        return found + [jnp.concatenate(far, axis=0)]

    def scatter(self, blocks, beside=()):
        last = self.last
        beside = list(beside) + [None] * last
        block = lambda d: blocks[0 if d == 0 else 2 * d if 0 < d < last else -2 * d - 1 if d < 0 else -1]
        half = blocks[0].shape[0] // 2
        right, left = block(last)[:half], block(last)[half:]
        for s in range(last - 1, -1, -1):
            ahead, behind = self.move(right, 1), self.move(left, -1)
            deps = [beside[last - 1 - s](right)] if beside[last - 1 - s] else []
            if s:
                like = [shape(block(s).shape, BF)] * 2
                right, left = vmem_call(
                    "ring_add", ring_add_kernel, like, [block(s), block(-s), ahead, behind], 0, deps
                )
        return [block(0), ahead, behind], deps


def ring_add_kernel(first, second, ahead, behind, right, left):
    rows, part = first.shape[0], ahead.shape[0]
    for block, arrived, out, at in (
        (first, ahead, right, slice(0, part)),
        (second, behind, left, slice(rows - part, rows)),
    ):
        if part < rows:
            out[...] = block[...]
        out[at, :] = (block[at, :].astype(F32) + arrived[...].astype(F32)).astype(BF)


def sum_kernel(x, y, z, out):
    out[...] = (x[...].astype(F32) + (y[...].astype(F32) + z[...].astype(F32))).astype(BF)


def assemble_kernel(rank, *refs):
    out, parts = refs[-1], refs[:-1]
    count = out.shape[1]
    cols = parts[0].shape[1] // count
    for j, part in enumerate(parts):
        at = pl.ds(pl.multiple_of((rank[0] ^ j) * cols, cols), cols)
        for i in range(count):
            out[:, i, at] = part[:, i * cols : (i + 1) * cols].astype(F32)


def add_kernel(x, y, out):
    out[...] = x[...] + y[...]


def exchange(blocks, rank):
    parts = []
    for j in range(lax.axis_size("ta")):
        block = lax.dynamic_index_in_dim(blocks, rank ^ j, 0, False)
        parts.append(swap(block, "ta", j) if j else block)
    return parts


def sum_over(x, axis, waits):
    size = lax.axis_size(axis)
    bit, n = 1, 0
    while bit < size:
        (x,) = vmem_call("add", add_kernel, [shape(x.shape)], [x, swap(x, axis, bit)], 0, waits[n : n + 1])
        bit, n = 2 * bit, n + 1
    return x


def scatter_sum(kept, sent, rank, beside=None):
    lanes = lax.axis_size("ta")
    made = None
    bit = 1
    while True:
        arrived = swap(sent, "ta", bit)
        bit *= 2
        if bit == lanes:
            if beside:
                made = beside(sent)
                arrived = gate(arrived, made[0])
            return kept[0], arrived[0], made
        blocks = kept.astype(F32) + arrived.astype(F32)
        pairs = blocks.reshape((blocks.shape[0] // 2, 2) + blocks.shape[1:])
        mine = (rank // bit) % 2
        kept = lax.dynamic_index_in_dim(pairs, mine, 1, False)
        sent = lax.dynamic_index_in_dim(pairs, 1 - mine, 1, False).astype(BF)


def rms_scale(values, gain):
    return values * lax.rsqrt(jnp.mean(values * values, axis=-1, keepdims=True) + NORM_EPS) * gain


def document_of(lengths, positions):
    starts = jnp.cumsum(lengths) - lengths
    above = (starts[None, :] <= positions[:, None]).astype(jnp.int32)
    return jnp.sum(above, axis=1) - 1


def contract_rows(left, right):
    return lax.dot_general(left, right, (((0,), (0,)), ((), ())), preferred_element_type=F32)


def contract_cols(left, right):
    return lax.dot_general(left, right, (((1,), (1,)), ((), ())), preferred_element_type=F32)


def dot(left, right):
    return jnp.dot(left, right, preferred_element_type=F32)


PAD = 8
VMEM_LIMIT = 48 * 1024 * 1024
FFN_VMEM = 56 * 1024 * 1024


def dims(a, b, ca, cb):
    return lax.dot_general(a, b, (((ca,), (cb,)), ((), ())), preferred_element_type=F32)


def d1(a, b, ca=1, cb=0):
    return dims(a.astype(BF), b.astype(BF), ca, cb)


def parts_of(a):
    high = a.astype(BF)
    return high, (a - high.astype(F32)).astype(BF)


def d3(a, b, ca=1, cb=0):
    ah, al = parts_of(a)
    bh, bl = parts_of(b)
    return dims(ah, bh, ca, cb) + (dims(ah, bl, ca, cb) + dims(al, bh, ca, cb))


def iotas(size):
    return (
        lax.broadcasted_iota(jnp.int32, (size, size), 0),
        lax.broadcasted_iota(jnp.int32, (size, size), 1),
    )


def inverses_of(lowers):
    size = lowers[0].shape[0]
    row, col = iotas(size)
    eye = (row == col).astype(F32)
    pair = (row // 2 == col // 2).astype(F32)
    found = [eye - low * pair for low in lowers]
    block = 2
    while block < size:
        joint = ((row // (2 * block) == col // (2 * block)) & (row // block != col // block)).astype(F32)
        steps = [d1(low * joint, x) for low, x in zip(lowers, found)]
        found = [x - d1(x, s) for x, s in zip(found, steps)]
        block *= 2
    errors = [d3(low, x) + (x - eye) for low, x in zip(lowers, found)]
    return [x - d1(x, e) for x, e in zip(found, errors)]


def unit_of(active):
    scale = lax.rsqrt(jnp.sum(active * active, axis=-1, keepdims=True) + UNIT_EPS)
    return active * scale, scale


def masks_of(aux, row, at, size):
    doc, doc_row = aux[at, 6:7], row[6:7, at]
    r, c = iotas(size)
    same = doc == doc_row
    weak = (same & (r >= c)).astype(F32)
    strict = (same & (r > c)).astype(F32)
    return weak, strict


def forward_kernel(size, xq, xk, xv, conv, aux_ref, row_ref, yq, yk, yv, inv, plain, reach, read, direct, trans, fresh, whole):
    count = inv.shape[1]
    depth = xq.shape[1]
    ksize = conv.shape[1]
    aux, row = aux_ref.at[0], row_ref.at[0]
    r, c = iotas(depth)
    eye = (r == c).astype(F32)
    spans = [slice(n * size, (n + 1) * size) for n in range(count)]
    saved = []
    lowers = []
    for n, at in enumerate(spans):
        active = []
        for i, (x, y) in enumerate(((xq, yq), (xk, yk), (xv, yv))):
            first = PAD - (ksize - 1) + n * size
            summed = x[first + ksize - 1 : first + ksize - 1 + size, :] * conv[i, ksize - 1 : ksize, :]
            for j in range(ksize - 1):
                summed = summed + x[first + j : first + j + size, :] * conv[i, j : j + 1, :] * aux[at, j : j + 1]
            y[at, :] = summed
            active.append(summed * jax.nn.sigmoid(summed))
        q = unit_of(active[0])[0] * depth ** (-0.5)
        k = unit_of(active[1])[0]
        weak, strict = masks_of(aux, row, at, size)
        rate = row[7:8, at]
        products = d3(jnp.concatenate([q, k], axis=0), k, 1, 1)
        lowers.append(products[size:] * rate * strict)
        saved.append((q, k, active[2], products[:size] * rate * weak))
    inverses = inverses_of(lowers)
    total = added = None
    for n, at in enumerate(spans):
        q, k, v, mix = saved[n]
        cont, clos, beta = aux[at, 3:4], aux[at, 4:5], aux[at, 7:8]
        both = d3(inverses[n], jnp.concatenate([v, k * cont], axis=1))
        spread = d1(mix, both)
        inv[0, n] = inverses[n]
        plain[0, at, :] = both[:, :depth]
        reach[0, at, :] = both[:, depth:]
        direct[0, at, :] = spread[:, :depth]
        read[0, at, :] = q * cont - spread[:, depth:]
        gained = d3(k * (beta * clos), both, 0, 0)
        map_n = aux[(n + 1) * size - 1 : (n + 1) * size, 3:4] * eye - gained[:, depth:]
        add_n = gained[:, :depth]
        trans[0, n] = map_n
        fresh[0, n] = add_n
        if n == 0:
            total, added = map_n, add_n
        else:
            new = d3(map_n, jnp.concatenate([added, total], axis=1))
            total, added = new[:, depth:], new[:, :depth] + add_n
    whole[0, 0] = total.astype(BF)
    whole[0, 1] = added.astype(BF)


def read_kernel(size, count_of, index, *refs):
    parts, refs = refs[:count_of], refs[count_of:]
    trans, fresh, read, direct, gain, both, states, outputs, normed = refs
    heads, count = trans.shape[0], trans.shape[1]
    depth = trans.shape[-1]
    for n, part in enumerate(parts):
        both[index[1 + n]] = part[...]

    def earlier(i, carry):
        return tuple(
            d3(both[i, h, 0].astype(F32), carry[h]) + both[i, h, 1].astype(F32) for h in range(heads)
        )

    carry = lax.fori_loop(0, index[0], earlier, tuple(jnp.zeros((depth, depth), F32) for _ in range(heads)))
    carry = list(carry)
    for n in range(count):
        at = slice(n * size, (n + 1) * size)
        for h in range(heads):
            state = carry[h]
            states[h, n] = state
            out = direct[h, at, :] + d3(read[h, at, :], state)
            cols = slice(h * depth, (h + 1) * depth)
            outputs[at, cols] = out
            scale = lax.rsqrt(jnp.mean(out * out, axis=-1, keepdims=True) + HEAD_EPS)
            normed[at, cols] = (out * scale * gain[...]).astype(BF)
            if n < count - 1:
                carry[h] = d3(trans[h, n], state) + fresh[h, n]


def leak_kernel(size, lanes, rank, *refs):
    parts, refs = refs[:lanes], refs[lanes:]
    outputs, gain, read, trans, grad_out, from_out, leak, grad_gain, mixed, grads = refs
    heads, count = trans.shape[0], trans.shape[1]
    depth = trans.shape[-1]
    for j, part in enumerate(parts):
        at = pl.ds(pl.multiple_of((rank[0] ^ j) * size, size), size)
        grads[at, :] = part[:, : heads * depth]
        mixed[at, :] = part[:, heads * depth :]
    gained = jnp.zeros((1, depth), F32)
    totals = [None] * heads
    for n in range(count - 1, -1, -1):
        at = slice(n * size, (n + 1) * size)
        for h in range(heads):
            cols = slice(h * depth, (h + 1) * depth)
            out, grad = outputs[at, cols], grads[at, cols].astype(F32)
            scale = lax.rsqrt(jnp.mean(out * out, axis=-1, keepdims=True) + HEAD_EPS)
            unit = out * scale
            gained = gained + jnp.sum(grad * unit, axis=0, keepdims=True)
            grad = grad * gain[...]
            grad = scale * (grad - unit * jnp.mean(grad * unit, axis=-1, keepdims=True))
            grad_out[h, at, :] = grad
            term = d3(read[h, at, :], grad, 0, 0)
            from_out[h, n] = term
            totals[h] = term if n == count - 1 else d3(trans[h, n], totals[h], 0, 0) + term
    for h in range(heads):
        leak[h] = totals[h].astype(BF)
    grad_gain[...] = gained


def chain_kernel(index, *refs):
    both, trans, from_out, grads = refs[-4:]
    leaks = refs[:-4]
    heads, count = trans.shape[0], trans.shape[1]
    depth = trans.shape[-1]
    devices = both.shape[0]
    carry = [jnp.zeros((depth, depth), F32) for _ in range(heads)]
    for k in range(devices - 1, 0, -1):
        at = jnp.minimum(index[0] + k, devices - 1)
        carry = [
            d3(both[at, h, 0].astype(F32), carry[h], 0, 0) + leaks[k - 1][h].astype(F32) for h in range(heads)
        ]
    for n in range(count - 1, -1, -1):
        for h in range(heads):
            grads[h, n] = carry[h]
            if n:
                carry[h] = d3(trans[h, n], carry[h], 0, 0) + from_out[h, n]


def backward_kernel(size, xq, xk, xv, yq, yk, yv, conv, aux_ref, row_ref, inv, plain, reach, states, grads, grad_out,
                    gq, gk, gv, tail, spill, grad_conv, grad_beta, zs):
    count = inv.shape[1]
    depth = xq.shape[1]
    ksize = conv.shape[1]
    aux, row = aux_ref.at[0], row_ref.at[0]
    length = count * size
    scale_q = depth ** (-0.5)
    for n in range(count):
        at = slice(n * size, (n + 1) * size)
        cont, clos, beta = aux[at, 3:4], aux[at, 4:5], aux[at, 7:8]
        weak, strict = masks_of(aux, row, at, size)
        rate = row[7:8, at]
        ys = [yq[at, :], yk[at, :], yv[at, :]]
        sigs = [jax.nn.sigmoid(y) for y in ys]
        uq, rq = unit_of(ys[0] * sigs[0])
        k, rk = unit_of(ys[1] * sigs[1])
        q = uq * scale_q
        products = d1(jnp.concatenate([q, k], axis=0), k, 1, 1)
        qk, kk = products[:size], products[size:]
        mix = qk * rate * weak
        state, grad_state, dout = states[0, n], grads[0, n], grad_out[0, at, :]
        u = plain[0, at, :] - d1(reach[0, at, :], state)
        kds = d1(k, grad_state)
        written = beta * clos
        du = d1(mix, dout, 0, 0) + written * kds
        dr = d1(inv[0, n], du, 0, 0)
        pair = jnp.concatenate([dout, dr], axis=0)
        outer = d1(pair, u, 1, 1)
        through = d1(pair, state, 1, 1)
        dp = outer[:size] * weak
        dl = -outer[size:] * strict
        per_key = jnp.sum(dp * qk + dl * kk, axis=0, keepdims=True)
        per_state = jnp.sum((kds * u).T, axis=0, keepdims=True)
        grad_beta[0, :, at] = per_key + row[4:5, at] * per_state
        dqk = dp * rate
        da = dl * rate
        dq = cont * through[:size] + d1(dqk, k)
        dk = d1(dqk, q, 0, 0) + written * d1(u, grad_state, 1, 1) - cont * through[size:] + d1(da + da.T, k)
        dq = dq * scale_q
        acts = [
            rq * (dq - uq * jnp.sum(uq * dq, axis=-1, keepdims=True)),
            rk * (dk - k * jnp.sum(k * dk, axis=-1, keepdims=True)),
            dr,
        ]
        for i, x in enumerate((xq, xk, xv)):
            dy = acts[i] * sigs[i] * (1.0 + ys[i] * (1.0 - sigs[i]))
            first = PAD - (ksize - 1) + n * size
            for j in range(ksize):
                dv = dy if j == ksize - 1 else dy * aux[at, j : j + 1]
                term = jnp.sum(dv * x[first + j : first + j + size, :], axis=0, keepdims=True)
                before = jnp.zeros_like(term) if n == 0 else grad_conv[i, j : j + 1, :]
                grad_conv[i, j : j + 1, :] = before + term
                zs[i, j, PAD + n * size : PAD + (n + 1) * size, :] = dv * conv[i, j : j + 1, :]
    for i, g in enumerate((gq, gk, gv)):
        for j in range(ksize):
            zs[i, j, 0:PAD, :] = jnp.zeros((PAD, depth), F32)
            zs[i, j, PAD + length : 2 * PAD + length, :] = jnp.zeros((PAD, depth), F32)

        def shifted_sum(first, rows):
            return sum(zs[i, j, first + ksize - 1 - j : first + ksize - 1 - j + rows, :] for j in range(ksize))

        for n in range(count):
            at = slice(n * size, (n + 1) * size)
            g[at, :] = (shifted_sum(PAD + n * size, size) * aux[at, 5:6]).astype(BF)
        tail[i] = shifted_sum(length, PAD)
        spill[i] = shifted_sum(0, PAD)


def vmem_call(name, kernel, out_shape, inputs, flops, deps=(), scratch=()):
    smem, vmem = (pl.BlockSpec(memory_space=m) for m in (pltpu.SMEM, pltpu.VMEM))

    def run(*refs):
        kernel(*refs[: len(inputs)], *refs[len(inputs) + len(deps) :])

    return pl.pallas_call(
        run,
        name=name,
        out_shape=out_shape,
        in_specs=[smem if x.dtype == jnp.int32 else vmem for x in inputs]
        + [pl.BlockSpec(memory_space=pl.ANY)] * len(deps),
        out_specs=[vmem] * len(out_shape),
        scratch_shapes=list(scratch),
        cost_estimate=cost(flops, inputs, out_shape),
        compiler_params=pltpu.CompilerParams(vmem_limit_bytes=FFN_VMEM),
    )(*inputs, *deps)


def cost(flops, inputs, outputs):
    moved = sum(x.size * x.dtype.itemsize for x in list(inputs) + list(outputs))
    return pl.CostEstimate(flops=int(flops), bytes_accessed=int(moved), transcendentals=0)


def shape(dims, dtype=F32):
    return jax.ShapeDtypeStruct(dims, dtype)


class Mixer:
    def __init__(self, projected, own_conv, aux, row, size):
        self.size = size
        self.heads, self.length = aux.shape[0], aux.shape[1]
        self.depth = own_conv.shape[2] // self.heads
        self.count = self.length // size
        self.projected, self.conv, self.aux, self.row = projected, own_conv, aux, row
        heads, length, depth, count = self.heads, self.length, self.depth, self.count
        ksize = own_conv.shape[1]
        self.token_specs = [
            pl.BlockSpec((length + PAD, depth), lambda h, i=i: (0, i * heads + h)) for i in range(3)
        ]
        self.head_cols = pl.BlockSpec((length, depth), lambda h: (0, h))
        self.conv_spec = pl.BlockSpec((3, ksize, depth), lambda h: (0, 0, h))
        self.aux_specs = [
            pl.BlockSpec((1, length, 8), lambda h: (h, 0, 0)),
            pl.BlockSpec((1, 8, length), lambda h: (h, 0, 0)),
        ]
        self.chunk_spec = pl.BlockSpec((1, count, depth, depth), lambda h: (h, 0, 0, 0))
        self.inv_spec = pl.BlockSpec((1, count, size, size), lambda h: (h, 0, 0, 0))
        self.rows_spec = pl.BlockSpec((1, length, depth), lambda h: (h, 0, 0))
        self.flops = 2 * heads * count * size * depth * depth
        inputs = [projected] * 3 + [own_conv, aux, row]
        square = shape((heads, count, depth, depth))
        tokens = shape((heads, length, depth))
        out_shape = (
            [shape((length, heads * depth))] * 3
            + [shape((heads, count, size, size))]
            + [tokens] * 4
            + [square] * 2
            + [shape((heads, 2, depth, depth), BF)]
        )
        (
            self.yq, self.yk, self.yv, self.inv, self.plain, self.reach, self.read, self.direct,
            self.trans, self.fresh, self.whole,
        ) = pl.pallas_call(
            functools.partial(forward_kernel, size),
            name="mixer_forward",
            out_shape=out_shape,
            grid=(heads,),
            in_specs=self.token_specs + [self.conv_spec] + self.aux_specs,
            out_specs=[self.head_cols] * 3
            + [self.inv_spec]
            + [self.rows_spec] * 4
            + [self.chunk_spec] * 2
            + [pl.BlockSpec((1, 2, depth, depth), lambda h: (h, 0, 0, 0))],
            cost_estimate=cost(60 * self.flops, inputs, out_shape),
            compiler_params=pltpu.CompilerParams(vmem_limit_bytes=VMEM_LIMIT),
        )(*inputs)

    def outputs(self, index, parts, head_gain):
        heads, length, depth, count = self.heads, self.length, self.depth, self.count
        self.index, self.gain = index, head_gain
        self.both, self.states, self.out, normed = vmem_call(
            "mixer_read",
            functools.partial(read_kernel, self.size, len(parts)),
            [
                shape((len(parts),) + parts[0].shape, BF),
                shape((heads, count, depth, depth)),
                shape((length, heads * depth)),
                shape((length, heads * depth), BF),
            ],
            [index, *parts, self.trans, self.fresh, self.read, self.direct, head_gain],
            12 * self.flops,
        )
        return normed

    def leak(self, rank, parts, deps=()):
        heads, length, depth, count = self.heads, self.length, self.depth, self.count
        self.grad_out, self.from_out, leak, grad_gain, mixed = vmem_call(
            "mixer_leak",
            functools.partial(leak_kernel, self.size, len(parts)),
            [
                shape((heads, length, depth)),
                shape((heads, count, depth, depth)),
                shape((heads, depth, depth), BF),
                shape((1, depth)),
                shape((length, heads * depth), BF),
            ],
            [rank, *parts, self.out, self.gain, self.read, self.trans],
            6 * self.flops,
            deps,
            scratch=[pltpu.VMEM((length, heads * depth), BF)],
        )
        return leak, grad_gain, mixed

    def back(self, leaks, deps=()):
        heads, length, depth, count = self.heads, self.length, self.depth, self.count
        ksize = self.conv.shape[1]
        (grads,) = vmem_call(
            "mixer_chain",
            chain_kernel,
            [shape((heads, count, depth, depth))],
            [self.index, *leaks, self.both, self.trans, self.from_out],
            6 * self.flops,
            deps,
        )
        inputs = [self.projected] * 3 + [self.yq, self.yk, self.yv, self.conv, self.aux, self.row]
        inputs += [self.inv, self.plain, self.reach, self.states, grads, self.grad_out]
        edge = shape((3, PAD, heads * depth))
        out_shape = [shape((length, heads * depth), BF)] * 3 + [edge] * 2
        out_shape += [shape((3, ksize, heads * depth)), shape((heads, 1, length))]
        edge_spec = pl.BlockSpec((3, PAD, depth), lambda h: (0, 0, h))
        return pl.pallas_call(
            functools.partial(backward_kernel, self.size),
            name="mixer_backward",
            out_shape=out_shape,
            grid=(heads,),
            in_specs=self.token_specs
            + [self.head_cols] * 3
            + [self.conv_spec]
            + self.aux_specs
            + [self.inv_spec, self.rows_spec, self.rows_spec, self.chunk_spec, self.chunk_spec, self.rows_spec],
            out_specs=[self.head_cols] * 3
            + [edge_spec] * 2
            + [self.conv_spec, pl.BlockSpec((1, 1, length), lambda h: (h, 0, 0))],
            scratch_shapes=[pltpu.VMEM((3, ksize, length + 2 * PAD, depth), F32)],
            cost_estimate=cost(30 * self.flops, inputs, out_shape),
            compiler_params=pltpu.CompilerParams(vmem_limit_bytes=VMEM_LIMIT),
        )(*inputs)


ANY = pl.BlockSpec(memory_space=pl.ANY)
TOKEN = shape((8, 128))


def resident(x):
    return pl.BlockSpec(x.shape, lambda *_: (0,) * x.ndim, pipeline_mode=pl.Buffered(1))


def activations(gate, lifted, grad_hidden):
    sig = jax.nn.sigmoid(gate)
    swish = gate * sig
    return (
        (swish * lifted).astype(BF),
        (grad_hidden * lifted * sig * (1.0 + gate * (1.0 - sig))).astype(BF),
        (grad_hidden * swish).astype(BF),
    )


def chunks_of(size, chunk=256):
    return [slice(at, min(at + chunk, size)) for at in range(0, size, chunk)]


def params(flops, moved):
    return dict(
        cost_estimate=pl.CostEstimate(flops=int(flops), bytes_accessed=int(moved), transcendentals=0),
        compiler_params=pltpu.CompilerParams(vmem_limit_bytes=FFN_VMEM),
    )


TOKEN_SPEC = pl.BlockSpec((8, 128), lambda *_: (0, 0))


def split_by_core(source, core, width, kept, sent):
    for p in range(kept.shape[0]):
        for ref, which in ((kept, core), (sent, 1 - core)):
            ref[p] = source[pl.ds(pl.multiple_of((2 * p + which) * width, width), width), :]


def own_kernel(index, feed, cot, wg, wu, wd, hidden, grad_gate, grad_lifted, kept, sent, branch, total):
    units, model = wd.shape
    for cut in chunks_of(units):
        gated = jnp.dot(feed[...], wg[:, cut], preferred_element_type=F32)
        lifted = jnp.dot(feed[...], wu[:, cut], preferred_element_type=F32)
        grad_hidden = dims(cot[...], wd[cut, :], 1, 1)
        hidden[:, cut], grad_gate[:, cut], grad_lifted[:, cut] = activations(gated, lifted, grad_hidden)
    for cut in chunks_of(model):
        grad_feed = dims(grad_gate[...], wg[cut, :], 1, 1) + dims(grad_lifted[...], wu[cut, :], 1, 1)
        total[:, cut] = grad_feed.astype(BF)
        branch[:, cut] = jnp.dot(hidden[...], wd[:, cut], preferred_element_type=F32).astype(BF)
    split_by_core(total, index[1], kept.shape[1], kept, sent)


def hidden_kernel(groups, cot, wd, *refs):
    out, token = refs[-2:]
    out[...] = dims(cot[...], wd[...], 1, 1).astype(BF)
    token[...] = jnp.zeros_like(token)


def rows_kernel(groups, feed, grad_hidden, wg, wu, *refs):
    *outs, token = refs[-4:]
    before = grad_hidden[...].reshape(feed.shape[0], -1)
    for cut in chunks_of(wg.shape[1]):
        gated = jnp.dot(feed[...], wg[:, cut], preferred_element_type=F32)
        lifted = jnp.dot(feed[...], wu[:, cut], preferred_element_type=F32)
        for out, value in zip(outs, activations(gated, lifted, before[:, cut].astype(F32))):
            out[:, :, :, cut] = value.reshape(out.shape[:-1] + (value.shape[-1],))
    token[...] = jnp.zeros_like(token)


def by_group(name, kernel, groups, size, inputs, weights, outs, held, deps, products, half=0):
    like = inputs[-1].shape
    count = groups.shape[0]

    def picked(x, width):
        if x.ndim == 2:
            return pl.BlockSpec((size, width), lambda i, g: (g[i], 0))
        return pl.BlockSpec((size // like[2], 1, like[2], width), lambda i, g: (g[i], half, 0, 0))

    first = 1 + len(inputs) + len(weights) + len(deps)
    return pl.pallas_call(
        kernel,
        name=name,
        out_shape=[shape(like[:-1] + (width,), BF) for width in outs] + [TOKEN],
        grid_spec=pltpu.PrefetchScalarGridSpec(
            num_scalar_prefetch=1,
            grid=(count,),
            in_specs=[picked(x, x.shape[-1]) for x in inputs]
            + [resident(w) for w in weights]
            + [ANY] * (len(deps) + len(held)),
            out_specs=[picked(inputs[-1], width) for width in outs] + [TOKEN_SPEC],
        ),
        input_output_aliases={first + n: n for n in range(len(held))},
        **params(
            2 * count * size * weights[0].size * products,
            sum(w.size for w in weights) * 2 + count * size * 2 * (sum(outs) + sum(x.shape[-1] for x in inputs)),
        ),
    )(groups, *inputs, *weights, *deps, *held)


def feed_own(index, feed, cot, weights, tokens, width):
    rows, model = feed.shape
    units = weights[0].shape[1]
    block = 2 * width
    count = rows // block
    wide = pl.BlockSpec((block, units), lambda i, g: (g[0] * count + i, 0))
    here = pl.BlockSpec((block, model), lambda i, g: (i, 0))
    half = pl.BlockSpec((1, width, model), lambda i, g: (i, 0, 0))
    return pl.pallas_call(
        own_kernel,
        name="feed_own",
        out_shape=[shape((tokens, units), BF)] * 3
        + [shape((count, width, model), BF)] * 2
        + [shape((rows, model), BF)],
        grid_spec=pltpu.PrefetchScalarGridSpec(
            num_scalar_prefetch=1,
            grid=(count,),
            in_specs=[here] * 2 + [resident(w) for w in weights],
            out_specs=[wide] * 3 + [half] * 2 + [here],
            scratch_shapes=[pltpu.VMEM((block, model), BF)],
        ),
        **params(12 * rows * model * units, 6 * model * units + rows * (3 * units + 4 * model) * 2),
    )(index, feed, cot, *weights)


GRAD_COLS = 256


def grad_kernel(transposed, count, *refs):
    lefts, right = refs[:count], refs[count]
    out, token = refs[-2:]
    units = right.shape[-1]
    if count == 1:
        term = dims(lefts[0][...], right[...].reshape(-1, units), 0, 0)
    else:
        term = sum(dims(left[...], right[:, n].reshape(-1, units), 0, 0) for n, left in enumerate(lefts))
    out[...] = term.T if transposed else term
    token[...] = jnp.zeros_like(token)


def weight_grad(part, parts, lefts, right, held, deps, transposed):
    rows, model = lefts[0].shape
    units = right.shape[-1]
    count = model // GRAD_COLS // parts
    if transposed:
        out_spec = pl.BlockSpec((units, GRAD_COLS), lambda m: (0, part * count + m))
    else:
        out_spec = pl.BlockSpec((GRAD_COLS, units), lambda m: (part * count + m, 0))
    first = len(lefts) + 1 + len(deps)
    tokens = rows * len(lefts)
    return pl.pallas_call(
        functools.partial(grad_kernel, transposed, len(lefts)),
        name="weight_grad",
        out_shape=[shape((units, model) if transposed else (model, units)), TOKEN],
        grid=(count,),
        in_specs=[pl.BlockSpec((rows, GRAD_COLS), lambda m: (0, part * count + m))] * len(lefts)
        + [resident(right)]
        + [ANY] * (len(deps) + len(held)),
        out_specs=[out_spec, TOKEN_SPEC],
        input_output_aliases={first + n: n for n in range(len(held))},
        **params(
            2 * tokens * count * GRAD_COLS * units,
            2 * tokens * (units + count * GRAD_COLS) + 4 * count * GRAD_COLS * units,
        ),
    )(*lefts, right, *deps, *held)


def order_kernel(rank, *refs):
    out = refs[-1]
    size = refs[0].shape[0]
    for j, part in enumerate(refs[:-1]):
        out[pl.ds(pl.multiple_of((rank[0] ^ j) * size, size), size), :] = part[...]


def in_order(parts, rank):
    rows, width = parts[0].shape
    return vmem_call(
        "in_order", order_kernel, [shape((rows * len(parts), width), parts[0].dtype)], [rank, *parts], 0
    )[0]


def norm_kernel(width, rank, *refs):
    gain, group, normed, extended, live = refs[-5:]
    parts = refs[:-5]

    def scaled(values):
        values = values.astype(F32)
        scale = lax.rsqrt(jnp.mean(values * values, axis=-1, keepdims=True) + NORM_EPS)
        return (values * scale * gain[...]).astype(BF)

    for j, part in enumerate(parts):
        at = rank[0] ^ j
        rows = part[0:width, :]
        group[pl.ds(pl.multiple_of(at * width, width), width), :] = rows
        rows = scaled(rows)
        normed[pl.ds(pl.multiple_of(at * width, width), width), :] = rows
        extended[pl.ds(pl.multiple_of(PAD + at * width, PAD), width), :] = rows
        live[at] = part[width : width + 8, 0 : 2 * width]

        @pl.when(at == 0)
        def _():
            extended[0:PAD, :] = scaled(part[width + 8 : width + 8 + PAD, :])


def weights_kernel(lanes, rank, *refs):
    out, parts = refs[-1], refs[:-1]
    rows = out.shape[0] - parts[0].shape[0]
    rows = rows // (lanes - 1)
    heads = parts[0].shape[0] - rows
    mine = lax.broadcasted_iota(jnp.int32, (heads, 128), 0) // (heads // lanes)
    tile = jnp.zeros((heads, 128), F32)
    for j, part in enumerate(parts):
        at = rank[0] ^ j
        out[pl.ds(pl.multiple_of(at * rows, rows), rows), :] = part[0:rows, :]
        tile = jnp.where(mine == at, part[rows:, 0:128].astype(F32), tile)
    out[lanes * rows :, :] = jnp.zeros((heads, out.shape[1]), BF)
    out[lanes * rows :, 0:128] = tile.astype(BF)


def project_kernel(lanes, slots, x, live, *refs):
    out, out_w, logit, wbeta = refs[-4:]
    parts, last = refs[: len(refs) // 2 - 2], refs[len(refs) // 2 - 2 : -4]
    size = out_w.shape[0] // len(parts)
    heads = parts[0].shape[0] - size
    own = heads // lanes
    total = None
    for n, part in enumerate(parts):
        at = pl.ds(pl.multiple_of(slots[n] * size, size), size)
        term = jnp.dot(x[:, at], part[0:size, :], preferred_element_type=F32)
        total = term if total is None else total + term
    out[...] = total * live[...]

    @pl.when(pl.program_id(0) == 0)
    def _():
        each = size // lanes
        row = lax.broadcasted_iota(jnp.int32, (heads, size), 0)
        col = lax.broadcasted_iota(jnp.int32, (heads, size), 1)
        own_row = lax.broadcasted_iota(jnp.int32, (8, heads), 0)
        own_col = lax.broadcasted_iota(jnp.int32, (8, heads), 1)
        picked = ((own_col % own == own_row) & (own_row < own)).astype(BF)
        for n, (part, columns) in enumerate(zip(parts, last)):
            out_w[n * size : (n + 1) * size, :] = columns[0:size, :]
            tile = jnp.concatenate([part[size:, 0:each]] * lanes, axis=1)
            tile = jnp.where(col // each == row // own, tile.astype(F32), 0.0).astype(BF)
            at = pl.ds(pl.multiple_of(slots[n] * size, size), size)
            wbeta[:, at] = jnp.dot(picked, tile, preferred_element_type=F32).astype(BF)
        logit[...] = dims(x[...], wbeta[...], 1, 1)


def project(slots, x, live, parts, lanes):
    rows, model = x.shape
    size, width = parts[0].shape
    cols = width // 4
    whole = lambda a: pl.BlockSpec(a.shape, lambda i, s: (0,) * len(a.shape))
    outs = [shape((rows, 3 * cols)), shape((model, cols), BF), shape((rows, 8)), shape((8, model), BF)]
    return pl.pallas_call(
        functools.partial(project_kernel, lanes),
        name="project",
        out_shape=outs,
        grid_spec=pltpu.PrefetchScalarGridSpec(
            num_scalar_prefetch=1,
            grid=(3,),
            in_specs=[whole(x), whole(live)]
            + [pl.BlockSpec((size, cols), lambda i, s: (0, i))] * len(parts)
            + [pl.BlockSpec((size, cols), lambda i, s: (0, 3))] * len(parts),
            out_specs=[pl.BlockSpec((rows, cols), lambda i, s: (0, i))] + [whole(a) for a in outs[1:]],
        ),
        **params(6 * rows * model * cols, 2 * x.size + 8 * model * cols),
    )(slots, x, live, *parts, *parts)


def out_kernel(lanes, index, *refs):
    heads, w, refs = refs[:lanes], refs[lanes : 2 * lanes], refs[2 * lanes :]
    tokens, gain, feed, *own_feed, own_residual, total = refs
    rank = index[0]
    width = own_residual.shape[0]
    cols = heads[0].shape[1]
    blocks = w[0].shape[0]
    size = w[0].shape[0] // (index.shape[0] - 1)
    per = cols // size
    for j in range(lanes):
        acc = None
        for i in range(lanes):
            for p in range(per):
                slot = index[1 + (rank ^ i) * per + p]
                rows = w[j][pl.ds(pl.multiple_of(slot * size, size), size), :]
                term = jnp.dot(heads[i][:, p * size : (p + 1) * size], rows, preferred_element_type=F32)
                acc = term if acc is None else acc + term
        at = pl.ds(pl.multiple_of((rank ^ j) * cols, cols), cols)
        total[:, at] = tokens[:, at].astype(F32) + acc
    for n in range(lanes):
        at = slice(n * width, (n + 1) * width)
        values = total[at, :]
        scale = lax.rsqrt(jnp.mean(values * values, axis=-1, keepdims=True) + NORM_EPS)
        feed[at, :] = (values * scale * gain[...]).astype(BF)
    own = pl.ds(pl.multiple_of(rank * width, width), width)
    own_residual[...] = total[own, :]
    for n, out in enumerate(own_feed):
        out[...] = feed[pl.ds(pl.multiple_of(rank * width + n * (width // 2), width // 2), width // 2), :]


def residual_kernel(lanes, index, *refs):
    w, refs = refs[:lanes], refs[lanes:]
    kept, arrived, residual, cot, gain, grad_residual, grad_gain = refs[:7]
    sent, mixed = refs[7 : 7 + lanes], refs[7 + lanes]
    rank = index[0]
    cols = w[0].shape[1]
    size = w[0].shape[0] // (index.shape[0] - 1)
    per = cols // size
    grad = kept[...].astype(F32) + arrived[...].astype(F32)
    values = residual[...]
    scale = lax.rsqrt(jnp.mean(values * values, axis=-1, keepdims=True) + NORM_EPS)
    unit = values * scale
    grad_gain[...] = jnp.sum(grad * unit, axis=0, keepdims=True)
    grad = grad * gain[...]
    grad = cot[...].astype(F32) + scale * (grad - unit * jnp.mean(grad * unit, axis=-1, keepdims=True))
    grad_residual[...] = grad
    mixed[...] = grad.astype(BF)
    columns = [pl.ds(pl.multiple_of((rank ^ j) * cols, cols), cols) for j in range(lanes)]
    for j in range(lanes):
        for p in range(per):
            slot = index[1 + (rank ^ j) * per + p]
            acc = None
            for i in range(lanes):
                rows = w[i][pl.ds(pl.multiple_of(slot * size, size), size), :]
                term = dims(mixed[:, columns[i]], rows, 1, 1)
                acc = term if acc is None else acc + term
            sent[j][:, p * size : (p + 1) * size] = acc.astype(BF)
        sent[j][:, cols:] = mixed[:, columns[j]]


def normed_back_kernel(blocks, index, *refs):
    w, refs = refs[:blocks], refs[blocks:]
    gq, gk, gv, tail, arrived, live, logit, wbeta, tokens, grads, kept, sent, gain, total = refs
    size = total.shape[1] // blocks
    cols = gq.shape[1]
    length = gq.shape[0]
    for i, g in enumerate((gq, gk, gv)):
        at = slice(i * cols, (i + 1) * cols)
        grads[:, at] = g[...]
        last = ((tail[i] + arrived[i].astype(F32)) * live[...]).astype(BF)
        grads[length - 16 :, at] = jnp.concatenate([g[length - 16 : length - PAD, :], last], axis=0)
    values = tokens[...].astype(F32)
    scale = lax.rsqrt(jnp.mean(values * values, axis=-1, keepdims=True) + NORM_EPS)
    for n in range(blocks):
        at = pl.ds(pl.multiple_of(index[1 + n] * size, size), size)
        part = dims(grads[...], w[n][0:size, : 3 * cols], 1, 1) + jnp.dot(
            logit[...], wbeta[:, at], preferred_element_type=F32
        )
        gain[:, at] = jnp.sum(part * (tokens[:, at].astype(F32) * scale), axis=0, keepdims=True)
        total[:, at] = part.astype(BF)
    split_by_core(total, index[0], kept.shape[1], kept, sent)


def weight_rows_kernel(lanes, index, *refs):
    heads, refs = refs[:lanes], refs[lanes:]
    normed, grads, mixed, logit = refs[:4]
    *outs, wbeta, joined = refs[4:]
    cols = mixed.shape[1]
    wide = grads.shape[1]
    size = outs[0].shape[0]
    rank = index[0]
    for j, part in enumerate(heads):
        joined[:, pl.ds(pl.multiple_of((rank ^ j) * cols, cols), cols)] = part[...]
    for n, out in enumerate(outs):
        at = pl.ds(pl.multiple_of(index[1 + n] * size, size), size)
        out[:, :wide] = dims(normed[:, at], grads[...], 0, 0).astype(BF)
        out[:, wide:] = dims(joined[:, at], mixed[...], 0, 0).astype(BF)
    wbeta[...] = dims(logit[...], normed[...], 0, 0)


def body(
    tokens,
    cotangent,
    lengths,
    pad_mask,
    attn_gain,
    projection_weight,
    w_beta,
    beta_bias,
    conv_weight,
    head_gain,
    mlp_gain,
    w_gate,
    w_up,
    w_down,
):
    width, model = tokens.shape
    heads = w_beta.shape[1]
    depth = head_gain.shape[0]
    ksize = conv_weight.shape[1]
    margin = ksize - 1
    lanes, blocks = lax.axis_size("ta"), lax.axis_size("dev")
    rank, place = lax.axis_index("ta"), lax.axis_index("dev")
    own_heads = heads // lanes
    cols = own_heads * depth
    rows = projection_weight.shape[0]
    group = lanes * width
    ring = Ring()

    positions = place * group + jnp.arange(group, dtype=jnp.int32)
    documents = document_of(lengths, positions)
    valid = jnp.stack(
        [
            (document_of(lengths, positions - margin + offset) == documents).astype(F32)
            for offset in range(ksize)
        ],
        axis=1,
    )
    previous = document_of(lengths, positions[::width] - 1)

    at_rank = rank.astype(jnp.int32).reshape(1)
    at_place = place.astype(jnp.int32).reshape(1)
    by_rank = jnp.concatenate([at_rank, ring.slot_of])

    flags = jnp.zeros((8, model), BF).at[0, 0:width].set(pad_mask.astype(BF))
    edge = jnp.concatenate([tokens[width - PAD :], flags], axis=0)
    route = [(i, i + 1) for i in range(lanes - 1, blocks * lanes - 1, lanes)]
    before = lax.ppermute(edge, BOTH, route)
    flags = flags.at[0, width : width + PAD].set(before[PAD, width - PAD : width])
    packed = gather_parts(jnp.concatenate([tokens, flags, before[0:PAD]], axis=0))
    cot_parts = gather_parts(cotangent)
    group_tokens, normed_group, normed, flags = vmem_call(
        "norm",
        functools.partial(norm_kernel, width),
        [
            shape((group, model), BF),
            shape((group, model), BF),
            shape((group + PAD, model), BF),
            shape((lanes, 8, 2 * width), BF),
        ],
        [at_rank, *packed, attn_gain[None]],
        0,
    )
    cot_group = in_order(cot_parts, at_rank)
    live = flags[:, 0, 0:width].reshape(group).astype(F32)
    live_ext = jnp.concatenate([flags[0, 0, width : width + PAD].astype(F32), live])[:, None]

    own_conv = lax.dynamic_slice_in_dim(conv_weight, rank * cols, cols, 2)
    own_bias = lax.dynamic_slice_in_dim(beta_bias, rank * own_heads, own_heads, 0)
    chunk_docs = documents.reshape(lanes, width)
    continuing = (chunk_docs == previous[:, None]).reshape(group).astype(F32)
    closing = (chunk_docs == chunk_docs[:, width - 1 :]).reshape(group).astype(F32)
    shared = jnp.stack(
        [valid[:, j] for j in range(margin)] + [continuing, closing, live, documents.astype(F32)], axis=0
    )
    shared = jnp.broadcast_to(shared, (own_heads,) + shared.shape)
    columns = jnp.transpose(shared, (0, 2, 1))

    split = jnp.transpose(projection_weight.reshape(rows, 4, lanes, cols), (2, 0, 1, 3)).reshape(lanes, rows, 4 * cols)
    turned = jnp.tile(w_beta.T.reshape(lanes, own_heads, rows), (1, lanes, 1))
    turned = jnp.pad(turned, ((0, 0), (0, 0), (0, 4 * cols - rows)))
    parts = exchange(jnp.concatenate([split, turned], axis=1), rank)
    (own_rows,) = vmem_call(
        "weights",
        functools.partial(weights_kernel, lanes),
        [shape((lanes * rows + heads, 4 * cols), BF)],
        [at_rank, *parts],
        0,
    )
    w = ring.collect(own_rows, [[packed[-1]], [normed, cot_group, live_ext], [columns, own_conv]])
    cot_all = lax.all_gather(gate(cotangent, w[-1]), BOTH, axis=0, tiled=True)
    projected, w_out, beta_logit, wbeta = project(ring.slots, normed, live_ext, w, lanes)
    beta_logit = beta_logit[PAD:, :own_heads]
    sig_beta = jax.nn.sigmoid(beta_logit + own_bias)
    beta = sig_beta * live[:, None]
    row = jnp.concatenate([shared, beta.T[:, None]], axis=1)
    columns = jnp.concatenate([columns, beta.T[:, :, None]], axis=2)
    mixer = Mixer(projected, own_conv, columns, row, width)
    head_normed = mixer.outputs(
        jnp.concatenate([at_place, ring.slots]), ring.collect(mixer.whole), head_gain[None]
    )
    w_out = gather_parts(w_out, head_normed)
    heads_low = gather_parts(head_normed)
    feed_rows, *own_feed, own_residual = vmem_call(
        "out",
        functools.partial(out_kernel, lanes),
        [shape((group, model), BF)] + [shape((width // 2, model), BF)] * 2 + [shape((width, model))],
        [by_rank, *heads_low, *w_out, group_tokens, mlp_gain[None]],
        2 * group * model * model,
        scratch=[pltpu.VMEM((group, model), F32)],
    )
    half_rows = width // 2
    feed_halves = [lax.all_gather(x, BOTH, axis=0, tiled=True) for x in own_feed]

    weights = [w_gate, w_up, w_down]
    units = w_gate.shape[1]
    core = (rank % 2).astype(jnp.int32).reshape(1)
    *arrays, kept, sent, partial_branch = feed_own(
        jnp.concatenate([at_place, core]), feed_rows, cot_group, weights, blocks * group, width
    )
    others = lax.rem(place + 1 + jnp.arange(blocks - 1, dtype=jnp.int32), blocks)
    row_parts = [others[: (blocks + 1) // 2], others[(blocks + 1) // 2 :]]

    def hidden_of(part, held, dep):
        return by_group(
            "feed_hidden", hidden_kernel, part, group, [cot_all], [w_down], [units], held, [dep], 1
        )[::-1]

    kept, arrived, (_, grad_hidden) = scatter_sum(
        kept, sent, rank, lambda sent: hidden_of(row_parts[0], [], sent)
    )

    halves_left = [0, 1]

    def by_halves(x):
        return x.reshape(blocks * lanes, 2, half_rows, x.shape[-1])

    def fill_rows(deps):
        half = halves_left.pop(0)
        *found, token = by_group(
            "feed_rows", rows_kernel, others, lanes * half_rows, [feed_halves[half], by_halves(grad_hidden)],
            weights[:2], [units] * 3, [by_halves(x) for x in arrays], deps, 2, half,
        )
        arrays[:] = [x.reshape(blocks * group, units) for x in found]
        return token

    order = [0, 1, 2]
    ffn_grads = [[], [], []]
    done = [0, 0, 0]

    def fill_grads(parts, dep):
        which = order[0]
        lefts = [cot_all] if which == 2 else feed_halves
        hidden, grad_gate, grad_lifted = arrays
        right = (grad_gate, grad_lifted, hidden)[which]
        right = by_halves(right)
        out, token = weight_grad(done[which], parts, lefts, right, ffn_grads[which], [dep], which == 2)
        ffn_grads[which] = [out]
        done[which] += 1
        if done[which] == parts:
            order.pop(0)
        return token

    grad_residual, grad_mlp_gain, *sent = vmem_call(
        "residual",
        functools.partial(residual_kernel, lanes),
        [shape((width, model)), shape((1, model))] + [shape((width, 2 * cols), BF)] * lanes,
        [by_rank, *w_out, kept, arrived, own_residual, cotangent, mlp_gain[None]],
        2 * width * model * model,
        scratch=[pltpu.VMEM((width, model), BF)],
    )
    by_heads = [swap(x, "ta", j) if j else x for j, x in enumerate(sent)]
    token, grad_hidden = hidden_of(row_parts[1], [grad_hidden], sent[0])
    leak, grad_head_gain, mixed_cols = mixer.leak(at_rank, by_heads, [token])
    leaks = [
        lax.ppermute(leak, "dev", [(i, i - k) for i in range(k, blocks)]) for k in range(1, blocks)
    ]
    token = fill_rows([leak])
    grad_q, grad_k, grad_v, tail, spill, grad_conv, grad_beta = mixer.back(leaks, [token])
    arrived = lax.ppermute(spill.astype(BF), "dev", [(i, i - 1) for i in range(1, blocks)])
    grad_logit = grad_beta[:, 0].T * beta * (1.0 - sig_beta)
    grad_bias = jnp.sum(grad_logit, axis=0)
    grad_logit_low = grad_logit.astype(BF)

    grad_logit_low = jnp.pad(grad_logit_low, ((0, 0), (0, 8 - own_heads)))

    half = (lanes // 2, width, model)
    grad_projected, kept, sent, grad_attn_gain = vmem_call(
        "normed_back",
        functools.partial(normed_back_kernel, blocks),
        [shape((group, 3 * cols), BF), shape(half, BF), shape(half, BF), shape((1, model))],
        [jnp.concatenate([core, ring.slots]), *w, grad_q, grad_k, grad_v, tail, arrived]
        + [live[group - PAD :, None], grad_logit_low, wbeta, group_tokens],
        2 * group * model * 3 * cols,
        scratch=[pltpu.VMEM((group, model), BF)],
    )

    *partial_rows, partial_wbeta = vmem_call(
        "weight_rows",
        functools.partial(weight_rows_kernel, lanes),
        [shape((model // blocks, 4 * cols), BF)] * blocks + [shape((8, model))],
        [jnp.concatenate([at_rank, ring.slots]), *heads_low, normed_group, grad_projected, mixed_cols]
        + [grad_logit_low],
        2 * group * model * 4 * cols,
        scratch=[pltpu.VMEM((group, model), BF)],
    )
    made = []

    def fill(function, *deps):
        made.append(function(*deps))
        return made[-1]

    terms, deps = ring.scatter(
        partial_rows,
        [
            lambda x: fill(fill_rows, [x]),
            lambda x: fill(fill_grads, 1, x),
            lambda x: fill(fill_grads, 1, x),
            lambda x: fill(fill_grads, 2, x),
        ],
    )
    (w_part,) = vmem_call("sum", sum_kernel, [shape(terms[0].shape, BF)], terms, 0, deps)
    w_parts = exchange(w_part.reshape(lanes, rows, 4 * cols), rank)
    token = fill_grads(2, w_part)
    (grad_projection,) = vmem_call(
        "assemble",
        assemble_kernel,
        [shape((rows, 4, model))],
        [at_rank, *w_parts],
        0,
        [token],
    )

    kept_b, sent_b = (
        lax.dynamic_index_in_dim(partial_branch.reshape(lanes // 2, 2, width, model), which, 1, False)
        for which in (rank % 2, 1 - rank % 2)
    )
    kept, arrived, _ = scatter_sum(
        jnp.concatenate([kept, kept_b], axis=1), jnp.concatenate([sent, sent_b], axis=1), rank,
        lambda sent: (made[0],),
    )
    both_sums = kept.astype(F32) + arrived.astype(F32)
    block_out = (own_residual + both_sums[width:]).astype(BF)
    _, attention_back = jax.vjp(lambda x: rms_scale(x, attn_gain), tokens.astype(F32))
    grad_tokens = grad_residual + attention_back(both_sums[:width])[0]

    gains = jnp.concatenate([grad_mlp_gain[0], grad_head_gain[0], grad_attn_gain[0]])
    pieces = [grad_conv.reshape(-1), partial_wbeta[:own_heads].reshape(-1), grad_bias, gains]
    ends = [0]
    for piece in pieces:
        ends.append(ends[-1] + piece.shape[0])
    flat = jnp.concatenate(pieces)
    flat = jnp.pad(flat, (0, -flat.shape[0] % 1024)).reshape(-1, 128)
    flat = sum_over(flat, "dev", made)
    flat = in_order(gather_parts(flat), at_rank).reshape(lanes, -1)
    conv_sum, wbeta_sum, bias_sum, gains = (flat[:, a:b] for a, b in zip(ends, ends[1:]))
    conv_sum = jnp.transpose(conv_sum.reshape(lanes, 3, ksize, cols), (1, 2, 0, 3))
    conv_sum = conv_sum.reshape(3, ksize, lanes * cols)
    wbeta_sum = lax.dynamic_slice_in_dim(
        wbeta_sum.reshape(heads, model), (place * lanes + rank) * rows, rows, 1
    )
    grad_w_beta = wbeta_sum.T
    bias_sum = bias_sum.reshape(heads)
    gains = jnp.sum(gains, axis=0)

    (grad_w_gate,), (grad_w_up,), (grad_w_down,) = ffn_grads
    return (
        block_out,
        grad_tokens,
        gains[model + depth : 2 * model + depth],
        grad_projection,
        grad_w_beta,
        bias_sum,
        conv_sum,
        gains[model : model + depth],
        gains[:model],
        grad_w_gate,
        grad_w_up,
        grad_w_down,
    )


def solution(mesh):
    rows = P(BOTH, None)
    three = P(BOTH, None, None)
    return jax.shard_map(
        body,
        mesh=mesh,
        in_specs=(
            rows,
            rows,
            P(),
            P(BOTH),
            P(),
            three,
            rows,
            P(),
            P(),
            P(),
            P(),
            P(None, "ta"),
            P(None, "ta"),
            P("ta", None),
        ),
        out_specs=(
            rows,
            rows,
            P(),
            three,
            rows,
            P(),
            P(),
            P(),
            P(),
            P(None, "ta"),
            P(None, "ta"),
            P("ta", None),
        ),
        check_vma=False,
    )
```

time: 801 us -> 703 us (0.88)
  Pallas kernels: 302 us -> 384 us
  matrix products: 46.9 us -> 0 us
  local copies, waits for them, and re-layouts: 107 us -> 61.7 us
  waiting for transfers between devices: 186 us -> 149 us
  other arithmetic: 49.9 us -> 22.1 us
  between operations: 29.7 us -> 15 us
  starting transfers between devices: 72.3 us -> 61.3 us
    pallas_call x12 -> x28, Pallas kernels: 232 us -> 315 us  [the longest x4 108 us: weight_grad(): pl.pallas_call(functools.partial(grad_kernel, transposed, len(lefts)), na...]
    dot_general x12 -> x0, matrix products: 46.9 us -> none  [the longest x3 20.2 us: dot(): return jnp.dot(left, right, preferred_element_type=F32)]
    ppermute x34 -> x31, waiting for transfers between devices: 94 us -> 48.2 us  [swap(): lax.ppermute(x, axis, [(i, i ^ bit) for i in range(lax.axis_size(axis))])]
    dynamic_update_slice x50 -> x0, local copies, waits for them, and re-layouts: 36.2 us -> none  [the longest x28 24.8 us: in_order(): lax.dynamic_update_slice_in_dim(joined, part, (rank ^ j) * size, axis)]
    convert_element_type x13 -> x3, other arithmetic: 16.7 us -> 1.39 us  [the longest x1 0.7 us: body(): live = flags[:, 0, 0:width].reshape(group).astype(F32)]
    ppermute x32 -> x24, starting transfers between devices: 38.7 us -> 27.8 us  [move(): lax.ppermute(x, 'dev', [(self.order[p], self.order[(p + step) % n]) for p...]
    dynamic_slice x11 -> x0, local copies, waits for them, and re-layouts: 9.23 us -> none  [the longest x2 4.24 us: body(): wbeta = lax.dynamic_index_in_dim(wbeta, rank, 1, False)]
    ppermute x34 -> x31, starting transfers between devices: 29 us -> 22.1 us  [swap(): lax.ppermute(x, axis, [(i, i ^ bit) for i in range(lax.axis_size(axis))])]
  transfers between devices with their start and end apart: 70 -> 67, of which waited for: 29 -> 24; matrix products, arithmetic and copies ran while one was open for 21% -> 7% of each run, Pallas kernels for 38% -> 54%
where the time goes in v3:
time: 703 us; the launch traced here: 693 us
  Pallas kernels  384 us (55%)
  waiting for transfers between devices  149 us (21%)
  local copies, waits for them, and re-layouts  61.7 us (9%)
  starting transfers between devices  61.3 us (9%)
  other arithmetic  22.1 us (3%)
  between operations  15 us (2%)
    pallas_call x4, Pallas kernels, weight_grad(): pl.pallas_call(functools.partial(grad_kernel, transposed, len(lefts)), na...  108 us
    pallas_call x4, Pallas kernels, by_group(): pl.pallas_call(kernel, name=name, out_shape=[shape(like[:-1] + (width,),...  103 us
    pallas_call x19, Pallas kernels, vmem_call(): pl.pallas_call(run, name=name, out_shape=out_shape, in_specs=[smem if x.d...  91.8 us
    ppermute x24, waiting for transfers between devices, move(): lax.ppermute(x, 'dev', [(self.order[p], self.order[(p + step) % n]) for p...  91.8 us
    ppermute x31, waiting for transfers between devices, swap(): lax.ppermute(x, axis, [(i, i ^ bit) for i in range(lax.axis_size(axis))])  48.2 us
    pallas_call x1, Pallas kernels, feed_own(): pl.pallas_call(own_kernel, name='feed_own', out_shape=[shape((tokens, uni...  29.6 us
    unnamed x157, local copies, waits for them, and re-layouts  28.5 us
    ppermute x24, starting transfers between devices, move(): lax.ppermute(x, 'dev', [(self.order[p], self.order[(p + step) % n]) for p...  27.8 us
  transfers between devices with their start and end apart: 67, of which 24 were waited for; matrix products, arithmetic and copies ran while one was open for 7% of the time, Pallas kernels for 54%

profile of v3, /device:TPU:0, one launch (start us, length us, event | category | flops | bytes accessed | tf_op | source)
XLA Modules:
  0.0 693.1 jit_solution(17017852041853844721)
XLA Ops:
  11.8 2.5 collective-permute-start.5
  16.4 2.0 broadcast_select_fusion
  22.9 6.7 collective-permute-done.6.refs_4_
  30.2 2.4 weights.1.refs_0_.refs_8_.refs_1_
  32.6 2.3 collective-permute-start.7
  36.4 6.2 collective-permute-done.2.refs_3_
  43.4 10.3 %collective-permute-done.11.refs_3_ = bf16[128,2048]{1,0:T(8,128)(2,1)} collective-permute-done((bf16[128,2048]{1,0:T(8,128)(2,1)S(1)}, bf16[128,2048]{1,0:T(8,128)(2,1)}, u32[]{:S(2)}, u32[]{:S(2)}) %collective-permute-start.11) | collective-permute-done | bytes 524320 | tf_op jit(solution)/shard_map/ppermute | solution.py:19
  54.2 6.2 collective-permute-done.7.refs_0_
  61.4 1.8 collective-permute-start.9
  65.4 3.0 in_order.2.refs_2_.cot
  68.4 5.5 norm.1
  76.2 11.8 %collective-permute-done.9.refs_0_ = bf16[272,2048]{1,0:T(8,128)(2,1)S(1)} collective-permute-done((bf16[272,2048]{1,0:T(8,128)(2,1)}, bf16[272,2048]{1,0:T(8,128)(2,1)S(1)}, u32[]{:S(2)}, u32[]{:S(2)}) %collective-permute-start.9) | collective-permute-done | bytes 1114144 | tf_op jit(solution)/shard_map/ppermute | solution.py:62
  94.2 20.7 %collective-permute-done.14.refs_0_ = bf16[272,2048]{1,0:T(8,128)(2,1)S(1)} collective-permute-done((bf16[272,2048]{1,0:T(8,128)(2,1)}, bf16[272,2048]{1,0:T(8,128)(2,1)S(1)}, u32[]{:S(2)}, u32[]{:S(2)}) %collective-permute-start.14) | collective-permute-done | bytes 1114144 | tf_op jit(solution)/shard_map/ppermute | solution.py:62
  122.1 7.7 %collective-permute-done.16 = bf16[136,2048]{1,0:T(8,128)(2,1)S(1)} collective-permute-done((bf16[136,2048]{1,0:T(8,128)(2,1)S(1)}, bf16[136,2048]{1,0:T(8,128)(2,1)S(1)}, u32[]{:S(2)}, u32[]{:S(2)}) %collective-permute-start.16) | collective-permute-done | bytes 557088 | tf_op jit(solution)/shard_map/ppermute | solution.py:62
  129.9 3.0 collective-permute-done.17
  134.6 11.5 %project.1 = (f32[520,1536]{1,0:T(8,128)}, bf16[2048,512]{1,0:T(8,128)(2,1)}, f32[520,8]{1,0:T(8,128)}, bf16[8,2048]{1,0:T(8,128)(2,1)}) custom-call(s32[8]{0:T(128)} %compare_select_fusion.slots, bf16[520,2048]{1,0:T(8,128)(2,1)} %get-tuple-element.126.refs_1_.x, f32[520,1]{1,0:T(8,128)} %broadcast_in_dim.55.refs_3_.live, ...), custom_call_target="tpu_custom_call" | custom-call | flops 3271557120 | bytes 10518528 | tf_op jit(solution)/shard_map/project/pallas_call | solution.py:844
  149.7 23.1 %mixer_forward.1 = (f32[512,512]{1,0:T(8,128)S(1)}, f32[512,512]{1,0:T(8,128)S(1)}, f32[512,512]{1,0:T(8,128)S(1)}, f32[4,4,128,128]{3,2,1,0:T(8,128)S(1)}, f32[...) custom-call(f32[520,1536]{1,0:T(8,128)} %get-tuple-element.128.xq.xk, ...), custom_call_target="tpu_custom_call" | custom-call | flops 4026531840 | bytes 20488192 | tf_op jit(solution)/shard_map/mixer_forward/pallas_call | solution.py:503
  174.8 2.0 collective-permute-start.18
  177.2 10.4 %collective-permute-done.18.refs_2_ = bf16[4,2,128,128]{3,2,1,0:T(8,128)(2,1)S(1)} collective-permute-done((bf16[4,2,128,128]{3,2,1,0:T(8,128)(2,1)S(1)}, bf16[4,2,128,128]{3,2,1,0:T(8,128)(2,1)S(1)}, u32[]{:S(2)}, u32[]{:S(2)}) %collective-permute-start.18) | collective-permute-done | bytes 262176 | tf_op jit(solution)/shard_map/ppermute | solution.py:62
  189.6 8.4 %collective-permute-done.20.refs_4_ = bf16[4,2,128,128]{3,2,1,0:T(8,128)(2,1)S(1)} collective-permute-done((bf16[4,2,128,128]{3,2,1,0:T(8,128)(2,1)S(1)}, bf16[4,2,128,128]{3,2,1,0:T(8,128)(2,1)S(1)}, u32[]{:S(2)}, u32[]{:S(2)}) %collective-permute-start.20) | collective-permute-done | bytes 262176 | tf_op jit(solution)/shard_map/ppermute | solution.py:62
  198.0 2.5 collective-permute-start.22
  201.9 5.8 collective-permute-done.22.refs_6_
  210.4 2.0 collective-permute-start.25
  213.1 4.6 collective-permute-done.24
  217.8 4.7 collective-permute-done.25
  224.2 5.3 mixer_read.1
  231.4 18.8 %collective-permute-done.27.refs_3_ = bf16[512,512]{1,0:T(8,128)(2,1)S(1)} collective-permute-done((bf16[512,512]{1,0:T(8,128)(2,1)}, bf16[512,512]{1,0:T(8,128)(2,1)S(1)}, u32[]{:S(2)}, u32[]{:S(2)}) %collective-permute-start.27) | collective-permute-done | bytes 524320 | tf_op jit(solution)/shard_map/ppermute | solution.py:19
  253.6 11.9 %out.1 = (bf16[512,2048]{1,0:T(8,128)(2,1)}, bf16[64,2048]{1,0:T(8,128)(2,1)}, bf16[64,2048]{1,0:T(8,128)(2,1)}, f32[128,2048]{1,0:T(8,128)}) custom-call(s32[9]{0:T(128)} %pad_add_fusion.refs_0_, bf16[512,512]{1,0:T(8,128)(2,1)} %get-tuple-element.135.refs_1_, bf16[512,512]{1,0:T(8,128)(2,1)} %copy-done.68, bf16[512,512]{1,0:T(8,128)(2,1)} %copy-done.67, ...), custom_call_target="tpu_custom_call" | custom-call | flops 4294967296 | bytes 16261156 | tf_op jit(solution)/shard_map/out/pallas_call | solution.py:446
  266.8 29.6 %feed_own.1 = (bf16[4096,1408]{1,0:T(8,128)(2,1)}, bf16[4096,1408]{1,0:T(8,128)(2,1)}, bf16[4096,1408]{1,0:T(8,128)(2,1)}, bf16[2,128,2048]{2,1,0:T(8,128)(2,1)}...) custom-call(s32[2]{0:T(128)} %pad_add_fusion.3.index, bf16[512,2048]{1,0:T(8,128)(2,1)} %get-tuple-element.146.feed, ...), custom_call_target="tpu_custom_call" | custom-call | flops 17716740096 | bytes 30015488 | tf_op jit(solution)/shard_map/feed_own/pallas_call | solution.py:697
  299.4 1.9 convert_add_fusion.2
  303.7 19.1 %feed_hidden.2 = (bf16[4096,1408]{1,0:T(8,128)(2,1)}, f32[8,128]{1,0:T(8,128)}) custom-call(s32[4]{0:T(128)} %bitcast.150, bf16[4096,2048]{1,0:T(8,128)(2,1)} %all-gather.4.cloned.1.call-done.cot.refs_0_, bf16[1408,2048]{1,0:T(8,128)(2,1)} %wd.5, bf16[1,128,2048]{2,1,0:T(8,128)(2,1)} %dynamic-slice_convert_fusion.1.refs_0_), custom_call_target="tpu_custom_call" | custom-call | flops 11811160064 | bytes 19922944 | tf_op jit(solution)/shard_map/feed_hidden/pallas_call | solution.py:669
  322.8 8.9 %residual.1 = (f32[128,2048]{1,0:T(8,128)}, f32[1,2048]{1,0:T(1,128)}, bf16[128,1024]{1,0:T(8,128)(2,1)}, bf16[128,1024]{1,0:T(8,128)(2,1)}, bf16[128,1024]{1,0:T(8,128)(2,1)}, /*index=5*/bf16[128,1024]{1,0:T(8,128)(2,1)}) custom-call(s32[9]{0:T(128)} %pad_add_fusion.refs_0_, bf16[2048,512]{1,0:T(8,128)(2,1)} %get-tuple-element.136.refs_5_.refs_1_, ...), custom_call_target="tpu_custom_call" | custom-call | flops 1073741824 | bytes 13647908 | tf_op jit(solution)/shard_map/residual/pallas_call | solution.py:446
  331.7 1.7 collective-permute-start.35
  333.5 15.5 %feed_hidden.3 = (bf16[4096,1408]{1,0:T(8,128)(2,1)}, f32[8,128]{1,0:T(8,128)}) custom-call(s32[3]{0:T(128)} %slice.140.groups, bf16[4096,2048]{1,0:T(8,128)(2,1)} %all-gather.4.cloned.1.call-done.cot.refs_0_, bf16[1408,2048]{1,0:T(8,128)(2,1)} %wd.5, bf16[128,1024]{1,0:T(8,128)(2,1)} %get-tuple-element.150.refs_0_.refs_1_, ...), custom_call_target="tpu_custom_call", output_to_operand_aliasing={{0}: (4, {})} | custom-call | flops 8858370048 | bytes 16384000 | tf_op jit(solution)/shard_map/feed_hidden/pallas_call | solution.py:669
  349.9 6.0 mixer_leak.1
  365.9 5.7 collective-permute-done.38.refs_2_
  372.9 34.4 %feed_rows.2 = (bf16[32,2,64,1408]{3,2,1,0:T(8,128)(2,1)}, bf16[32,2,64,1408]{3,2,1,0:T(8,128)(2,1)}, bf16[32,2,64,1408]{3,2,1,0:T(8,128)(2,1)}, f32[8,128]{1,0:T(8,128)}) custom-call(s32[7]{0:T(128)} %copy-done.74, bf16[2048,2048]{1,0:T(8,128)(2,1)} %all-gather.6.cloned.1.call-done.feed.refs_0_, ...), custom_call_target="tpu_custom_call", output_to_operand_aliasing={{0}: (6, {}), {1}: (7, {}), {2}: (8, {})} | custom-call | flops 20669530112 | bytes 39059456 | tf_op jit(solution)/shard_map/feed_rows/pallas_call | solution.py:669
  407.4 5.6 mixer_chain.1.grads
  413.0 16.3 %mixer_backward.1 = (bf16[512,512]{1,0:T(8,128)(2,1)S(1)}, bf16[512,512]{1,0:T(8,128)(2,1)S(1)}, bf16[512,512]{1,0:T(8,128)(2,1)S(1)}, f32[3,8,512]{2,1,0:T(8,12...) custom-call(f32[520,1536]{1,0:T(8,128)} %get-tuple-element.128.xq.xk.xv, ...), custom_call_target="tpu_custom_call" | custom-call | flops 2013265920 | bytes 20881408 | tf_op jit(solution)/shard_map/mixer_backward/pallas_call | solution.py:571
  436.0 2.2 collective-permute-done.44.refs_13_
  438.9 10.7 %normed_back.1 = (bf16[512,1536]{1,0:T(8,128)(2,1)}, bf16[2,128,2048]{2,1,0:T(8,128)(2,1)}, bf16[2,128,2048]{2,1,0:T(8,128)(2,1)}, f32[1,2048]{1,0:T(1,128)}) custom-call(s32[9]{0:T(128)} %get-tuple-element.254.refs_0_, bf16[272,2048]{1,0:T(8,128)(2,1)} %weights.1.refs_0_.refs_8_.refs_1_, bf16[272,2048]{1,0:T(8,128)(2,1)} %gate.10.refs_1_.refs_9_.refs_2_, ...), custom_call_target="tpu_custom_call" | custom-call | flops 3221225472 | bytes 16375876 | tf_op jit(solution)/shard_map/normed_back/pallas_call | solution.py:446
  449.5 9.0 %weight_rows.1 = (bf16[256,2048]{1,0:T(8,128)(2,1)}, bf16[256,2048]{1,0:T(8,128)(2,1)}, bf16[256,2048]{1,0:T(8,128)(2,1)}, bf16[256,2048]{1,0:T(8,128)(2,1)}, bf...) custom-call(s32[9]{0:T(128)} %get-tuple-element.253.refs_0_, ...), custom_call_target="tpu_custom_call" | custom-call | flops 4294967296 | bytes 14753828 | tf_op jit(solution)/shard_map/weight_rows/pallas_call | solution.py:446
  458.6 2.4 fusion.22
  463.1 1.8 collective-permute-start.47
  466.5 34.0 %feed_rows.3 = (bf16[32,2,64,1408]{3,2,1,0:T(8,128)(2,1)}, bf16[32,2,64,1408]{3,2,1,0:T(8,128)(2,1)}, bf16[32,2,64,1408]{3,2,1,0:T(8,128)(2,1)}, f32[8,128]{1,0:T(8,128)}) custom-call(s32[7]{0:T(128)} %copy-done.74, bf16[2048,2048]{1,0:T(8,128)(2,1)} %all-gather.8.cloned.1.call-done.feed.refs_1_, ...), custom_call_target="tpu_custom_call", output_to_operand_aliasing={{0}: (6, {}), {1}: (7, {}), {2}: (8, {})} | custom-call | flops 20669530112 | bytes 39059456 | tf_op jit(solution)/shard_map/feed_rows/pallas_call | solution.py:669
  502.7 2.0 collective-permute-start.48
  504.7 3.4 ring_add.3
  508.2 2.1 collective-permute-start.53
  510.3 33.8 %weight_grad.4 = (f32[2048,1408]{1,0:T(8,128)}, f32[8,128]{1,0:T(8,128)}) custom-call(bf16[2048,2048]{1,0:T(8,128)(2,1)} %all-gather.6.cloned.1.call-done.feed.refs_0_, bf16[2048,2048]{1,0:T(8,128)(2,1)} %all-gather.8.cloned.1.call-done.feed.refs_1_, bf16[32,2,64,1408]{3,2,1,0:T(8,128)(2,1)} %get-tuple-element.192.refs_2_, ...), custom_call_target="tpu_custom_call" | custom-call | flops 23622320128 | bytes 39845888 | tf_op jit(solution)/shard_map/weight_grad/pallas_call | solution.py:739
  549.2 3.8 ring_add.4
  553.0 33.8 %weight_grad.5 = (f32[2048,1408]{1,0:T(8,128)}, f32[8,128]{1,0:T(8,128)}) custom-call(bf16[2048,2048]{1,0:T(8,128)(2,1)} %all-gather.6.cloned.1.call-done.feed.refs_0_, bf16[2048,2048]{1,0:T(8,128)(2,1)} %all-gather.8.cloned.1.call-done.feed.refs_1_, bf16[32,2,64,1408]{3,2,1,0:T(8,128)(2,1)} %get-tuple-element.197.refs_2_, ...), custom_call_target="tpu_custom_call" | custom-call | flops 23622320128 | bytes 39845888 | tf_op jit(solution)/shard_map/weight_grad/pallas_call | solution.py:739
  590.4 3.2 collective-permute-done.55.refs_3_
  593.6 2.0 collective-permute-start.57
  607.2 2.6 convert_add_fusion
  609.9 1.9 copy-done.18
  613.4 6.0 collective-permute-done.57.refs_2_
  621.2 3.8 ring_add.5
  625.2 1.9 collective-permute-start.60
  627.2 20.3 %weight_grad.6 = (f32[1408,2048]{1,0:T(8,128)}, f32[8,128]{1,0:T(8,128)}) custom-call(bf16[4096,2048]{1,0:T(8,128)(2,1)} %all-gather.4.cloned.1.call-done.cot.refs_0_, bf16[32,2,64,1408]{3,2,1,0:T(8,128)(2,1)} %get-tuple-element.209.refs_1_, bf16[256,2048]{1,0:T(8,128)(2,1)} %get-tuple-element.207.refs_2_), custom_call_target="tpu_custom_call" | custom-call | flops 11811160064 | bytes 25690112 | tf_op jit(solution)/shard_map/weight_grad/pallas_call | solution.py:739
  648.5 2.3 convert_add_fusion.1
  654.9 3.2 sum.1.refs_2_
  658.1 2.0 dynamic-slice_bitcast_fusion.7
  662.0 20.3 %weight_grad.7 = (f32[1408,2048]{1,0:T(8,128)}, f32[8,128]{1,0:T(8,128)}) custom-call(bf16[4096,2048]{1,0:T(8,128)(2,1)} %all-gather.4.cloned.1.call-done.cot.refs_0_, bf16[32,2,64,1408]{3,2,1,0:T(8,128)(2,1)} %get-tuple-element.209.refs_1_, bf16[256,2048]{1,0:T(8,128)(2,1)} %sum.1.refs_2_, ...), custom_call_target="tpu_custom_call", output_to_operand_aliasing={{0}: (3, {})} | custom-call | flops 11811160064 | bytes 25690112 | tf_op jit(solution)/shard_map/weight_grad/pallas_call | solution.py:739
  683.2 3.1 assemble.1
  (368 shorter events, 118.5 us)
Async XLA Ops:
  7.2 296.5 %all-gather.4.cloned.1.call-start = ((), (), s32[]{:S(2)}) async-start(), calls=%async_computation | async-start | bytes 17301504 | tf_op jit(solution)/shard_map/all_gather | solution.py:1050
  11.3 11.2 %collective-permute-start.4 = (bf16[80,2048]{1,0:T(8,128)(2,1)S(1)}, bf16[80,2048]{1,0:T(8,128)(2,1)S(1)}, u32[]{:S(2)}, u32[]{:S(2)}) collective-permute-start(bf16[80,2048]{1,0:T(8,128)(2,1)S(1)} %get-tuple-element.228), channel_id=1, source_target_pairs={{0,1},{1,0},{2,3},{3,2},{4,5},{5,4},{6,7},{7,6},{8,9},{9,8},{10,11... | collective-permute-start | bytes 983048 | tf_op jit(solution)/shard_map/ppermute | solution.py:19
  11.8 11.1 %collective-permute-start.5 = (bf16[80,2048]{1,0:T(8,128)(2,1)S(1)}, bf16[80,2048]{1,0:T(8,128)(2,1)S(1)}, u32[]{:S(2)}, u32[]{:S(2)}) collective-permute-start(bf16[80,2048]{1,0:T(8,128)(2,1)S(1)} %get-tuple-element.227), channel_id=1, source_target_pairs={{0,2},{1,3},{2,0},{3,1},{4,6},{5,7},{6,4},{7,5},{8,10},{9,11},{10,... | collective-permute-start | bytes 983048 | tf_op jit(solution)/shard_map/ppermute | solution.py:19
  14.3 15.2 %collective-permute-start.6 = (bf16[80,2048]{1,0:T(8,128)(2,1)S(1)}, bf16[80,2048]{1,0:T(8,128)(2,1)S(1)}, u32[]{:S(2)}, u32[]{:S(2)}) collective-permute-start(bf16[80,2048]{1,0:T(8,128)(2,1)S(1)} %get-tuple-element.226), channel_id=1, source_target_pairs={{0,3},{1,2},{2,1},{3,0},{4,7},{5,6},{6,5},{7,4},{8,11},{9,10},{10,... | collective-permute-start | bytes 983048 | tf_op jit(solution)/shard_map/ppermute | solution.py:19
  20.8 21.9 %collective-permute-start.2 = (bf16[144,2048]{1,0:T(8,128)(2,1)}, bf16[144,2048]{1,0:T(8,128)(2,1)}, u32[]{:S(2)}, u32[]{:S(2)}) collective-permute-start(bf16[144,2048]{1,0:T(8,128)(2,1)} %pad_maximum_fusion.1.refs_1_), channel_id=1, source_target_pairs={{0,2},{1,3},{2,0},{3,1},{4,6},{5,7},{6,4},{7,5},{8,10},{9,11},{10,... | collective-permute-start | bytes 1769480 | tf_op jit(solution)/shard_map/ppermute | solution.py:19
  32.6 27.7 %collective-permute-start.7 = (bf16[272,2048]{1,0:T(8,128)(2,1)}, bf16[272,2048]{1,0:T(8,128)(2,1)S(1)}, u32[]{:S(2)}, u32[]{:S(2)}) collective-permute-start(bf16[272,2048]{1,0:T(8,128)(2,1)} %weights.1.refs_0_.refs_8_.refs_1_), channel_id=1, source_target_pairs={{0,8},{8,16},{16,24},{24,28},{28,20},{20,12},{12,4},{4,0},{1,9},{9... | collective-permute-start | bytes 3342344 | tf_op jit(solution)/shard_map/ppermute | solution.py:62
  34.9 18.8 %collective-permute-start.11 = (bf16[128,2048]{1,0:T(8,128)(2,1)S(1)}, bf16[128,2048]{1,0:T(8,128)(2,1)}, u32[]{:S(2)}, u32[]{:S(2)}) collective-permute-start(bf16[128,2048]{1,0:T(8,128)(2,1)S(1)} %copy-done.22), channel_id=1, source_target_pairs={{0,2},{1,3},{2,0},{3,1},{4,6},{5,7},{6,4},{7,5},{8,10},{9,11},{10,... | collective-permute-start | bytes 1572872 | tf_op jit(solution)/shard_map/ppermute | solution.py:19
  35.9 28.1 %collective-permute-start.8 = (bf16[272,2048]{1,0:T(8,128)(2,1)}, bf16[272,2048]{1,0:T(8,128)(2,1)S(1)}, u32[]{:S(2)}, u32[]{:S(2)}) collective-permute-start(bf16[272,2048]{1,0:T(8,128)(2,1)} %weights.1.refs_0_.refs_8_.refs_1_), channel_id=1, source_target_pairs={{0,4},{8,0},{16,8},{24,16},{28,24},{20,28},{12,20},{4,12},{1,5},{9... | collective-permute-start | bytes 3342344 | tf_op jit(solution)/shard_map/ppermute | solution.py:62
  42.6 11.1 %collective-permute-start.3 = (bf16[144,2048]{1,0:T(8,128)(2,1)}, bf16[144,2048]{1,0:T(8,128)(2,1)S(1)}, u32[]{:S(2)}, u32[]{:S(2)}) collective-permute-start(bf16[144,2048]{1,0:T(8,128)(2,1)} %collective-permute-done.2.refs_3_), channel_id=1, source_target_pairs={{0,1},{1,0},{2,3},{3,2},{4,5},{5,4},{6,7},{7,6},{8,9},{9,8},{10,11... | collective-permute-start | bytes 1769480 | tf_op jit(solution)/shard_map/ppermute | solution.py:19
  42.8 25.6 %collective-permute-start.1 = (bf16[144,2048]{1,0:T(8,128)(2,1)}, bf16[144,2048]{1,0:T(8,128)(2,1)}, u32[]{:S(2)}, u32[]{:S(2)}) collective-permute-start(bf16[144,2048]{1,0:T(8,128)(2,1)} %pad_maximum_fusion.1.refs_1_), channel_id=1, source_target_pairs={{0,1},{1,0},{2,3},{3,2},{4,5},{5,4},{6,7},{7,6},{8,9},{9,8},{10,11... | collective-permute-start | bytes 1769480 | tf_op jit(solution)/shard_map/ppermute | solution.py:19
  53.7 11.7 %collective-permute-start.10 = (bf16[128,2048]{1,0:T(8,128)(2,1)S(1)}, bf16[128,2048]{1,0:T(8,128)(2,1)}, u32[]{:S(2)}, u32[]{:S(2)}) collective-permute-start(bf16[128,2048]{1,0:T(8,128)(2,1)S(1)} %copy-done.22), channel_id=1, source_target_pairs={{0,1},{1,0},{2,3},{3,2},{4,5},{5,4},{6,7},{7,6},{8,9},{9,8},{10,11... | collective-permute-start | bytes 1572872 | tf_op jit(solution)/shard_map/ppermute | solution.py:19
  53.7 11.7 %collective-permute-start.12 = (bf16[128,2048]{1,0:T(8,128)(2,1)}, bf16[128,2048]{1,0:T(8,128)(2,1)}, u32[]{:S(2)}, u32[]{:S(2)}) collective-permute-start(bf16[128,2048]{1,0:T(8,128)(2,1)} %collective-permute-done.11.refs_3_), channel_id=1, source_target_pairs={{0,1},{1,0},{2,3},{3,2},{4,5},{5,4},{6,7},{7,6},{8,9},{9,8},{10,11... | collective-permute-start | bytes 1572872 | tf_op jit(solution)/shard_map/ppermute | solution.py:19
  61.4 26.7 %collective-permute-start.9 = (bf16[272,2048]{1,0:T(8,128)(2,1)}, bf16[272,2048]{1,0:T(8,128)(2,1)S(1)}, u32[]{:S(2)}, u32[]{:S(2)}) collective-permute-start(bf16[272,2048]{1,0:T(8,128)(2,1)} %gate.10.refs_1_.refs_9_.refs_2_), channel_id=1, source_target_pairs={{0,8},{8,16},{16,24},{24,28},{28,20},{20,12},{12,4},{4,0},{1,9},{9... | collective-permute-start | bytes 3342344 | tf_op jit(solution)/shard_map/ppermute | solution.py:62
  65.0 26.2 %collective-permute-start.13 = (bf16[272,2048]{1,0:T(8,128)(2,1)}, bf16[272,2048]{1,0:T(8,128)(2,1)S(1)}, u32[]{:S(2)}, u32[]{:S(2)}) collective-permute-start(bf16[272,2048]{1,0:T(8,128)(2,1)} %gate.11.refs_2_.refs_10_.refs_3_), channel_id=1, source_target_pairs={{0,4},{8,0},{16,8},{24,16},{28,24},{20,28},{12,20},{4,12},{1,5},{9... | collective-permute-start | bytes 3342344 | tf_op jit(solution)/shard_map/ppermute | solution.py:62
  89.0 25.9 %collective-permute-start.14 = (bf16[272,2048]{1,0:T(8,128)(2,1)}, bf16[272,2048]{1,0:T(8,128)(2,1)S(1)}, u32[]{:S(2)}, u32[]{:S(2)}) collective-permute-start(bf16[272,2048]{1,0:T(8,128)(2,1)} %gate.12.refs_3_.refs_11_.refs_4_), channel_id=1, source_target_pairs={{0,8},{8,16},{16,24},{24,28},{28,20},{20,12},{12,4},{4,0},{1,9},{9... | collective-permute-start | bytes 3342344 | tf_op jit(solution)/shard_map/ppermute | solution.py:62
  92.2 26.2 %collective-permute-start.15 = (bf16[272,2048]{1,0:T(8,128)(2,1)}, bf16[272,2048]{1,0:T(8,128)(2,1)S(1)}, u32[]{:S(2)}, u32[]{:S(2)}) collective-permute-start(bf16[272,2048]{1,0:T(8,128)(2,1)} %gate.13.refs_4_.refs_12_.refs_5_), channel_id=1, source_target_pairs={{0,4},{8,0},{16,8},{24,16},{28,24},{20,28},{12,20},{4,12},{1,5},{9... | collective-permute-start | bytes 3342344 | tf_op jit(solution)/shard_map/ppermute | solution.py:62
  117.0 12.8 %collective-permute-start.16 = (bf16[136,2048]{1,0:T(8,128)(2,1)S(1)}, bf16[136,2048]{1,0:T(8,128)(2,1)S(1)}, u32[]{:S(2)}, u32[]{:S(2)}) collective-permute-start(bf16[136,2048]{1,0:T(8,128)(2,1)S(1)} %slice.158), channel_id=1, source_target_pairs={{0,8},{8,16},{16,24},{24,28},{28,20},{20,12},{12,4},{4,0},{1,9},{9... | collective-permute-start | bytes 1671176 | tf_op jit(solution)/shard_map/ppermute | solution.py:62
  120.5 12.3 %collective-permute-start.17 = (bf16[136,2048]{1,0:T(8,128)(2,1)S(1)}, bf16[136,2048]{1,0:T(8,128)(2,1)S(1)}, u32[]{:S(2)}, u32[]{:S(2)}) collective-permute-start(bf16[136,2048]{1,0:T(8,128)(2,1)S(1)} %slice.159), channel_id=1, source_target_pairs={{0,4},{8,0},{16,8},{24,16},{28,24},{20,28},{12,20},{4,12},{1,5},{9... | collective-permute-start | bytes 1671176 | tf_op jit(solution)/shard_map/ppermute | solution.py:62
  134.0 239.0 %all-gather.6.cloned.1.call-start = ((), (), s32[]{:S(2)}) async-start(), calls=%async_computation.1 | async-start | bytes 8650752 | tf_op jit(solution)/shard_map/all_gather | solution.py:1072
  146.0 83.4 %collective-permute-start.30 = (bf16[2048,512]{1,0:T(8,128)(2,1)}, bf16[2048,512]{1,0:T(8,128)(2,1)}, u32[]{:S(2)}, u32[]{:S(2)}) collective-permute-start(bf16[2048,512]{1,0:T(8,128)(2,1)} %get-tuple-element.136.refs_5_.refs_1_), channel_id=1, source_target_pairs={{0,2},{1,3},{2,0},{3,1},{4,6},{5,7},{6,4},{7,5},{8,10},{9,11},{10,... | collective-permute-start | bytes 6291464 | tf_op jit(solution)/shard_map/ppermute | solution.py:19
  174.8 12.8 %collective-permute-start.18 = (bf16[4,2,128,128]{3,2,1,0:T(8,128)(2,1)S(1)}, bf16[4,2,128,128]{3,2,1,0:T(8,128)(2,1)S(1)}, u32[]{:S(2)}, u32[]{:S(2)}) collective-permute-start(bf16[4,2,128,128]{3,2,1,0:T(8,128)(2,1)S(1)} %get-tuple-element.130.refs_1_), channel_id=1, source_target_pairs={{0,8},{8,16},{16,24},{24,28},{28,20},{20,12},{12,4},{4,0},{1,9},{9... | collective-permute-start | bytes 786440 | tf_op jit(solution)/shard_map/ppermute | solution.py:62
  176.7 11.7 %collective-permute-start.19 = (bf16[4,2,128,128]{3,2,1,0:T(8,128)(2,1)S(1)}, bf16[4,2,128,128]{3,2,1,0:T(8,128)(2,1)S(1)}, u32[]{:S(2)}, u32[]{:S(2)}) collective-permute-start(bf16[4,2,128,128]{3,2,1,0:T(8,128)(2,1)S(1)} %get-tuple-element.130.refs_1_), channel_id=1, source_target_pairs={{0,4},{8,0},{16,8},{24,16},{28,24},{20,28},{12,20},{4,12},{1,5},{9... | collective-permute-start | bytes 786440 | tf_op jit(solution)/shard_map/ppermute | solution.py:62
  187.6 10.4 %collective-permute-start.20 = (bf16[4,2,128,128]{3,2,1,0:T(8,128)(2,1)S(1)}, bf16[4,2,128,128]{3,2,1,0:T(8,128)(2,1)S(1)}, u32[]{:S(2)}, u32[]{:S(2)}) collective-permute-start(bf16[4,2,128,128]{3,2,1,0:T(8,128)(2,1)S(1)} %collective-permute-done.18.refs_2_), channel_id=1, source_target_pairs={{0,8},{8,16},{16,24},{24,28},{28,20},{20,12},{12,4},{4,0},{1,9},{9... | collective-permute-start | bytes 786440 | tf_op jit(solution)/shard_map/ppermute | solution.py:62
  188.4 12.1 %collective-permute-start.21 = (bf16[4,2,128,128]{3,2,1,0:T(8,128)(2,1)S(1)}, bf16[4,2,128,128]{3,2,1,0:T(8,128)(2,1)S(1)}, u32[]{:S(2)}, u32[]{:S(2)}) collective-permute-start(bf16[4,2,128,128]{3,2,1,0:T(8,128)(2,1)S(1)} %collective-permute-done.19.refs_3_), channel_id=1, source_target_pairs={{0,4},{8,0},{16,8},{24,16},{28,24},{20,28},{12,20},{4,12},{1,5},{9... | collective-permute-start | bytes 786440 | tf_op jit(solution)/shard_map/ppermute | solution.py:62
  198.0 9.7 %collective-permute-start.22 = (bf16[4,2,128,128]{3,2,1,0:T(8,128)(2,1)S(1)}, bf16[4,2,128,128]{3,2,1,0:T(8,128)(2,1)S(1)}, u32[]{:S(2)}, u32[]{:S(2)}) collective-permute-start(bf16[4,2,128,128]{3,2,1,0:T(8,128)(2,1)S(1)} %collective-permute-done.20.refs_4_), channel_id=1, source_target_pairs={{0,8},{8,16},{16,24},{24,28},{28,20},{20,12},{12,4},{4,0},{1,9},{9... | collective-permute-start | bytes 786440 | tf_op jit(solution)/shard_map/ppermute | solution.py:62
  200.5 8.5 %collective-permute-start.23 = (bf16[4,2,128,128]{3,2,1,0:T(8,128)(2,1)S(1)}, bf16[4,2,128,128]{3,2,1,0:T(8,128)(2,1)S(1)}, u32[]{:S(2)}, u32[]{:S(2)}) collective-permute-start(bf16[4,2,128,128]{3,2,1,0:T(8,128)(2,1)S(1)} %collective-permute-done.21.refs_5_), channel_id=1, source_target_pairs={{0,4},{8,0},{16,8},{24,16},{28,24},{20,28},{12,20},{4,12},{1,5},{9... | collective-permute-start | bytes 786440 | tf_op jit(solution)/shard_map/ppermute | solution.py:62
  209.1 8.7 %collective-permute-start.24 = (bf16[2,2,128,128]{3,2,1,0:T(8,128)(2,1)}, bf16[2,2,128,128]{3,2,1,0:T(8,128)(2,1)}, u32[]{:S(2)}, u32[]{:S(2)}) collective-permute-start(bf16[2,2,128,128]{3,2,1,0:T(8,128)(2,1)} %slice.160), channel_id=1, source_target_pairs={{0,8},{8,16},{16,24},{24,28},{28,20},{20,12},{12,4},{4,0},{1,9},{9... | collective-permute-start | bytes 393224 | tf_op jit(solution)/shard_map/ppermute | solution.py:62
  210.4 12.1 %collective-permute-start.25 = (bf16[2,2,128,128]{3,2,1,0:T(8,128)(2,1)}, bf16[2,2,128,128]{3,2,1,0:T(8,128)(2,1)}, u32[]{:S(2)}, u32[]{:S(2)}) collective-permute-start(bf16[2,2,128,128]{3,2,1,0:T(8,128)(2,1)} %slice.161), channel_id=1, source_target_pairs={{0,4},{8,0},{16,8},{24,16},{28,24},{20,28},{12,20},{4,12},{1,5},{9... | collective-permute-start | bytes 393224 | tf_op jit(solution)/shard_map/ppermute | solution.py:62
  213.1 39.0 %collective-permute-start.29 = (bf16[2048,512]{1,0:T(8,128)(2,1)}, bf16[2048,512]{1,0:T(8,128)(2,1)}, u32[]{:S(2)}, u32[]{:S(2)}) collective-permute-start(bf16[2048,512]{1,0:T(8,128)(2,1)} %get-tuple-element.136.refs_5_.refs_1_), channel_id=1, source_target_pairs={{0,1},{1,0},{2,3},{3,2},{4,5},{5,4},{6,7},{7,6},{8,9},{9,8},{10,11... | collective-permute-start | bytes 6291464 | tf_op jit(solution)/shard_map/ppermute | solution.py:19
  229.5 22.6 %collective-permute-start.31 = (bf16[2048,512]{1,0:T(8,128)(2,1)}, bf16[2048,512]{1,0:T(8,128)(2,1)S(1)}, u32[]{:S(2)}, u32[]{:S(2)}) collective-permute-start(bf16[2048,512]{1,0:T(8,128)(2,1)} %gate.16.refs_7_.refs_3_), channel_id=1, source_target_pairs={{0,1},{1,0},{2,3},{3,2},{4,5},{5,4},{6,7},{7,6},{8,9},{9,8},{10,11... | collective-permute-start | bytes 6291464 | tf_op jit(solution)/shard_map/ppermute | solution.py:19
  229.6 20.6 %collective-permute-start.27 = (bf16[512,512]{1,0:T(8,128)(2,1)}, bf16[512,512]{1,0:T(8,128)(2,1)S(1)}, u32[]{:S(2)}, u32[]{:S(2)}) collective-permute-start(bf16[512,512]{1,0:T(8,128)(2,1)} %get-tuple-element.135.refs_1_), channel_id=1, source_target_pairs={{0,2},{1,3},{2,0},{3,1},{4,6},{5,7},{6,4},{7,5},{8,10},{9,11},{10,... | collective-permute-start | bytes 1572872 | tf_op jit(solution)/shard_map/ppermute | solution.py:19
  231.2 19.7 %collective-permute-start.26 = (bf16[512,512]{1,0:T(8,128)(2,1)}, bf16[512,512]{1,0:T(8,128)(2,1)S(1)}, u32[]{:S(2)}, u32[]{:S(2)}) collective-permute-start(bf16[512,512]{1,0:T(8,128)(2,1)} %get-tuple-element.135.refs_1_), channel_id=1, source_target_pairs={{0,1},{1,0},{2,3},{3,2},{4,5},{5,4},{6,7},{7,6},{8,9},{9,8},{10,11... | collective-permute-start | bytes 1572872 | tf_op jit(solution)/shard_map/ppermute | solution.py:19
  265.5 201.0 %all-gather.8.cloned.1.call-start = ((), (), s32[]{:S(2)}) async-start(), calls=%async_computation.2 | async-start | bytes 8650752 | tf_op jit(solution)/shard_map/all_gather | solution.py:1072
  296.4 3.1 collective-permute-start.32
  302.2 20.6 %collective-permute-start.33 = (bf16[1,128,2048]{2,1,0:T(8,128)(2,1)}, bf16[1,128,2048]{2,1,0:T(8,128)(2,1)}, u32[]{:S(2)}, u32[]{:S(2)}) collective-permute-start(bf16[1,128,2048]{2,1,0:T(8,128)(2,1)} %dynamic-slice_convert_fusion.1.refs_0_), channel_id=1, source_target_pairs={{0,2},{1,3},{2,0},{3,1},{4,6},{5,7},{6,4},{7,5},{8,10},{9,11},{10,... | collective-permute-start | bytes 1572872 | tf_op jit(solution)/shard_map/ppermute | solution.py:19
  331.7 17.3 %collective-permute-start.34 = (bf16[128,1024]{1,0:T(8,128)(2,1)}, bf16[128,1024]{1,0:T(8,128)(2,1)S(1)}, u32[]{:S(2)}, u32[]{:S(2)}) collective-permute-start(bf16[128,1024]{1,0:T(8,128)(2,1)} %get-tuple-element.151), channel_id=1, source_target_pairs={{0,1},{1,0},{2,3},{3,2},{4,5},{5,4},{6,7},{7,6},{8,9},{9,8},{10,11... | collective-permute-start | bytes 786440 | tf_op jit(solution)/shard_map/ppermute | solution.py:19
  331.7 17.3 %collective-permute-start.35 = (bf16[128,1024]{1,0:T(8,128)(2,1)}, bf16[128,1024]{1,0:T(8,128)(2,1)S(1)}, u32[]{:S(2)}, u32[]{:S(2)}) collective-permute-start(bf16[128,1024]{1,0:T(8,128)(2,1)} %get-tuple-element.152), channel_id=1, source_target_pairs={{0,2},{1,3},{2,0},{3,1},{4,6},{5,7},{6,4},{7,5},{8,10},{9,11},{10,... | collective-permute-start | bytes 786440 | tf_op jit(solution)/shard_map/ppermute | solution.py:19
  333.4 15.6 %collective-permute-start.36 = (bf16[128,1024]{1,0:T(8,128)(2,1)}, bf16[128,1024]{1,0:T(8,128)(2,1)S(1)}, u32[]{:S(2)}, u32[]{:S(2)}) collective-permute-start(bf16[128,1024]{1,0:T(8,128)(2,1)} %get-tuple-element.153), channel_id=1, source_target_pairs={{0,3},{1,2},{2,1},{3,0},{4,7},{5,6},{6,5},{7,4},{8,11},{9,10},{10,... | collective-permute-start | bytes 786440 | tf_op jit(solution)/shard_map/ppermute | solution.py:19
  356.0 8.7 %collective-permute-start.37 = (bf16[4,128,128]{2,1,0:T(8,128)(2,1)}, bf16[4,128,128]{2,1,0:T(8,128)(2,1)S(1)}, u32[]{:S(2)}, u32[]{:S(2)}) collective-permute-start(bf16[4,128,128]{2,1,0:T(8,128)(2,1)} %get-tuple-element.157.refs_0_), channel_id=1, source_target_pairs={{4,0},{8,4},{12,8},{16,12},{20,16},{24,20},{28,24},{5,1},{9,5},{13... | collective-permute-start | bytes 393224 | tf_op jit(solution)/shard_map/ppermute | solution.py:1135
  357.2 14.4 %collective-permute-start.38 = (bf16[4,128,128]{2,1,0:T(8,128)(2,1)}, bf16[4,128,128]{2,1,0:T(8,128)(2,1)S(1)}, u32[]{:S(2)}, u32[]{:S(2)}) collective-permute-start(bf16[4,128,128]{2,1,0:T(8,128)(2,1)} %get-tuple-element.157.refs_0_), channel_id=1, source_target_pairs={{8,0},{12,4},{16,8},{20,12},{24,16},{28,20},{9,1},{13,5},{17,9},{2... | collective-permute-start | bytes 393224 | tf_op jit(solution)/shard_map/ppermute | solution.py:1135
  360.2 47.2 %collective-permute-start.39 = (bf16[4,128,128]{2,1,0:T(8,128)(2,1)}, bf16[4,128,128]{2,1,0:T(8,128)(2,1)}, u32[]{:S(2)}, u32[]{:S(2)}) collective-permute-start(bf16[4,128,128]{2,1,0:T(8,128)(2,1)} %get-tuple-element.157.refs_0_), channel_id=1, source_target_pairs={{12,0},{16,4},{20,8},{24,12},{28,16},{13,1},{17,5},{21,9},{25,13},... | collective-permute-start | bytes 393224 | tf_op jit(solution)/shard_map/ppermute | solution.py:1135
  361.5 45.9 %collective-permute-start.40 = (bf16[4,128,128]{2,1,0:T(8,128)(2,1)}, bf16[4,128,128]{2,1,0:T(8,128)(2,1)}, u32[]{:S(2)}, u32[]{:S(2)}) collective-permute-start(bf16[4,128,128]{2,1,0:T(8,128)(2,1)} %get-tuple-element.157.refs_0_), channel_id=1, source_target_pairs={{16,0},{20,4},{24,8},{28,12},{17,1},{21,5},{25,9},{29,13},{18,2},{... | collective-permute-start | bytes 393224 | tf_op jit(solution)/shard_map/ppermute | solution.py:1135
  362.8 44.6 %collective-permute-start.41 = (bf16[4,128,128]{2,1,0:T(8,128)(2,1)}, bf16[4,128,128]{2,1,0:T(8,128)(2,1)}, u32[]{:S(2)}, u32[]{:S(2)}) collective-permute-start(bf16[4,128,128]{2,1,0:T(8,128)(2,1)} %get-tuple-element.157.refs_0_), channel_id=1, source_target_pairs={{20,0},{24,4},{28,8},{21,1},{25,5},{29,9},{22,2},{26,6},{30,10},{2... | collective-permute-start | bytes 393224 | tf_op jit(solution)/shard_map/ppermute | solution.py:1135
  364.6 42.8 %collective-permute-start.42 = (bf16[4,128,128]{2,1,0:T(8,128)(2,1)}, bf16[4,128,128]{2,1,0:T(8,128)(2,1)}, u32[]{:S(2)}, u32[]{:S(2)}) collective-permute-start(bf16[4,128,128]{2,1,0:T(8,128)(2,1)} %get-tuple-element.157.refs_0_), channel_id=1, source_target_pairs={{24,0},{28,4},{25,1},{29,5},{26,2},{30,6},{27,3},{31,7}} | collective-permute-start | bytes 393224 | tf_op jit(solution)/shard_map/ppermute | solution.py:1135
  371.6 35.8 %collective-permute-start.43 = (bf16[4,128,128]{2,1,0:T(8,128)(2,1)}, bf16[4,128,128]{2,1,0:T(8,128)(2,1)}, u32[]{:S(2)}, u32[]{:S(2)}) collective-permute-start(bf16[4,128,128]{2,1,0:T(8,128)(2,1)} %get-tuple-element.157.refs_0_), channel_id=1, source_target_pairs={{28,0},{29,1},{30,2},{31,3}} | collective-permute-start | bytes 393224 | tf_op jit(solution)/shard_map/ppermute | solution.py:1135
  432.5 5.7 collective-permute-start.44
  460.9 43.8 %collective-permute-start.49 = (bf16[128,2048]{1,0:T(8,128)(2,1)}, bf16[128,2048]{1,0:T(8,128)(2,1)}, u32[]{:S(2)}, u32[]{:S(2)}) collective-permute-start(bf16[128,2048]{1,0:T(8,128)(2,1)} %get-tuple-element.235.refs_0_), channel_id=1, source_target_pairs={{0,8},{8,16},{16,24},{24,28},{28,20},{20,12},{12,4},{4,0},{1,9},{9... | collective-permute-start | bytes 1572872 | tf_op jit(solution)/shard_map/ppermute | solution.py:62
  462.5 42.2 %collective-permute-start.50 = (bf16[128,2048]{1,0:T(8,128)(2,1)}, bf16[128,2048]{1,0:T(8,128)(2,1)}, u32[]{:S(2)}, u32[]{:S(2)}) collective-permute-start(bf16[128,2048]{1,0:T(8,128)(2,1)} %get-tuple-element.234), channel_id=1, source_target_pairs={{0,4},{8,0},{16,8},{24,16},{28,24},{20,28},{12,20},{4,12},{1,5},{9... | collective-permute-start | bytes 1572872 | tf_op jit(solution)/shard_map/ppermute | solution.py:62
  463.1 37.4 %collective-permute-start.47 = (f32[152,128]{1,0:T(8,128)S(1)}, f32[152,128]{1,0:T(8,128)S(1)}, u32[]{:S(2)}, u32[]{:S(2)}) collective-permute-start(f32[152,128]{1,0:T(8,128)S(1)} %pad_bitcast_fusion.refs_0_), channel_id=1, source_target_pairs={{0,4},{4,0},{8,12},{12,8},{16,20},{20,16},{24,28},{28,24},{1,5},{5... | collective-permute-start | bytes 233480 | tf_op jit(solution)/shard_map/ppermute | solution.py:19
  466.4 140.8 %collective-permute-start.45 = (bf16[2,256,2048]{2,1,0:T(8,128)(2,1)S(1)}, bf16[2,256,2048]{2,1,0:T(8,128)(2,1)}, u32[]{:S(2)}, u32[]{:S(2)}) collective-permute-start(bf16[2,256,2048]{2,1,0:T(8,128)(2,1)S(1)} %pad_maximum_fusion), channel_id=1, source_target_pairs={{0,1},{1,0},{2,3},{3,2},{4,5},{5,4},{6,7},{7,6},{8,9},{9,8},{10,11... | collective-permute-start | bytes 6291464 | tf_op jit(solution)/shard_map/ppermute | solution.py:19
  502.7 41.4 %collective-permute-start.48 = (f32[152,128]{1,0:T(8,128)}, f32[152,128]{1,0:T(8,128)S(1)}, u32[]{:S(2)}, u32[]{:S(2)}) collective-permute-start(f32[152,128]{1,0:T(8,128)} %add.406.refs_0_), channel_id=1, source_target_pairs={{0,8},{4,12},{8,0},{12,4},{16,24},{20,28},{24,16},{28,20},{1,9},{5... | collective-permute-start | bytes 233480 | tf_op jit(solution)/shard_map/ppermute | solution.py:19
  508.2 39.7 %collective-permute-start.52 = (bf16[256,2048]{1,0:T(8,128)(2,1)}, bf16[256,2048]{1,0:T(8,128)(2,1)S(1)}, u32[]{:S(2)}, u32[]{:S(2)}) collective-permute-start(bf16[256,2048]{1,0:T(8,128)(2,1)} %get-tuple-element.195.refs_3_), channel_id=1, source_target_pairs={{0,8},{8,16},{16,24},{24,28},{28,20},{20,12},{12,4},{4,0},{1,9},{9... | collective-permute-start | bytes 3145736 | tf_op jit(solution)/shard_map/ppermute | solution.py:62
  508.2 39.7 %collective-permute-start.53 = (bf16[256,2048]{1,0:T(8,128)(2,1)}, bf16[256,2048]{1,0:T(8,128)(2,1)S(1)}, u32[]{:S(2)}, u32[]{:S(2)}) collective-permute-start(bf16[256,2048]{1,0:T(8,128)(2,1)} %get-tuple-element.200), channel_id=1, source_target_pairs={{0,4},{8,0},{16,8},{24,16},{28,24},{20,28},{12,20},{4,12},{1,5},{9... | collective-permute-start | bytes 3145736 | tf_op jit(solution)/shard_map/ppermute | solution.py:62
  546.4 40.4 %collective-permute-start.51 = (f32[152,128]{1,0:T(8,128)}, f32[152,128]{1,0:T(8,128)S(1)}, u32[]{:S(2)}, u32[]{:S(2)}) collective-permute-start(f32[152,128]{1,0:T(8,128)} %add.407.refs_0_), channel_id=1, source_target_pairs={{0,16},{4,20},{8,24},{12,28},{16,0},{20,4},{24,8},{28,12},{1,17},{... | collective-permute-start | bytes 233480 | tf_op jit(solution)/shard_map/ppermute | solution.py:19
  589.0 4.6 collective-permute-start.55
  590.4 5.2 collective-permute-start.54
  593.6 25.9 %collective-permute-start.57 = (bf16[256,2048]{1,0:T(8,128)(2,1)}, bf16[256,2048]{1,0:T(8,128)(2,1)}, u32[]{:S(2)}, u32[]{:S(2)}) collective-permute-start(bf16[256,2048]{1,0:T(8,128)(2,1)} %get-tuple-element.201.refs_3_), channel_id=1, source_target_pairs={{0,8},{8,16},{16,24},{24,28},{28,20},{20,12},{12,4},{4,0},{1,9},{9... | collective-permute-start | bytes 3145736 | tf_op jit(solution)/shard_map/ppermute | solution.py:62
  595.6 25.6 %collective-permute-start.58 = (bf16[256,2048]{1,0:T(8,128)(2,1)}, bf16[256,2048]{1,0:T(8,128)(2,1)}, u32[]{:S(2)}, u32[]{:S(2)}) collective-permute-start(bf16[256,2048]{1,0:T(8,128)(2,1)} %get-tuple-element.206), channel_id=1, source_target_pairs={{0,4},{8,0},{16,8},{24,16},{28,24},{20,28},{12,20},{4,12},{1,5},{9... | collective-permute-start | bytes 3145736 | tf_op jit(solution)/shard_map/ppermute | solution.py:62
  611.9 35.5 %collective-permute-start.46 = (bf16[1,256,2048]{2,1,0:T(8,128)(2,1)S(1)}, bf16[1,256,2048]{2,1,0:T(8,128)(2,1)S(1)}, u32[]{:S(2)}, u32[]{:S(2)}) collective-permute-start(bf16[1,256,2048]{2,1,0:T(8,128)(2,1)S(1)} %dynamic-slice_convert_fusion), channel_id=1, source_target_pairs={{0,2},{1,3},{2,0},{3,1},{4,6},{5,7},{6,4},{7,5},{8,10},{9,11},{10,... | collective-permute-start | bytes 3145736 | tf_op jit(solution)/shard_map/ppermute | solution.py:19
  625.0 28.6 %collective-permute-start.59 = (bf16[256,2048]{1,0:T(8,128)(2,1)}, bf16[256,2048]{1,0:T(8,128)(2,1)S(1)}, u32[]{:S(2)}, u32[]{:S(2)}) collective-permute-start(bf16[256,2048]{1,0:T(8,128)(2,1)} %get-tuple-element.207.refs_2_), channel_id=1, source_target_pairs={{0,8},{8,16},{16,24},{24,28},{28,20},{20,12},{12,4},{4,0},{1,9},{9... | collective-permute-start | bytes 3145736 | tf_op jit(solution)/shard_map/ppermute | solution.py:62
  625.2 28.3 %collective-permute-start.60 = (bf16[256,2048]{1,0:T(8,128)(2,1)}, bf16[256,2048]{1,0:T(8,128)(2,1)S(1)}, u32[]{:S(2)}, u32[]{:S(2)}) collective-permute-start(bf16[256,2048]{1,0:T(8,128)(2,1)} %get-tuple-element.208), channel_id=1, source_target_pairs={{0,4},{8,0},{16,8},{24,16},{28,24},{20,28},{12,20},{4,12},{1,5},{9... | collective-permute-start | bytes 3145736 | tf_op jit(solution)/shard_map/ppermute | solution.py:62
  660.1 22.2 %collective-permute-start.61 = (bf16[64,2048]{1,0:T(8,128)(2,1)S(1)}, bf16[64,2048]{1,0:T(8,128)(2,1)S(1)}, u32[]{:S(2)}, u32[]{:S(2)}) collective-permute-start(bf16[64,2048]{1,0:T(8,128)(2,1)S(1)} %get-tuple-element.232), channel_id=1, source_target_pairs={{0,1},{1,0},{2,3},{3,2},{4,5},{5,4},{6,7},{7,6},{8,9},{9,8},{10,11... | collective-permute-start | bytes 786440 | tf_op jit(solution)/shard_map/ppermute | solution.py:19
  660.1 22.2 %collective-permute-start.62 = (bf16[64,2048]{1,0:T(8,128)(2,1)S(1)}, bf16[64,2048]{1,0:T(8,128)(2,1)S(1)}, u32[]{:S(2)}, u32[]{:S(2)}) collective-permute-start(bf16[64,2048]{1,0:T(8,128)(2,1)S(1)} %get-tuple-element.231), channel_id=1, source_target_pairs={{0,2},{1,3},{2,0},{3,1},{4,6},{5,7},{6,4},{7,5},{8,10},{9,11},{10,... | collective-permute-start | bytes 786440 | tf_op jit(solution)/shard_map/ppermute | solution.py:19
  661.3 21.0 %collective-permute-start.63 = (bf16[64,2048]{1,0:T(8,128)(2,1)S(1)}, bf16[64,2048]{1,0:T(8,128)(2,1)S(1)}, u32[]{:S(2)}, u32[]{:S(2)}) collective-permute-start(bf16[64,2048]{1,0:T(8,128)(2,1)S(1)} %get-tuple-element.230), channel_id=1, source_target_pairs={{0,3},{1,2},{2,1},{3,0},{4,7},{5,6},{6,5},{7,4},{8,11},{9,10},{10,... | collective-permute-start | bytes 786440 | tf_op jit(solution)/shard_map/ppermute | solution.py:19
  (80 other events, 547.0 us)
Sparse Core Ops, SparseCore 0:
  134.1 133.7 all-gather.3
  270.8 74.3 all-gather.5
  348.0 87.9 all-gather.7

commit v4 on v3

--- a/solution.py
+++ b/solution.py
@@ -76,9 +76,8 @@
     def scatter(self, blocks, beside=()):
         last = self.last
         beside = list(beside) + [None] * last
-        block = lambda d: blocks[0 if d == 0 else 2 * d if 0 < d < last else -2 * d - 1 if d < 0 else -1]
-        half = blocks[0].shape[0] // 2
-        right, left = block(last)[:half], block(last)[half:]
+        block = lambda d: blocks[0 if d == 0 else 2 * d if d > 0 else -2 * d - 1]
+        right, left = blocks[-2:]
         for s in range(last - 1, -1, -1):
             ahead, behind = self.move(right, 1), self.move(left, -1)
             deps = [beside[last - 1 - s](right)] if beside[last - 1 - s] else []
@@ -101,8 +100,11 @@
         out[at, :] = (block[at, :].astype(F32) + arrived[...].astype(F32)).astype(BF)
 
 
-def sum_kernel(x, y, z, out):
-    out[...] = (x[...].astype(F32) + (y[...].astype(F32) + z[...].astype(F32))).astype(BF)
+def sum_kernel(rank, x, y, z, *outs):
+    rows = outs[0].shape[0]
+    for j, out in enumerate(outs):
+        at = pl.ds(pl.multiple_of((rank[0] ^ j) * rows, rows), rows)
+        out[...] = (x[at, :].astype(F32) + (y[at, :].astype(F32) + z[at, :].astype(F32))).astype(BF)
 
 
 def assemble_kernel(rank, *refs):
@@ -115,25 +117,12 @@
             out[:, i, at] = part[:, i * cols : (i + 1) * cols].astype(F32)
 
 
-def add_kernel(x, y, out):
-    out[...] = x[...] + y[...]
-
-
 def exchange(blocks, rank):
     parts = []
     for j in range(lax.axis_size("ta")):
         block = lax.dynamic_index_in_dim(blocks, rank ^ j, 0, False)
         parts.append(swap(block, "ta", j) if j else block)
     return parts
-
-
-def sum_over(x, axis, waits):
-    size = lax.axis_size(axis)
-    bit, n = 1, 0
-    while bit < size:
-        (x,) = vmem_call("add", add_kernel, [shape(x.shape)], [x, swap(x, axis, bit)], 0, waits[n : n + 1])
-        bit, n = 2 * bit, n + 1
-    return x
 
 
 def scatter_sum(kept, sent, rank, beside=None):
@@ -148,11 +137,16 @@
                 made = beside(sent)
                 arrived = gate(arrived, made[0])
             return kept[0], arrived[0], made
-        blocks = kept.astype(F32) + arrived.astype(F32)
-        pairs = blocks.reshape((blocks.shape[0] // 2, 2) + blocks.shape[1:])
-        mine = (rank // bit) % 2
-        kept = lax.dynamic_index_in_dim(pairs, mine, 1, False)
-        sent = lax.dynamic_index_in_dim(pairs, 1 - mine, 1, False).astype(BF)
+        half = (kept.shape[0] // 2,) + kept.shape[1:]
+        mine = ((rank // bit) % 2).astype(jnp.int32).reshape(1)
+        kept, sent = vmem_call("stage", stage_kernel, [shape(half), shape(half, BF)], [mine, kept, arrived], 0)
+
+
+def stage_kernel(mine, first, second, kept, sent):
+    for n in range(kept.shape[0]):
+        for out, which in ((kept, mine[0]), (sent, 1 - mine[0])):
+            at = 2 * n + which
+            out[n] = (first[at].astype(F32) + second[at].astype(F32)).astype(out.dtype)
 
 
 def rms_scale(values, gain):
@@ -178,6 +172,7 @@
 
 
 PAD = 8
+HEADS_A_STEP = 2
 VMEM_LIMIT = 48 * 1024 * 1024
 FFN_VMEM = 56 * 1024 * 1024
 
@@ -239,55 +234,60 @@
 
 
 def forward_kernel(size, xq, xk, xv, conv, aux_ref, row_ref, yq, yk, yv, inv, plain, reach, read, direct, trans, fresh, whole):
-    count = inv.shape[1]
-    depth = xq.shape[1]
+    heads, count = inv.shape[0], inv.shape[1]
+    depth = xq.shape[1] // heads
     ksize = conv.shape[1]
-    aux, row = aux_ref.at[0], row_ref.at[0]
     r, c = iotas(depth)
     eye = (r == c).astype(F32)
     spans = [slice(n * size, (n + 1) * size) for n in range(count)]
     saved = []
     lowers = []
-    for n, at in enumerate(spans):
-        active = []
-        for i, (x, y) in enumerate(((xq, yq), (xk, yk), (xv, yv))):
-            first = PAD - (ksize - 1) + n * size
-            summed = x[first + ksize - 1 : first + ksize - 1 + size, :] * conv[i, ksize - 1 : ksize, :]
-            for j in range(ksize - 1):
-                summed = summed + x[first + j : first + j + size, :] * conv[i, j : j + 1, :] * aux[at, j : j + 1]
-            y[at, :] = summed
-            active.append(summed * jax.nn.sigmoid(summed))
-        q = unit_of(active[0])[0] * depth ** (-0.5)
-        k = unit_of(active[1])[0]
-        weak, strict = masks_of(aux, row, at, size)
-        rate = row[7:8, at]
-        products = d3(jnp.concatenate([q, k], axis=0), k, 1, 1)
-        lowers.append(products[size:] * rate * strict)
-        saved.append((q, k, active[2], products[:size] * rate * weak))
+    for h in range(heads):
+        aux, row = aux_ref.at[h], row_ref.at[h]
+        col = slice(h * depth, (h + 1) * depth)
+        for n, at in enumerate(spans):
+            active = []
+            for i, (x, y) in enumerate(((xq, yq), (xk, yk), (xv, yv))):
+                first = PAD - (ksize - 1) + n * size
+                summed = x[first + ksize - 1 : first + ksize - 1 + size, col] * conv[i, ksize - 1 : ksize, col]
+                for j in range(ksize - 1):
+                    moved = x[first + j : first + j + size, col]
+                    summed = summed + moved * conv[i, j : j + 1, col] * aux[at, j : j + 1]
+                y[at, col] = summed
+                active.append(summed * jax.nn.sigmoid(summed))
+            q = unit_of(active[0])[0] * depth ** (-0.5)
+            k = unit_of(active[1])[0]
+            weak, strict = masks_of(aux, row, at, size)
+            rate = row[7:8, at]
+            products = d3(jnp.concatenate([q, k], axis=0), k, 1, 1)
+            lowers.append(products[size:] * rate * strict)
+            saved.append((h, n, q, k, active[2], products[:size] * rate * weak))
     inverses = inverses_of(lowers)
-    total = added = None
-    for n, at in enumerate(spans):
-        q, k, v, mix = saved[n]
+    total, added = [None] * heads, [None] * heads
+    for inverse, (h, n, q, k, v, mix) in zip(inverses, saved):
+        at = spans[n]
+        aux = aux_ref.at[h]
         cont, clos, beta = aux[at, 3:4], aux[at, 4:5], aux[at, 7:8]
-        both = d3(inverses[n], jnp.concatenate([v, k * cont], axis=1))
+        both = d3(inverse, jnp.concatenate([v, k * cont], axis=1))
         spread = d1(mix, both)
-        inv[0, n] = inverses[n]
-        plain[0, at, :] = both[:, :depth]
-        reach[0, at, :] = both[:, depth:]
-        direct[0, at, :] = spread[:, :depth]
-        read[0, at, :] = q * cont - spread[:, depth:]
+        inv[h, n] = inverse
+        plain[h, at, :] = both[:, :depth]
+        reach[h, at, :] = both[:, depth:]
+        direct[h, at, :] = spread[:, :depth]
+        read[h, at, :] = q * cont - spread[:, depth:]
         gained = d3(k * (beta * clos), both, 0, 0)
         map_n = aux[(n + 1) * size - 1 : (n + 1) * size, 3:4] * eye - gained[:, depth:]
         add_n = gained[:, :depth]
-        trans[0, n] = map_n
-        fresh[0, n] = add_n
+        trans[h, n] = map_n
+        fresh[h, n] = add_n
         if n == 0:
-            total, added = map_n, add_n
+            total[h], added[h] = map_n, add_n
         else:
-            new = d3(map_n, jnp.concatenate([added, total], axis=1))
-            total, added = new[:, depth:], new[:, :depth] + add_n
-    whole[0, 0] = total.astype(BF)
-    whole[0, 1] = added.astype(BF)
+            new = d3(map_n, jnp.concatenate([added[h], total[h]], axis=1))
+            total[h], added[h] = new[:, depth:], new[:, :depth] + add_n
+    for h in range(heads):
+        whole[h, 0] = total[h].astype(BF)
+        whole[h, 1] = added[h].astype(BF)
 
 
 def read_kernel(size, count_of, index, *refs):
@@ -349,18 +349,26 @@
     grad_gain[...] = gained
 
 
-def chain_kernel(index, *refs):
+def chain_kernel(index, beside, *refs):
     both, trans, from_out, grads = refs[-4:]
-    leaks = refs[:-4]
+    pairs = refs[:-4]
     heads, count = trans.shape[0], trans.shape[1]
     depth = trans.shape[-1]
     devices = both.shape[0]
+    odd = index[0] % 2
     carry = [jnp.zeros((depth, depth), F32) for _ in range(heads)]
-    for k in range(devices - 1, 0, -1):
-        at = jnp.minimum(index[0] + k, devices - 1)
-        carry = [
-            d3(both[at, h, 0].astype(F32), carry[h], 0, 0) + leaks[k - 1][h].astype(F32) for h in range(heads)
-        ]
+
+    def follow(at, leak):
+        at = jnp.minimum(at, devices - 1)
+        return [d3(both[at, h, 0].astype(F32), carry[h], 0, 0) + leak(h).astype(F32) for h in range(heads)]
+
+    for k in range(len(pairs), 0, -1):
+        pair = pairs[k - 1]
+        first = index[0] - odd + 2 * k
+        carry = follow(first + 1, lambda h: pair[1 - odd, h])
+        carry = follow(first, lambda h: pair[odd, h])
+    later = follow(index[0] + 1, lambda h: beside[h])
+    carry = [jnp.where(odd == 0, x, y) for x, y in zip(later, carry)]
     for n in range(count - 1, -1, -1):
         for h in range(heads):
             grads[h, n] = carry[h]
@@ -497,6 +505,9 @@
             + [square] * 2
             + [shape((heads, 2, depth, depth), BF)]
         )
+        step = HEADS_A_STEP if heads % HEADS_A_STEP == 0 else 1
+        each = lambda x: pl.BlockSpec((step,) + x.shape[1:], lambda h: (h,) + (0,) * (len(x.shape) - 1))
+        column = pl.BlockSpec((length, step * depth), lambda h: (0, h))
         (
             self.yq, self.yk, self.yv, self.inv, self.plain, self.reach, self.read, self.direct,
             self.trans, self.fresh, self.whole,
@@ -504,13 +515,13 @@
             functools.partial(forward_kernel, size),
             name="mixer_forward",
             out_shape=out_shape,
-            grid=(heads,),
-            in_specs=self.token_specs + [self.conv_spec] + self.aux_specs,
-            out_specs=[self.head_cols] * 3
-            + [self.inv_spec]
-            + [self.rows_spec] * 4
-            + [self.chunk_spec] * 2
-            + [pl.BlockSpec((1, 2, depth, depth), lambda h: (h, 0, 0, 0))],
+            grid=(heads // step,),
+            in_specs=[
+                pl.BlockSpec((length + PAD, step * depth), lambda h, i=i: (0, i * (heads // step) + h))
+                for i in range(3)
+            ]
+            + [pl.BlockSpec((3, ksize, step * depth), lambda h: (0, 0, h)), each(aux), each(row)],
+            out_specs=[column] * 3 + [each(x) for x in out_shape[3:]],
             cost_estimate=cost(60 * self.flops, inputs, out_shape),
             compiler_params=pltpu.CompilerParams(vmem_limit_bytes=VMEM_LIMIT),
         )(*inputs)
@@ -622,10 +633,11 @@
 def split_by_core(source, core, width, kept, sent):
     for p in range(kept.shape[0]):
         for ref, which in ((kept, core), (sent, 1 - core)):
-            ref[p] = source[pl.ds(pl.multiple_of((2 * p + which) * width, width), width), :]
-
-
-def own_kernel(index, feed, cot, wg, wu, wd, hidden, grad_gate, grad_lifted, kept, sent, branch, total):
+            ref[p, 0:width, :] = source[pl.ds(pl.multiple_of((2 * p + which) * width, width), width), :]
+
+
+def own_kernel(index, feed, cot, wg, wu, wd, hidden, grad_gate, grad_lifted, *refs):
+    (kept, sent, kept_result, sent_result), (total, result) = refs[:4], refs[4:]
     units, model = wd.shape
     for cut in chunks_of(units):
         gated = jnp.dot(feed[...], wg[:, cut], preferred_element_type=F32)
@@ -635,8 +647,9 @@
     for cut in chunks_of(model):
         grad_feed = dims(grad_gate[...], wg[cut, :], 1, 1) + dims(grad_lifted[...], wu[cut, :], 1, 1)
         total[:, cut] = grad_feed.astype(BF)
-        branch[:, cut] = jnp.dot(hidden[...], wd[:, cut], preferred_element_type=F32).astype(BF)
+        result[:, cut] = jnp.dot(hidden[...], wd[:, cut], preferred_element_type=F32).astype(BF)
     split_by_core(total, index[1], kept.shape[1], kept, sent)
+    split_by_core(result, index[1], kept.shape[1], kept_result, sent_result)
 
 
 def hidden_kernel(groups, cot, wd, *refs):
@@ -698,14 +711,13 @@
         own_kernel,
         name="feed_own",
         out_shape=[shape((tokens, units), BF)] * 3
-        + [shape((count, width, model), BF)] * 2
-        + [shape((rows, model), BF)],
+        + [shape((count, width, model), BF)] * 4,
         grid_spec=pltpu.PrefetchScalarGridSpec(
             num_scalar_prefetch=1,
             grid=(count,),
             in_specs=[here] * 2 + [resident(w) for w in weights],
-            out_specs=[wide] * 3 + [half] * 2 + [here],
-            scratch_shapes=[pltpu.VMEM((block, model), BF)],
+            out_specs=[wide] * 3 + [half] * 4,
+            scratch_shapes=[pltpu.VMEM((block, model), BF)] * 2,
         ),
         **params(12 * rows * model * units, 6 * model * units + rows * (3 * units + 4 * model) * 2),
     )(index, feed, cot, *weights)
@@ -855,6 +867,19 @@
         ),
         **params(6 * rows * model * cols, 2 * x.size + 8 * model * cols),
     )(slots, x, live, *parts, *parts)
+
+
+def finish_kernel(kept, arrived, residual, grad_residual, tokens, gain, block_out, grad_tokens):
+    width = tokens.shape[0]
+    both = kept[...].astype(F32) + arrived[...].astype(F32)
+    block_out[...] = (residual[...] + both[width:]).astype(BF)
+    values = tokens[...].astype(F32)
+    scale = lax.rsqrt(jnp.mean(values * values, axis=-1, keepdims=True) + NORM_EPS)
+    unit = values * scale
+    grad = both[:width] * gain[...]
+    grad_tokens[...] = grad_residual[...] + scale * (
+        grad - unit * jnp.mean(grad * unit, axis=-1, keepdims=True)
+    )
 
 
 def out_kernel(lanes, index, *refs):
@@ -919,7 +944,8 @@
 
 def normed_back_kernel(blocks, index, *refs):
     w, refs = refs[:blocks], refs[blocks:]
-    gq, gk, gv, tail, arrived, live, logit, wbeta, tokens, grads, kept, sent, gain, total = refs
+    gq, gk, gv, tail, arrived, live, logit, wbeta, tokens, kept_result, sent_result = refs[:11]
+    grads, kept, sent, gain, total = refs[11:]
     size = total.shape[1] // blocks
     cols = gq.shape[1]
     length = gq.shape[0]
@@ -932,12 +958,14 @@
     scale = lax.rsqrt(jnp.mean(values * values, axis=-1, keepdims=True) + NORM_EPS)
     for n in range(blocks):
         at = pl.ds(pl.multiple_of(index[1 + n] * size, size), size)
-        part = dims(grads[...], w[n][0:size, : 3 * cols], 1, 1) + jnp.dot(
-            logit[...], wbeta[:, at], preferred_element_type=F32
-        )
+        part = dims(grads[...], w[n][0:size, : 3 * cols], 1, 1) + dims(logit[...], wbeta[:, at], 0, 0)
         gain[:, at] = jnp.sum(part * (tokens[:, at].astype(F32) * scale), axis=0, keepdims=True)
         total[:, at] = part.astype(BF)
-    split_by_core(total, index[0], kept.shape[1], kept, sent)
+    width = kept_result.shape[1]
+    split_by_core(total, index[0], width, kept, sent)
+    for out, result in ((kept, kept_result), (sent, sent_result)):
+        for n in range(out.shape[0]):
+            out[n, width:, :] = result[n]
 
 
 def weight_rows_kernel(lanes, index, *refs):
@@ -948,13 +976,19 @@
     wide = grads.shape[1]
     size = outs[0].shape[0]
     rank = index[0]
+    outs[-2:] = [outs[-2:]]
     for j, part in enumerate(heads):
         joined[:, pl.ds(pl.multiple_of((rank ^ j) * cols, cols), cols)] = part[...]
     for n, out in enumerate(outs):
         at = pl.ds(pl.multiple_of(index[1 + n] * size, size), size)
-        out[:, :wide] = dims(normed[:, at], grads[...], 0, 0).astype(BF)
-        out[:, wide:] = dims(joined[:, at], mixed[...], 0, 0).astype(BF)
-    wbeta[...] = dims(logit[...], normed[...], 0, 0)
+        first = dims(normed[:, at], grads[...], 0, 0).astype(BF)
+        second = dims(joined[:, at], mixed[...], 0, 0).astype(BF)
+        pieces = out if isinstance(out, list) else [out]
+        for n, piece in enumerate(pieces):
+            rows = slice(n * piece.shape[0], (n + 1) * piece.shape[0])
+            piece[:, :wide] = first[rows]
+            piece[:, wide:] = second[rows]
+    wbeta[...] = dims(logit[...], normed[...], 1, 0)
 
 
 def body(
@@ -1049,11 +1083,10 @@
     w = ring.collect(own_rows, [[packed[-1]], [normed, cot_group, live_ext], [columns, own_conv]])
     cot_all = lax.all_gather(gate(cotangent, w[-1]), BOTH, axis=0, tiled=True)
     projected, w_out, beta_logit, wbeta = project(ring.slots, normed, live_ext, w, lanes)
-    beta_logit = beta_logit[PAD:, :own_heads]
-    sig_beta = jax.nn.sigmoid(beta_logit + own_bias)
-    beta = sig_beta * live[:, None]
-    row = jnp.concatenate([shared, beta.T[:, None]], axis=1)
-    columns = jnp.concatenate([columns, beta.T[:, :, None]], axis=2)
+    sig_beta = jax.nn.sigmoid(beta_logit[PAD:, :own_heads].T + own_bias[:, None])
+    beta = sig_beta * live[None]
+    row = jnp.concatenate([shared, beta[:, None]], axis=1)
+    columns = jnp.concatenate([columns, beta[:, :, None]], axis=2)
     mixer = Mixer(projected, own_conv, columns, row, width)
     head_normed = mixer.outputs(
         jnp.concatenate([at_place, ring.slots]), ring.collect(mixer.whole), head_gain[None]
@@ -1074,7 +1107,7 @@
     weights = [w_gate, w_up, w_down]
     units = w_gate.shape[1]
     core = (rank % 2).astype(jnp.int32).reshape(1)
-    *arrays, kept, sent, partial_branch = feed_own(
+    *arrays, kept, sent, kept_result, sent_result = feed_own(
         jnp.concatenate([at_place, core]), feed_rows, cot_group, weights, blocks * group, width
     )
     others = lax.rem(place + 1 + jnp.arange(blocks - 1, dtype=jnp.int32), blocks)
@@ -1131,25 +1164,25 @@
     by_heads = [swap(x, "ta", j) if j else x for j, x in enumerate(sent)]
     token, grad_hidden = hidden_of(row_parts[1], [grad_hidden], sent[0])
     leak, grad_head_gain, mixed_cols = mixer.leak(at_rank, by_heads, [token])
-    leaks = [
-        lax.ppermute(leak, "dev", [(i, i - k) for i in range(k, blocks)]) for k in range(1, blocks)
+    beside = swap(leak, "dev", 1)
+    pair = jnp.stack([leak, beside])
+    pairs = [
+        lax.ppermute(pair, "dev", [(i, i - 2 * k) for i in range(2 * k, blocks)]) for k in range(1, blocks // 2)
     ]
-    token = fill_rows([leak])
-    grad_q, grad_k, grad_v, tail, spill, grad_conv, grad_beta = mixer.back(leaks, [token])
+    token = fill_rows([pair])
+    grad_q, grad_k, grad_v, tail, spill, grad_conv, grad_beta = mixer.back([beside, *pairs], [token])
     arrived = lax.ppermute(spill.astype(BF), "dev", [(i, i - 1) for i in range(1, blocks)])
-    grad_logit = grad_beta[:, 0].T * beta * (1.0 - sig_beta)
-    grad_bias = jnp.sum(grad_logit, axis=0)
-    grad_logit_low = grad_logit.astype(BF)
-
-    grad_logit_low = jnp.pad(grad_logit_low, ((0, 0), (0, 8 - own_heads)))
-
-    half = (lanes // 2, width, model)
+    grad_logit = grad_beta[:, 0] * beta * (1.0 - sig_beta)
+    grad_bias = jnp.sum(grad_logit, axis=1)
+    grad_logit_low = jnp.pad(grad_logit.astype(BF), ((0, 8 - own_heads), (0, 0)))
+
+    half = (lanes // 2, 2 * width, model)
     grad_projected, kept, sent, grad_attn_gain = vmem_call(
         "normed_back",
         functools.partial(normed_back_kernel, blocks),
         [shape((group, 3 * cols), BF), shape(half, BF), shape(half, BF), shape((1, model))],
         [jnp.concatenate([core, ring.slots]), *w, grad_q, grad_k, grad_v, tail, arrived]
-        + [live[group - PAD :, None], grad_logit_low, wbeta, group_tokens],
+        + [live[group - PAD :, None], grad_logit_low, wbeta, group_tokens, kept_result, sent_result],
         2 * group * model * 3 * cols,
         scratch=[pltpu.VMEM((group, model), BF)],
     )
@@ -1157,7 +1190,9 @@
     *partial_rows, partial_wbeta = vmem_call(
         "weight_rows",
         functools.partial(weight_rows_kernel, lanes),
-        [shape((model // blocks, 4 * cols), BF)] * blocks + [shape((8, model))],
+        [shape((model // blocks, 4 * cols), BF)] * (blocks - 1)
+        + [shape((model // blocks // 2, 4 * cols), BF)] * 2
+        + [shape((8, model))],
         [jnp.concatenate([at_rank, ring.slots]), *heads_low, normed_group, grad_projected, mixed_cols]
         + [grad_logit_low],
         2 * group * model * 4 * cols,
@@ -1175,52 +1210,44 @@
             lambda x: fill(fill_rows, [x]),
             lambda x: fill(fill_grads, 1, x),
             lambda x: fill(fill_grads, 1, x),
-            lambda x: fill(fill_grads, 2, x),
+            lambda x: fill(fill_grads, 1, x),
         ],
     )
-    (w_part,) = vmem_call("sum", sum_kernel, [shape(terms[0].shape, BF)], terms, 0, deps)
-    w_parts = exchange(w_part.reshape(lanes, rows, 4 * cols), rank)
-    token = fill_grads(2, w_part)
+    w_parts = vmem_call("sum", sum_kernel, [shape((rows, 4 * cols), BF)] * lanes, [at_rank, *terms], 0, deps)
+    w_parts = [swap(x, "ta", j) if j else x for j, x in enumerate(w_parts)]
     (grad_projection,) = vmem_call(
         "assemble",
         assemble_kernel,
         [shape((rows, 4, model))],
         [at_rank, *w_parts],
         0,
-        [token],
-    )
-
-    kept_b, sent_b = (
-        lax.dynamic_index_in_dim(partial_branch.reshape(lanes // 2, 2, width, model), which, 1, False)
-        for which in (rank % 2, 1 - rank % 2)
-    )
-    kept, arrived, _ = scatter_sum(
-        jnp.concatenate([kept, kept_b], axis=1), jnp.concatenate([sent, sent_b], axis=1), rank,
-        lambda sent: (made[0],),
-    )
-    both_sums = kept.astype(F32) + arrived.astype(F32)
-    block_out = (own_residual + both_sums[width:]).astype(BF)
-    _, attention_back = jax.vjp(lambda x: rms_scale(x, attn_gain), tokens.astype(F32))
-    grad_tokens = grad_residual + attention_back(both_sums[:width])[0]
-
+    )
+
+    kept, arrived, _ = scatter_sum(kept, sent, rank, lambda sent: (made[0],))
+    block_out, grad_tokens = vmem_call(
+        "finish",
+        finish_kernel,
+        [shape((width, model), BF), shape((width, model))],
+        [kept, arrived, own_residual, grad_residual, tokens, attn_gain[None]],
+        0,
+    )
+
+    own = jnp.concatenate([grad_conv.reshape(-1), partial_wbeta[:own_heads].reshape(-1), grad_bias])
     gains = jnp.concatenate([grad_mlp_gain[0], grad_head_gain[0], grad_attn_gain[0]])
-    pieces = [grad_conv.reshape(-1), partial_wbeta[:own_heads].reshape(-1), grad_bias, gains]
-    ends = [0]
-    for piece in pieces:
-        ends.append(ends[-1] + piece.shape[0])
-    flat = jnp.concatenate(pieces)
-    flat = jnp.pad(flat, (0, -flat.shape[0] % 1024)).reshape(-1, 128)
-    flat = sum_over(flat, "dev", made)
-    flat = in_order(gather_parts(flat), at_rank).reshape(lanes, -1)
-    conv_sum, wbeta_sum, bias_sum, gains = (flat[:, a:b] for a, b in zip(ends, ends[1:]))
-    conv_sum = jnp.transpose(conv_sum.reshape(lanes, 3, ksize, cols), (1, 2, 0, 3))
+    length = own.shape[0]
+    apart = length + (-length % 1024)
+    flat = jnp.zeros((lanes, apart), F32)
+    flat = lax.dynamic_update_slice(flat, jnp.pad(own, (0, apart - length))[None], (rank, 0))
+    flat = jnp.concatenate([flat.reshape(-1, 128), jnp.pad(gains, (0, -gains.shape[0] % 1024)).reshape(-1, 128)])
+    flat = gate(lax.psum(flat, BOTH), made[-1]).reshape(-1)
+    gains = flat[lanes * apart :]
+    flat = flat[: lanes * apart].reshape(lanes, apart)
+    convs = 3 * ksize * cols
+    conv_sum = jnp.transpose(flat[:, :convs].reshape(lanes, 3, ksize, cols), (1, 2, 0, 3))
     conv_sum = conv_sum.reshape(3, ksize, lanes * cols)
-    wbeta_sum = lax.dynamic_slice_in_dim(
-        wbeta_sum.reshape(heads, model), (place * lanes + rank) * rows, rows, 1
-    )
-    grad_w_beta = wbeta_sum.T
-    bias_sum = bias_sum.reshape(heads)
-    gains = jnp.sum(gains, axis=0)
+    wbeta_sum = flat[:, convs : convs + own_heads * model].reshape(heads, model)
+    grad_w_beta = lax.dynamic_slice_in_dim(wbeta_sum, (place * lanes + rank) * rows, rows, 1).T
+    bias_sum = flat[:, convs + own_heads * model : length].reshape(heads)
 
     (grad_w_gate,), (grad_w_up,), (grad_w_down,) = ffn_grads
     return (

time: 703 us -> 666 us (0.947)
  other arithmetic: 22.1 us -> 11.5 us
  local copies, waits for them, and re-layouts: 61.7 us -> 52 us
  starting transfers between devices: 61.3 us -> 53.7 us
    add x4 -> x0, other arithmetic: 8.35 us -> none  [the longest x2 4.51 us: scatter_sum(): blocks = kept.astype(F32) + arrived.astype(F32)]
    ppermute x31 -> x26, waiting for transfers between devices: 48.2 us -> 56 us  [swap(): lax.ppermute(x, axis, [(i, i ^ bit) for i in range(lax.axis_size(axis))])]
    ppermute x24, waiting for transfers between devices: 91.8 us -> 84.7 us  [move(): lax.ppermute(x, 'dev', [(self.order[p], self.order[(p + step) % n]) for p...]
    pallas_call x19 -> x18, Pallas kernels: 91.8 us -> 98.4 us  [vmem_call(): pl.pallas_call(run, name=name, out_shape=out_shape, in_specs=[smem if x.d...]
    pallas_call x4 -> x3, Pallas kernels: 108 us -> 102 us  [weight_grad(): pl.pallas_call(functools.partial(grad_kernel, transposed, len(lefts)), na...]
    ppermute x31 -> x26, starting transfers between devices: 22.1 us -> 16.8 us  [swap(): lax.ppermute(x, axis, [(i, i ^ bit) for i in range(lax.axis_size(axis))])]
    unnamed x157 -> x133, local copies, waits for them, and re-layouts: 28.5 us -> 26.2 us
  transfers between devices with their start and end apart: 67 -> 59, of which waited for: 24 -> 24; matrix products, arithmetic and copies ran while one was open for 7% -> 5% of each run, Pallas kernels for 54% -> 57%
where the time goes in v4:
time: 666 us; the launch traced here: 660 us
  Pallas kernels  382 us (57%)
  waiting for transfers between devices  146 us (22%)
  starting transfers between devices  53.7 us (8%)
  local copies, waits for them, and re-layouts  52 us (8%)
  between operations  15.1 us (2%)
  other arithmetic  11.5 us (2%)
    pallas_call x4, Pallas kernels, by_group(): pl.pallas_call(kernel, name=name, out_shape=[shape(like[:-1] + (width,),...  103 us
    pallas_call x3, Pallas kernels, weight_grad(): pl.pallas_call(functools.partial(grad_kernel, transposed, len(lefts)), na...  102 us
    pallas_call x18, Pallas kernels, vmem_call(): pl.pallas_call(run, name=name, out_shape=out_shape, in_specs=[smem if x.d...  98.4 us
    ppermute x24, waiting for transfers between devices, move(): lax.ppermute(x, 'dev', [(self.order[p], self.order[(p + step) % n]) for p...  84.7 us
    ppermute x26, waiting for transfers between devices, swap(): lax.ppermute(x, axis, [(i, i ^ bit) for i in range(lax.axis_size(axis))])  56 us
    ppermute x24, starting transfers between devices, move(): lax.ppermute(x, 'dev', [(self.order[p], self.order[(p + step) % n]) for p...  30.6 us
    pallas_call x1, Pallas kernels, feed_own(): pl.pallas_call(own_kernel, name='feed_own', out_shape=[shape((tokens, uni...  30.3 us
    unnamed x133, local copies, waits for them, and re-layouts  26.2 us
  transfers between devices with their start and end apart: 59, of which 24 were waited for; matrix products, arithmetic and copies ran while one was open for 5% of the time, Pallas kernels for 57%

profile of v4, /device:TPU:0, one launch (start us, length us, event | category | flops | bytes accessed | tf_op | source)
XLA Modules:
  0.0 660.2 jit_solution(16141515024785161730)
XLA Ops:
  7.3 1.7 reshape.331
  11.8 2.5 collective-permute-start.1
  16.4 2.0 broadcast_select_fusion
  20.0 1.8 collective-permute-start.5
  22.9 6.8 %collective-permute-done.2.refs_4_ = bf16[80,2048]{1,0:T(8,128)(2,1)} collective-permute-done((bf16[80,2048]{1,0:T(8,128)(2,1)S(1)}, bf16[80,2048]{1,0:T(8,128)(2,1)}, u32[]{:S(2)}, u32[]{:S(2)}) %collective-permute-start.2) | collective-permute-done | bytes 327712 | tf_op jit(solution)/shard_map/ppermute | solution.py:19
  29.6 2.3 weights.1.refs_0_.refs_8_.refs_1_
  32.0 2.3 collective-permute-start.3
  35.8 6.9 %collective-permute-done.5.refs_3_ = bf16[144,2048]{1,0:T(8,128)(2,1)} collective-permute-done((bf16[144,2048]{1,0:T(8,128)(2,1)S(1)}, bf16[144,2048]{1,0:T(8,128)(2,1)}, u32[]{:S(2)}, u32[]{:S(2)}) %collective-permute-start.5) | collective-permute-done | bytes 589856 | tf_op jit(solution)/shard_map/ppermute | solution.py:19
  43.4 10.3 %collective-permute-done.11.refs_3_ = bf16[128,2048]{1,0:T(8,128)(2,1)} collective-permute-done((bf16[128,2048]{1,0:T(8,128)(2,1)S(1)}, bf16[128,2048]{1,0:T(8,128)(2,1)}, u32[]{:S(2)}, u32[]{:S(2)}) %collective-permute-start.11) | collective-permute-done | bytes 524320 | tf_op jit(solution)/shard_map/ppermute | solution.py:19
  54.2 5.5 collective-permute-done.3.refs_0_
  60.8 1.8 collective-permute-start.8
  64.8 3.0 in_order.1.refs_2_.cot
  67.8 5.5 norm.1
  75.6 11.9 %collective-permute-done.8.refs_0_ = bf16[272,2048]{1,0:T(8,128)(2,1)S(1)} collective-permute-done((bf16[272,2048]{1,0:T(8,128)(2,1)}, bf16[272,2048]{1,0:T(8,128)(2,1)S(1)}, u32[]{:S(2)}, u32[]{:S(2)}) %collective-permute-start.8) | collective-permute-done | bytes 1114144 | tf_op jit(solution)/shard_map/ppermute | solution.py:62
  93.6 20.7 %collective-permute-done.14.refs_0_ = bf16[272,2048]{1,0:T(8,128)(2,1)S(1)} collective-permute-done((bf16[272,2048]{1,0:T(8,128)(2,1)}, bf16[272,2048]{1,0:T(8,128)(2,1)S(1)}, u32[]{:S(2)}, u32[]{:S(2)}) %collective-permute-start.14) | collective-permute-done | bytes 1114144 | tf_op jit(solution)/shard_map/ppermute | solution.py:62
  121.5 7.8 %collective-permute-done.16 = bf16[136,2048]{1,0:T(8,128)(2,1)S(1)} collective-permute-done((bf16[136,2048]{1,0:T(8,128)(2,1)S(1)}, bf16[136,2048]{1,0:T(8,128)(2,1)S(1)}, u32[]{:S(2)}, u32[]{:S(2)}) %collective-permute-start.16) | collective-permute-done | bytes 557088 | tf_op jit(solution)/shard_map/ppermute | solution.py:62
  129.4 3.0 collective-permute-done.17
  134.3 11.4 %project.1 = (f32[520,1536]{1,0:T(8,128)}, bf16[2048,512]{1,0:T(8,128)(2,1)}, f32[520,8]{1,0:T(8,128)}, bf16[8,2048]{1,0:T(8,128)(2,1)}) custom-call(s32[8]{0:T(128)} %compare_select_fusion.slots, bf16[520,2048]{1,0:T(8,128)(2,1)} %get-tuple-element.136.refs_1_.x, f32[520,1]{1,0:T(8,128)} %broadcast_in_dim.58.refs_3_.live, ...), custom_call_target="tpu_custom_call" | custom-call | flops 3271557120 | bytes 10518528 | tf_op jit(solution)/shard_map/project/pallas_call | solution.py:856
  149.2 19.9 %mixer_forward.1 = (f32[512,512]{1,0:T(8,128)S(1)}, f32[512,512]{1,0:T(8,128)S(1)}, f32[512,512]{1,0:T(8,128)S(1)}, f32[4,4,128,128]{3,2,1,0:T(8,128)S(1)}, f32[...) custom-call(f32[520,1536]{1,0:T(8,128)} %get-tuple-element.138.xq.xk, ...), custom_call_target="tpu_custom_call" | custom-call | flops 4026531840 | bytes 20488192 | tf_op jit(solution)/shard_map/mixer_forward/pallas_call | solution.py:514
  173.1 11.2 %collective-permute-done.18.refs_2_ = bf16[4,2,128,128]{3,2,1,0:T(8,128)(2,1)S(1)} collective-permute-done((bf16[4,2,128,128]{3,2,1,0:T(8,128)(2,1)S(1)}, bf16[4,2,128,128]{3,2,1,0:T(8,128)(2,1)S(1)}, u32[]{:S(2)}, u32[]{:S(2)}) %collective-permute-start.18) | collective-permute-done | bytes 262176 | tf_op jit(solution)/shard_map/ppermute | solution.py:62
  184.8 2.8 collective-permute-done.19.refs_3_
  189.0 5.2 collective-permute-done.20.refs_4_
  194.2 4.5 collective-permute-start.22
  201.0 5.8 collective-permute-done.22.refs_6_
  209.5 2.0 collective-permute-start.25
  212.1 4.7 collective-permute-done.24
  216.8 4.9 collective-permute-done.25
  221.7 1.7 pad_maximum_fusion.2.refs_8_
  223.4 5.5 mixer_read.1
  228.9 1.7 collective-permute-start.30
  230.8 18.6 %collective-permute-done.30.refs_3_ = bf16[512,512]{1,0:T(8,128)(2,1)S(1)} collective-permute-done((bf16[512,512]{1,0:T(8,128)(2,1)}, bf16[512,512]{1,0:T(8,128)(2,1)S(1)}, u32[]{:S(2)}, u32[]{:S(2)}) %collective-permute-start.30) | collective-permute-done | bytes 524320 | tf_op jit(solution)/shard_map/ppermute | solution.py:19
  250.1 1.7 collective-permute-done.31.refs_4_
  253.3 11.9 %out.1 = (bf16[512,2048]{1,0:T(8,128)(2,1)}, bf16[64,2048]{1,0:T(8,128)(2,1)}, bf16[64,2048]{1,0:T(8,128)(2,1)}, f32[128,2048]{1,0:T(8,128)}) custom-call(s32[9]{0:T(128)} %pad_add_fusion.2.refs_0_, bf16[512,512]{1,0:T(8,128)(2,1)} %get-tuple-element.153.refs_1_, bf16[512,512]{1,0:T(8,128)(2,1)} %copy-done.56, bf16[512,512]{1,0:T(8,128)(2,1)} %copy-done.55, ...), custom_call_target="tpu_custom_call" | custom-call | flops 4294967296 | bytes 16261156 | tf_op jit(solution)/shard_map/out/pallas_call | solution.py:454
  266.6 30.3 %feed_own.1 = (bf16[4096,1408]{1,0:T(8,128)(2,1)}, bf16[4096,1408]{1,0:T(8,128)(2,1)}, bf16[4096,1408]{1,0:T(8,128)(2,1)}, bf16[2,128,2048]{2,1,0:T(8,128)(2,1)}...) custom-call(s32[2]{0:T(128)} %pad_add_fusion.3.index, ...), custom_call_target="tpu_custom_call" | custom-call | flops 17716740096 | bytes 30015488 | tf_op jit(solution)/shard_map/feed_own/pallas_call | solution.py:710
  297.7 2.2 collective-permute-done.32.refs_2_
  299.9 2.9 stage.2
  302.8 19.3 %feed_hidden.2 = (bf16[4096,1408]{1,0:T(8,128)(2,1)}, f32[8,128]{1,0:T(8,128)}) custom-call(s32[4]{0:T(128)} %bitcast.144, bf16[4096,2048]{1,0:T(8,128)(2,1)} %all-gather.4.cloned.1.call-done.cot.refs_0_, bf16[1408,2048]{1,0:T(8,128)(2,1)} %wd.5, bf16[1,128,2048]{2,1,0:T(8,128)(2,1)} %get-tuple-element.159.refs_0_), custom_call_target="tpu_custom_call" | custom-call | flops 11811160064 | bytes 19922944 | tf_op jit(solution)/shard_map/feed_hidden/pallas_call | solution.py:682
  322.1 8.9 %residual.1 = (f32[128,2048]{1,0:T(8,128)}, f32[1,2048]{1,0:T(1,128)}, bf16[128,1024]{1,0:T(8,128)(2,1)}, bf16[128,1024]{1,0:T(8,128)(2,1)}, bf16[128,1024]{1,0:T(8,128)(2,1)}, /*index=5*/bf16[128,1024]{1,0:T(8,128)(2,1)}) custom-call(s32[9]{0:T(128)} %pad_add_fusion.2.refs_0_, bf16[2048,512]{1,0:T(8,128)(2,1)} %get-tuple-element.152.refs_5_.refs_1_, ...), custom_call_target="tpu_custom_call" | custom-call | flops 1073741824 | bytes 13647908 | tf_op jit(solution)/shard_map/residual/pallas_call | solution.py:454
  331.2 1.8 collective-permute-start.35
  333.1 15.5 %feed_hidden.3 = (bf16[4096,1408]{1,0:T(8,128)(2,1)}, f32[8,128]{1,0:T(8,128)}) custom-call(s32[3]{0:T(128)} %slice.137.groups, bf16[4096,2048]{1,0:T(8,128)(2,1)} %all-gather.4.cloned.1.call-done.cot.refs_0_, bf16[1408,2048]{1,0:T(8,128)(2,1)} %wd.5, bf16[128,1024]{1,0:T(8,128)(2,1)} %get-tuple-element.162.refs_0_.refs_1_, ...), custom_call_target="tpu_custom_call", output_to_operand_aliasing={{0}: (4, {})} | custom-call | flops 8858370048 | bytes 16384000 | tf_op jit(solution)/shard_map/feed_hidden/pallas_call | solution.py:682
  349.5 6.0 mixer_leak.1
  357.6 5.1 collective-permute-done.37.refs_1_
  362.7 1.7 pad_maximum_fusion.3.refs_0_
  368.3 34.2 %feed_rows.2 = (bf16[32,2,64,1408]{3,2,1,0:T(8,128)(2,1)}, bf16[32,2,64,1408]{3,2,1,0:T(8,128)(2,1)}, bf16[32,2,64,1408]{3,2,1,0:T(8,128)(2,1)}, f32[8,128]{1,0:T(8,128)}) custom-call(s32[7]{0:T(128)} %copy-done.62, bf16[2048,2048]{1,0:T(8,128)(2,1)} %all-gather.6.cloned.1.call-done.feed.refs_0_, ...), custom_call_target="tpu_custom_call", output_to_operand_aliasing={{0}: (6, {}), {1}: (7, {}), {2}: (8, {})} | custom-call | flops 20669530112 | bytes 39059456 | tf_op jit(solution)/shard_map/feed_rows/pallas_call | solution.py:682
  403.6 5.6 mixer_chain.1.grads
  409.2 16.3 %mixer_backward.1 = (bf16[512,512]{1,0:T(8,128)(2,1)S(1)}, bf16[512,512]{1,0:T(8,128)(2,1)S(1)}, bf16[512,512]{1,0:T(8,128)(2,1)S(1)}, f32[3,8,512]{2,1,0:T(8,12...) custom-call(f32[520,1536]{1,0:T(8,128)} %get-tuple-element.138.xq.xk.xv, ...), custom_call_target="tpu_custom_call" | custom-call | flops 2013265920 | bytes 20881408 | tf_op jit(solution)/shard_map/mixer_backward/pallas_call | solution.py:582
  430.8 3.5 collective-permute-done.41.refs_13_
  434.9 12.2 %normed_back.1 = (bf16[512,1536]{1,0:T(8,128)(2,1)}, bf16[2,256,2048]{2,1,0:T(8,128)(2,1)}, bf16[2,256,2048]{2,1,0:T(8,128)(2,1)}, f32[1,2048]{1,0:T(1,128)}) custom-call(s32[9]{0:T(128)} %get-tuple-element.261.refs_0_, bf16[272,2048]{1,0:T(8,128)(2,1)} %weights.1.refs_0_.refs_8_.refs_1_, bf16[272,2048]{1,0:T(8,128)(2,1)} %gate.11.refs_1_.refs_9_.refs_2_, ...), custom_call_target="tpu_custom_call" | custom-call | flops 3221225472 | bytes 20570180 | tf_op jit(solution)/shard_map/normed_back/pallas_call | solution.py:454
  447.1 9.0 %weight_rows.1 = (bf16[256,2048]{1,0:T(8,128)(2,1)}, bf16[256,2048]{1,0:T(8,128)(2,1)}, bf16[256,2048]{1,0:T(8,128)(2,1)}, bf16[256,2048]{1,0:T(8,128)(2,1)}, bf...) custom-call(s32[9]{0:T(128)} %get-tuple-element.259.refs_0_, ...), custom_call_target="tpu_custom_call" | custom-call | flops 4294967296 | bytes 14753828 | tf_op jit(solution)/shard_map/weight_rows/pallas_call | solution.py:454
  456.0 1.7 collective-permute-start.44
  462.1 34.0 %feed_rows.3 = (bf16[32,2,64,1408]{3,2,1,0:T(8,128)(2,1)}, bf16[32,2,64,1408]{3,2,1,0:T(8,128)(2,1)}, bf16[32,2,64,1408]{3,2,1,0:T(8,128)(2,1)}, f32[8,128]{1,0:T(8,128)}) custom-call(s32[7]{0:T(128)} %copy-done.62, bf16[2048,2048]{1,0:T(8,128)(2,1)} %all-gather.8.cloned.1.call-done.feed.refs_1_, ...), custom_call_target="tpu_custom_call", output_to_operand_aliasing={{0}: (6, {}), {1}: (7, {}), {2}: (8, {})} | custom-call | flops 20669530112 | bytes 39059456 | tf_op jit(solution)/shard_map/feed_rows/pallas_call | solution.py:682
  497.1 3.3 ring_add.3
  502.5 33.9 %weight_grad.3 = (f32[2048,1408]{1,0:T(8,128)}, f32[8,128]{1,0:T(8,128)}) custom-call(bf16[2048,2048]{1,0:T(8,128)(2,1)} %all-gather.6.cloned.1.call-done.feed.refs_0_, bf16[2048,2048]{1,0:T(8,128)(2,1)} %all-gather.8.cloned.1.call-done.feed.refs_1_, bf16[32,2,64,1408]{3,2,1,0:T(8,128)(2,1)} %get-tuple-element.219.refs_2_, ...), custom_call_target="tpu_custom_call" | custom-call | flops 23622320128 | bytes 39845888 | tf_op jit(solution)/shard_map/weight_grad/pallas_call | solution.py:751
  537.7 3.8 ring_add.4
  541.4 2.5 collective-permute-start.48
  543.9 33.8 %weight_grad.4 = (f32[2048,1408]{1,0:T(8,128)}, f32[8,128]{1,0:T(8,128)}) custom-call(bf16[2048,2048]{1,0:T(8,128)(2,1)} %all-gather.6.cloned.1.call-done.feed.refs_0_, bf16[2048,2048]{1,0:T(8,128)(2,1)} %all-gather.8.cloned.1.call-done.feed.refs_1_, bf16[32,2,64,1408]{3,2,1,0:T(8,128)(2,1)} %get-tuple-element.223.refs_2_, ...), custom_call_target="tpu_custom_call" | custom-call | flops 23622320128 | bytes 39845888 | tf_op jit(solution)/shard_map/weight_grad/pallas_call | solution.py:751
  579.1 4.3 stage.3
  586.2 3.8 ring_add.5
  589.9 2.0 collective-permute-start.50
  592.2 34.6 %weight_grad.5 = (f32[1408,2048]{1,0:T(8,128)}, f32[8,128]{1,0:T(8,128)}) custom-call(bf16[4096,2048]{1,0:T(8,128)(2,1)} %all-gather.4.cloned.1.call-done.cot.refs_0_, bf16[32,2,64,1408]{3,2,1,0:T(8,128)(2,1)} %get-tuple-element.209.refs_1_, bf16[256,2048]{1,0:T(8,128)(2,1)} %get-tuple-element.225.refs_2_), custom_call_target="tpu_custom_call" | custom-call | flops 23622320128 | bytes 39845888 | tf_op jit(solution)/shard_map/weight_grad/pallas_call | solution.py:751
  632.1 3.0 sum.1
  641.3 4.5 finish.1
  645.8 3.5 collective-permute-done.54.refs_4_
  650.0 3.1 assemble.1
  (323 shorter events, 89.7 us)
Async XLA Ops:
  7.2 55.4 %copy-start = (f32[3,4,2048]{2,1,0:T(4,128)S(1)}, f32[3,4,2048]{2,1,0:T(4,128)}, u32[]{:S(2)}) copy-start(f32[3,4,2048]{2,1,0:T(4,128)} %param.27) | copy-start | bytes 294916
  7.2 295.6 %all-gather.4.cloned.1.call-start = ((), (), s32[]{:S(2)}) async-start(), calls=%async_computation | async-start | bytes 17301504 | tf_op jit(solution)/shard_map/all_gather | solution.py:1084
  11.3 23.8 %copy-start.59 = (s32[6]{0:T(128)S(1)}, s32[6]{0:T(128)}, u32[]{:S(2)}) copy-start(s32[6]{0:T(128)} %param.21) | copy-start | bytes 76
  11.3 10.4 %collective-permute-start = (bf16[80,2048]{1,0:T(8,128)(2,1)S(1)}, bf16[80,2048]{1,0:T(8,128)(2,1)S(1)}, u32[]{:S(2)}, u32[]{:S(2)}) collective-permute-start(bf16[80,2048]{1,0:T(8,128)(2,1)S(1)} %get-tuple-element.244), channel_id=1, source_target_pairs={{0,1},{1,0},{2,3},{3,2},{4,5},{5,4},{6,7},{7,6},{8,9},{9,8},{10,11... | collective-permute-start | bytes 983048 | tf_op jit(solution)/shard_map/ppermute | solution.py:19
  11.8 11.1 %collective-permute-start.1 = (bf16[80,2048]{1,0:T(8,128)(2,1)S(1)}, bf16[80,2048]{1,0:T(8,128)(2,1)S(1)}, u32[]{:S(2)}, u32[]{:S(2)}) collective-permute-start(bf16[80,2048]{1,0:T(8,128)(2,1)S(1)} %get-tuple-element.243), channel_id=1, source_target_pairs={{0,2},{1,3},{2,0},{3,1},{4,6},{5,7},{6,4},{7,5},{8,10},{9,11},{10,... | collective-permute-start | bytes 983048 | tf_op jit(solution)/shard_map/ppermute | solution.py:19
  14.3 15.3 %collective-permute-start.2 = (bf16[80,2048]{1,0:T(8,128)(2,1)S(1)}, bf16[80,2048]{1,0:T(8,128)(2,1)}, u32[]{:S(2)}, u32[]{:S(2)}) collective-permute-start(bf16[80,2048]{1,0:T(8,128)(2,1)S(1)} %get-tuple-element.242), channel_id=1, source_target_pairs={{0,3},{1,2},{2,1},{3,0},{4,7},{5,6},{6,5},{7,4},{8,11},{9,10},{10,... | collective-permute-start | bytes 983048 | tf_op jit(solution)/shard_map/ppermute | solution.py:19
  14.5 1.9 collective-permute-start.4
  20.0 22.6 %collective-permute-start.5 = (bf16[144,2048]{1,0:T(8,128)(2,1)S(1)}, bf16[144,2048]{1,0:T(8,128)(2,1)}, u32[]{:S(2)}, u32[]{:S(2)}) collective-permute-start(bf16[144,2048]{1,0:T(8,128)(2,1)S(1)} %pad_maximum_fusion.refs_1_), channel_id=1, source_target_pairs={{0,2},{1,3},{2,0},{3,1},{4,6},{5,7},{6,4},{7,5},{8,10},{9,11},{10,... | collective-permute-start | bytes 1769480 | tf_op jit(solution)/shard_map/ppermute | solution.py:19
  32.0 27.7 %collective-permute-start.3 = (bf16[272,2048]{1,0:T(8,128)(2,1)}, bf16[272,2048]{1,0:T(8,128)(2,1)S(1)}, u32[]{:S(2)}, u32[]{:S(2)}) collective-permute-start(bf16[272,2048]{1,0:T(8,128)(2,1)} %weights.1.refs_0_.refs_8_.refs_1_), channel_id=1, source_target_pairs={{0,8},{8,16},{16,24},{24,28},{28,20},{20,12},{12,4},{4,0},{1,9},{9... | collective-permute-start | bytes 3342344 | tf_op jit(solution)/shard_map/ppermute | solution.py:62
  34.3 19.4 %collective-permute-start.11 = (bf16[128,2048]{1,0:T(8,128)(2,1)S(1)}, bf16[128,2048]{1,0:T(8,128)(2,1)}, u32[]{:S(2)}, u32[]{:S(2)}) collective-permute-start(bf16[128,2048]{1,0:T(8,128)(2,1)S(1)} %copy-done.19), channel_id=1, source_target_pairs={{0,2},{1,3},{2,0},{3,1},{4,6},{5,7},{6,4},{7,5},{8,10},{9,11},{10,... | collective-permute-start | bytes 1572872 | tf_op jit(solution)/shard_map/ppermute | solution.py:19
  35.3 28.1 %collective-permute-start.7 = (bf16[272,2048]{1,0:T(8,128)(2,1)}, bf16[272,2048]{1,0:T(8,128)(2,1)S(1)}, u32[]{:S(2)}, u32[]{:S(2)}) collective-permute-start(bf16[272,2048]{1,0:T(8,128)(2,1)} %weights.1.refs_0_.refs_8_.refs_1_), channel_id=1, source_target_pairs={{0,4},{8,0},{16,8},{24,16},{28,24},{20,28},{12,20},{4,12},{1,5},{9... | collective-permute-start | bytes 3342344 | tf_op jit(solution)/shard_map/ppermute | solution.py:62
  42.6 11.1 %collective-permute-start.6 = (bf16[144,2048]{1,0:T(8,128)(2,1)}, bf16[144,2048]{1,0:T(8,128)(2,1)S(1)}, u32[]{:S(2)}, u32[]{:S(2)}) collective-permute-start(bf16[144,2048]{1,0:T(8,128)(2,1)} %collective-permute-done.5.refs_3_), channel_id=1, source_target_pairs={{0,1},{1,0},{2,3},{3,2},{4,5},{5,4},{6,7},{7,6},{8,9},{9,8},{10,11... | collective-permute-start | bytes 1769480 | tf_op jit(solution)/shard_map/ppermute | solution.py:19
  42.8 24.9 %collective-permute-start.9 = (bf16[144,2048]{1,0:T(8,128)(2,1)}, bf16[144,2048]{1,0:T(8,128)(2,1)}, u32[]{:S(2)}, u32[]{:S(2)}) collective-permute-start(bf16[144,2048]{1,0:T(8,128)(2,1)} %copy-done.22), channel_id=1, source_target_pairs={{0,1},{1,0},{2,3},{3,2},{4,5},{5,4},{6,7},{7,6},{8,9},{9,8},{10,11... | collective-permute-start | bytes 1769480 | tf_op jit(solution)/shard_map/ppermute | solution.py:19
  53.7 11.1 %collective-permute-start.10 = (bf16[128,2048]{1,0:T(8,128)(2,1)S(1)}, bf16[128,2048]{1,0:T(8,128)(2,1)}, u32[]{:S(2)}, u32[]{:S(2)}) collective-permute-start(bf16[128,2048]{1,0:T(8,128)(2,1)S(1)} %copy-done.19), channel_id=1, source_target_pairs={{0,1},{1,0},{2,3},{3,2},{4,5},{5,4},{6,7},{7,6},{8,9},{9,8},{10,11... | collective-permute-start | bytes 1572872 | tf_op jit(solution)/shard_map/ppermute | solution.py:19
  53.7 11.1 %collective-permute-start.12 = (bf16[128,2048]{1,0:T(8,128)(2,1)}, bf16[128,2048]{1,0:T(8,128)(2,1)}, u32[]{:S(2)}, u32[]{:S(2)}) collective-permute-start(bf16[128,2048]{1,0:T(8,128)(2,1)} %collective-permute-done.11.refs_3_), channel_id=1, source_target_pairs={{0,1},{1,0},{2,3},{3,2},{4,5},{5,4},{6,7},{7,6},{8,9},{9,8},{10,11... | collective-permute-start | bytes 1572872 | tf_op jit(solution)/shard_map/ppermute | solution.py:19
  60.8 26.7 %collective-permute-start.8 = (bf16[272,2048]{1,0:T(8,128)(2,1)}, bf16[272,2048]{1,0:T(8,128)(2,1)S(1)}, u32[]{:S(2)}, u32[]{:S(2)}) collective-permute-start(bf16[272,2048]{1,0:T(8,128)(2,1)} %gate.11.refs_1_.refs_9_.refs_2_), channel_id=1, source_target_pairs={{0,8},{8,16},{16,24},{24,28},{28,20},{20,12},{12,4},{4,0},{1,9},{9... | collective-permute-start | bytes 3342344 | tf_op jit(solution)/shard_map/ppermute | solution.py:62
  64.4 26.2 %collective-permute-start.13 = (bf16[272,2048]{1,0:T(8,128)(2,1)}, bf16[272,2048]{1,0:T(8,128)(2,1)S(1)}, u32[]{:S(2)}, u32[]{:S(2)}) collective-permute-start(bf16[272,2048]{1,0:T(8,128)(2,1)} %gate.12.refs_2_.refs_10_.refs_3_), channel_id=1, source_target_pairs={{0,4},{8,0},{16,8},{24,16},{28,24},{20,28},{12,20},{4,12},{1,5},{9... | collective-permute-start | bytes 3342344 | tf_op jit(solution)/shard_map/ppermute | solution.py:62
  88.5 25.9 %collective-permute-start.14 = (bf16[272,2048]{1,0:T(8,128)(2,1)}, bf16[272,2048]{1,0:T(8,128)(2,1)S(1)}, u32[]{:S(2)}, u32[]{:S(2)}) collective-permute-start(bf16[272,2048]{1,0:T(8,128)(2,1)} %gate.13.refs_3_.refs_11_.refs_4_), channel_id=1, source_target_pairs={{0,8},{8,16},{16,24},{24,28},{28,20},{20,12},{12,4},{4,0},{1,9},{9... | collective-permute-start | bytes 3342344 | tf_op jit(solution)/shard_map/ppermute | solution.py:62
  91.7 26.3 %collective-permute-start.15 = (bf16[272,2048]{1,0:T(8,128)(2,1)}, bf16[272,2048]{1,0:T(8,128)(2,1)S(1)}, u32[]{:S(2)}, u32[]{:S(2)}) collective-permute-start(bf16[272,2048]{1,0:T(8,128)(2,1)} %gate.14.refs_4_.refs_12_.refs_5_), channel_id=1, source_target_pairs={{0,4},{8,0},{16,8},{24,16},{28,24},{20,28},{12,20},{4,12},{1,5},{9... | collective-permute-start | bytes 3342344 | tf_op jit(solution)/shard_map/ppermute | solution.py:62
  116.4 12.8 %collective-permute-start.16 = (bf16[136,2048]{1,0:T(8,128)(2,1)S(1)}, bf16[136,2048]{1,0:T(8,128)(2,1)S(1)}, u32[]{:S(2)}, u32[]{:S(2)}) collective-permute-start(bf16[136,2048]{1,0:T(8,128)(2,1)S(1)} %slice.152), channel_id=1, source_target_pairs={{0,8},{8,16},{16,24},{24,28},{28,20},{20,12},{12,4},{4,0},{1,9},{9... | collective-permute-start | bytes 1671176 | tf_op jit(solution)/shard_map/ppermute | solution.py:62
  120.0 12.3 %collective-permute-start.17 = (bf16[136,2048]{1,0:T(8,128)(2,1)S(1)}, bf16[136,2048]{1,0:T(8,128)(2,1)S(1)}, u32[]{:S(2)}, u32[]{:S(2)}) collective-permute-start(bf16[136,2048]{1,0:T(8,128)(2,1)S(1)} %slice.153), channel_id=1, source_target_pairs={{0,4},{8,0},{16,8},{24,16},{28,24},{20,28},{12,20},{4,12},{1,5},{9... | collective-permute-start | bytes 1671176 | tf_op jit(solution)/shard_map/ppermute | solution.py:62
  133.5 234.8 %all-gather.6.cloned.1.call-start = ((), (), s32[]{:S(2)}) async-start(), calls=%async_computation.1 | async-start | bytes 8650752 | tf_op jit(solution)/shard_map/all_gather | solution.py:1105
  146.8 82.0 %collective-permute-start.27 = (bf16[2048,512]{1,0:T(8,128)(2,1)}, bf16[2048,512]{1,0:T(8,128)(2,1)}, u32[]{:S(2)}, u32[]{:S(2)}) collective-permute-start(bf16[2048,512]{1,0:T(8,128)(2,1)} %get-tuple-element.152.refs_5_.refs_1_), channel_id=1, source_target_pairs={{0,2},{1,3},{2,0},{3,1},{4,6},{5,7},{6,4},{7,5},{8,10},{9,11},{10,... | collective-permute-start | bytes 6291464 | tf_op jit(solution)/shard_map/ppermute | solution.py:19
  149.2 62.3 %copy-start.53 = (s32[8]{0:T(128)S(1)}, s32[8]{0:T(128)}, u32[]{:S(2)}) copy-start(s32[8]{0:T(128)} %compare_select_fusion.slots) | copy-start | bytes 100
  171.1 52.3 %copy-start.9 = (bf16[4,2,128,128]{3,2,1,0:T(8,128)(2,1)}, bf16[4,2,128,128]{3,2,1,0:T(8,128)(2,1)S(1)}, u32[]{:S(2)}) copy-start(bf16[4,2,128,128]{3,2,1,0:T(8,128)(2,1)S(1)} %get-tuple-element.146.refs_1_) | copy-start | bytes 786436
  171.1 13.3 %collective-permute-start.18 = (bf16[4,2,128,128]{3,2,1,0:T(8,128)(2,1)S(1)}, bf16[4,2,128,128]{3,2,1,0:T(8,128)(2,1)S(1)}, u32[]{:S(2)}, u32[]{:S(2)}) collective-permute-start(bf16[4,2,128,128]{3,2,1,0:T(8,128)(2,1)S(1)} %get-tuple-element.146.refs_1_), channel_id=1, source_target_pairs={{0,8},{8,16},{16,24},{24,28},{28,20},{20,12},{12,4},{4,0},{1,9},{9... | collective-permute-start | bytes 786440 | tf_op jit(solution)/shard_map/ppermute | solution.py:62
  172.7 14.9 %collective-permute-start.19 = (bf16[4,2,128,128]{3,2,1,0:T(8,128)(2,1)S(1)}, bf16[4,2,128,128]{3,2,1,0:T(8,128)(2,1)S(1)}, u32[]{:S(2)}, u32[]{:S(2)}) collective-permute-start(bf16[4,2,128,128]{3,2,1,0:T(8,128)(2,1)S(1)} %get-tuple-element.146.refs_1_), channel_id=1, source_target_pairs={{0,4},{8,0},{16,8},{24,16},{28,24},{20,28},{12,20},{4,12},{1,5},{9... | collective-permute-start | bytes 786440 | tf_op jit(solution)/shard_map/ppermute | solution.py:62
  184.3 9.9 %collective-permute-start.20 = (bf16[4,2,128,128]{3,2,1,0:T(8,128)(2,1)S(1)}, bf16[4,2,128,128]{3,2,1,0:T(8,128)(2,1)S(1)}, u32[]{:S(2)}, u32[]{:S(2)}) collective-permute-start(bf16[4,2,128,128]{3,2,1,0:T(8,128)(2,1)S(1)} %collective-permute-done.18.refs_2_), channel_id=1, source_target_pairs={{0,8},{8,16},{16,24},{24,28},{28,20},{20,12},{12,4},{4,0},{1,9},{9... | collective-permute-start | bytes 786440 | tf_op jit(solution)/shard_map/ppermute | solution.py:62
  187.6 11.8 %collective-permute-start.21 = (bf16[4,2,128,128]{3,2,1,0:T(8,128)(2,1)S(1)}, bf16[4,2,128,128]{3,2,1,0:T(8,128)(2,1)S(1)}, u32[]{:S(2)}, u32[]{:S(2)}) collective-permute-start(bf16[4,2,128,128]{3,2,1,0:T(8,128)(2,1)S(1)} %collective-permute-done.19.refs_3_), channel_id=1, source_target_pairs={{0,4},{8,0},{16,8},{24,16},{28,24},{20,28},{12,20},{4,12},{1,5},{9... | collective-permute-start | bytes 786440 | tf_op jit(solution)/shard_map/ppermute | solution.py:62
  194.2 12.5 %collective-permute-start.22 = (bf16[4,2,128,128]{3,2,1,0:T(8,128)(2,1)S(1)}, bf16[4,2,128,128]{3,2,1,0:T(8,128)(2,1)S(1)}, u32[]{:S(2)}, u32[]{:S(2)}) collective-permute-start(bf16[4,2,128,128]{3,2,1,0:T(8,128)(2,1)S(1)} %collective-permute-done.20.refs_4_), channel_id=1, source_target_pairs={{0,8},{8,16},{16,24},{24,28},{28,20},{20,12},{12,4},{4,0},{1,9},{9... | collective-permute-start | bytes 786440 | tf_op jit(solution)/shard_map/ppermute | solution.py:62
  199.4 8.7 %collective-permute-start.23 = (bf16[4,2,128,128]{3,2,1,0:T(8,128)(2,1)S(1)}, bf16[4,2,128,128]{3,2,1,0:T(8,128)(2,1)S(1)}, u32[]{:S(2)}, u32[]{:S(2)}) collective-permute-start(bf16[4,2,128,128]{3,2,1,0:T(8,128)(2,1)S(1)} %collective-permute-done.21.refs_5_), channel_id=1, source_target_pairs={{0,4},{8,0},{16,8},{24,16},{28,24},{20,28},{12,20},{4,12},{1,5},{9... | collective-permute-start | bytes 786440 | tf_op jit(solution)/shard_map/ppermute | solution.py:62
  208.1 8.7 %collective-permute-start.24 = (bf16[2,2,128,128]{3,2,1,0:T(8,128)(2,1)}, bf16[2,2,128,128]{3,2,1,0:T(8,128)(2,1)}, u32[]{:S(2)}, u32[]{:S(2)}) collective-permute-start(bf16[2,2,128,128]{3,2,1,0:T(8,128)(2,1)} %slice.155), channel_id=1, source_target_pairs={{0,8},{8,16},{16,24},{24,28},{28,20},{20,12},{12,4},{4,0},{1,9},{9... | collective-permute-start | bytes 393224 | tf_op jit(solution)/shard_map/ppermute | solution.py:62
  209.5 12.2 %collective-permute-start.25 = (bf16[2,2,128,128]{3,2,1,0:T(8,128)(2,1)}, bf16[2,2,128,128]{3,2,1,0:T(8,128)(2,1)}, u32[]{:S(2)}, u32[]{:S(2)}) collective-permute-start(bf16[2,2,128,128]{3,2,1,0:T(8,128)(2,1)} %slice.156), channel_id=1, source_target_pairs={{0,4},{8,0},{16,8},{24,16},{28,24},{20,28},{12,20},{4,12},{1,5},{9... | collective-permute-start | bytes 393224 | tf_op jit(solution)/shard_map/ppermute | solution.py:62
  212.1 39.7 %collective-permute-start.26 = (bf16[2048,512]{1,0:T(8,128)(2,1)}, bf16[2048,512]{1,0:T(8,128)(2,1)}, u32[]{:S(2)}, u32[]{:S(2)}) collective-permute-start(bf16[2048,512]{1,0:T(8,128)(2,1)} %get-tuple-element.152.refs_5_.refs_1_), channel_id=1, source_target_pairs={{0,1},{1,0},{2,3},{3,2},{4,5},{5,4},{6,7},{7,6},{8,9},{9,8},{10,11... | collective-permute-start | bytes 6291464 | tf_op jit(solution)/shard_map/ppermute | solution.py:19
  228.9 22.9 %collective-permute-start.28 = (bf16[2048,512]{1,0:T(8,128)(2,1)}, bf16[2048,512]{1,0:T(8,128)(2,1)S(1)}, u32[]{:S(2)}, u32[]{:S(2)}) collective-permute-start(bf16[2048,512]{1,0:T(8,128)(2,1)} %gate.17.refs_7_.refs_3_), channel_id=1, source_target_pairs={{0,1},{1,0},{2,3},{3,2},{4,5},{5,4},{6,7},{7,6},{8,9},{9,8},{10,11... | collective-permute-start | bytes 6291464 | tf_op jit(solution)/shard_map/ppermute | solution.py:19
  228.9 20.5 %collective-permute-start.30 = (bf16[512,512]{1,0:T(8,128)(2,1)}, bf16[512,512]{1,0:T(8,128)(2,1)S(1)}, u32[]{:S(2)}, u32[]{:S(2)}) collective-permute-start(bf16[512,512]{1,0:T(8,128)(2,1)} %get-tuple-element.153.refs_1_), channel_id=1, source_target_pairs={{0,2},{1,3},{2,0},{3,1},{4,6},{5,7},{6,4},{7,5},{8,10},{9,11},{10,... | collective-permute-start | bytes 1572872 | tf_op jit(solution)/shard_map/ppermute | solution.py:19
  230.6 19.5 %collective-permute-start.29 = (bf16[512,512]{1,0:T(8,128)(2,1)}, bf16[512,512]{1,0:T(8,128)(2,1)S(1)}, u32[]{:S(2)}, u32[]{:S(2)}) collective-permute-start(bf16[512,512]{1,0:T(8,128)(2,1)} %get-tuple-element.153.refs_1_), channel_id=1, source_target_pairs={{0,1},{1,0},{2,3},{3,2},{4,5},{5,4},{6,7},{7,6},{8,9},{9,8},{10,11... | collective-permute-start | bytes 1572872 | tf_op jit(solution)/shard_map/ppermute | solution.py:19
  249.4 2.3 collective-permute-start.31
  265.2 196.9 %all-gather.8.cloned.1.call-start = ((), (), s32[]{:S(2)}) async-start(), calls=%async_computation.2 | async-start | bytes 8650752 | tf_op jit(solution)/shard_map/all_gather | solution.py:1105
  265.9 360.9 %all-reduce.7.cloned.1.call-start = ((), (), s32[]{:S(2)}) async-start(), calls=%async_computation.3 | async-start | bytes 532480 | tf_op jit(solution)/shard_map/psum | solution.py:1242
  296.9 3.0 collective-permute-start.32
  302.8 19.4 %collective-permute-start.33 = (bf16[1,128,2048]{2,1,0:T(8,128)(2,1)}, bf16[1,128,2048]{2,1,0:T(8,128)(2,1)}, u32[]{:S(2)}, u32[]{:S(2)}) collective-permute-start(bf16[1,128,2048]{2,1,0:T(8,128)(2,1)} %get-tuple-element.159.refs_0_), channel_id=1, source_target_pairs={{0,2},{1,3},{2,0},{3,1},{4,6},{5,7},{6,4},{7,5},{8,10},{9,11},{10,... | collective-permute-start | bytes 1572872 | tf_op jit(solution)/shard_map/ppermute | solution.py:19
  331.0 17.6 %collective-permute-start.34 = (bf16[128,1024]{1,0:T(8,128)(2,1)}, bf16[128,1024]{1,0:T(8,128)(2,1)S(1)}, u32[]{:S(2)}, u32[]{:S(2)}) collective-permute-start(bf16[128,1024]{1,0:T(8,128)(2,1)} %get-tuple-element.163), channel_id=1, source_target_pairs={{0,1},{1,0},{2,3},{3,2},{4,5},{5,4},{6,7},{7,6},{8,9},{9,8},{10,11... | collective-permute-start | bytes 786440 | tf_op jit(solution)/shard_map/ppermute | solution.py:19
  331.2 17.4 %collective-permute-start.35 = (bf16[128,1024]{1,0:T(8,128)(2,1)}, bf16[128,1024]{1,0:T(8,128)(2,1)S(1)}, u32[]{:S(2)}, u32[]{:S(2)}) collective-permute-start(bf16[128,1024]{1,0:T(8,128)(2,1)} %get-tuple-element.164), channel_id=1, source_target_pairs={{0,2},{1,3},{2,0},{3,1},{4,6},{5,7},{6,4},{7,5},{8,10},{9,11},{10,... | collective-permute-start | bytes 786440 | tf_op jit(solution)/shard_map/ppermute | solution.py:19
  333.1 15.6 %collective-permute-start.36 = (bf16[128,1024]{1,0:T(8,128)(2,1)}, bf16[128,1024]{1,0:T(8,128)(2,1)S(1)}, u32[]{:S(2)}, u32[]{:S(2)}) collective-permute-start(bf16[128,1024]{1,0:T(8,128)(2,1)} %get-tuple-element.165), channel_id=1, source_target_pairs={{0,3},{1,2},{2,1},{3,0},{4,7},{5,6},{6,5},{7,4},{8,11},{9,10},{10,... | collective-permute-start | bytes 786440 | tf_op jit(solution)/shard_map/ppermute | solution.py:19
  355.5 7.2 %collective-permute-start.37 = (bf16[4,128,128]{2,1,0:T(8,128)(2,1)}, bf16[4,128,128]{2,1,0:T(8,128)(2,1)S(1)}, u32[]{:S(2)}, u32[]{:S(2)}) collective-permute-start(bf16[4,128,128]{2,1,0:T(8,128)(2,1)} %get-tuple-element.169), channel_id=1, source_target_pairs={{0,4},{4,0},{8,12},{12,8},{16,20},{20,16},{24,28},{28,24},{1,5},{5... | collective-permute-start | bytes 393224 | tf_op jit(solution)/shard_map/ppermute | solution.py:19
  362.7 39.8 %copy-start.34 = (bf16[4,128,128]{2,1,0:T(8,128)(2,1)}, bf16[4,128,128]{2,1,0:T(8,128)(2,1)S(1)}, u32[]{:S(2)}) copy-start(bf16[4,128,128]{2,1,0:T(8,128)(2,1)S(1)} %collective-permute-done.37.refs_1_) | copy-start | bytes 393220
  364.4 38.1 %collective-permute-start.38 = (bf16[2,4,128,128]{3,2,1,0:T(8,128)(2,1)}, bf16[2,4,128,128]{3,2,1,0:T(8,128)(2,1)}, u32[]{:S(2)}, u32[]{:S(2)}) collective-permute-start(bf16[2,4,128,128]{3,2,1,0:T(8,128)(2,1)} %pad_maximum_fusion.3.refs_0_), channel_id=1, source_target_pairs={{8,0},{12,4},{16,8},{20,12},{24,16},{28,20},{9,1},{13,5},{17,9},{2... | collective-permute-start | bytes 786440 | tf_op jit(solution)/shard_map/ppermute | solution.py:1170
  365.7 37.9 %collective-permute-start.39 = (bf16[2,4,128,128]{3,2,1,0:T(8,128)(2,1)}, bf16[2,4,128,128]{3,2,1,0:T(8,128)(2,1)}, u32[]{:S(2)}, u32[]{:S(2)}) collective-permute-start(bf16[2,4,128,128]{3,2,1,0:T(8,128)(2,1)} %pad_maximum_fusion.3.refs_0_), channel_id=1, source_target_pairs={{16,0},{20,4},{24,8},{28,12},{17,1},{21,5},{25,9},{29,13},{18,2},{... | collective-permute-start | bytes 786440 | tf_op jit(solution)/shard_map/ppermute | solution.py:1170
  367.0 36.6 %collective-permute-start.40 = (bf16[2,4,128,128]{3,2,1,0:T(8,128)(2,1)}, bf16[2,4,128,128]{3,2,1,0:T(8,128)(2,1)}, u32[]{:S(2)}, u32[]{:S(2)}) collective-permute-start(bf16[2,4,128,128]{3,2,1,0:T(8,128)(2,1)} %pad_maximum_fusion.3.refs_0_), channel_id=1, source_target_pairs={{24,0},{28,4},{25,1},{29,5},{26,2},{30,6},{27,3},{31,7}} | collective-permute-start | bytes 786440 | tf_op jit(solution)/shard_map/ppermute | solution.py:1170
  428.5 5.7 collective-permute-start.41
  456.0 40.1 %collective-permute-start.44 = (bf16[128,2048]{1,0:T(8,128)(2,1)}, bf16[128,2048]{1,0:T(8,128)(2,1)S(1)}, u32[]{:S(2)}, u32[]{:S(2)}) collective-permute-start(bf16[128,2048]{1,0:T(8,128)(2,1)} %get-tuple-element.196.refs_0_), channel_id=1, source_target_pairs={{0,8},{8,16},{16,24},{24,28},{28,20},{20,12},{12,4},{4,0},{1,9},{9... | collective-permute-start | bytes 1572872 | tf_op jit(solution)/shard_map/ppermute | solution.py:62
  457.7 38.4 %collective-permute-start.45 = (bf16[128,2048]{1,0:T(8,128)(2,1)}, bf16[128,2048]{1,0:T(8,128)(2,1)S(1)}, u32[]{:S(2)}, u32[]{:S(2)}) collective-permute-start(bf16[128,2048]{1,0:T(8,128)(2,1)} %get-tuple-element.216), channel_id=1, source_target_pairs={{0,4},{8,0},{16,8},{24,16},{28,24},{20,28},{12,20},{4,12},{1,5},{9... | collective-permute-start | bytes 1572872 | tf_op jit(solution)/shard_map/ppermute | solution.py:62
  461.1 116.6 %collective-permute-start.42 = (bf16[2,256,2048]{2,1,0:T(8,128)(2,1)}, bf16[2,256,2048]{2,1,0:T(8,128)(2,1)S(1)}, u32[]{:S(2)}, u32[]{:S(2)}) collective-permute-start(bf16[2,256,2048]{2,1,0:T(8,128)(2,1)} %get-tuple-element.189), channel_id=1, source_target_pairs={{0,1},{1,0},{2,3},{3,2},{4,5},{5,4},{6,7},{7,6},{8,9},{9,8},{10,11... | collective-permute-start | bytes 6291464 | tf_op jit(solution)/shard_map/ppermute | solution.py:19
  500.4 35.9 %collective-permute-start.46 = (bf16[256,2048]{1,0:T(8,128)(2,1)}, bf16[256,2048]{1,0:T(8,128)(2,1)S(1)}, u32[]{:S(2)}, u32[]{:S(2)}) collective-permute-start(bf16[256,2048]{1,0:T(8,128)(2,1)} %get-tuple-element.217.refs_3_), channel_id=1, source_target_pairs={{0,8},{8,16},{16,24},{24,28},{28,20},{20,12},{12,4},{4,0},{1,9},{9... | collective-permute-start | bytes 3145736 | tf_op jit(solution)/shard_map/ppermute | solution.py:62
  501.8 34.6 %collective-permute-start.47 = (bf16[256,2048]{1,0:T(8,128)(2,1)}, bf16[256,2048]{1,0:T(8,128)(2,1)S(1)}, u32[]{:S(2)}, u32[]{:S(2)}) collective-permute-start(bf16[256,2048]{1,0:T(8,128)(2,1)} %get-tuple-element.218), channel_id=1, source_target_pairs={{0,4},{8,0},{16,8},{24,16},{28,24},{20,28},{12,20},{4,12},{1,5},{9... | collective-permute-start | bytes 3145736 | tf_op jit(solution)/shard_map/ppermute | solution.py:62
  541.4 43.4 %collective-permute-start.48 = (bf16[256,2048]{1,0:T(8,128)(2,1)}, bf16[256,2048]{1,0:T(8,128)(2,1)S(1)}, u32[]{:S(2)}, u32[]{:S(2)}) collective-permute-start(bf16[256,2048]{1,0:T(8,128)(2,1)} %get-tuple-element.221.refs_3_), channel_id=1, source_target_pairs={{0,8},{8,16},{16,24},{24,28},{28,20},{20,12},{12,4},{4,0},{1,9},{9... | collective-permute-start | bytes 3145736 | tf_op jit(solution)/shard_map/ppermute | solution.py:62
  543.9 40.9 %collective-permute-start.49 = (bf16[256,2048]{1,0:T(8,128)(2,1)}, bf16[256,2048]{1,0:T(8,128)(2,1)S(1)}, u32[]{:S(2)}, u32[]{:S(2)}) collective-permute-start(bf16[256,2048]{1,0:T(8,128)(2,1)} %get-tuple-element.222), channel_id=1, source_target_pairs={{0,4},{8,0},{16,8},{24,16},{28,24},{20,28},{12,20},{4,12},{1,5},{9... | collective-permute-start | bytes 3145736 | tf_op jit(solution)/shard_map/ppermute | solution.py:62
  583.4 57.0 %collective-permute-start.43 = (bf16[1,256,2048]{2,1,0:T(8,128)(2,1)}, bf16[1,256,2048]{2,1,0:T(8,128)(2,1)S(1)}, u32[]{:S(2)}, u32[]{:S(2)}) collective-permute-start(bf16[1,256,2048]{2,1,0:T(8,128)(2,1)} %get-tuple-element.191), channel_id=1, source_target_pairs={{0,2},{1,3},{2,0},{3,1},{4,6},{5,7},{6,4},{7,5},{8,10},{9,11},{10,... | collective-permute-start | bytes 3145736 | tf_op jit(solution)/shard_map/ppermute | solution.py:19
  589.9 40.9 %collective-permute-start.50 = (bf16[256,2048]{1,0:T(8,128)(2,1)}, bf16[256,2048]{1,0:T(8,128)(2,1)S(1)}, u32[]{:S(2)}, u32[]{:S(2)}) collective-permute-start(bf16[256,2048]{1,0:T(8,128)(2,1)} %get-tuple-element.225.refs_2_), channel_id=1, source_target_pairs={{0,8},{8,16},{16,24},{24,28},{28,20},{20,12},{12,4},{4,0},{1,9},{9... | collective-permute-start | bytes 3145736 | tf_op jit(solution)/shard_map/ppermute | solution.py:62
  591.9 38.9 %collective-permute-start.51 = (bf16[256,2048]{1,0:T(8,128)(2,1)}, bf16[256,2048]{1,0:T(8,128)(2,1)S(1)}, u32[]{:S(2)}, u32[]{:S(2)}) collective-permute-start(bf16[256,2048]{1,0:T(8,128)(2,1)} %get-tuple-element.228), channel_id=1, source_target_pairs={{0,4},{8,0},{16,8},{24,16},{28,24},{20,28},{12,20},{4,12},{1,5},{9... | collective-permute-start | bytes 3145736 | tf_op jit(solution)/shard_map/ppermute | solution.py:62
  635.1 10.7 %collective-permute-start.52 = (bf16[64,2048]{1,0:T(8,128)(2,1)}, bf16[64,2048]{1,0:T(8,128)(2,1)S(1)}, u32[]{:S(2)}, u32[]{:S(2)}) collective-permute-start(bf16[64,2048]{1,0:T(8,128)(2,1)} %get-tuple-element.230), channel_id=1, source_target_pairs={{0,1},{1,0},{2,3},{3,2},{4,5},{5,4},{6,7},{7,6},{8,9},{9,8},{10,11... | collective-permute-start | bytes 786440 | tf_op jit(solution)/shard_map/ppermute | solution.py:19
  635.1 10.7 %collective-permute-start.53 = (bf16[64,2048]{1,0:T(8,128)(2,1)}, bf16[64,2048]{1,0:T(8,128)(2,1)S(1)}, u32[]{:S(2)}, u32[]{:S(2)}) collective-permute-start(bf16[64,2048]{1,0:T(8,128)(2,1)} %get-tuple-element.231), channel_id=1, source_target_pairs={{0,2},{1,3},{2,0},{3,1},{4,6},{5,7},{6,4},{7,5},{8,10},{9,11},{10,... | collective-permute-start | bytes 786440 | tf_op jit(solution)/shard_map/ppermute | solution.py:19
  635.7 13.6 %collective-permute-start.54 = (bf16[64,2048]{1,0:T(8,128)(2,1)}, bf16[64,2048]{1,0:T(8,128)(2,1)S(1)}, u32[]{:S(2)}, u32[]{:S(2)}) collective-permute-start(bf16[64,2048]{1,0:T(8,128)(2,1)} %get-tuple-element.232), channel_id=1, source_target_pairs={{0,3},{1,2},{2,1},{3,0},{4,7},{5,6},{6,5},{7,4},{8,11},{9,10},{10,... | collective-permute-start | bytes 786440 | tf_op jit(solution)/shard_map/ppermute | solution.py:19
  (62 other events, 282.6 us)
Sparse Core Ops, SparseCore 0:
  133.6 131.0 all-gather.3
  267.5 77.3 all-gather.5
  347.8 91.1 all-gather.7
  462.2 128.3 all-reduce.6

commit v5 on v4

--- a/solution.py
+++ b/solution.py
@@ -636,14 +636,25 @@
             ref[p, 0:width, :] = source[pl.ds(pl.multiple_of((2 * p + which) * width, width), width), :]
 
 
-def own_kernel(index, feed, cot, wg, wu, wd, hidden, grad_gate, grad_lifted, *refs):
-    (kept, sent, kept_result, sent_result), (total, result) = refs[:4], refs[4:]
-    units, model = wd.shape
-    for cut in chunks_of(units):
-        gated = jnp.dot(feed[...], wg[:, cut], preferred_element_type=F32)
-        lifted = jnp.dot(feed[...], wu[:, cut], preferred_element_type=F32)
-        grad_hidden = dims(cot[...], wd[cut, :], 1, 1)
-        hidden[:, cut], grad_gate[:, cut], grad_lifted[:, cut] = activations(gated, lifted, grad_hidden)
+def first_step(act):
+    pl.when(pl.program_id(0) == 0)(act)
+
+
+def own_kernel(index, feed, cot, wg, wu_source, wd_source, hidden, grad_gate, grad_lifted, *refs):
+    (kept, sent, kept_result, sent_result), (total, result, wu, wd, sems) = refs[:4], refs[4:]
+    up, down = (
+        pltpu.make_async_copy(source, held, sems.at[n])
+        for n, (source, held) in enumerate(((wu_source, wu), (wd_source, wd)))
+    )
+    first_step(up.start)
+    first_step(down.start)
+    model = wd.shape[1]
+    gated = jnp.dot(feed[...], wg[...], preferred_element_type=F32)
+    first_step(up.wait)
+    lifted = jnp.dot(feed[...], wu[...], preferred_element_type=F32)
+    first_step(down.wait)
+    grad_hidden = dims(cot[...], wd[...], 1, 1)
+    hidden[...], grad_gate[...], grad_lifted[...] = activations(gated, lifted, grad_hidden)
     for cut in chunks_of(model):
         grad_feed = dims(grad_gate[...], wg[cut, :], 1, 1) + dims(grad_lifted[...], wu[cut, :], 1, 1)
         total[:, cut] = grad_feed.astype(BF)
@@ -661,11 +672,10 @@
 def rows_kernel(groups, feed, grad_hidden, wg, wu, *refs):
     *outs, token = refs[-4:]
     before = grad_hidden[...].reshape(feed.shape[0], -1)
-    for cut in chunks_of(wg.shape[1]):
-        gated = jnp.dot(feed[...], wg[:, cut], preferred_element_type=F32)
-        lifted = jnp.dot(feed[...], wu[:, cut], preferred_element_type=F32)
-        for out, value in zip(outs, activations(gated, lifted, before[:, cut].astype(F32))):
-            out[:, :, :, cut] = value.reshape(out.shape[:-1] + (value.shape[-1],))
+    gated = jnp.dot(feed[...], wg[...], preferred_element_type=F32)
+    lifted = jnp.dot(feed[...], wu[...], preferred_element_type=F32)
+    for out, value in zip(outs, activations(gated, lifted, before.astype(F32))):
+        out[...] = value.reshape(out.shape)
     token[...] = jnp.zeros_like(token)
 
 
@@ -715,9 +725,11 @@
         grid_spec=pltpu.PrefetchScalarGridSpec(
             num_scalar_prefetch=1,
             grid=(count,),
-            in_specs=[here] * 2 + [resident(w) for w in weights],
+            in_specs=[here] * 2 + [resident(weights[0])] + [ANY] * 2,
             out_specs=[wide] * 3 + [half] * 4,
-            scratch_shapes=[pltpu.VMEM((block, model), BF)] * 2,
+            scratch_shapes=[pltpu.VMEM((block, model), BF)] * 2
+            + [pltpu.VMEM(w.shape, w.dtype) for w in weights[1:]]
+            + [pltpu.SemaphoreType.DMA((2,))],
         ),
         **params(12 * rows * model * units, 6 * model * units + rows * (3 * units + 4 * model) * 2),
     )(index, feed, cot, *weights)
@@ -1214,12 +1226,12 @@
         ],
     )
     w_parts = vmem_call("sum", sum_kernel, [shape((rows, 4 * cols), BF)] * lanes, [at_rank, *terms], 0, deps)
-    w_parts = [swap(x, "ta", j) if j else x for j, x in enumerate(w_parts)]
+    moved_parts = [swap(x, "ta", j) if j else x for j, x in enumerate(w_parts)]
     (grad_projection,) = vmem_call(
         "assemble",
         assemble_kernel,
         [shape((rows, 4, model))],
-        [at_rank, *w_parts],
+        [at_rank, *moved_parts],
         0,
     )
 
@@ -1230,6 +1242,7 @@
         [shape((width, model), BF), shape((width, model))],
         [kept, arrived, own_residual, grad_residual, tokens, attn_gain[None]],
         0,
+        w_parts[:1],
     )
 
     own = jnp.concatenate([grad_conv.reshape(-1), partial_wbeta[:own_heads].reshape(-1), grad_bias])
@@ -1239,7 +1252,7 @@
     flat = jnp.zeros((lanes, apart), F32)
     flat = lax.dynamic_update_slice(flat, jnp.pad(own, (0, apart - length))[None], (rank, 0))
     flat = jnp.concatenate([flat.reshape(-1, 128), jnp.pad(gains, (0, -gains.shape[0] % 1024)).reshape(-1, 128)])
-    flat = gate(lax.psum(flat, BOTH), made[-1]).reshape(-1)
+    flat = gate(lax.psum(flat, BOTH), w_parts[0]).reshape(-1)
     gains = flat[lanes * apart :]
     flat = flat[: lanes * apart].reshape(lanes, apart)
     convs = 3 * ksize * cols

time: 666 us -> 664 us (level)
  no operation moved by 1% of the time
where the time goes in v5:
time: 664 us; the launch traced here: 657 us
  Pallas kernels  378 us (57%)
  waiting for transfers between devices  148 us (22%)
  starting transfers between devices  53.2 us (8%)
  local copies, waits for them, and re-layouts  50.4 us (8%)
  between operations  15.2 us (2%)
  other arithmetic  11.7 us (2%)
    pallas_call x3, Pallas kernels, weight_grad(): pl.pallas_call(functools.partial(grad_kernel, transposed, len(lefts)), na...  102 us
    pallas_call x4, Pallas kernels, by_group(): pl.pallas_call(kernel, name=name, out_shape=[shape(like[:-1] + (width,),...  101 us
    pallas_call x18, Pallas kernels, vmem_call(): pl.pallas_call(run, name=name, out_shape=out_shape, in_specs=[smem if x.d...  98.3 us
    ppermute x24, waiting for transfers between devices, move(): lax.ppermute(x, 'dev', [(self.order[p], self.order[(p + step) % n]) for p...  84.7 us
    ppermute x26, waiting for transfers between devices, swap(): lax.ppermute(x, axis, [(i, i ^ bit) for i in range(lax.axis_size(axis))])  57.1 us
    ppermute x24, starting transfers between devices, move(): lax.ppermute(x, 'dev', [(self.order[p], self.order[(p + step) % n]) for p...  30.2 us
    pallas_call x1, Pallas kernels, feed_own(): pl.pallas_call(own_kernel, name='feed_own', out_shape=[shape((tokens, uni...  28.2 us
    unnamed x133, local copies, waits for them, and re-layouts  26.3 us
  transfers between devices with their start and end apart: 59, of which 24 were waited for; matrix products, arithmetic and copies ran while one was open for 5% of the time, Pallas kernels for 57%

profile of v5, /device:TPU:0, one launch (start us, length us, event | category | flops | bytes accessed | tf_op | source)
XLA Modules:
  0.0 656.5 jit_solution(4032752426677636558)
XLA Ops:
  7.3 1.7 reshape.331
  11.8 2.5 collective-permute-start.1
  16.4 2.0 broadcast_select_fusion
  20.0 1.8 collective-permute-start.5
  22.9 6.8 %collective-permute-done.2.refs_4_ = bf16[80,2048]{1,0:T(8,128)(2,1)} collective-permute-done((bf16[80,2048]{1,0:T(8,128)(2,1)S(1)}, bf16[80,2048]{1,0:T(8,128)(2,1)}, u32[]{:S(2)}, u32[]{:S(2)}) %collective-permute-start.2) | collective-permute-done | bytes 327712 | tf_op jit(solution)/shard_map/ppermute | solution.py:19
  29.6 2.3 weights.1.refs_0_.refs_8_.refs_1_
  32.0 2.3 collective-permute-start.3
  35.8 6.9 %collective-permute-done.5.refs_3_ = bf16[144,2048]{1,0:T(8,128)(2,1)} collective-permute-done((bf16[144,2048]{1,0:T(8,128)(2,1)S(1)}, bf16[144,2048]{1,0:T(8,128)(2,1)}, u32[]{:S(2)}, u32[]{:S(2)}) %collective-permute-start.5) | collective-permute-done | bytes 589856 | tf_op jit(solution)/shard_map/ppermute | solution.py:19
  43.4 10.3 %collective-permute-done.11.refs_3_ = bf16[128,2048]{1,0:T(8,128)(2,1)} collective-permute-done((bf16[128,2048]{1,0:T(8,128)(2,1)S(1)}, bf16[128,2048]{1,0:T(8,128)(2,1)}, u32[]{:S(2)}, u32[]{:S(2)}) %collective-permute-start.11) | collective-permute-done | bytes 524320 | tf_op jit(solution)/shard_map/ppermute | solution.py:19
  54.2 5.5 collective-permute-done.3.refs_0_
  60.8 1.8 collective-permute-start.8
  64.8 3.0 in_order.1.refs_2_.cot
  67.8 5.5 norm.1
  75.6 11.9 %collective-permute-done.8.refs_0_ = bf16[272,2048]{1,0:T(8,128)(2,1)S(1)} collective-permute-done((bf16[272,2048]{1,0:T(8,128)(2,1)}, bf16[272,2048]{1,0:T(8,128)(2,1)S(1)}, u32[]{:S(2)}, u32[]{:S(2)}) %collective-permute-start.8) | collective-permute-done | bytes 1114144 | tf_op jit(solution)/shard_map/ppermute | solution.py:62
  88.5 1.6 collective-permute-start.14
  93.6 20.7 %collective-permute-done.14.refs_0_ = bf16[272,2048]{1,0:T(8,128)(2,1)S(1)} collective-permute-done((bf16[272,2048]{1,0:T(8,128)(2,1)}, bf16[272,2048]{1,0:T(8,128)(2,1)S(1)}, u32[]{:S(2)}, u32[]{:S(2)}) %collective-permute-start.14) | collective-permute-done | bytes 1114144 | tf_op jit(solution)/shard_map/ppermute | solution.py:62
  121.5 7.8 %collective-permute-done.16 = bf16[136,2048]{1,0:T(8,128)(2,1)S(1)} collective-permute-done((bf16[136,2048]{1,0:T(8,128)(2,1)S(1)}, bf16[136,2048]{1,0:T(8,128)(2,1)S(1)}, u32[]{:S(2)}, u32[]{:S(2)}) %collective-permute-start.16) | collective-permute-done | bytes 557088 | tf_op jit(solution)/shard_map/ppermute | solution.py:62
  129.4 3.0 collective-permute-done.17
  134.4 11.4 %project.1 = (f32[520,1536]{1,0:T(8,128)}, bf16[2048,512]{1,0:T(8,128)(2,1)}, f32[520,8]{1,0:T(8,128)}, bf16[8,2048]{1,0:T(8,128)(2,1)}) custom-call(s32[8]{0:T(128)} %compare_select_fusion.slots, bf16[520,2048]{1,0:T(8,128)(2,1)} %get-tuple-element.136.refs_1_.x, f32[520,1]{1,0:T(8,128)} %broadcast_in_dim.58.refs_3_.live, ...), custom_call_target="tpu_custom_call" | custom-call | flops 3271557120 | bytes 10518528 | tf_op jit(solution)/shard_map/project/pallas_call | solution.py:868
  149.2 19.9 %mixer_forward.1 = (f32[512,512]{1,0:T(8,128)S(1)}, f32[512,512]{1,0:T(8,128)S(1)}, f32[512,512]{1,0:T(8,128)S(1)}, f32[4,4,128,128]{3,2,1,0:T(8,128)S(1)}, f32[...) custom-call(f32[520,1536]{1,0:T(8,128)} %get-tuple-element.138.xq.xk, ...), custom_call_target="tpu_custom_call" | custom-call | flops 4026531840 | bytes 20488192 | tf_op jit(solution)/shard_map/mixer_forward/pallas_call | solution.py:514
  173.2 11.2 %collective-permute-done.18.refs_2_ = bf16[4,2,128,128]{3,2,1,0:T(8,128)(2,1)S(1)} collective-permute-done((bf16[4,2,128,128]{3,2,1,0:T(8,128)(2,1)S(1)}, bf16[4,2,128,128]{3,2,1,0:T(8,128)(2,1)S(1)}, u32[]{:S(2)}, u32[]{:S(2)}) %collective-permute-start.18) | collective-permute-done | bytes 262176 | tf_op jit(solution)/shard_map/ppermute | solution.py:62
  184.9 2.8 collective-permute-done.19.refs_3_
  189.0 5.3 collective-permute-done.20.refs_4_
  194.3 4.5 collective-permute-start.22
  201.0 5.8 collective-permute-done.22.refs_6_
  209.6 2.0 collective-permute-start.25
  212.3 4.6 collective-permute-done.24
  216.9 4.9 collective-permute-done.25
  221.7 1.7 pad_maximum_fusion.2.refs_8_
  223.5 5.5 mixer_read.1
  229.0 1.7 collective-permute-start.30
  230.9 18.6 %collective-permute-done.30.refs_3_ = bf16[512,512]{1,0:T(8,128)(2,1)S(1)} collective-permute-done((bf16[512,512]{1,0:T(8,128)(2,1)}, bf16[512,512]{1,0:T(8,128)(2,1)S(1)}, u32[]{:S(2)}, u32[]{:S(2)}) %collective-permute-start.30) | collective-permute-done | bytes 524320 | tf_op jit(solution)/shard_map/ppermute | solution.py:19
  250.2 1.6 collective-permute-done.31.refs_4_
  253.3 11.9 %out.1 = (bf16[512,2048]{1,0:T(8,128)(2,1)}, bf16[64,2048]{1,0:T(8,128)(2,1)}, bf16[64,2048]{1,0:T(8,128)(2,1)}, f32[128,2048]{1,0:T(8,128)}) custom-call(s32[9]{0:T(128)} %pad_add_fusion.2.refs_0_, bf16[512,512]{1,0:T(8,128)(2,1)} %get-tuple-element.153.refs_1_, bf16[512,512]{1,0:T(8,128)(2,1)} %copy-done.56, bf16[512,512]{1,0:T(8,128)(2,1)} %copy-done.55, ...), custom_call_target="tpu_custom_call" | custom-call | flops 4294967296 | bytes 16261156 | tf_op jit(solution)/shard_map/out/pallas_call | solution.py:454
  266.6 28.2 %feed_own.1 = (bf16[4096,1408]{1,0:T(8,128)(2,1)}, bf16[4096,1408]{1,0:T(8,128)(2,1)}, bf16[4096,1408]{1,0:T(8,128)(2,1)}, bf16[2,128,2048]{2,1,0:T(8,128)(2,1)}...) custom-call(s32[2]{0:T(128)} %pad_add_fusion.3.index, ...), custom_call_target="tpu_custom_call" | custom-call | flops 17716740096 | bytes 30015488 | tf_op jit(solution)/shard_map/feed_own/pallas_call | solution.py:720
  295.6 2.2 collective-permute-done.32.refs_2_
  297.8 2.9 stage.2
  300.7 19.3 %feed_hidden.2 = (bf16[4096,1408]{1,0:T(8,128)(2,1)}, f32[8,128]{1,0:T(8,128)}) custom-call(s32[4]{0:T(128)} %bitcast.144, bf16[4096,2048]{1,0:T(8,128)(2,1)} %all-gather.4.cloned.1.call-done.cot.refs_0_, bf16[1408,2048]{1,0:T(8,128)(2,1)} %wd.3, bf16[1,128,2048]{2,1,0:T(8,128)(2,1)} %get-tuple-element.159.refs_0_), custom_call_target="tpu_custom_call" | custom-call | flops 11811160064 | bytes 19922944 | tf_op jit(solution)/shard_map/feed_hidden/pallas_call | solution.py:692
  320.1 8.9 %residual.1 = (f32[128,2048]{1,0:T(8,128)}, f32[1,2048]{1,0:T(1,128)}, bf16[128,1024]{1,0:T(8,128)(2,1)}, bf16[128,1024]{1,0:T(8,128)(2,1)}, bf16[128,1024]{1,0:T(8,128)(2,1)}, /*index=5*/bf16[128,1024]{1,0:T(8,128)(2,1)}) custom-call(s32[9]{0:T(128)} %pad_add_fusion.2.refs_0_, bf16[2048,512]{1,0:T(8,128)(2,1)} %get-tuple-element.152.refs_5_.refs_1_, ...), custom_call_target="tpu_custom_call" | custom-call | flops 1073741824 | bytes 13647908 | tf_op jit(solution)/shard_map/residual/pallas_call | solution.py:454
  329.2 1.9 collective-permute-start.35
  331.1 15.7 %feed_hidden.3 = (bf16[4096,1408]{1,0:T(8,128)(2,1)}, f32[8,128]{1,0:T(8,128)}) custom-call(s32[3]{0:T(128)} %slice.137.groups, bf16[4096,2048]{1,0:T(8,128)(2,1)} %all-gather.4.cloned.1.call-done.cot.refs_0_, bf16[1408,2048]{1,0:T(8,128)(2,1)} %wd.3, bf16[128,1024]{1,0:T(8,128)(2,1)} %get-tuple-element.162.refs_0_.refs_1_, ...), custom_call_target="tpu_custom_call", output_to_operand_aliasing={{0}: (4, {})} | custom-call | flops 8858370048 | bytes 16384000 | tf_op jit(solution)/shard_map/feed_hidden/pallas_call | solution.py:692
  347.7 6.0 mixer_leak.1
  355.7 5.5 collective-permute-done.37.refs_1_
  361.3 1.7 pad_maximum_fusion.3.refs_0_
  366.9 33.2 %feed_rows.2 = (bf16[32,2,64,1408]{3,2,1,0:T(8,128)(2,1)}, bf16[32,2,64,1408]{3,2,1,0:T(8,128)(2,1)}, bf16[32,2,64,1408]{3,2,1,0:T(8,128)(2,1)}, f32[8,128]{1,0:T(8,128)}) custom-call(s32[7]{0:T(128)} %copy-done.62, bf16[2048,2048]{1,0:T(8,128)(2,1)} %all-gather.6.cloned.1.call-done.feed.refs_0_, ...), custom_call_target="tpu_custom_call", output_to_operand_aliasing={{0}: (6, {}), {1}: (7, {}), {2}: (8, {})} | custom-call | flops 20669530112 | bytes 39059456 | tf_op jit(solution)/shard_map/feed_rows/pallas_call | solution.py:692
  400.1 2.1 collective-permute-done.39.refs_3_
  402.2 5.5 mixer_chain.1.grads
  407.8 16.5 %mixer_backward.1 = (bf16[512,512]{1,0:T(8,128)(2,1)S(1)}, bf16[512,512]{1,0:T(8,128)(2,1)S(1)}, bf16[512,512]{1,0:T(8,128)(2,1)S(1)}, f32[3,8,512]{2,1,0:T(8,12...) custom-call(f32[520,1536]{1,0:T(8,128)} %get-tuple-element.138.xq.xk.xv, ...), custom_call_target="tpu_custom_call" | custom-call | flops 2013265920 | bytes 20881408 | tf_op jit(solution)/shard_map/mixer_backward/pallas_call | solution.py:582
  429.5 3.5 collective-permute-done.41.refs_13_
  433.6 12.2 %normed_back.1 = (bf16[512,1536]{1,0:T(8,128)(2,1)}, bf16[2,256,2048]{2,1,0:T(8,128)(2,1)}, bf16[2,256,2048]{2,1,0:T(8,128)(2,1)}, f32[1,2048]{1,0:T(1,128)}) custom-call(s32[9]{0:T(128)} %get-tuple-element.261.refs_0_, bf16[272,2048]{1,0:T(8,128)(2,1)} %weights.1.refs_0_.refs_8_.refs_1_, bf16[272,2048]{1,0:T(8,128)(2,1)} %gate.11.refs_1_.refs_9_.refs_2_, ...), custom_call_target="tpu_custom_call" | custom-call | flops 3221225472 | bytes 20570180 | tf_op jit(solution)/shard_map/normed_back/pallas_call | solution.py:454
  445.8 8.9 %weight_rows.1 = (bf16[256,2048]{1,0:T(8,128)(2,1)}, bf16[256,2048]{1,0:T(8,128)(2,1)}, bf16[256,2048]{1,0:T(8,128)(2,1)}, bf16[256,2048]{1,0:T(8,128)(2,1)}, bf...) custom-call(s32[9]{0:T(128)} %get-tuple-element.259.refs_0_, ...), custom_call_target="tpu_custom_call" | custom-call | flops 4294967296 | bytes 14753828 | tf_op jit(solution)/shard_map/weight_rows/pallas_call | solution.py:454
  456.0 1.7 collective-permute-start.45
  461.0 33.1 %feed_rows.3 = (bf16[32,2,64,1408]{3,2,1,0:T(8,128)(2,1)}, bf16[32,2,64,1408]{3,2,1,0:T(8,128)(2,1)}, bf16[32,2,64,1408]{3,2,1,0:T(8,128)(2,1)}, f32[8,128]{1,0:T(8,128)}) custom-call(s32[7]{0:T(128)} %copy-done.62, bf16[2048,2048]{1,0:T(8,128)(2,1)} %all-gather.8.cloned.1.call-done.feed.refs_1_, ...), custom_call_target="tpu_custom_call", output_to_operand_aliasing={{0}: (6, {}), {1}: (7, {}), {2}: (8, {})} | custom-call | flops 20669530112 | bytes 39059456 | tf_op jit(solution)/shard_map/feed_rows/pallas_call | solution.py:692
  495.1 3.3 ring_add.3
  500.4 33.9 %weight_grad.3 = (f32[2048,1408]{1,0:T(8,128)}, f32[8,128]{1,0:T(8,128)}) custom-call(bf16[2048,2048]{1,0:T(8,128)(2,1)} %all-gather.6.cloned.1.call-done.feed.refs_0_, bf16[2048,2048]{1,0:T(8,128)(2,1)} %all-gather.8.cloned.1.call-done.feed.refs_1_, bf16[32,2,64,1408]{3,2,1,0:T(8,128)(2,1)} %get-tuple-element.212.refs_2_, ...), custom_call_target="tpu_custom_call" | custom-call | flops 23622320128 | bytes 39845888 | tf_op jit(solution)/shard_map/weight_grad/pallas_call | solution.py:763
  535.6 3.8 ring_add.4
  541.4 33.8 %weight_grad.4 = (f32[2048,1408]{1,0:T(8,128)}, f32[8,128]{1,0:T(8,128)}) custom-call(bf16[2048,2048]{1,0:T(8,128)(2,1)} %all-gather.6.cloned.1.call-done.feed.refs_0_, bf16[2048,2048]{1,0:T(8,128)(2,1)} %all-gather.8.cloned.1.call-done.feed.refs_1_, bf16[32,2,64,1408]{3,2,1,0:T(8,128)(2,1)} %get-tuple-element.216.refs_2_, ...), custom_call_target="tpu_custom_call" | custom-call | flops 23622320128 | bytes 39845888 | tf_op jit(solution)/shard_map/weight_grad/pallas_call | solution.py:763
  576.6 4.3 stage.3
  583.4 3.8 ring_add.5
  589.5 34.6 %weight_grad.5 = (f32[1408,2048]{1,0:T(8,128)}, f32[8,128]{1,0:T(8,128)}) custom-call(bf16[4096,2048]{1,0:T(8,128)(2,1)} %all-gather.4.cloned.1.call-done.cot.refs_0_, bf16[32,2,64,1408]{3,2,1,0:T(8,128)(2,1)} %get-tuple-element.220.refs_1_, bf16[256,2048]{1,0:T(8,128)(2,1)} %get-tuple-element.218.refs_2_), custom_call_target="tpu_custom_call" | custom-call | flops 23622320128 | bytes 39845888 | tf_op jit(solution)/shard_map/weight_grad/pallas_call | solution.py:763
  626.4 3.0 sum.1
  635.6 4.5 finish.1
  641.4 4.2 collective-permute-done.54.refs_4_
  646.4 3.1 assemble.1
  (321 shorter events, 89.3 us)
Async XLA Ops:
  7.2 55.4 %copy-start = (f32[3,4,2048]{2,1,0:T(4,128)S(1)}, f32[3,4,2048]{2,1,0:T(4,128)}, u32[]{:S(2)}) copy-start(f32[3,4,2048]{2,1,0:T(4,128)} %param.27) | copy-start | bytes 294916
  7.2 293.5 %all-gather.4.cloned.1.call-start = ((), (), s32[]{:S(2)}) async-start(), calls=%async_computation | async-start | bytes 17301504 | tf_op jit(solution)/shard_map/all_gather | solution.py:1096
  11.3 23.8 %copy-start.59 = (s32[6]{0:T(128)S(1)}, s32[6]{0:T(128)}, u32[]{:S(2)}) copy-start(s32[6]{0:T(128)} %param.21) | copy-start | bytes 76
  11.3 10.4 %collective-permute-start = (bf16[80,2048]{1,0:T(8,128)(2,1)S(1)}, bf16[80,2048]{1,0:T(8,128)(2,1)S(1)}, u32[]{:S(2)}, u32[]{:S(2)}) collective-permute-start(bf16[80,2048]{1,0:T(8,128)(2,1)S(1)} %get-tuple-element.244), channel_id=1, source_target_pairs={{0,1},{1,0},{2,3},{3,2},{4,5},{5,4},{6,7},{7,6},{8,9},{9,8},{10,11... | collective-permute-start | bytes 983048 | tf_op jit(solution)/shard_map/ppermute | solution.py:19
  11.8 11.1 %collective-permute-start.1 = (bf16[80,2048]{1,0:T(8,128)(2,1)S(1)}, bf16[80,2048]{1,0:T(8,128)(2,1)S(1)}, u32[]{:S(2)}, u32[]{:S(2)}) collective-permute-start(bf16[80,2048]{1,0:T(8,128)(2,1)S(1)} %get-tuple-element.243), channel_id=1, source_target_pairs={{0,2},{1,3},{2,0},{3,1},{4,6},{5,7},{6,4},{7,5},{8,10},{9,11},{10,... | collective-permute-start | bytes 983048 | tf_op jit(solution)/shard_map/ppermute | solution.py:19
  14.3 15.3 %collective-permute-start.2 = (bf16[80,2048]{1,0:T(8,128)(2,1)S(1)}, bf16[80,2048]{1,0:T(8,128)(2,1)}, u32[]{:S(2)}, u32[]{:S(2)}) collective-permute-start(bf16[80,2048]{1,0:T(8,128)(2,1)S(1)} %get-tuple-element.242), channel_id=1, source_target_pairs={{0,3},{1,2},{2,1},{3,0},{4,7},{5,6},{6,5},{7,4},{8,11},{9,10},{10,... | collective-permute-start | bytes 983048 | tf_op jit(solution)/shard_map/ppermute | solution.py:19
  14.5 1.9 collective-permute-start.4
  20.0 22.6 %collective-permute-start.5 = (bf16[144,2048]{1,0:T(8,128)(2,1)S(1)}, bf16[144,2048]{1,0:T(8,128)(2,1)}, u32[]{:S(2)}, u32[]{:S(2)}) collective-permute-start(bf16[144,2048]{1,0:T(8,128)(2,1)S(1)} %pad_maximum_fusion.refs_1_), channel_id=1, source_target_pairs={{0,2},{1,3},{2,0},{3,1},{4,6},{5,7},{6,4},{7,5},{8,10},{9,11},{10,... | collective-permute-start | bytes 1769480 | tf_op jit(solution)/shard_map/ppermute | solution.py:19
  32.0 27.7 %collective-permute-start.3 = (bf16[272,2048]{1,0:T(8,128)(2,1)}, bf16[272,2048]{1,0:T(8,128)(2,1)S(1)}, u32[]{:S(2)}, u32[]{:S(2)}) collective-permute-start(bf16[272,2048]{1,0:T(8,128)(2,1)} %weights.1.refs_0_.refs_8_.refs_1_), channel_id=1, source_target_pairs={{0,8},{8,16},{16,24},{24,28},{28,20},{20,12},{12,4},{4,0},{1,9},{9... | collective-permute-start | bytes 3342344 | tf_op jit(solution)/shard_map/ppermute | solution.py:62
  34.3 19.4 %collective-permute-start.11 = (bf16[128,2048]{1,0:T(8,128)(2,1)S(1)}, bf16[128,2048]{1,0:T(8,128)(2,1)}, u32[]{:S(2)}, u32[]{:S(2)}) collective-permute-start(bf16[128,2048]{1,0:T(8,128)(2,1)S(1)} %copy-done.19), channel_id=1, source_target_pairs={{0,2},{1,3},{2,0},{3,1},{4,6},{5,7},{6,4},{7,5},{8,10},{9,11},{10,... | collective-permute-start | bytes 1572872 | tf_op jit(solution)/shard_map/ppermute | solution.py:19
  35.3 28.1 %collective-permute-start.7 = (bf16[272,2048]{1,0:T(8,128)(2,1)}, bf16[272,2048]{1,0:T(8,128)(2,1)S(1)}, u32[]{:S(2)}, u32[]{:S(2)}) collective-permute-start(bf16[272,2048]{1,0:T(8,128)(2,1)} %weights.1.refs_0_.refs_8_.refs_1_), channel_id=1, source_target_pairs={{0,4},{8,0},{16,8},{24,16},{28,24},{20,28},{12,20},{4,12},{1,5},{9... | collective-permute-start | bytes 3342344 | tf_op jit(solution)/shard_map/ppermute | solution.py:62
  42.6 11.1 %collective-permute-start.6 = (bf16[144,2048]{1,0:T(8,128)(2,1)}, bf16[144,2048]{1,0:T(8,128)(2,1)S(1)}, u32[]{:S(2)}, u32[]{:S(2)}) collective-permute-start(bf16[144,2048]{1,0:T(8,128)(2,1)} %collective-permute-done.5.refs_3_), channel_id=1, source_target_pairs={{0,1},{1,0},{2,3},{3,2},{4,5},{5,4},{6,7},{7,6},{8,9},{9,8},{10,11... | collective-permute-start | bytes 1769480 | tf_op jit(solution)/shard_map/ppermute | solution.py:19
  42.8 25.0 %collective-permute-start.9 = (bf16[144,2048]{1,0:T(8,128)(2,1)}, bf16[144,2048]{1,0:T(8,128)(2,1)}, u32[]{:S(2)}, u32[]{:S(2)}) collective-permute-start(bf16[144,2048]{1,0:T(8,128)(2,1)} %copy-done.22), channel_id=1, source_target_pairs={{0,1},{1,0},{2,3},{3,2},{4,5},{5,4},{6,7},{7,6},{8,9},{9,8},{10,11... | collective-permute-start | bytes 1769480 | tf_op jit(solution)/shard_map/ppermute | solution.py:19
  53.7 11.1 %collective-permute-start.10 = (bf16[128,2048]{1,0:T(8,128)(2,1)S(1)}, bf16[128,2048]{1,0:T(8,128)(2,1)}, u32[]{:S(2)}, u32[]{:S(2)}) collective-permute-start(bf16[128,2048]{1,0:T(8,128)(2,1)S(1)} %copy-done.19), channel_id=1, source_target_pairs={{0,1},{1,0},{2,3},{3,2},{4,5},{5,4},{6,7},{7,6},{8,9},{9,8},{10,11... | collective-permute-start | bytes 1572872 | tf_op jit(solution)/shard_map/ppermute | solution.py:19
  53.7 11.1 %collective-permute-start.12 = (bf16[128,2048]{1,0:T(8,128)(2,1)}, bf16[128,2048]{1,0:T(8,128)(2,1)}, u32[]{:S(2)}, u32[]{:S(2)}) collective-permute-start(bf16[128,2048]{1,0:T(8,128)(2,1)} %collective-permute-done.11.refs_3_), channel_id=1, source_target_pairs={{0,1},{1,0},{2,3},{3,2},{4,5},{5,4},{6,7},{7,6},{8,9},{9,8},{10,11... | collective-permute-start | bytes 1572872 | tf_op jit(solution)/shard_map/ppermute | solution.py:19
  60.8 26.7 %collective-permute-start.8 = (bf16[272,2048]{1,0:T(8,128)(2,1)}, bf16[272,2048]{1,0:T(8,128)(2,1)S(1)}, u32[]{:S(2)}, u32[]{:S(2)}) collective-permute-start(bf16[272,2048]{1,0:T(8,128)(2,1)} %gate.11.refs_1_.refs_9_.refs_2_), channel_id=1, source_target_pairs={{0,8},{8,16},{16,24},{24,28},{28,20},{20,12},{12,4},{4,0},{1,9},{9... | collective-permute-start | bytes 3342344 | tf_op jit(solution)/shard_map/ppermute | solution.py:62
  64.4 26.2 %collective-permute-start.13 = (bf16[272,2048]{1,0:T(8,128)(2,1)}, bf16[272,2048]{1,0:T(8,128)(2,1)S(1)}, u32[]{:S(2)}, u32[]{:S(2)}) collective-permute-start(bf16[272,2048]{1,0:T(8,128)(2,1)} %gate.12.refs_2_.refs_10_.refs_3_), channel_id=1, source_target_pairs={{0,4},{8,0},{16,8},{24,16},{28,24},{20,28},{12,20},{4,12},{1,5},{9... | collective-permute-start | bytes 3342344 | tf_op jit(solution)/shard_map/ppermute | solution.py:62
  88.5 25.9 %collective-permute-start.14 = (bf16[272,2048]{1,0:T(8,128)(2,1)}, bf16[272,2048]{1,0:T(8,128)(2,1)S(1)}, u32[]{:S(2)}, u32[]{:S(2)}) collective-permute-start(bf16[272,2048]{1,0:T(8,128)(2,1)} %gate.13.refs_3_.refs_11_.refs_4_), channel_id=1, source_target_pairs={{0,8},{8,16},{16,24},{24,28},{28,20},{20,12},{12,4},{4,0},{1,9},{9... | collective-permute-start | bytes 3342344 | tf_op jit(solution)/shard_map/ppermute | solution.py:62
  91.7 26.3 %collective-permute-start.15 = (bf16[272,2048]{1,0:T(8,128)(2,1)}, bf16[272,2048]{1,0:T(8,128)(2,1)S(1)}, u32[]{:S(2)}, u32[]{:S(2)}) collective-permute-start(bf16[272,2048]{1,0:T(8,128)(2,1)} %gate.14.refs_4_.refs_12_.refs_5_), channel_id=1, source_target_pairs={{0,4},{8,0},{16,8},{24,16},{28,24},{20,28},{12,20},{4,12},{1,5},{9... | collective-permute-start | bytes 3342344 | tf_op jit(solution)/shard_map/ppermute | solution.py:62
  116.5 12.8 %collective-permute-start.16 = (bf16[136,2048]{1,0:T(8,128)(2,1)S(1)}, bf16[136,2048]{1,0:T(8,128)(2,1)S(1)}, u32[]{:S(2)}, u32[]{:S(2)}) collective-permute-start(bf16[136,2048]{1,0:T(8,128)(2,1)S(1)} %slice.152), channel_id=1, source_target_pairs={{0,8},{8,16},{16,24},{24,28},{28,20},{20,12},{12,4},{4,0},{1,9},{9... | collective-permute-start | bytes 1671176 | tf_op jit(solution)/shard_map/ppermute | solution.py:62
  120.1 12.3 %collective-permute-start.17 = (bf16[136,2048]{1,0:T(8,128)(2,1)S(1)}, bf16[136,2048]{1,0:T(8,128)(2,1)S(1)}, u32[]{:S(2)}, u32[]{:S(2)}) collective-permute-start(bf16[136,2048]{1,0:T(8,128)(2,1)S(1)} %slice.153), channel_id=1, source_target_pairs={{0,4},{8,0},{16,8},{24,16},{28,24},{20,28},{12,20},{4,12},{1,5},{9... | collective-permute-start | bytes 1671176 | tf_op jit(solution)/shard_map/ppermute | solution.py:62
  133.5 233.4 %all-gather.6.cloned.1.call-start = ((), (), s32[]{:S(2)}) async-start(), calls=%async_computation.1 | async-start | bytes 8650752 | tf_op jit(solution)/shard_map/all_gather | solution.py:1117
  146.9 82.1 %collective-permute-start.27 = (bf16[2048,512]{1,0:T(8,128)(2,1)}, bf16[2048,512]{1,0:T(8,128)(2,1)}, u32[]{:S(2)}, u32[]{:S(2)}) collective-permute-start(bf16[2048,512]{1,0:T(8,128)(2,1)} %get-tuple-element.152.refs_5_.refs_1_), channel_id=1, source_target_pairs={{0,2},{1,3},{2,0},{3,1},{4,6},{5,7},{6,4},{7,5},{8,10},{9,11},{10,... | collective-permute-start | bytes 6291464 | tf_op jit(solution)/shard_map/ppermute | solution.py:19
  149.2 62.4 %copy-start.53 = (s32[8]{0:T(128)S(1)}, s32[8]{0:T(128)}, u32[]{:S(2)}) copy-start(s32[8]{0:T(128)} %compare_select_fusion.slots) | copy-start | bytes 100
  171.1 52.3 %copy-start.9 = (bf16[4,2,128,128]{3,2,1,0:T(8,128)(2,1)}, bf16[4,2,128,128]{3,2,1,0:T(8,128)(2,1)S(1)}, u32[]{:S(2)}) copy-start(bf16[4,2,128,128]{3,2,1,0:T(8,128)(2,1)S(1)} %get-tuple-element.146.refs_1_) | copy-start | bytes 786436
  171.1 13.2 %collective-permute-start.18 = (bf16[4,2,128,128]{3,2,1,0:T(8,128)(2,1)S(1)}, bf16[4,2,128,128]{3,2,1,0:T(8,128)(2,1)S(1)}, u32[]{:S(2)}, u32[]{:S(2)}) collective-permute-start(bf16[4,2,128,128]{3,2,1,0:T(8,128)(2,1)S(1)} %get-tuple-element.146.refs_1_), channel_id=1, source_target_pairs={{0,8},{8,16},{16,24},{24,28},{28,20},{20,12},{12,4},{4,0},{1,9},{9... | collective-permute-start | bytes 786440 | tf_op jit(solution)/shard_map/ppermute | solution.py:62
  172.7 14.9 %collective-permute-start.19 = (bf16[4,2,128,128]{3,2,1,0:T(8,128)(2,1)S(1)}, bf16[4,2,128,128]{3,2,1,0:T(8,128)(2,1)S(1)}, u32[]{:S(2)}, u32[]{:S(2)}) collective-permute-start(bf16[4,2,128,128]{3,2,1,0:T(8,128)(2,1)S(1)} %get-tuple-element.146.refs_1_), channel_id=1, source_target_pairs={{0,4},{8,0},{16,8},{24,16},{28,24},{20,28},{12,20},{4,12},{1,5},{9... | collective-permute-start | bytes 786440 | tf_op jit(solution)/shard_map/ppermute | solution.py:62
  184.4 9.9 %collective-permute-start.20 = (bf16[4,2,128,128]{3,2,1,0:T(8,128)(2,1)S(1)}, bf16[4,2,128,128]{3,2,1,0:T(8,128)(2,1)S(1)}, u32[]{:S(2)}, u32[]{:S(2)}) collective-permute-start(bf16[4,2,128,128]{3,2,1,0:T(8,128)(2,1)S(1)} %collective-permute-done.18.refs_2_), channel_id=1, source_target_pairs={{0,8},{8,16},{16,24},{24,28},{28,20},{20,12},{12,4},{4,0},{1,9},{9... | collective-permute-start | bytes 786440 | tf_op jit(solution)/shard_map/ppermute | solution.py:62
  187.6 11.8 %collective-permute-start.21 = (bf16[4,2,128,128]{3,2,1,0:T(8,128)(2,1)S(1)}, bf16[4,2,128,128]{3,2,1,0:T(8,128)(2,1)S(1)}, u32[]{:S(2)}, u32[]{:S(2)}) collective-permute-start(bf16[4,2,128,128]{3,2,1,0:T(8,128)(2,1)S(1)} %collective-permute-done.19.refs_3_), channel_id=1, source_target_pairs={{0,4},{8,0},{16,8},{24,16},{28,24},{20,28},{12,20},{4,12},{1,5},{9... | collective-permute-start | bytes 786440 | tf_op jit(solution)/shard_map/ppermute | solution.py:62
  194.3 12.6 %collective-permute-start.22 = (bf16[4,2,128,128]{3,2,1,0:T(8,128)(2,1)S(1)}, bf16[4,2,128,128]{3,2,1,0:T(8,128)(2,1)S(1)}, u32[]{:S(2)}, u32[]{:S(2)}) collective-permute-start(bf16[4,2,128,128]{3,2,1,0:T(8,128)(2,1)S(1)} %collective-permute-done.20.refs_4_), channel_id=1, source_target_pairs={{0,8},{8,16},{16,24},{24,28},{28,20},{20,12},{12,4},{4,0},{1,9},{9... | collective-permute-start | bytes 786440 | tf_op jit(solution)/shard_map/ppermute | solution.py:62
  199.5 8.7 %collective-permute-start.23 = (bf16[4,2,128,128]{3,2,1,0:T(8,128)(2,1)S(1)}, bf16[4,2,128,128]{3,2,1,0:T(8,128)(2,1)S(1)}, u32[]{:S(2)}, u32[]{:S(2)}) collective-permute-start(bf16[4,2,128,128]{3,2,1,0:T(8,128)(2,1)S(1)} %collective-permute-done.21.refs_5_), channel_id=1, source_target_pairs={{0,4},{8,0},{16,8},{24,16},{28,24},{20,28},{12,20},{4,12},{1,5},{9... | collective-permute-start | bytes 786440 | tf_op jit(solution)/shard_map/ppermute | solution.py:62
  208.2 8.7 %collective-permute-start.24 = (bf16[2,2,128,128]{3,2,1,0:T(8,128)(2,1)}, bf16[2,2,128,128]{3,2,1,0:T(8,128)(2,1)}, u32[]{:S(2)}, u32[]{:S(2)}) collective-permute-start(bf16[2,2,128,128]{3,2,1,0:T(8,128)(2,1)} %slice.155), channel_id=1, source_target_pairs={{0,8},{8,16},{16,24},{24,28},{28,20},{20,12},{12,4},{4,0},{1,9},{9... | collective-permute-start | bytes 393224 | tf_op jit(solution)/shard_map/ppermute | solution.py:62
  209.6 12.2 %collective-permute-start.25 = (bf16[2,2,128,128]{3,2,1,0:T(8,128)(2,1)}, bf16[2,2,128,128]{3,2,1,0:T(8,128)(2,1)}, u32[]{:S(2)}, u32[]{:S(2)}) collective-permute-start(bf16[2,2,128,128]{3,2,1,0:T(8,128)(2,1)} %slice.156), channel_id=1, source_target_pairs={{0,4},{8,0},{16,8},{24,16},{28,24},{20,28},{12,20},{4,12},{1,5},{9... | collective-permute-start | bytes 393224 | tf_op jit(solution)/shard_map/ppermute | solution.py:62
  212.3 39.5 %collective-permute-start.26 = (bf16[2048,512]{1,0:T(8,128)(2,1)}, bf16[2048,512]{1,0:T(8,128)(2,1)}, u32[]{:S(2)}, u32[]{:S(2)}) collective-permute-start(bf16[2048,512]{1,0:T(8,128)(2,1)} %get-tuple-element.152.refs_5_.refs_1_), channel_id=1, source_target_pairs={{0,1},{1,0},{2,3},{3,2},{4,5},{5,4},{6,7},{7,6},{8,9},{9,8},{10,11... | collective-permute-start | bytes 6291464 | tf_op jit(solution)/shard_map/ppermute | solution.py:19
  229.0 22.9 %collective-permute-start.28 = (bf16[2048,512]{1,0:T(8,128)(2,1)}, bf16[2048,512]{1,0:T(8,128)(2,1)S(1)}, u32[]{:S(2)}, u32[]{:S(2)}) collective-permute-start(bf16[2048,512]{1,0:T(8,128)(2,1)} %gate.17.refs_7_.refs_3_), channel_id=1, source_target_pairs={{0,1},{1,0},{2,3},{3,2},{4,5},{5,4},{6,7},{7,6},{8,9},{9,8},{10,11... | collective-permute-start | bytes 6291464 | tf_op jit(solution)/shard_map/ppermute | solution.py:19
  229.0 20.5 %collective-permute-start.30 = (bf16[512,512]{1,0:T(8,128)(2,1)}, bf16[512,512]{1,0:T(8,128)(2,1)S(1)}, u32[]{:S(2)}, u32[]{:S(2)}) collective-permute-start(bf16[512,512]{1,0:T(8,128)(2,1)} %get-tuple-element.153.refs_1_), channel_id=1, source_target_pairs={{0,2},{1,3},{2,0},{3,1},{4,6},{5,7},{6,4},{7,5},{8,10},{9,11},{10,... | collective-permute-start | bytes 1572872 | tf_op jit(solution)/shard_map/ppermute | solution.py:19
  230.8 19.4 %collective-permute-start.29 = (bf16[512,512]{1,0:T(8,128)(2,1)}, bf16[512,512]{1,0:T(8,128)(2,1)S(1)}, u32[]{:S(2)}, u32[]{:S(2)}) collective-permute-start(bf16[512,512]{1,0:T(8,128)(2,1)} %get-tuple-element.153.refs_1_), channel_id=1, source_target_pairs={{0,1},{1,0},{2,3},{3,2},{4,5},{5,4},{6,7},{7,6},{8,9},{9,8},{10,11... | collective-permute-start | bytes 1572872 | tf_op jit(solution)/shard_map/ppermute | solution.py:19
  249.5 2.3 collective-permute-start.31
  265.2 195.7 %all-gather.8.cloned.1.call-start = ((), (), s32[]{:S(2)}) async-start(), calls=%async_computation.2 | async-start | bytes 8650752 | tf_op jit(solution)/shard_map/all_gather | solution.py:1117
  265.9 363.4 %all-reduce.7.cloned.1.call-start = ((), (), s32[]{:S(2)}) async-start(), calls=%async_computation.3 | async-start | bytes 532480 | tf_op jit(solution)/shard_map/psum | solution.py:1255
  294.7 3.1 collective-permute-start.32
  300.7 19.4 %collective-permute-start.33 = (bf16[1,128,2048]{2,1,0:T(8,128)(2,1)}, bf16[1,128,2048]{2,1,0:T(8,128)(2,1)}, u32[]{:S(2)}, u32[]{:S(2)}) collective-permute-start(bf16[1,128,2048]{2,1,0:T(8,128)(2,1)} %get-tuple-element.159.refs_0_), channel_id=1, source_target_pairs={{0,2},{1,3},{2,0},{3,1},{4,6},{5,7},{6,4},{7,5},{8,10},{9,11},{10,... | collective-permute-start | bytes 1572872 | tf_op jit(solution)/shard_map/ppermute | solution.py:19
  329.0 17.8 %collective-permute-start.34 = (bf16[128,1024]{1,0:T(8,128)(2,1)}, bf16[128,1024]{1,0:T(8,128)(2,1)S(1)}, u32[]{:S(2)}, u32[]{:S(2)}) collective-permute-start(bf16[128,1024]{1,0:T(8,128)(2,1)} %get-tuple-element.163), channel_id=1, source_target_pairs={{0,1},{1,0},{2,3},{3,2},{4,5},{5,4},{6,7},{7,6},{8,9},{9,8},{10,11... | collective-permute-start | bytes 786440 | tf_op jit(solution)/shard_map/ppermute | solution.py:19
  329.2 17.6 %collective-permute-start.35 = (bf16[128,1024]{1,0:T(8,128)(2,1)}, bf16[128,1024]{1,0:T(8,128)(2,1)S(1)}, u32[]{:S(2)}, u32[]{:S(2)}) collective-permute-start(bf16[128,1024]{1,0:T(8,128)(2,1)} %get-tuple-element.164), channel_id=1, source_target_pairs={{0,2},{1,3},{2,0},{3,1},{4,6},{5,7},{6,4},{7,5},{8,10},{9,11},{10,... | collective-permute-start | bytes 786440 | tf_op jit(solution)/shard_map/ppermute | solution.py:19
  331.0 15.8 %collective-permute-start.36 = (bf16[128,1024]{1,0:T(8,128)(2,1)}, bf16[128,1024]{1,0:T(8,128)(2,1)S(1)}, u32[]{:S(2)}, u32[]{:S(2)}) collective-permute-start(bf16[128,1024]{1,0:T(8,128)(2,1)} %get-tuple-element.165), channel_id=1, source_target_pairs={{0,3},{1,2},{2,1},{3,0},{4,7},{5,6},{6,5},{7,4},{8,11},{9,10},{10,... | collective-permute-start | bytes 786440 | tf_op jit(solution)/shard_map/ppermute | solution.py:19
  353.6 7.6 %collective-permute-start.37 = (bf16[4,128,128]{2,1,0:T(8,128)(2,1)}, bf16[4,128,128]{2,1,0:T(8,128)(2,1)S(1)}, u32[]{:S(2)}, u32[]{:S(2)}) collective-permute-start(bf16[4,128,128]{2,1,0:T(8,128)(2,1)} %get-tuple-element.169), channel_id=1, source_target_pairs={{0,4},{4,0},{8,12},{12,8},{16,20},{20,16},{24,28},{28,24},{1,5},{5... | collective-permute-start | bytes 393224 | tf_op jit(solution)/shard_map/ppermute | solution.py:19
  361.3 38.9 %copy-start.34 = (bf16[4,128,128]{2,1,0:T(8,128)(2,1)}, bf16[4,128,128]{2,1,0:T(8,128)(2,1)S(1)}, u32[]{:S(2)}) copy-start(bf16[4,128,128]{2,1,0:T(8,128)(2,1)S(1)} %collective-permute-done.37.refs_1_) | copy-start | bytes 393220
  363.0 37.2 %collective-permute-start.38 = (bf16[2,4,128,128]{3,2,1,0:T(8,128)(2,1)}, bf16[2,4,128,128]{3,2,1,0:T(8,128)(2,1)}, u32[]{:S(2)}, u32[]{:S(2)}) collective-permute-start(bf16[2,4,128,128]{3,2,1,0:T(8,128)(2,1)} %pad_maximum_fusion.3.refs_0_), channel_id=1, source_target_pairs={{8,0},{12,4},{16,8},{20,12},{24,16},{28,20},{9,1},{13,5},{17,9},{2... | collective-permute-start | bytes 786440 | tf_op jit(solution)/shard_map/ppermute | solution.py:1182
  364.3 37.9 %collective-permute-start.39 = (bf16[2,4,128,128]{3,2,1,0:T(8,128)(2,1)}, bf16[2,4,128,128]{3,2,1,0:T(8,128)(2,1)}, u32[]{:S(2)}, u32[]{:S(2)}) collective-permute-start(bf16[2,4,128,128]{3,2,1,0:T(8,128)(2,1)} %pad_maximum_fusion.3.refs_0_), channel_id=1, source_target_pairs={{16,0},{20,4},{24,8},{28,12},{17,1},{21,5},{25,9},{29,13},{18,2},{... | collective-permute-start | bytes 786440 | tf_op jit(solution)/shard_map/ppermute | solution.py:1182
  365.6 36.6 %collective-permute-start.40 = (bf16[2,4,128,128]{3,2,1,0:T(8,128)(2,1)}, bf16[2,4,128,128]{3,2,1,0:T(8,128)(2,1)}, u32[]{:S(2)}, u32[]{:S(2)}) collective-permute-start(bf16[2,4,128,128]{3,2,1,0:T(8,128)(2,1)} %pad_maximum_fusion.3.refs_0_), channel_id=1, source_target_pairs={{24,0},{28,4},{25,1},{29,5},{26,2},{30,6},{27,3},{31,7}} | collective-permute-start | bytes 786440 | tf_op jit(solution)/shard_map/ppermute | solution.py:1182
  427.3 5.7 collective-permute-start.41
  454.8 39.3 %collective-permute-start.44 = (bf16[128,2048]{1,0:T(8,128)(2,1)}, bf16[128,2048]{1,0:T(8,128)(2,1)S(1)}, u32[]{:S(2)}, u32[]{:S(2)}) collective-permute-start(bf16[128,2048]{1,0:T(8,128)(2,1)} %get-tuple-element.196.refs_0_), channel_id=1, source_target_pairs={{0,8},{8,16},{16,24},{24,28},{28,20},{20,12},{12,4},{4,0},{1,9},{9... | collective-permute-start | bytes 1572872 | tf_op jit(solution)/shard_map/ppermute | solution.py:62
  456.0 38.1 %collective-permute-start.45 = (bf16[128,2048]{1,0:T(8,128)(2,1)}, bf16[128,2048]{1,0:T(8,128)(2,1)S(1)}, u32[]{:S(2)}, u32[]{:S(2)}) collective-permute-start(bf16[128,2048]{1,0:T(8,128)(2,1)} %get-tuple-element.209), channel_id=1, source_target_pairs={{0,4},{8,0},{16,8},{24,16},{28,24},{20,28},{12,20},{4,12},{1,5},{9... | collective-permute-start | bytes 1572872 | tf_op jit(solution)/shard_map/ppermute | solution.py:62
  460.0 115.2 %collective-permute-start.42 = (bf16[2,256,2048]{2,1,0:T(8,128)(2,1)}, bf16[2,256,2048]{2,1,0:T(8,128)(2,1)S(1)}, u32[]{:S(2)}, u32[]{:S(2)}) collective-permute-start(bf16[2,256,2048]{2,1,0:T(8,128)(2,1)} %get-tuple-element.189), channel_id=1, source_target_pairs={{0,1},{1,0},{2,3},{3,2},{4,5},{5,4},{6,7},{7,6},{8,9},{9,8},{10,11... | collective-permute-start | bytes 6291464 | tf_op jit(solution)/shard_map/ppermute | solution.py:19
  498.4 35.9 %collective-permute-start.46 = (bf16[256,2048]{1,0:T(8,128)(2,1)}, bf16[256,2048]{1,0:T(8,128)(2,1)S(1)}, u32[]{:S(2)}, u32[]{:S(2)}) collective-permute-start(bf16[256,2048]{1,0:T(8,128)(2,1)} %get-tuple-element.210.refs_3_), channel_id=1, source_target_pairs={{0,8},{8,16},{16,24},{24,28},{28,20},{20,12},{12,4},{4,0},{1,9},{9... | collective-permute-start | bytes 3145736 | tf_op jit(solution)/shard_map/ppermute | solution.py:62
  499.0 35.3 %collective-permute-start.47 = (bf16[256,2048]{1,0:T(8,128)(2,1)}, bf16[256,2048]{1,0:T(8,128)(2,1)S(1)}, u32[]{:S(2)}, u32[]{:S(2)}) collective-permute-start(bf16[256,2048]{1,0:T(8,128)(2,1)} %get-tuple-element.211), channel_id=1, source_target_pairs={{0,4},{8,0},{16,8},{24,16},{28,24},{20,28},{12,20},{4,12},{1,5},{9... | collective-permute-start | bytes 3145736 | tf_op jit(solution)/shard_map/ppermute | solution.py:62
  539.4 42.7 %collective-permute-start.48 = (bf16[256,2048]{1,0:T(8,128)(2,1)}, bf16[256,2048]{1,0:T(8,128)(2,1)S(1)}, u32[]{:S(2)}, u32[]{:S(2)}) collective-permute-start(bf16[256,2048]{1,0:T(8,128)(2,1)} %get-tuple-element.214.refs_3_), channel_id=1, source_target_pairs={{0,8},{8,16},{16,24},{24,28},{28,20},{20,12},{12,4},{4,0},{1,9},{9... | collective-permute-start | bytes 3145736 | tf_op jit(solution)/shard_map/ppermute | solution.py:62
  540.5 41.6 %collective-permute-start.49 = (bf16[256,2048]{1,0:T(8,128)(2,1)}, bf16[256,2048]{1,0:T(8,128)(2,1)S(1)}, u32[]{:S(2)}, u32[]{:S(2)}) collective-permute-start(bf16[256,2048]{1,0:T(8,128)(2,1)} %get-tuple-element.215), channel_id=1, source_target_pairs={{0,4},{8,0},{16,8},{24,16},{28,24},{20,28},{12,20},{4,12},{1,5},{9... | collective-permute-start | bytes 3145736 | tf_op jit(solution)/shard_map/ppermute | solution.py:62
  580.8 43.2 %collective-permute-start.43 = (bf16[1,256,2048]{2,1,0:T(8,128)(2,1)}, bf16[1,256,2048]{2,1,0:T(8,128)(2,1)S(1)}, u32[]{:S(2)}, u32[]{:S(2)}) collective-permute-start(bf16[1,256,2048]{2,1,0:T(8,128)(2,1)} %get-tuple-element.191), channel_id=1, source_target_pairs={{0,2},{1,3},{2,0},{3,1},{4,6},{5,7},{6,4},{7,5},{8,10},{9,11},{10,... | collective-permute-start | bytes 3145736 | tf_op jit(solution)/shard_map/ppermute | solution.py:19
  587.2 37.9 %collective-permute-start.50 = (bf16[256,2048]{1,0:T(8,128)(2,1)}, bf16[256,2048]{1,0:T(8,128)(2,1)S(1)}, u32[]{:S(2)}, u32[]{:S(2)}) collective-permute-start(bf16[256,2048]{1,0:T(8,128)(2,1)} %get-tuple-element.218.refs_2_), channel_id=1, source_target_pairs={{0,8},{8,16},{16,24},{24,28},{28,20},{20,12},{12,4},{4,0},{1,9},{9... | collective-permute-start | bytes 3145736 | tf_op jit(solution)/shard_map/ppermute | solution.py:62
  588.8 36.3 %collective-permute-start.51 = (bf16[256,2048]{1,0:T(8,128)(2,1)}, bf16[256,2048]{1,0:T(8,128)(2,1)S(1)}, u32[]{:S(2)}, u32[]{:S(2)}) collective-permute-start(bf16[256,2048]{1,0:T(8,128)(2,1)} %get-tuple-element.219), channel_id=1, source_target_pairs={{0,4},{8,0},{16,8},{24,16},{28,24},{20,28},{12,20},{4,12},{1,5},{9... | collective-permute-start | bytes 3145736 | tf_op jit(solution)/shard_map/ppermute | solution.py:62
  631.5 9.9 %collective-permute-start.52 = (bf16[64,2048]{1,0:T(8,128)(2,1)}, bf16[64,2048]{1,0:T(8,128)(2,1)S(1)}, u32[]{:S(2)}, u32[]{:S(2)}) collective-permute-start(bf16[64,2048]{1,0:T(8,128)(2,1)} %get-tuple-element.230), channel_id=1, source_target_pairs={{0,1},{1,0},{2,3},{3,2},{4,5},{5,4},{6,7},{7,6},{8,9},{9,8},{10,11... | collective-permute-start | bytes 786440 | tf_op jit(solution)/shard_map/ppermute | solution.py:19
  631.5 9.9 %collective-permute-start.53 = (bf16[64,2048]{1,0:T(8,128)(2,1)}, bf16[64,2048]{1,0:T(8,128)(2,1)S(1)}, u32[]{:S(2)}, u32[]{:S(2)}) collective-permute-start(bf16[64,2048]{1,0:T(8,128)(2,1)} %get-tuple-element.231), channel_id=1, source_target_pairs={{0,2},{1,3},{2,0},{3,1},{4,6},{5,7},{6,4},{7,5},{8,10},{9,11},{10,... | collective-permute-start | bytes 786440 | tf_op jit(solution)/shard_map/ppermute | solution.py:19
  632.3 13.4 %collective-permute-start.54 = (bf16[64,2048]{1,0:T(8,128)(2,1)}, bf16[64,2048]{1,0:T(8,128)(2,1)S(1)}, u32[]{:S(2)}, u32[]{:S(2)}) collective-permute-start(bf16[64,2048]{1,0:T(8,128)(2,1)} %get-tuple-element.232), channel_id=1, source_target_pairs={{0,3},{1,2},{2,1},{3,0},{4,7},{5,6},{6,5},{7,4},{8,11},{9,10},{10,... | collective-permute-start | bytes 786440 | tf_op jit(solution)/shard_map/ppermute | solution.py:19
  (60 other events, 267.7 us)
Sparse Core Ops, SparseCore 0:
  133.6 130.9 all-gather.3
  267.5 76.5 all-gather.5
  347.0 90.7 all-gather.7
  461.1 127.1 all-reduce.6

commit v6 on v5

--- a/solution.py
+++ b/solution.py
@@ -445,7 +445,7 @@
         spill[i] = shifted_sum(0, PAD)
 
 
-def vmem_call(name, kernel, out_shape, inputs, flops, deps=(), scratch=()):
+def vmem_call(name, kernel, out_shape, inputs, flops, deps=(), scratch=(), grant=FFN_VMEM):
     smem, vmem = (pl.BlockSpec(memory_space=m) for m in (pltpu.SMEM, pltpu.VMEM))
 
     def run(*refs):
@@ -460,7 +460,7 @@
         out_specs=[vmem] * len(out_shape),
         scratch_shapes=list(scratch),
         cost_estimate=cost(flops, inputs, out_shape),
-        compiler_params=pltpu.CompilerParams(vmem_limit_bytes=FFN_VMEM),
+        compiler_params=pltpu.CompilerParams(vmem_limit_bytes=grant),
     )(*inputs, *deps)
 
 
@@ -540,6 +540,7 @@
             ],
             [index, *parts, self.trans, self.fresh, self.read, self.direct, head_gain],
             12 * self.flops,
+            grant=32 * 1024 * 1024,
         )
         return normed
 

time: 664 us -> 671 us (1.011)
  local copies, waits for them, and re-layouts: 50.4 us -> 66.6 us
  waiting for transfers between devices: 148 us -> 138 us
    unnamed x133 -> x167, local copies, waits for them, and re-layouts: 26.3 us -> 42.4 us
  transfers between devices with their start and end apart: 59 -> 59, of which waited for: 24 -> 24; matrix products, arithmetic and copies ran while one was open for 5% -> 5% of each run, Pallas kernels for 57% -> 56%
where the time goes in v6:
time: 671 us; the launch traced here: 660 us
  Pallas kernels  374 us (56%)
  waiting for transfers between devices  138 us (21%)
  local copies, waits for them, and re-layouts  66.6 us (10%)
  starting transfers between devices  54.8 us (8%)
  between operations  15.3 us (2%)
  other arithmetic  10.9 us (2%)
    pallas_call x3, Pallas kernels, weight_grad(): pl.pallas_call(functools.partial(grad_kernel, transposed, len(lefts)), na...  102 us
    pallas_call x4, Pallas kernels, by_group(): pl.pallas_call(kernel, name=name, out_shape=[shape(like[:-1] + (width,),...  101 us
    pallas_call x18, Pallas kernels, vmem_call(): pl.pallas_call(run, name=name, out_shape=out_shape, in_specs=[smem if x.d...  94.9 us
    ppermute x24, waiting for transfers between devices, move(): lax.ppermute(x, 'dev', [(self.order[p], self.order[(p + step) % n]) for p...  80.2 us
    ppermute x26, waiting for transfers between devices, swap(): lax.ppermute(x, axis, [(i, i ^ bit) for i in range(lax.axis_size(axis))])  51.9 us
    unnamed x167, local copies, waits for them, and re-layouts  42.4 us
    ppermute x24, starting transfers between devices, move(): lax.ppermute(x, 'dev', [(self.order[p], self.order[(p + step) % n]) for p...  32 us
    pallas_call x1, Pallas kernels, feed_own(): pl.pallas_call(own_kernel, name='feed_own', out_shape=[shape((tokens, uni...  28.1 us
  transfers between devices with their start and end apart: 59, of which 24 were waited for; matrix products, arithmetic and copies ran while one was open for 5% of the time, Pallas kernels for 56%

profile of v6, /device:TPU:0, one launch (start us, length us, event | category | flops | bytes accessed | tf_op | source)
XLA Modules:
  0.0 659.9 jit_solution(14822387415045966207)
XLA Ops:
  7.3 1.7 reshape.331
  11.8 2.5 collective-permute-start.1
  16.4 2.0 broadcast_select_fusion
  20.0 1.8 collective-permute-start.5
  22.9 6.8 %collective-permute-done.2.refs_4_ = bf16[80,2048]{1,0:T(8,128)(2,1)} collective-permute-done((bf16[80,2048]{1,0:T(8,128)(2,1)S(1)}, bf16[80,2048]{1,0:T(8,128)(2,1)}, u32[]{:S(2)}, u32[]{:S(2)}) %collective-permute-start.2) | collective-permute-done | bytes 327712 | tf_op jit(solution)/shard_map/ppermute | solution.py:19
  29.6 2.3 weights.1.refs_0_.refs_8_.refs_1_
  32.0 2.3 collective-permute-start.3
  35.8 6.9 %collective-permute-done.5.refs_3_ = bf16[144,2048]{1,0:T(8,128)(2,1)} collective-permute-done((bf16[144,2048]{1,0:T(8,128)(2,1)S(1)}, bf16[144,2048]{1,0:T(8,128)(2,1)}, u32[]{:S(2)}, u32[]{:S(2)}) %collective-permute-start.5) | collective-permute-done | bytes 589856 | tf_op jit(solution)/shard_map/ppermute | solution.py:19
  43.4 10.3 %collective-permute-done.11.refs_3_ = bf16[128,2048]{1,0:T(8,128)(2,1)} collective-permute-done((bf16[128,2048]{1,0:T(8,128)(2,1)S(1)}, bf16[128,2048]{1,0:T(8,128)(2,1)}, u32[]{:S(2)}, u32[]{:S(2)}) %collective-permute-start.11) | collective-permute-done | bytes 524320 | tf_op jit(solution)/shard_map/ppermute | solution.py:19
  54.2 5.5 collective-permute-done.3.refs_0_
  60.7 1.8 collective-permute-start.8
  64.7 3.0 in_order.1.refs_2_.cot
  67.7 5.5 norm.1
  75.5 11.9 %collective-permute-done.8.refs_0_ = bf16[272,2048]{1,0:T(8,128)(2,1)S(1)} collective-permute-done((bf16[272,2048]{1,0:T(8,128)(2,1)}, bf16[272,2048]{1,0:T(8,128)(2,1)S(1)}, u32[]{:S(2)}, u32[]{:S(2)}) %collective-permute-start.8) | collective-permute-done | bytes 1114144 | tf_op jit(solution)/shard_map/ppermute | solution.py:62
  88.4 1.6 collective-permute-start.14
  93.6 20.7 %collective-permute-done.14.refs_0_ = bf16[272,2048]{1,0:T(8,128)(2,1)S(1)} collective-permute-done((bf16[272,2048]{1,0:T(8,128)(2,1)}, bf16[272,2048]{1,0:T(8,128)(2,1)S(1)}, u32[]{:S(2)}, u32[]{:S(2)}) %collective-permute-start.14) | collective-permute-done | bytes 1114144 | tf_op jit(solution)/shard_map/ppermute | solution.py:62
  121.5 7.7 %collective-permute-done.16 = bf16[136,2048]{1,0:T(8,128)(2,1)S(1)} collective-permute-done((bf16[136,2048]{1,0:T(8,128)(2,1)S(1)}, bf16[136,2048]{1,0:T(8,128)(2,1)S(1)}, u32[]{:S(2)}, u32[]{:S(2)}) %collective-permute-start.16) | collective-permute-done | bytes 557088 | tf_op jit(solution)/shard_map/ppermute | solution.py:62
  129.3 3.0 collective-permute-done.17
  134.3 11.4 %project.1 = (f32[520,1536]{1,0:T(8,128)}, bf16[2048,512]{1,0:T(8,128)(2,1)}, f32[520,8]{1,0:T(8,128)}, bf16[8,2048]{1,0:T(8,128)(2,1)}) custom-call(s32[8]{0:T(128)} %compare_select_fusion.slots, bf16[520,2048]{1,0:T(8,128)(2,1)} %get-tuple-element.136.refs_1_.x, f32[520,1]{1,0:T(8,128)} %broadcast_in_dim.58.refs_3_.live, ...), custom_call_target="tpu_custom_call" | custom-call | flops 3271557120 | bytes 10518528 | tf_op jit(solution)/shard_map/project/pallas_call | solution.py:869
  149.1 19.9 %mixer_forward.1 = (f32[512,512]{1,0:T(8,128)S(1)}, f32[512,512]{1,0:T(8,128)S(1)}, f32[512,512]{1,0:T(8,128)S(1)}, f32[4,4,128,128]{3,2,1,0:T(8,128)S(1)}, f32[...) custom-call(f32[520,1536]{1,0:T(8,128)} %get-tuple-element.138.xq.xk, ...), custom_call_target="tpu_custom_call" | custom-call | flops 4026531840 | bytes 20488192 | tf_op jit(solution)/shard_map/mixer_forward/pallas_call | solution.py:514
  171.1 1.6 collective-permute-start.18
  173.8 10.5 %collective-permute-done.18.refs_2_ = bf16[4,2,128,128]{3,2,1,0:T(8,128)(2,1)S(1)} collective-permute-done((bf16[4,2,128,128]{3,2,1,0:T(8,128)(2,1)S(1)}, bf16[4,2,128,128]{3,2,1,0:T(8,128)(2,1)S(1)}, u32[]{:S(2)}, u32[]{:S(2)}) %collective-permute-start.18) | collective-permute-done | bytes 262176 | tf_op jit(solution)/shard_map/ppermute | solution.py:62
  185.4 1.9 collective-permute-done.19.refs_3_
  187.4 2.1 collective-permute-start.21
  190.2 3.9 collective-permute-done.20.refs_4_
  194.1 4.5 collective-permute-start.22
  199.4 2.2 collective-permute-start.23
  201.5 5.2 collective-permute-done.22.refs_6_
  209.0 2.5 collective-permute-start.25
  212.1 3.8 collective-permute-done.24
  216.0 5.2 collective-permute-done.25
  232.8 2.0 mixer_read.1
  240.6 12.9 %collective-permute-done.30.refs_3_ = bf16[512,512]{1,0:T(8,128)(2,1)S(1)} collective-permute-done((bf16[512,512]{1,0:T(8,128)(2,1)}, bf16[512,512]{1,0:T(8,128)(2,1)S(1)}, u32[]{:S(2)}, u32[]{:S(2)}) %collective-permute-start.30) | collective-permute-done | bytes 524320 | tf_op jit(solution)/shard_map/ppermute | solution.py:19
  257.0 11.8 %out.1 = (bf16[512,2048]{1,0:T(8,128)(2,1)}, bf16[64,2048]{1,0:T(8,128)(2,1)}, bf16[64,2048]{1,0:T(8,128)(2,1)}, f32[128,2048]{1,0:T(8,128)}) custom-call(s32[9]{0:T(128)} %pad_add_fusion.2.refs_0_, bf16[512,512]{1,0:T(8,128)(2,1)} %copy-done.14, bf16[512,512]{1,0:T(8,128)(2,1)} %copy-done.73, bf16[512,512]{1,0:T(8,128)(2,1)} %copy-done.72, ...), custom_call_target="tpu_custom_call" | custom-call | flops 4294967296 | bytes 16261156 | tf_op jit(solution)/shard_map/out/pallas_call | solution.py:454
  270.2 28.1 %feed_own.1 = (bf16[4096,1408]{1,0:T(8,128)(2,1)}, bf16[4096,1408]{1,0:T(8,128)(2,1)}, bf16[4096,1408]{1,0:T(8,128)(2,1)}, bf16[2,128,2048]{2,1,0:T(8,128)(2,1)}...) custom-call(s32[2]{0:T(128)} %pad_add_fusion.3.index, ...), custom_call_target="tpu_custom_call" | custom-call | flops 17716740096 | bytes 30015488 | tf_op jit(solution)/shard_map/feed_own/pallas_call | solution.py:721
  299.0 2.3 collective-permute-done.32.refs_2_
  301.4 2.9 stage.2
  305.6 19.3 %feed_hidden.2 = (bf16[4096,1408]{1,0:T(8,128)(2,1)}, f32[8,128]{1,0:T(8,128)}) custom-call(s32[4]{0:T(128)} %bitcast.144, bf16[4096,2048]{1,0:T(8,128)(2,1)} %all-gather.4.cloned.1.call-done.cot.refs_0_, bf16[1408,2048]{1,0:T(8,128)(2,1)} %wd.3, bf16[1,128,2048]{2,1,0:T(8,128)(2,1)} %get-tuple-element.159.refs_0_), custom_call_target="tpu_custom_call" | custom-call | flops 11811160064 | bytes 19922944 | tf_op jit(solution)/shard_map/feed_hidden/pallas_call | solution.py:693
  325.0 8.9 %residual.1 = (f32[128,2048]{1,0:T(8,128)}, f32[1,2048]{1,0:T(1,128)}, bf16[128,1024]{1,0:T(8,128)(2,1)}, bf16[128,1024]{1,0:T(8,128)(2,1)}, bf16[128,1024]{1,0:T(8,128)(2,1)}, /*index=5*/bf16[128,1024]{1,0:T(8,128)(2,1)}) custom-call(s32[9]{0:T(128)} %pad_add_fusion.2.refs_0_, bf16[2048,512]{1,0:T(8,128)(2,1)} %get-tuple-element.152.refs_5_.refs_1_, ...), custom_call_target="tpu_custom_call" | custom-call | flops 1073741824 | bytes 13647908 | tf_op jit(solution)/shard_map/residual/pallas_call | solution.py:454
  335.8 15.5 %feed_hidden.3 = (bf16[4096,1408]{1,0:T(8,128)(2,1)}, f32[8,128]{1,0:T(8,128)}) custom-call(s32[3]{0:T(128)} %slice.137.groups, bf16[4096,2048]{1,0:T(8,128)(2,1)} %all-gather.4.cloned.1.call-done.cot.refs_0_, bf16[1408,2048]{1,0:T(8,128)(2,1)} %wd.3, bf16[128,1024]{1,0:T(8,128)(2,1)} %get-tuple-element.162.refs_0_.refs_1_, ...), custom_call_target="tpu_custom_call", output_to_operand_aliasing={{0}: (4, {})} | custom-call | flops 8858370048 | bytes 16384000 | tf_op jit(solution)/shard_map/feed_hidden/pallas_call | solution.py:693
  352.2 6.0 mixer_leak.1
  359.6 6.1 collective-permute-done.37.refs_1_
  365.7 1.7 pad_maximum_fusion.3.refs_0_
  371.4 33.3 %feed_rows.2 = (bf16[32,2,64,1408]{3,2,1,0:T(8,128)(2,1)}, bf16[32,2,64,1408]{3,2,1,0:T(8,128)(2,1)}, bf16[32,2,64,1408]{3,2,1,0:T(8,128)(2,1)}, f32[8,128]{1,0:T(8,128)}) custom-call(s32[7]{0:T(128)} %copy-done.79, bf16[2048,2048]{1,0:T(8,128)(2,1)} %all-gather.6.cloned.1.call-done.feed.refs_0_, ...), custom_call_target="tpu_custom_call", output_to_operand_aliasing={{0}: (6, {}), {1}: (7, {}), {2}: (8, {})} | custom-call | flops 20669530112 | bytes 39059456 | tf_op jit(solution)/shard_map/feed_rows/pallas_call | solution.py:693
  404.6 1.5 collective-permute-done.39.refs_3_
  406.1 5.5 mixer_chain.1.grads
  411.7 16.6 %mixer_backward.1 = (bf16[512,512]{1,0:T(8,128)(2,1)S(1)}, bf16[512,512]{1,0:T(8,128)(2,1)S(1)}, bf16[512,512]{1,0:T(8,128)(2,1)S(1)}, f32[3,8,512]{2,1,0:T(8,12...) custom-call(f32[520,1536]{1,0:T(8,128)} %get-tuple-element.138.xq.xk.xv, ...), custom_call_target="tpu_custom_call" | custom-call | flops 2013265920 | bytes 20881408 | tf_op jit(solution)/shard_map/mixer_backward/pallas_call | solution.py:583
  430.7 1.5 collective-permute-start.41
  432.9 3.5 collective-permute-done.41.refs_13_
  437.0 12.3 %normed_back.1 = (bf16[512,1536]{1,0:T(8,128)(2,1)}, bf16[2,256,2048]{2,1,0:T(8,128)(2,1)}, bf16[2,256,2048]{2,1,0:T(8,128)(2,1)}, f32[1,2048]{1,0:T(1,128)}) custom-call(s32[9]{0:T(128)} %get-tuple-element.261.refs_0_, bf16[272,2048]{1,0:T(8,128)(2,1)} %weights.1.refs_0_.refs_8_.refs_1_, bf16[272,2048]{1,0:T(8,128)(2,1)} %gate.11.refs_1_.refs_9_.refs_2_, ...), custom_call_target="tpu_custom_call" | custom-call | flops 3221225472 | bytes 20570180 | tf_op jit(solution)/shard_map/normed_back/pallas_call | solution.py:454
  449.4 8.9 %weight_rows.1 = (bf16[256,2048]{1,0:T(8,128)(2,1)}, bf16[256,2048]{1,0:T(8,128)(2,1)}, bf16[256,2048]{1,0:T(8,128)(2,1)}, bf16[256,2048]{1,0:T(8,128)(2,1)}, bf...) custom-call(s32[9]{0:T(128)} %get-tuple-element.259.refs_0_, ...), custom_call_target="tpu_custom_call" | custom-call | flops 4294967296 | bytes 14753828 | tf_op jit(solution)/shard_map/weight_rows/pallas_call | solution.py:454
  459.7 1.6 collective-permute-start.45
  464.4 33.1 %feed_rows.3 = (bf16[32,2,64,1408]{3,2,1,0:T(8,128)(2,1)}, bf16[32,2,64,1408]{3,2,1,0:T(8,128)(2,1)}, bf16[32,2,64,1408]{3,2,1,0:T(8,128)(2,1)}, f32[8,128]{1,0:T(8,128)}) custom-call(s32[7]{0:T(128)} %copy-done.79, bf16[2048,2048]{1,0:T(8,128)(2,1)} %all-gather.8.cloned.1.call-done.feed.refs_1_, ...), custom_call_target="tpu_custom_call", output_to_operand_aliasing={{0}: (6, {}), {1}: (7, {}), {2}: (8, {})} | custom-call | flops 20669530112 | bytes 39059456 | tf_op jit(solution)/shard_map/feed_rows/pallas_call | solution.py:693
  498.5 3.3 ring_add.3
  503.9 33.9 %weight_grad.3 = (f32[2048,1408]{1,0:T(8,128)}, f32[8,128]{1,0:T(8,128)}) custom-call(bf16[2048,2048]{1,0:T(8,128)(2,1)} %all-gather.6.cloned.1.call-done.feed.refs_0_, bf16[2048,2048]{1,0:T(8,128)(2,1)} %all-gather.8.cloned.1.call-done.feed.refs_1_, bf16[32,2,64,1408]{3,2,1,0:T(8,128)(2,1)} %get-tuple-element.212.refs_2_, ...), custom_call_target="tpu_custom_call" | custom-call | flops 23622320128 | bytes 39845888 | tf_op jit(solution)/shard_map/weight_grad/pallas_call | solution.py:764
  539.1 3.8 ring_add.4
  544.9 33.8 %weight_grad.4 = (f32[2048,1408]{1,0:T(8,128)}, f32[8,128]{1,0:T(8,128)}) custom-call(bf16[2048,2048]{1,0:T(8,128)(2,1)} %all-gather.6.cloned.1.call-done.feed.refs_0_, bf16[2048,2048]{1,0:T(8,128)(2,1)} %all-gather.8.cloned.1.call-done.feed.refs_1_, bf16[32,2,64,1408]{3,2,1,0:T(8,128)(2,1)} %get-tuple-element.216.refs_2_, ...), custom_call_target="tpu_custom_call" | custom-call | flops 23622320128 | bytes 39845888 | tf_op jit(solution)/shard_map/weight_grad/pallas_call | solution.py:764
  580.0 4.3 stage.3
  586.8 3.7 ring_add.5
  592.8 34.6 %weight_grad.5 = (f32[1408,2048]{1,0:T(8,128)}, f32[8,128]{1,0:T(8,128)}) custom-call(bf16[4096,2048]{1,0:T(8,128)(2,1)} %all-gather.4.cloned.1.call-done.cot.refs_0_, bf16[32,2,64,1408]{3,2,1,0:T(8,128)(2,1)} %get-tuple-element.220.refs_1_, bf16[256,2048]{1,0:T(8,128)(2,1)} %get-tuple-element.218.refs_2_), custom_call_target="tpu_custom_call" | custom-call | flops 23622320128 | bytes 39845888 | tf_op jit(solution)/shard_map/weight_grad/pallas_call | solution.py:764
  629.7 3.0 sum.1
  638.9 4.5 finish.1
  644.8 4.2 collective-permute-done.54.refs_4_
  649.7 3.1 assemble.1
  (355 shorter events, 104.8 us)
Async XLA Ops:
  7.2 55.4 %copy-start = (f32[3,4,2048]{2,1,0:T(4,128)S(1)}, f32[3,4,2048]{2,1,0:T(4,128)}, u32[]{:S(2)}) copy-start(f32[3,4,2048]{2,1,0:T(4,128)} %param.27) | copy-start | bytes 294916
  7.2 298.4 %all-gather.4.cloned.1.call-start = ((), (), s32[]{:S(2)}) async-start(), calls=%async_computation | async-start | bytes 17301504 | tf_op jit(solution)/shard_map/all_gather | solution.py:1097
  11.3 23.8 %copy-start.76 = (s32[6]{0:T(128)S(1)}, s32[6]{0:T(128)}, u32[]{:S(2)}) copy-start(s32[6]{0:T(128)} %param.21) | copy-start | bytes 76
  11.3 10.4 %collective-permute-start = (bf16[80,2048]{1,0:T(8,128)(2,1)S(1)}, bf16[80,2048]{1,0:T(8,128)(2,1)S(1)}, u32[]{:S(2)}, u32[]{:S(2)}) collective-permute-start(bf16[80,2048]{1,0:T(8,128)(2,1)S(1)} %get-tuple-element.244), channel_id=1, source_target_pairs={{0,1},{1,0},{2,3},{3,2},{4,5},{5,4},{6,7},{7,6},{8,9},{9,8},{10,11... | collective-permute-start | bytes 983048 | tf_op jit(solution)/shard_map/ppermute | solution.py:19
  11.8 11.1 %collective-permute-start.1 = (bf16[80,2048]{1,0:T(8,128)(2,1)S(1)}, bf16[80,2048]{1,0:T(8,128)(2,1)S(1)}, u32[]{:S(2)}, u32[]{:S(2)}) collective-permute-start(bf16[80,2048]{1,0:T(8,128)(2,1)S(1)} %get-tuple-element.243), channel_id=1, source_target_pairs={{0,2},{1,3},{2,0},{3,1},{4,6},{5,7},{6,4},{7,5},{8,10},{9,11},{10,... | collective-permute-start | bytes 983048 | tf_op jit(solution)/shard_map/ppermute | solution.py:19
  14.3 15.3 %collective-permute-start.2 = (bf16[80,2048]{1,0:T(8,128)(2,1)S(1)}, bf16[80,2048]{1,0:T(8,128)(2,1)}, u32[]{:S(2)}, u32[]{:S(2)}) collective-permute-start(bf16[80,2048]{1,0:T(8,128)(2,1)S(1)} %get-tuple-element.242), channel_id=1, source_target_pairs={{0,3},{1,2},{2,1},{3,0},{4,7},{5,6},{6,5},{7,4},{8,11},{9,10},{10,... | collective-permute-start | bytes 983048 | tf_op jit(solution)/shard_map/ppermute | solution.py:19
  14.5 1.9 collective-permute-start.4
  20.0 22.6 %collective-permute-start.5 = (bf16[144,2048]{1,0:T(8,128)(2,1)S(1)}, bf16[144,2048]{1,0:T(8,128)(2,1)}, u32[]{:S(2)}, u32[]{:S(2)}) collective-permute-start(bf16[144,2048]{1,0:T(8,128)(2,1)S(1)} %pad_maximum_fusion.refs_1_), channel_id=1, source_target_pairs={{0,2},{1,3},{2,0},{3,1},{4,6},{5,7},{6,4},{7,5},{8,10},{9,11},{10,... | collective-permute-start | bytes 1769480 | tf_op jit(solution)/shard_map/ppermute | solution.py:19
  32.0 27.7 %collective-permute-start.3 = (bf16[272,2048]{1,0:T(8,128)(2,1)}, bf16[272,2048]{1,0:T(8,128)(2,1)S(1)}, u32[]{:S(2)}, u32[]{:S(2)}) collective-permute-start(bf16[272,2048]{1,0:T(8,128)(2,1)} %weights.1.refs_0_.refs_8_.refs_1_), channel_id=1, source_target_pairs={{0,8},{8,16},{16,24},{24,28},{28,20},{20,12},{12,4},{4,0},{1,9},{9... | collective-permute-start | bytes 3342344 | tf_op jit(solution)/shard_map/ppermute | solution.py:62
  34.3 19.4 %collective-permute-start.11 = (bf16[128,2048]{1,0:T(8,128)(2,1)S(1)}, bf16[128,2048]{1,0:T(8,128)(2,1)}, u32[]{:S(2)}, u32[]{:S(2)}) collective-permute-start(bf16[128,2048]{1,0:T(8,128)(2,1)S(1)} %copy-done.42), channel_id=1, source_target_pairs={{0,2},{1,3},{2,0},{3,1},{4,6},{5,7},{6,4},{7,5},{8,10},{9,11},{10,... | collective-permute-start | bytes 1572872 | tf_op jit(solution)/shard_map/ppermute | solution.py:19
  35.3 28.1 %collective-permute-start.7 = (bf16[272,2048]{1,0:T(8,128)(2,1)}, bf16[272,2048]{1,0:T(8,128)(2,1)S(1)}, u32[]{:S(2)}, u32[]{:S(2)}) collective-permute-start(bf16[272,2048]{1,0:T(8,128)(2,1)} %weights.1.refs_0_.refs_8_.refs_1_), channel_id=1, source_target_pairs={{0,4},{8,0},{16,8},{24,16},{28,24},{20,28},{12,20},{4,12},{1,5},{9... | collective-permute-start | bytes 3342344 | tf_op jit(solution)/shard_map/ppermute | solution.py:62
  42.6 11.1 %collective-permute-start.6 = (bf16[144,2048]{1,0:T(8,128)(2,1)}, bf16[144,2048]{1,0:T(8,128)(2,1)S(1)}, u32[]{:S(2)}, u32[]{:S(2)}) collective-permute-start(bf16[144,2048]{1,0:T(8,128)(2,1)} %collective-permute-done.5.refs_3_), channel_id=1, source_target_pairs={{0,1},{1,0},{2,3},{3,2},{4,5},{5,4},{6,7},{7,6},{8,9},{9,8},{10,11... | collective-permute-start | bytes 1769480 | tf_op jit(solution)/shard_map/ppermute | solution.py:19
  42.8 24.9 %collective-permute-start.9 = (bf16[144,2048]{1,0:T(8,128)(2,1)}, bf16[144,2048]{1,0:T(8,128)(2,1)}, u32[]{:S(2)}, u32[]{:S(2)}) collective-permute-start(bf16[144,2048]{1,0:T(8,128)(2,1)} %copy-done.45), channel_id=1, source_target_pairs={{0,1},{1,0},{2,3},{3,2},{4,5},{5,4},{6,7},{7,6},{8,9},{9,8},{10,11... | collective-permute-start | bytes 1769480 | tf_op jit(solution)/shard_map/ppermute | solution.py:19
  53.7 11.1 %collective-permute-start.10 = (bf16[128,2048]{1,0:T(8,128)(2,1)S(1)}, bf16[128,2048]{1,0:T(8,128)(2,1)}, u32[]{:S(2)}, u32[]{:S(2)}) collective-permute-start(bf16[128,2048]{1,0:T(8,128)(2,1)S(1)} %copy-done.42), channel_id=1, source_target_pairs={{0,1},{1,0},{2,3},{3,2},{4,5},{5,4},{6,7},{7,6},{8,9},{9,8},{10,11... | collective-permute-start | bytes 1572872 | tf_op jit(solution)/shard_map/ppermute | solution.py:19
  53.7 11.0 %collective-permute-start.12 = (bf16[128,2048]{1,0:T(8,128)(2,1)}, bf16[128,2048]{1,0:T(8,128)(2,1)}, u32[]{:S(2)}, u32[]{:S(2)}) collective-permute-start(bf16[128,2048]{1,0:T(8,128)(2,1)} %collective-permute-done.11.refs_3_), channel_id=1, source_target_pairs={{0,1},{1,0},{2,3},{3,2},{4,5},{5,4},{6,7},{7,6},{8,9},{9,8},{10,11... | collective-permute-start | bytes 1572872 | tf_op jit(solution)/shard_map/ppermute | solution.py:19
  60.7 26.7 %collective-permute-start.8 = (bf16[272,2048]{1,0:T(8,128)(2,1)}, bf16[272,2048]{1,0:T(8,128)(2,1)S(1)}, u32[]{:S(2)}, u32[]{:S(2)}) collective-permute-start(bf16[272,2048]{1,0:T(8,128)(2,1)} %gate.11.refs_1_.refs_9_.refs_2_), channel_id=1, source_target_pairs={{0,8},{8,16},{16,24},{24,28},{28,20},{20,12},{12,4},{4,0},{1,9},{9... | collective-permute-start | bytes 3342344 | tf_op jit(solution)/shard_map/ppermute | solution.py:62
  64.3 26.2 %collective-permute-start.13 = (bf16[272,2048]{1,0:T(8,128)(2,1)}, bf16[272,2048]{1,0:T(8,128)(2,1)S(1)}, u32[]{:S(2)}, u32[]{:S(2)}) collective-permute-start(bf16[272,2048]{1,0:T(8,128)(2,1)} %gate.12.refs_2_.refs_10_.refs_3_), channel_id=1, source_target_pairs={{0,4},{8,0},{16,8},{24,16},{28,24},{20,28},{12,20},{4,12},{1,5},{9... | collective-permute-start | bytes 3342344 | tf_op jit(solution)/shard_map/ppermute | solution.py:62
  88.4 25.9 %collective-permute-start.14 = (bf16[272,2048]{1,0:T(8,128)(2,1)}, bf16[272,2048]{1,0:T(8,128)(2,1)S(1)}, u32[]{:S(2)}, u32[]{:S(2)}) collective-permute-start(bf16[272,2048]{1,0:T(8,128)(2,1)} %gate.13.refs_3_.refs_11_.refs_4_), channel_id=1, source_target_pairs={{0,8},{8,16},{16,24},{24,28},{28,20},{20,12},{12,4},{4,0},{1,9},{9... | collective-permute-start | bytes 3342344 | tf_op jit(solution)/shard_map/ppermute | solution.py:62
  91.6 26.2 %collective-permute-start.15 = (bf16[272,2048]{1,0:T(8,128)(2,1)}, bf16[272,2048]{1,0:T(8,128)(2,1)S(1)}, u32[]{:S(2)}, u32[]{:S(2)}) collective-permute-start(bf16[272,2048]{1,0:T(8,128)(2,1)} %gate.14.refs_4_.refs_12_.refs_5_), channel_id=1, source_target_pairs={{0,4},{8,0},{16,8},{24,16},{28,24},{20,28},{12,20},{4,12},{1,5},{9... | collective-permute-start | bytes 3342344 | tf_op jit(solution)/shard_map/ppermute | solution.py:62
  116.4 12.8 %collective-permute-start.16 = (bf16[136,2048]{1,0:T(8,128)(2,1)S(1)}, bf16[136,2048]{1,0:T(8,128)(2,1)S(1)}, u32[]{:S(2)}, u32[]{:S(2)}) collective-permute-start(bf16[136,2048]{1,0:T(8,128)(2,1)S(1)} %slice.152), channel_id=1, source_target_pairs={{0,8},{8,16},{16,24},{24,28},{28,20},{20,12},{12,4},{4,0},{1,9},{9... | collective-permute-start | bytes 1671176 | tf_op jit(solution)/shard_map/ppermute | solution.py:62
  119.9 12.3 %collective-permute-start.17 = (bf16[136,2048]{1,0:T(8,128)(2,1)S(1)}, bf16[136,2048]{1,0:T(8,128)(2,1)S(1)}, u32[]{:S(2)}, u32[]{:S(2)}) collective-permute-start(bf16[136,2048]{1,0:T(8,128)(2,1)S(1)} %slice.153), channel_id=1, source_target_pairs={{0,4},{8,0},{16,8},{24,16},{28,24},{20,28},{12,20},{4,12},{1,5},{9... | collective-permute-start | bytes 1671176 | tf_op jit(solution)/shard_map/ppermute | solution.py:62
  133.4 238.0 %all-gather.6.cloned.1.call-start = ((), (), s32[]{:S(2)}) async-start(), calls=%async_computation.1 | async-start | bytes 8650752 | tf_op jit(solution)/shard_map/all_gather | solution.py:1118
  146.7 92.2 %collective-permute-start.27 = (bf16[2048,512]{1,0:T(8,128)(2,1)}, bf16[2048,512]{1,0:T(8,128)(2,1)}, u32[]{:S(2)}, u32[]{:S(2)}) collective-permute-start(bf16[2048,512]{1,0:T(8,128)(2,1)} %get-tuple-element.152.refs_5_.refs_1_), channel_id=1, source_target_pairs={{0,2},{1,3},{2,0},{3,1},{4,6},{5,7},{6,4},{7,5},{8,10},{9,11},{10,... | collective-permute-start | bytes 6291464 | tf_op jit(solution)/shard_map/ppermute | solution.py:19
  149.1 62.4 %copy-start.70 = (s32[8]{0:T(128)S(1)}, s32[8]{0:T(128)}, u32[]{:S(2)}) copy-start(s32[8]{0:T(128)} %compare_select_fusion.slots) | copy-start | bytes 100
  149.1 73.1 %copy-start.33 = (f32[128]{0:T(128)S(1)}, f32[128]{0:T(128)}, u32[]{:S(2)}) copy-start(f32[128]{0:T(128)} %param.28) | copy-start | bytes 1540
  171.1 13.3 %collective-permute-start.18 = (bf16[4,2,128,128]{3,2,1,0:T(8,128)(2,1)S(1)}, bf16[4,2,128,128]{3,2,1,0:T(8,128)(2,1)S(1)}, u32[]{:S(2)}, u32[]{:S(2)}) collective-permute-start(bf16[4,2,128,128]{3,2,1,0:T(8,128)(2,1)S(1)} %get-tuple-element.146.refs_1_), channel_id=1, source_target_pairs={{0,8},{8,16},{16,24},{24,28},{28,20},{20,12},{12,4},{4,0},{1,9},{9... | collective-permute-start | bytes 786440 | tf_op jit(solution)/shard_map/ppermute | solution.py:62
  172.6 14.7 %collective-permute-start.19 = (bf16[4,2,128,128]{3,2,1,0:T(8,128)(2,1)S(1)}, bf16[4,2,128,128]{3,2,1,0:T(8,128)(2,1)S(1)}, u32[]{:S(2)}, u32[]{:S(2)}) collective-permute-start(bf16[4,2,128,128]{3,2,1,0:T(8,128)(2,1)S(1)} %get-tuple-element.146.refs_1_), channel_id=1, source_target_pairs={{0,4},{8,0},{16,8},{24,16},{28,24},{20,28},{12,20},{4,12},{1,5},{9... | collective-permute-start | bytes 786440 | tf_op jit(solution)/shard_map/ppermute | solution.py:62
  184.3 9.8 %collective-permute-start.20 = (bf16[4,2,128,128]{3,2,1,0:T(8,128)(2,1)S(1)}, bf16[4,2,128,128]{3,2,1,0:T(8,128)(2,1)S(1)}, u32[]{:S(2)}, u32[]{:S(2)}) collective-permute-start(bf16[4,2,128,128]{3,2,1,0:T(8,128)(2,1)S(1)} %collective-permute-done.18.refs_2_), channel_id=1, source_target_pairs={{0,8},{8,16},{16,24},{24,28},{28,20},{20,12},{12,4},{4,0},{1,9},{9... | collective-permute-start | bytes 786440 | tf_op jit(solution)/shard_map/ppermute | solution.py:62
  187.4 12.0 %collective-permute-start.21 = (bf16[4,2,128,128]{3,2,1,0:T(8,128)(2,1)S(1)}, bf16[4,2,128,128]{3,2,1,0:T(8,128)(2,1)S(1)}, u32[]{:S(2)}, u32[]{:S(2)}) collective-permute-start(bf16[4,2,128,128]{3,2,1,0:T(8,128)(2,1)S(1)} %collective-permute-done.19.refs_3_), channel_id=1, source_target_pairs={{0,4},{8,0},{16,8},{24,16},{28,24},{20,28},{12,20},{4,12},{1,5},{9... | collective-permute-start | bytes 786440 | tf_op jit(solution)/shard_map/ppermute | solution.py:62
  194.1 12.6 %collective-permute-start.22 = (bf16[4,2,128,128]{3,2,1,0:T(8,128)(2,1)S(1)}, bf16[4,2,128,128]{3,2,1,0:T(8,128)(2,1)S(1)}, u32[]{:S(2)}, u32[]{:S(2)}) collective-permute-start(bf16[4,2,128,128]{3,2,1,0:T(8,128)(2,1)S(1)} %collective-permute-done.20.refs_4_), channel_id=1, source_target_pairs={{0,8},{8,16},{16,24},{24,28},{28,20},{20,12},{12,4},{4,0},{1,9},{9... | collective-permute-start | bytes 786440 | tf_op jit(solution)/shard_map/ppermute | solution.py:62
  199.4 8.3 %collective-permute-start.23 = (bf16[4,2,128,128]{3,2,1,0:T(8,128)(2,1)S(1)}, bf16[4,2,128,128]{3,2,1,0:T(8,128)(2,1)S(1)}, u32[]{:S(2)}, u32[]{:S(2)}) collective-permute-start(bf16[4,2,128,128]{3,2,1,0:T(8,128)(2,1)S(1)} %collective-permute-done.21.refs_5_), channel_id=1, source_target_pairs={{0,4},{8,0},{16,8},{24,16},{28,24},{20,28},{12,20},{4,12},{1,5},{9... | collective-permute-start | bytes 786440 | tf_op jit(solution)/shard_map/ppermute | solution.py:62
  207.4 8.6 %collective-permute-start.24 = (bf16[2,2,128,128]{3,2,1,0:T(8,128)(2,1)}, bf16[2,2,128,128]{3,2,1,0:T(8,128)(2,1)}, u32[]{:S(2)}, u32[]{:S(2)}) collective-permute-start(bf16[2,2,128,128]{3,2,1,0:T(8,128)(2,1)} %slice.155), channel_id=1, source_target_pairs={{0,8},{8,16},{16,24},{24,28},{28,20},{20,12},{12,4},{4,0},{1,9},{9... | collective-permute-start | bytes 393224 | tf_op jit(solution)/shard_map/ppermute | solution.py:62
  209.0 12.2 %collective-permute-start.25 = (bf16[2,2,128,128]{3,2,1,0:T(8,128)(2,1)}, bf16[2,2,128,128]{3,2,1,0:T(8,128)(2,1)}, u32[]{:S(2)}, u32[]{:S(2)}) collective-permute-start(bf16[2,2,128,128]{3,2,1,0:T(8,128)(2,1)} %slice.156), channel_id=1, source_target_pairs={{0,4},{8,0},{16,8},{24,16},{28,24},{20,28},{12,20},{4,12},{1,5},{9... | collective-permute-start | bytes 393224 | tf_op jit(solution)/shard_map/ppermute | solution.py:62
  212.1 43.3 %collective-permute-start.26 = (bf16[2048,512]{1,0:T(8,128)(2,1)}, bf16[2048,512]{1,0:T(8,128)(2,1)}, u32[]{:S(2)}, u32[]{:S(2)}) collective-permute-start(bf16[2048,512]{1,0:T(8,128)(2,1)} %get-tuple-element.152.refs_5_.refs_1_), channel_id=1, source_target_pairs={{0,1},{1,0},{2,3},{3,2},{4,5},{5,4},{6,7},{7,6},{8,9},{9,8},{10,11... | collective-permute-start | bytes 6291464 | tf_op jit(solution)/shard_map/ppermute | solution.py:19
  239.0 16.5 %collective-permute-start.28 = (bf16[2048,512]{1,0:T(8,128)(2,1)}, bf16[2048,512]{1,0:T(8,128)(2,1)S(1)}, u32[]{:S(2)}, u32[]{:S(2)}) collective-permute-start(bf16[2048,512]{1,0:T(8,128)(2,1)} %gate.17.refs_7_.refs_3_), channel_id=1, source_target_pairs={{0,1},{1,0},{2,3},{3,2},{4,5},{5,4},{6,7},{7,6},{8,9},{9,8},{10,11... | collective-permute-start | bytes 6291464 | tf_op jit(solution)/shard_map/ppermute | solution.py:19
  239.0 14.5 %collective-permute-start.30 = (bf16[512,512]{1,0:T(8,128)(2,1)}, bf16[512,512]{1,0:T(8,128)(2,1)S(1)}, u32[]{:S(2)}, u32[]{:S(2)}) collective-permute-start(bf16[512,512]{1,0:T(8,128)(2,1)} %copy-done.14), channel_id=1, source_target_pairs={{0,2},{1,3},{2,0},{3,1},{4,6},{5,7},{6,4},{7,5},{8,10},{9,11},{10,... | collective-permute-start | bytes 1572872 | tf_op jit(solution)/shard_map/ppermute | solution.py:19
  240.3 13.9 %collective-permute-start.29 = (bf16[512,512]{1,0:T(8,128)(2,1)}, bf16[512,512]{1,0:T(8,128)(2,1)S(1)}, u32[]{:S(2)}, u32[]{:S(2)}) collective-permute-start(bf16[512,512]{1,0:T(8,128)(2,1)} %copy-done.14), channel_id=1, source_target_pairs={{0,1},{1,0},{2,3},{3,2},{4,5},{5,4},{6,7},{7,6},{8,9},{9,8},{10,11... | collective-permute-start | bytes 1572872 | tf_op jit(solution)/shard_map/ppermute | solution.py:19
  253.5 1.9 collective-permute-start.31
  268.8 195.6 %all-gather.8.cloned.1.call-start = ((), (), s32[]{:S(2)}) async-start(), calls=%async_computation.2 | async-start | bytes 8650752 | tf_op jit(solution)/shard_map/all_gather | solution.py:1118
  269.5 363.1 %all-reduce.7.cloned.1.call-start = ((), (), s32[]{:S(2)}) async-start(), calls=%async_computation.3 | async-start | bytes 532480 | tf_op jit(solution)/shard_map/psum | solution.py:1256
  298.3 3.1 collective-permute-start.32
  304.3 20.7 %collective-permute-start.33 = (bf16[1,128,2048]{2,1,0:T(8,128)(2,1)}, bf16[1,128,2048]{2,1,0:T(8,128)(2,1)}, u32[]{:S(2)}, u32[]{:S(2)}) collective-permute-start(bf16[1,128,2048]{2,1,0:T(8,128)(2,1)} %get-tuple-element.159.refs_0_), channel_id=1, source_target_pairs={{0,2},{1,3},{2,0},{3,1},{4,6},{5,7},{6,4},{7,5},{8,10},{9,11},{10,... | collective-permute-start | bytes 1572872 | tf_op jit(solution)/shard_map/ppermute | solution.py:19
  333.9 17.3 %collective-permute-start.34 = (bf16[128,1024]{1,0:T(8,128)(2,1)}, bf16[128,1024]{1,0:T(8,128)(2,1)S(1)}, u32[]{:S(2)}, u32[]{:S(2)}) collective-permute-start(bf16[128,1024]{1,0:T(8,128)(2,1)} %get-tuple-element.163), channel_id=1, source_target_pairs={{0,1},{1,0},{2,3},{3,2},{4,5},{5,4},{6,7},{7,6},{8,9},{9,8},{10,11... | collective-permute-start | bytes 786440 | tf_op jit(solution)/shard_map/ppermute | solution.py:19
  333.9 17.3 %collective-permute-start.35 = (bf16[128,1024]{1,0:T(8,128)(2,1)}, bf16[128,1024]{1,0:T(8,128)(2,1)S(1)}, u32[]{:S(2)}, u32[]{:S(2)}) collective-permute-start(bf16[128,1024]{1,0:T(8,128)(2,1)} %get-tuple-element.164), channel_id=1, source_target_pairs={{0,2},{1,3},{2,0},{3,1},{4,6},{5,7},{6,4},{7,5},{8,10},{9,11},{10,... | collective-permute-start | bytes 786440 | tf_op jit(solution)/shard_map/ppermute | solution.py:19
  334.6 16.7 %collective-permute-start.36 = (bf16[128,1024]{1,0:T(8,128)(2,1)}, bf16[128,1024]{1,0:T(8,128)(2,1)S(1)}, u32[]{:S(2)}, u32[]{:S(2)}) collective-permute-start(bf16[128,1024]{1,0:T(8,128)(2,1)} %get-tuple-element.165), channel_id=1, source_target_pairs={{0,3},{1,2},{2,1},{3,0},{4,7},{5,6},{6,5},{7,4},{8,11},{9,10},{10,... | collective-permute-start | bytes 786440 | tf_op jit(solution)/shard_map/ppermute | solution.py:19
  358.2 7.6 %collective-permute-start.37 = (bf16[4,128,128]{2,1,0:T(8,128)(2,1)}, bf16[4,128,128]{2,1,0:T(8,128)(2,1)S(1)}, u32[]{:S(2)}, u32[]{:S(2)}) collective-permute-start(bf16[4,128,128]{2,1,0:T(8,128)(2,1)} %get-tuple-element.169), channel_id=1, source_target_pairs={{0,4},{4,0},{8,12},{12,8},{16,20},{20,16},{24,28},{28,24},{1,5},{5... | collective-permute-start | bytes 393224 | tf_op jit(solution)/shard_map/ppermute | solution.py:19
  365.7 38.9 %copy-start.55 = (bf16[4,128,128]{2,1,0:T(8,128)(2,1)}, bf16[4,128,128]{2,1,0:T(8,128)(2,1)S(1)}, u32[]{:S(2)}) copy-start(bf16[4,128,128]{2,1,0:T(8,128)(2,1)S(1)} %collective-permute-done.37.refs_1_) | copy-start | bytes 393220
  367.4 37.2 %collective-permute-start.38 = (bf16[2,4,128,128]{3,2,1,0:T(8,128)(2,1)}, bf16[2,4,128,128]{3,2,1,0:T(8,128)(2,1)}, u32[]{:S(2)}, u32[]{:S(2)}) collective-permute-start(bf16[2,4,128,128]{3,2,1,0:T(8,128)(2,1)} %pad_maximum_fusion.3.refs_0_), channel_id=1, source_target_pairs={{8,0},{12,4},{16,8},{20,12},{24,16},{28,20},{9,1},{13,5},{17,9},{2... | collective-permute-start | bytes 786440 | tf_op jit(solution)/shard_map/ppermute | solution.py:1183
  368.7 37.4 %collective-permute-start.39 = (bf16[2,4,128,128]{3,2,1,0:T(8,128)(2,1)}, bf16[2,4,128,128]{3,2,1,0:T(8,128)(2,1)}, u32[]{:S(2)}, u32[]{:S(2)}) collective-permute-start(bf16[2,4,128,128]{3,2,1,0:T(8,128)(2,1)} %pad_maximum_fusion.3.refs_0_), channel_id=1, source_target_pairs={{16,0},{20,4},{24,8},{28,12},{17,1},{21,5},{25,9},{29,13},{18,2},{... | collective-permute-start | bytes 786440 | tf_op jit(solution)/shard_map/ppermute | solution.py:1183
  370.0 36.1 %collective-permute-start.40 = (bf16[2,4,128,128]{3,2,1,0:T(8,128)(2,1)}, bf16[2,4,128,128]{3,2,1,0:T(8,128)(2,1)}, u32[]{:S(2)}, u32[]{:S(2)}) collective-permute-start(bf16[2,4,128,128]{3,2,1,0:T(8,128)(2,1)} %pad_maximum_fusion.3.refs_0_), channel_id=1, source_target_pairs={{24,0},{28,4},{25,1},{29,5},{26,2},{30,6},{27,3},{31,7}} | collective-permute-start | bytes 786440 | tf_op jit(solution)/shard_map/ppermute | solution.py:1183
  430.7 5.7 collective-permute-start.41
  458.3 39.2 %collective-permute-start.44 = (bf16[128,2048]{1,0:T(8,128)(2,1)}, bf16[128,2048]{1,0:T(8,128)(2,1)S(1)}, u32[]{:S(2)}, u32[]{:S(2)}) collective-permute-start(bf16[128,2048]{1,0:T(8,128)(2,1)} %get-tuple-element.196.refs_0_), channel_id=1, source_target_pairs={{0,8},{8,16},{16,24},{24,28},{28,20},{20,12},{12,4},{4,0},{1,9},{9... | collective-permute-start | bytes 1572872 | tf_op jit(solution)/shard_map/ppermute | solution.py:62
  459.7 37.9 %collective-permute-start.45 = (bf16[128,2048]{1,0:T(8,128)(2,1)}, bf16[128,2048]{1,0:T(8,128)(2,1)S(1)}, u32[]{:S(2)}, u32[]{:S(2)}) collective-permute-start(bf16[128,2048]{1,0:T(8,128)(2,1)} %get-tuple-element.209), channel_id=1, source_target_pairs={{0,4},{8,0},{16,8},{24,16},{28,24},{20,28},{12,20},{4,12},{1,5},{9... | collective-permute-start | bytes 1572872 | tf_op jit(solution)/shard_map/ppermute | solution.py:62
  463.5 115.2 %collective-permute-start.42 = (bf16[2,256,2048]{2,1,0:T(8,128)(2,1)}, bf16[2,256,2048]{2,1,0:T(8,128)(2,1)S(1)}, u32[]{:S(2)}, u32[]{:S(2)}) collective-permute-start(bf16[2,256,2048]{2,1,0:T(8,128)(2,1)} %get-tuple-element.189), channel_id=1, source_target_pairs={{0,1},{1,0},{2,3},{3,2},{4,5},{5,4},{6,7},{7,6},{8,9},{9,8},{10,11... | collective-permute-start | bytes 6291464 | tf_op jit(solution)/shard_map/ppermute | solution.py:19
  501.8 35.9 %collective-permute-start.46 = (bf16[256,2048]{1,0:T(8,128)(2,1)}, bf16[256,2048]{1,0:T(8,128)(2,1)S(1)}, u32[]{:S(2)}, u32[]{:S(2)}) collective-permute-start(bf16[256,2048]{1,0:T(8,128)(2,1)} %get-tuple-element.210.refs_3_), channel_id=1, source_target_pairs={{0,8},{8,16},{16,24},{24,28},{28,20},{20,12},{12,4},{4,0},{1,9},{9... | collective-permute-start | bytes 3145736 | tf_op jit(solution)/shard_map/ppermute | solution.py:62
  502.5 35.2 %collective-permute-start.47 = (bf16[256,2048]{1,0:T(8,128)(2,1)}, bf16[256,2048]{1,0:T(8,128)(2,1)S(1)}, u32[]{:S(2)}, u32[]{:S(2)}) collective-permute-start(bf16[256,2048]{1,0:T(8,128)(2,1)} %get-tuple-element.211), channel_id=1, source_target_pairs={{0,4},{8,0},{16,8},{24,16},{28,24},{20,28},{12,20},{4,12},{1,5},{9... | collective-permute-start | bytes 3145736 | tf_op jit(solution)/shard_map/ppermute | solution.py:62
  542.9 42.6 %collective-permute-start.48 = (bf16[256,2048]{1,0:T(8,128)(2,1)}, bf16[256,2048]{1,0:T(8,128)(2,1)S(1)}, u32[]{:S(2)}, u32[]{:S(2)}) collective-permute-start(bf16[256,2048]{1,0:T(8,128)(2,1)} %get-tuple-element.214.refs_3_), channel_id=1, source_target_pairs={{0,8},{8,16},{16,24},{24,28},{28,20},{20,12},{12,4},{4,0},{1,9},{9... | collective-permute-start | bytes 3145736 | tf_op jit(solution)/shard_map/ppermute | solution.py:62
  544.3 41.2 %collective-permute-start.49 = (bf16[256,2048]{1,0:T(8,128)(2,1)}, bf16[256,2048]{1,0:T(8,128)(2,1)S(1)}, u32[]{:S(2)}, u32[]{:S(2)}) collective-permute-start(bf16[256,2048]{1,0:T(8,128)(2,1)} %get-tuple-element.215), channel_id=1, source_target_pairs={{0,4},{8,0},{16,8},{24,16},{28,24},{20,28},{12,20},{4,12},{1,5},{9... | collective-permute-start | bytes 3145736 | tf_op jit(solution)/shard_map/ppermute | solution.py:62
  584.3 43.1 %collective-permute-start.43 = (bf16[1,256,2048]{2,1,0:T(8,128)(2,1)}, bf16[1,256,2048]{2,1,0:T(8,128)(2,1)S(1)}, u32[]{:S(2)}, u32[]{:S(2)}) collective-permute-start(bf16[1,256,2048]{2,1,0:T(8,128)(2,1)} %get-tuple-element.191), channel_id=1, source_target_pairs={{0,2},{1,3},{2,0},{3,1},{4,6},{5,7},{6,4},{7,5},{8,10},{9,11},{10,... | collective-permute-start | bytes 3145736 | tf_op jit(solution)/shard_map/ppermute | solution.py:19
  590.5 37.9 %collective-permute-start.50 = (bf16[256,2048]{1,0:T(8,128)(2,1)}, bf16[256,2048]{1,0:T(8,128)(2,1)S(1)}, u32[]{:S(2)}, u32[]{:S(2)}) collective-permute-start(bf16[256,2048]{1,0:T(8,128)(2,1)} %get-tuple-element.218.refs_2_), channel_id=1, source_target_pairs={{0,8},{8,16},{16,24},{24,28},{28,20},{20,12},{12,4},{4,0},{1,9},{9... | collective-permute-start | bytes 3145736 | tf_op jit(solution)/shard_map/ppermute | solution.py:62
  591.8 36.6 %collective-permute-start.51 = (bf16[256,2048]{1,0:T(8,128)(2,1)}, bf16[256,2048]{1,0:T(8,128)(2,1)S(1)}, u32[]{:S(2)}, u32[]{:S(2)}) collective-permute-start(bf16[256,2048]{1,0:T(8,128)(2,1)} %get-tuple-element.219), channel_id=1, source_target_pairs={{0,4},{8,0},{16,8},{24,16},{28,24},{20,28},{12,20},{4,12},{1,5},{9... | collective-permute-start | bytes 3145736 | tf_op jit(solution)/shard_map/ppermute | solution.py:62
  634.9 9.9 %collective-permute-start.52 = (bf16[64,2048]{1,0:T(8,128)(2,1)}, bf16[64,2048]{1,0:T(8,128)(2,1)S(1)}, u32[]{:S(2)}, u32[]{:S(2)}) collective-permute-start(bf16[64,2048]{1,0:T(8,128)(2,1)} %get-tuple-element.230), channel_id=1, source_target_pairs={{0,1},{1,0},{2,3},{3,2},{4,5},{5,4},{6,7},{7,6},{8,9},{9,8},{10,11... | collective-permute-start | bytes 786440 | tf_op jit(solution)/shard_map/ppermute | solution.py:19
  634.9 9.9 %collective-permute-start.53 = (bf16[64,2048]{1,0:T(8,128)(2,1)}, bf16[64,2048]{1,0:T(8,128)(2,1)S(1)}, u32[]{:S(2)}, u32[]{:S(2)}) collective-permute-start(bf16[64,2048]{1,0:T(8,128)(2,1)} %get-tuple-element.231), channel_id=1, source_target_pairs={{0,2},{1,3},{2,0},{3,1},{4,6},{5,7},{6,4},{7,5},{8,10},{9,11},{10,... | collective-permute-start | bytes 786440 | tf_op jit(solution)/shard_map/ppermute | solution.py:19
  635.7 13.3 %collective-permute-start.54 = (bf16[64,2048]{1,0:T(8,128)(2,1)}, bf16[64,2048]{1,0:T(8,128)(2,1)S(1)}, u32[]{:S(2)}, u32[]{:S(2)}) collective-permute-start(bf16[64,2048]{1,0:T(8,128)(2,1)} %get-tuple-element.232), channel_id=1, source_target_pairs={{0,3},{1,2},{2,1},{3,0},{4,7},{5,6},{6,5},{7,4},{8,11},{9,10},{10,... | collective-permute-start | bytes 786440 | tf_op jit(solution)/shard_map/ppermute | solution.py:19
  (77 other events, 302.0 us)
Sparse Core Ops, SparseCore 0:
  133.5 126.0 all-gather.3
  268.9 78.6 all-gather.5
  350.5 91.3 all-gather.7
  464.5 126.7 all-reduce.6
